TPU v7x, 256 devices: a whole 4x4x8 slice. The times are simulated.
256 devices in a mesh: gx: 32 (over z, y_lo, core), gy: 8 (over y_hi, x).
Axes of the slice: x: 4, y: 4 (y_hi: 2, y_lo: 2; y = y_hi * 2 + y_lo), z: 8, core: 2. Of those that a mesh axis runs over, the one named last changes fastest.
Arguments:
- coords: float32 [32, 8, 8, 1024], P('gx', 'gy'), may hold values from 0 to 1, as said below
- probes: float32 [32, 8, 16, 1024], P('gx', 'gy'), may hold values from -6 to 6
- precond: float32 [32, 8, 1024], P('gx', 'gy'), may hold values from 0.25 to 1
- counts: int32 [32, 8], P('gx', 'gy'), may hold values from 192 to 1024, as said below
- neighbours: int32 [32, 8, 8, 8], P('gx', 'gy'), may hold values from 0 to 72, as said below
- inducing: int32 [32, 8, 16], P('gx', 'gy'), may hold values from 0 to 1023, as said below
- factor: float32 [4096, 4096], P('gy'), may hold values from -0.00390625 to 0.00390625
Outputs:
- solution: float32 [32, 8, 16, 1024], P('gx', 'gy')
- residual: float32 [32, 8, 16, 1024], P('gx', 'gy')
Inputs may be any that keep to these rules, and one draw needn't show every extreme that they name: `counts`: slots at or past a cell's count are padding; some cell holds exactly 1024 points in every draw. `neighbours`: the listing is symmetric and lists each block itself; the distinct blocks of one cell listed by all blocks of the cell beside it along one grid axis number at most 4, by a diagonal neighbour cell at most 2, and both bounds are reached; no entry leaves the grid. `inducing`: distinct slots below the cell's count. `coords`: the first two inputs place each point inside its cell's box, (cx + a) / 32 and (cy + b) / 8 with a, b in [0, 1).
All inputs are finite; a program needn't handle non-finite values.
Results may differ from a plain program's by a relative error of at most 0.0048.
The roundings to bfloat16 on the way count: a program that leaves them out, or rounds other values in their place, can miss the bound.
Values may be sent and summed in bfloat16 or wider, within the bound.
No kernel may reach another device: no remote copies, remote signals or barrier semaphores. Data moves between devices by JAX's collectives and lax.ppermute only.
A program may use at most 64 MiB of HBM per device.

v0:
```python
import jax
import jax.numpy as jnp
from jax import lax
from jax.sharding import PartitionSpec as P

FEAT = 8
BLOCK = 128
ITERS = 2


noise_level = 1.0
sparse_amp = 1.0
support_radius = 0.32
width_sq = 0.045
group_blocks = 4


def padded(block, sides, width):
    for axis, dim in sides:
        count = lax.axis_size(axis)
        forward = [(i, i + 1) for i in range(count - 1)]
        backward = [(target, source) for source, target in forward]
        low = lax.ppermute(
            lax.slice_in_dim(block, block.shape[dim] - width, None, axis=dim), axis, forward
        )
        high = lax.ppermute(lax.slice_in_dim(block, 0, width, axis=dim), axis, backward)
        block = jnp.concatenate([low, block, high], axis=dim)
    return block


def wendland(dist_sq):
    ratio = jnp.sqrt(dist_sq) / support_radius
    remain = jnp.maximum(1.0 - ratio, 0.0)
    square = remain * remain
    return sparse_amp * square * square * square * remain * (7.0 * ratio + 1.0)


def inducing_rows(points, centres):
    total = jnp.zeros((points.shape[1], centres.shape[1]), jnp.float32)
    for feature in range(points.shape[0]):
        spacing = points[feature][:, None] - centres[feature][None, :]
        total = total + spacing * spacing
    return jnp.exp(-total / width_sq).astype(jnp.bfloat16)


def block_table(region):
    feats = region.shape[2]
    slots = region.shape[3] // BLOCK
    table = (
        region.reshape(9, feats, slots, BLOCK)
        .transpose(0, 2, 1, 3)
        .reshape(9 * slots, feats, BLOCK)
    )
    return jnp.concatenate([table, jnp.zeros((1, feats, BLOCK), region.dtype)], axis=0)


def kernel_tiles(own_points, partner_points):
    total = jnp.zeros((own_points.shape[0], BLOCK, partner_points.shape[1], BLOCK), jnp.float32)
    for feature in range(own_points.shape[1]):
        spacing = own_points[:, feature, :, None, None] - partner_points[:, None, :, feature, :]
        total = total + spacing * spacing
    return wendland(total).astype(jnp.bfloat16)


def on_device(coords, probes, precond, counts, neighbours, inducing, factor):
    slots = coords.shape[3]
    blocks_cell = slots // BLOCK
    groups = blocks_cell // group_blocks
    probe_count = probes.shape[2]
    share_rows = factor.shape[0]
    live_count = counts[0, 0]
    live = (jnp.arange(slots, dtype=jnp.int32) < live_count).astype(jnp.float32)[None, :]
    own_points = coords[0, 0]
    entry_codes = neighbours[0, 0]
    near_points = padded(coords, (("gx", 0), ("gy", 1)), 1)
    point_table = block_table(near_points)
    own_blocks = own_points.reshape(FEAT, blocks_cell, BLOCK).transpose(1, 0, 2)

    def tile_group(index):
        start = index * group_blocks
        own = lax.dynamic_slice_in_dim(own_blocks, start, group_blocks, 0)
        picks = lax.dynamic_slice_in_dim(entry_codes, start, group_blocks, 0)
        return kernel_tiles(own, point_table[picks])

    stored_tiles = lax.map(tile_group, jnp.arange(groups, dtype=jnp.int32))
    centre_local = jnp.take(own_points, inducing[0, 0], axis=1)
    centres = lax.all_gather(centre_local, ("gx", "gy"), axis=1, tiled=True)
    grouped = own_points.reshape(FEAT, blocks_cell // group_blocks, group_blocks * BLOCK).transpose(
        1, 0, 2
    )
    kernel_rows = lax.map(lambda portion: inducing_rows(portion, centres), grouped).reshape(
        slots, centres.shape[1]
    )

    def residual_norm(left, right):
        return lax.psum(jnp.sum(left * right, axis=1), ("gx", "gy"))

    scaling = precond[0, 0][None, :]
    residual = probes[0, 0] * live
    solution = jnp.zeros_like(residual)
    search = scaling * residual
    rz_now = residual_norm(residual, search)
    for step_index in range(ITERS):
        operate_packed = search.astype(jnp.bfloat16)
        near_values = padded(operate_packed[None, None], (("gx", 0), ("gy", 1)), 1)
        operate_value_table = block_table(near_values)
        value_table = operate_value_table

        def one_group(index, result):
            start = index * group_blocks
            picks = lax.dynamic_slice_in_dim(entry_codes, start, group_blocks, 0)
            tiles = lax.dynamic_index_in_dim(stored_tiles, index, 0, keepdims=False)
            partial_out = jnp.einsum(
                "giej,gecj->gci", tiles, value_table[picks], preferred_element_type=jnp.float32
            )
            return lax.dynamic_update_slice_in_dim(result, partial_out, start, 0)

        result = lax.fori_loop(
            0, groups, one_group, jnp.zeros((blocks_cell, probe_count, BLOCK), jnp.float32)
        )
        sparse = result.transpose(1, 0, 2).reshape(probe_count, slots)
        terms = jnp.dot(operate_packed, kernel_rows, preferred_element_type=jnp.float32)
        total = lax.psum(terms, ("gx", "gy"))
        row_share = lax.dynamic_slice_in_dim(
            total, lax.axis_index("gy") * share_rows, share_rows, 1
        )
        coeff_terms = jnp.dot(
            row_share, factor, precision=lax.Precision.HIGHEST, preferred_element_type=jnp.float32
        )
        coeffs = lax.psum(coeff_terms, "gy")
        weights = lax.dot_general(
            coeffs,
            factor,
            (((1,), (1,)), ((), ())),
            precision=lax.Precision.HIGHEST,
            preferred_element_type=jnp.float32,
        ).astype(jnp.bfloat16)
        low = lax.dot_general(
            lax.all_gather(weights, "gy", axis=1, tiled=True),
            kernel_rows,
            (((1,), (1,)), ((), ())),
            preferred_element_type=jnp.float32,
        )
        image = live * (noise_level * search + sparse + low)
        curve = lax.psum(jnp.sum(search * image, axis=1), ("gx", "gy"))
        alpha = (rz_now / curve)[:, None]
        solution = solution + alpha * search
        residual = residual - alpha * image
        if step_index + 1 < ITERS:
            precon = scaling * residual
            rz_next = residual_norm(residual, precon)
            search = precon + (rz_next / rz_now)[:, None] * search
            rz_now = rz_next
    return (solution[None, None], residual[None, None])


def solution(mesh):
    placed = (
        P("gx", "gy", None, None),
        P("gx", "gy", None, None),
        P("gx", "gy", None),
        P("gx", "gy"),
        P("gx", "gy", None, None),
        P("gx", "gy", None),
        P("gy", None),
    )
    return jax.shard_map(
        on_device,
        mesh=mesh,
        in_specs=placed,
        out_specs=(P("gx", "gy", None, None), P("gx", "gy", None, None)),
        check_vma=False,
    )
```

profile of v0, /device:TPU:1, one launch (start us, length us, event | category | flops | bytes accessed | tf_op | source)
XLA Modules:
  0.0 1711.0 jit_solution(9221189245831148234)
XLA Ops:
  7.9 0.9 multiply_convert_fusion
  8.7 5.1 collective-permute-start.1
  13.9 1.9 collective-permute-start
  15.8 1.9 collective-permute-start.4
  17.7 2.4 collective-permute-start.5
  20.2 1.0 copy.53
  21.1 0.7 fusion.36
  21.8 0.7 compare_and_fusion
  22.5 0.6 gather_fusion.3
  23.2 618.3 %all-gather = f32[256,16,8]{1,2,0:T(8,128)S(1)} all-gather(f32[1,16,8]{1,2,0:T(8,128)S(1)} %bitcast.305), channel_id=1, replica_groups=mesh['gx'=32,'gy'=8] {'gx','gy'}, dimensions={0}, use_global_device_ids=true | all-gather | bytes 131584 | tf_op jit(solution)/shard_map/all_gather | solution.py:87
  641.4 0.2 copy.55
  641.6 0.6 reshape.791
  642.3 21.0 %while.50 = (s32[]{:T(128)}, bf16[2,512,4096]{2,1,0:T(8,128)(2,1)}, f32[2,8,512]{2,1,0:T(8,128)}, f32[8,4096]{1,0:T(8,128)S(1)}, s32[]{:T(128)}, /*index=5*/s32[...) while((s32[]{:T(128)}, bf16[2,512,4096]{2,1,0:T(8,128)(2,1)}, f32[2,8,512]{2,1,0:T(8,128)}, ...), condition=%wide.region_7.8_spmd, body=%wide.region_6.7_spmd.sunk | while | flops 54525960 | bytes 4636925 | solution.py:91
  642.4 1.0 constant_dynamic-slice_fusion.18
  643.4 9.3 fusion.75
  652.8 1.0 constant_dynamic-slice_fusion.18
  653.9 9.4 fusion.75
  663.3 5.3 fusion.27
  668.7 1.3 collective-permute-start.3
  670.0 4.0 collective-permute-start.2
  674.1 1.3 collective-permute-start.7
  675.4 4.0 collective-permute-start.6
  679.4 248.2 %all-reduce.9.cloned.1.call-done = f32[16,4096]{1,0:T(8,128)} async-done(((f32[16,4096]{1,0:T(8,128)}), f32[16,4096]{1,0:T(8,128)}) %all-reduce.9.cloned.1.call-update) | async-done | bytes 262160 | tf_op jit(solution)/shard_map/psum | solution.py:123
  927.6 8.2 fusion.31
  935.8 0.5 all-reduce.13.cloned.1.call-start
  936.6 15.2 while.48
  936.6 0.6 dynamic_slice.84
  937.9 0.6 gather_fusion
  938.6 5.2 fusion.70
  943.8 0.4 copy_dynamic-update-slice_fusion.2
  944.2 0.6 dynamic_slice.84
  945.5 0.6 gather_fusion
  946.2 5.2 fusion.70
  951.5 0.4 copy_dynamic-update-slice_fusion.2
  951.9 2.2 while.49
  952.0 0.6 gather_fusion.1
  952.6 0.4 fusion.73
  953.1 0.6 gather_fusion.1
  953.7 0.4 fusion.73
  954.1 66.2 %all-reduce.11.cloned.1.call-done = f32[16,4096]{1,0:T(8,128)} async-done(((f32[16,4096]{1,0:T(8,128)}), f32[16,4096]{1,0:T(8,128)}) %all-reduce.11.cloned.1.call-update) | async-done | bytes 262160 | tf_op jit(solution)/shard_map/psum | solution.py:130
  1020.3 10.3 convolution_convert_fusion.1
  1030.6 27.8 %all_gather.10 = bf16[16,4096]{1,0:T(8,128)(2,1)S(1)} all-gather(bf16[16,512]{1,0:T(8,128)(2,1)S(1)} %convolution_convert_fusion.1), channel_id=1, replica_groups=mesh['gx'=32,'gy'=8] {'gy'}, dimensions={1}, use_global_device_ids=true | all-gather | bytes 147456 | tf_op jit(solution)/shard_map/all_gather | solution.py:139
  1058.4 5.8 fusion.23
  1064.2 85.8 %all-reduce.3 = (f32[16]{0:T(128)S(1)}, f32[16]{0:T(128)S(1)}) all-reduce(f32[16]{0:T(128)S(1)} %get-tuple-element.324, f32[16]{0:T(128)S(1)} %get-tuple-element.323), channel_id=1, replica_groups=mesh['gx'=32,'gy'=8] {'gx','gy'}, use_global_device_ids=true, to_apply=%region_1.2 | all-reduce | flops 32 | bytes 256 | tf_op jit(solution)/shard_map/psum | solution.py:96
  1150.0 0.2 fusion.26
  1150.2 74.1 %psum.60 = f32[16]{0:T(128)S(1)} all-reduce(f32[16]{0:T(128)S(1)} %fusion.26), channel_id=1, replica_groups=mesh['gx'=32,'gy'=8] {'gx','gy'}, use_global_device_ids=true, to_apply=%region_13.14 | all-reduce | flops 16 | bytes 128 | tf_op jit(solution)/shard_map/psum | solution.py:96
  1224.4 2.6 collective-permute-start.9
  1227.0 3.2 collective-permute-start.8
  1230.1 5.3 fusion.33
  1235.6 1.3 collective-permute-start.11
  1236.9 4.0 collective-permute-start.10
  1240.9 240.2 %all-reduce.13.cloned.1.call-done = f32[16,4096]{1,0:T(8,128)} async-done(((f32[16,4096]{1,0:T(8,128)}), f32[16,4096]{1,0:T(8,128)}) %all-reduce.13.cloned.1.call-update) | async-done | bytes 262160 | tf_op jit(solution)/shard_map/psum | solution.py:123
  1481.1 8.1 fusion.29
  1489.5 2.2 while.51
  1489.6 0.6 gather_fusion.2
  1490.2 0.4 fusion.78
  1490.7 0.6 gather_fusion.2
  1491.3 0.4 fusion.78
  1491.7 81.9 %all-reduce.15.cloned.1.call-done = f32[16,4096]{1,0:T(8,128)} async-done(((f32[16,4096]{1,0:T(8,128)}), f32[16,4096]{1,0:T(8,128)}) %all-reduce.15.cloned.1.call-update) | async-done | bytes 262160 | tf_op jit(solution)/shard_map/psum | solution.py:130
  1573.5 10.3 convolution_convert_fusion
  1583.8 28.0 %all_gather.11 = bf16[16,4096]{1,0:T(8,128)(2,1)S(1)} all-gather(bf16[16,512]{1,0:T(8,128)(2,1)S(1)} %convolution_convert_fusion), channel_id=1, replica_groups=mesh['gx'=32,'gy'=8] {'gy'}, dimensions={1}, use_global_device_ids=true | all-gather | bytes 147456 | tf_op jit(solution)/shard_map/all_gather | solution.py:139
  1611.9 5.8 multiply_reduce_fusion
  1617.6 85.8 %psum.63 = f32[16]{0:T(128)S(1)} all-reduce(f32[16]{0:T(128)S(1)} %get-tuple-element.404), channel_id=1, replica_groups=mesh['gx'=32,'gy'=8] {'gx','gy'}, use_global_device_ids=true, to_apply=%region_19.20 | all-reduce | flops 16 | bytes 128 | tf_op jit(solution)/shard_map/psum | solution.py:145
  1703.5 0.7 subtract_bitcast_fusion
  (81 shorter events, 2.0 us)
Async XLA Ops:
  7.2 920.5 %all-reduce.9.cloned.1.call-start = ((), (), s32[]{:S(2)}) async-start(), calls=%async_computation | async-start | bytes 524288 | tf_op jit(solution)/shard_map/psum | solution.py:123
  8.7 660.0 %collective-permute-start.1 = (bf16[1,1,16,1024]{3,2,1,0:T(8,128)(2,1)S(1)}, bf16[1,1,16,1024]{3,2,1,0:T(8,128)(2,1)S(1)}, u32[]{:S(2)}, u32[]{:S(2)}) collective-permute-start(bf16[1,1,16,1024]{3,2,1,0:T(8,128)(2,1)S(1)} %multiply_convert_fusion), channel_id=1, source_target_pairs={{8,0},{16,8},{24,16},{32,24},{40,32},{48,40},{56,48},{64,56},{72,6... | collective-permute-start | bytes 98312 | tf_op jit(solution)/shard_map/ppermute | solution.py:26
  13.9 654.8 %collective-permute-start = (bf16[1,1,16,1024]{3,2,1,0:T(8,128)(2,1)S(1)}, bf16[1,1,16,1024]{3,2,1,0:T(8,128)(2,1)S(1)}, u32[]{:S(2)}, u32[]{:S(2)}) collective-permute-start(bf16[1,1,16,1024]{3,2,1,0:T(8,128)(2,1)S(1)} %multiply_convert_fusion), channel_id=1, source_target_pairs={{0,8},{8,16},{16,24},{24,32},{32,40},{40,48},{48,56},{56,64},{64,7... | collective-permute-start | bytes 98312 | tf_op jit(solution)/shard_map/ppermute | solution.py:23
  15.8 658.2 %collective-permute-start.4 = (f32[1,1,8,1024]{3,2,1,0:T(8,128)}, f32[1,1,8,1024]{3,2,1,0:T(8,128)S(1)}, u32[]{:S(2)}, u32[]{:S(2)}) collective-permute-start(f32[1,1,8,1024]{3,2,1,0:T(8,128)} %param.15), channel_id=1, source_target_pairs={{0,8},{8,16},{16,24},{24,32},{32,40},{40,48},{48,56},{56,64},{64,7... | collective-permute-start | bytes 98312 | tf_op jit(solution)/shard_map/ppermute | solution.py:23
  17.7 656.3 %collective-permute-start.5 = (f32[1,1,8,1024]{3,2,1,0:T(8,128)}, f32[1,1,8,1024]{3,2,1,0:T(8,128)S(1)}, u32[]{:S(2)}, u32[]{:S(2)}) collective-permute-start(f32[1,1,8,1024]{3,2,1,0:T(8,128)} %param.15), channel_id=1, source_target_pairs={{8,0},{16,8},{24,16},{32,24},{40,32},{48,40},{56,48},{64,56},{72,6... | collective-permute-start | bytes 98312 | tf_op jit(solution)/shard_map/ppermute | solution.py:26
  663.3 5.4 copy-start.1
  668.6 268.0 %copy-start.2 = (s32[1,1,8,8]{3,2,1,0:T(8,128)S(1)}, s32[1,1,8,8]{3,2,1,0:T(8,128)}, u32[]{:S(2)}) copy-start(s32[1,1,8,8]{3,2,1,0:T(8,128)} %param.19) | copy-start | bytes 772
  668.6 351.7 %all-reduce.11.cloned.1.call-start = ((), (), s32[]{:S(2)}) async-start(), calls=%async_computation.1 | async-start | bytes 524288 | tf_op jit(solution)/shard_map/psum | solution.py:130
  668.7 267.6 %collective-permute-start.3 = (bf16[3,1,16,1024]{3,2,1,0:T(8,128)(2,1)S(1)}, bf16[3,1,16,1024]{3,2,1,0:T(8,128)(2,1)S(1)}, u32[]{:S(2)}, u32[]{:S(2)}) collective-permute-start(bf16[3,1,16,1024]{3,2,1,0:T(8,128)(2,1)S(1)} %pad_maximum_fusion.3), channel_id=1, source_target_pairs={{1,0},{2,1},{3,2},{4,3},{5,4},{6,5},{7,6},{9,8},{10,9},{11,10},{12... | collective-permute-start | bytes 294920 | tf_op jit(solution)/shard_map/ppermute | solution.py:26
  670.0 266.3 %collective-permute-start.2 = (bf16[3,1,16,1024]{3,2,1,0:T(8,128)(2,1)S(1)}, bf16[3,1,16,1024]{3,2,1,0:T(8,128)(2,1)S(1)}, u32[]{:S(2)}, u32[]{:S(2)}) collective-permute-start(bf16[3,1,16,1024]{3,2,1,0:T(8,128)(2,1)S(1)} %pad_maximum_fusion.3), channel_id=1, source_target_pairs={{0,1},{1,2},{2,3},{3,4},{4,5},{5,6},{6,7},{8,9},{9,10},{10,11},{11... | collective-permute-start | bytes 294920 | tf_op jit(solution)/shard_map/ppermute | solution.py:23
  674.1 262.4 %collective-permute-start.7 = (f32[3,1,8,1024]{3,2,1,0:T(8,128)S(1)}, f32[3,1,8,1024]{3,2,1,0:T(8,128)S(1)}, u32[]{:S(2)}, u32[]{:S(2)}) collective-permute-start(f32[3,1,8,1024]{3,2,1,0:T(8,128)S(1)} %constant_dynamic-update-slice_fusion), channel_id=1, source_target_pairs={{1,0},{2,1},{3,2},{4,3},{5,4},{6,5},{7,6},{9,8},{10,9},{11,10},{12... | collective-permute-start | bytes 294920 | tf_op jit(solution)/shard_map/ppermute | solution.py:26
  675.4 261.1 %collective-permute-start.6 = (f32[3,1,8,1024]{3,2,1,0:T(8,128)S(1)}, f32[3,1,8,1024]{3,2,1,0:T(8,128)S(1)}, u32[]{:S(2)}, u32[]{:S(2)}) collective-permute-start(f32[3,1,8,1024]{3,2,1,0:T(8,128)S(1)} %constant_dynamic-update-slice_fusion), channel_id=1, source_target_pairs={{0,1},{1,2},{2,3},{3,4},{4,5},{5,6},{6,7},{8,9},{9,10},{10,11},{11... | collective-permute-start | bytes 294920 | tf_op jit(solution)/shard_map/ppermute | solution.py:23
  935.8 545.2 %all-reduce.13.cloned.1.call-start = ((), (), s32[]{:S(2)}) async-start(), calls=%async_computation.2 | async-start | bytes 524288 | tf_op jit(solution)/shard_map/psum | solution.py:123
  951.9 106.5 %copy-start = (f32[1,1,16,1024]{3,2,1,0:T(8,128)S(1)}, f32[1,1,16,1024]{3,2,1,0:T(8,128)}, u32[]{:S(2)}) copy-start(f32[1,1,16,1024]{3,2,1,0:T(8,128)} %param.16) | copy-start | bytes 196612
  951.9 106.5 %copy-start.3 = (f32[1,1,1024]{2,1,0:T(1,128)S(1)}, f32[1,1,1024]{2,1,0:T(1,128)}, u32[]{:S(2)}) copy-start(f32[1,1,1024]{2,1,0:T(1,128)} %param.17) | copy-start | bytes 12292
  1224.4 11.1 collective-permute-start.9
  1227.0 8.5 collective-permute-start.8
  1235.5 338.1 %all-reduce.15.cloned.1.call-start = ((), (), s32[]{:S(2)}) async-start(), calls=%async_computation.3 | async-start | bytes 524288 | tf_op jit(solution)/shard_map/psum | solution.py:130
  1235.6 253.7 %collective-permute-start.11 = (bf16[3,1,16,1024]{3,2,1,0:T(8,128)(2,1)S(1)}, bf16[3,1,16,1024]{3,2,1,0:T(8,128)(2,1)S(1)}, u32[]{:S(2)}, u32[]{:S(2)}) collective-permute-start(bf16[3,1,16,1024]{3,2,1,0:T(8,128)(2,1)S(1)} %pad_maximum_fusion.4), channel_id=1, source_target_pairs={{1,0},{2,1},{3,2},{4,3},{5,4},{6,5},{7,6},{9,8},{10,9},{11,10},{12... | collective-permute-start | bytes 294920 | tf_op jit(solution)/shard_map/ppermute | solution.py:26
  1236.9 252.4 %collective-permute-start.10 = (bf16[3,1,16,1024]{3,2,1,0:T(8,128)(2,1)S(1)}, bf16[3,1,16,1024]{3,2,1,0:T(8,128)(2,1)S(1)}, u32[]{:S(2)}, u32[]{:S(2)}) collective-permute-start(bf16[3,1,16,1024]{3,2,1,0:T(8,128)(2,1)S(1)} %pad_maximum_fusion.4), channel_id=1, source_target_pairs={{0,1},{1,2},{2,3},{3,4},{4,5},{5,6},{6,7},{8,9},{9,10},{10,11},{11... | collective-permute-start | bytes 294920 | tf_op jit(solution)/shard_map/ppermute | solution.py:23
Sparse Core Ops, SparseCore 0:
  668.7 258.8 all-reduce.8
  935.9 84.2 all-reduce.10
  1235.6 245.4 all-reduce.12
  1489.3 84.1 all-reduce.14
where the time goes:
time: 1720 us; the launch traced here: 1710 us
  blocking collectives  920 us (53%)
  waiting for transfers between devices  637 us (37%)
  matrix products  60.6 us (4%)
  starting transfers between devices  33.6 us (2%)
  other arithmetic  32.7 us (2%)
    all_gather x1, blocking collectives, on_device(): centres = lax.all_gather(centre_local, ('gx', 'gy'), axis=1, tiled=True)  618 us
    psum x2, waiting for transfers between devices, on_device(): total = lax.psum(terms, ('gx', 'gy'))  488 us
    psum x2, blocking collectives, residual_norm(): return lax.psum(jnp.sum(left * right, axis=1), ('gx', 'gy'))  160 us
    psum x2, waiting for transfers between devices, on_device(): coeffs = lax.psum(coeff_terms, 'gy')  148 us
    psum x1, blocking collectives, on_device(): curve = lax.psum(jnp.sum(search * image, axis=1), ('gx', 'gy'))  85.8 us
    all_gather x2, blocking collectives, on_device(): lax.all_gather(weights, 'gy', axis=1, tiled=True)  55.9 us
  transfers between devices with their start and end apart: 16, of which 4 were waited for; matrix products, arithmetic and copies ran while one was open for 4% of the time, Pallas kernels for 0%

commit v1 on v0

v1 whole, which is shorter than its diff:
```python
import jax
import jax.numpy as jnp
from jax import lax
from jax.sharding import Mesh, PartitionSpec as P

FEAT = 8
BLOCK = 128
ITERS = 2
PROBES = 16
SHARE = 128

noise_level = 1.0
sparse_amp = 1.0
support_radius = 0.32
width_sq = 0.045
group_blocks = 4

ALL = ("z", "yl", "c", "yh", "x")
PLANE = ("yh", "x", "yl", "c")
CELLS = ("yl", "c", "yh", "x")
GX = ("z", "yl", "c")
GY = ("yh", "x")


def padded(block, sides, width):
    for axis, dim in sides:
        count = lax.axis_size(axis)
        forward = [(i, i + 1) for i in range(count - 1)]
        backward = [(target, source) for source, target in forward]
        low = lax.ppermute(
            lax.slice_in_dim(block, block.shape[dim] - width, None, axis=dim), axis, forward
        )
        high = lax.ppermute(lax.slice_in_dim(block, 0, width, axis=dim), axis, backward)
        block = jnp.concatenate([low, block, high], axis=dim)
    return block


def wendland(dist_sq):
    ratio = jnp.sqrt(dist_sq) / support_radius
    remain = jnp.maximum(1.0 - ratio, 0.0)
    square = remain * remain
    return sparse_amp * square * square * square * remain * (7.0 * ratio + 1.0)


def inducing_rows(points, centres):
    total = jnp.zeros((points.shape[1], centres.shape[1]), jnp.float32)
    for feature in range(points.shape[0]):
        spacing = points[feature][:, None] - centres[feature][None, :]
        total = total + spacing * spacing
    return jnp.exp(-total / width_sq).astype(jnp.bfloat16)


def block_table(region):
    feats = region.shape[2]
    slots = region.shape[3] // BLOCK
    table = (
        region.reshape(9, feats, slots, BLOCK)
        .transpose(0, 2, 1, 3)
        .reshape(9 * slots, feats, BLOCK)
    )
    return jnp.concatenate([table, jnp.zeros((1, feats, BLOCK), region.dtype)], axis=0)


def kernel_tiles(own_points, partner_points):
    total = jnp.zeros((own_points.shape[0], BLOCK, partner_points.shape[1], BLOCK), jnp.float32)
    for feature in range(own_points.shape[1]):
        spacing = own_points[:, feature, :, None, None] - partner_points[:, None, :, feature, :]
        total = total + spacing * spacing
    return wendland(total).astype(jnp.bfloat16)


def exchange(parts, axes):
    return lax.all_to_all(parts, axes, 0, 0, tiled=True)


def spread(value, axes):
    count = lax.axis_size(axes)
    return exchange(jnp.broadcast_to(value[None], (count,) + value.shape), axes)


def total_scalars(row):
    row = jnp.sum(spread(row, CELLS), axis=0)
    return jnp.sum(spread(row, "z"), axis=0)


def quad_partner(value, step):
    pairs = [(i, i ^ step) for i in range(4)]
    return lax.ppermute(value, ("yl", "c"), pairs)


def on_device(coords, probes, precond, counts, neighbours, inducing, factor):
    slots = coords.shape[3]
    blocks_cell = slots // BLOCK
    groups = blocks_cell // group_blocks
    quad = lax.axis_index("yl") * 2 + lax.axis_index("c")
    live_count = counts[0, 0]
    live = (jnp.arange(slots, dtype=jnp.int32) < live_count).astype(jnp.float32)[None, :]
    own_points = coords[0, 0]
    entry_codes = neighbours[0, 0]
    scaling = precond[0, 0][None, :]
    residual = probes[0, 0] * live
    solution = jnp.zeros_like(residual)
    search = scaling * residual

    centre_local = jnp.take(own_points, inducing[0, 0], axis=1)
    plane_centres = spread(centre_local.reshape(1, 128), CELLS).reshape(32, 128)
    centres = spread(plane_centres, "z").reshape(256, FEAT, 16)
    centres = centres.transpose(1, 0, 2).reshape(FEAT, 4096)

    columns = factor.shape[1] // 4
    factor_cols = lax.dynamic_slice_in_dim(factor, quad * columns, columns, 1)
    factor_part = jnp.concatenate(
        [
            lax.dynamic_slice_in_dim(factor_cols, (quad ^ step) * SHARE, SHARE, 0)
            for step in range(4)
        ],
        axis=0,
    )

    near_points = padded(coords, ((GX, 0), (GY, 1)), 1)
    point_table = block_table(near_points)
    own_blocks = own_points.reshape(FEAT, blocks_cell, BLOCK).transpose(1, 0, 2)

    def tile_group(index):
        start = index * group_blocks
        own = lax.dynamic_slice_in_dim(own_blocks, start, group_blocks, 0)
        picks = lax.dynamic_slice_in_dim(entry_codes, start, group_blocks, 0)
        return kernel_tiles(own, point_table[picks])

    stored_tiles = lax.map(tile_group, jnp.arange(groups, dtype=jnp.int32))
    grouped = own_points.reshape(FEAT, blocks_cell // group_blocks, group_blocks * BLOCK).transpose(
        1, 0, 2
    )
    kernel_rows = lax.map(lambda portion: inducing_rows(portion, centres), grouped).reshape(
        slots, centres.shape[1]
    )

    def inner(left, right):
        return jnp.sum(left * right, axis=1)

    def pack(*sums):
        row = jnp.concatenate(sums)
        return jnp.pad(row, (0, 128 - row.shape[0]))[None, :]

    rz_part = inner(residual, search)
    for step_index in range(ITERS):
        packed = search.astype(jnp.bfloat16)
        near_values = padded(packed[None, None], ((GX, 0), (GY, 1)), 1)
        value_table = block_table(near_values)

        def one_group(index, result):
            start = index * group_blocks
            picks = lax.dynamic_slice_in_dim(entry_codes, start, group_blocks, 0)
            tiles = lax.dynamic_index_in_dim(stored_tiles, index, 0, keepdims=False)
            partial_out = jnp.einsum(
                "giej,gecj->gci", tiles, value_table[picks], preferred_element_type=jnp.float32
            )
            return lax.dynamic_update_slice_in_dim(result, partial_out, start, 0)

        result = lax.fori_loop(
            0, groups, one_group, jnp.zeros((blocks_cell, PROBES, BLOCK), jnp.float32)
        )
        sparse = result.transpose(1, 0, 2).reshape(PROBES, slots)

        terms = jnp.dot(packed, kernel_rows, preferred_element_type=jnp.float32)
        parts = terms.reshape(PROBES, 32, SHARE).transpose(1, 0, 2)
        share = jnp.sum(exchange(parts, PLANE), axis=0)
        share = jnp.sum(spread(share, "z"), axis=0)
        quad_shares = jnp.concatenate(
            [share] + [quad_partner(share, step) for step in (1, 2, 3)], axis=1
        )
        coeff_terms = jnp.dot(
            quad_shares,
            factor_part,
            precision=lax.Precision.HIGHEST,
            preferred_element_type=jnp.float32,
        )
        coeffs = jnp.sum(spread(coeff_terms, GY), axis=0)
        weight_terms = lax.dot_general(
            coeffs,
            factor_part,
            (((1,), (1,)), ((), ())),
            precision=lax.Precision.HIGHEST,
            preferred_element_type=jnp.float32,
        )
        weights = weight_terms[:, :SHARE]
        for step in (1, 2, 3):
            weights = weights + quad_partner(
                weight_terms[:, step * SHARE : (step + 1) * SHARE], step
            )
        weights = spread(weights.astype(jnp.bfloat16), PLANE)
        weights = weights.transpose(1, 0, 2).reshape(PROBES, 4096)
        low = lax.dot_general(
            weights,
            kernel_rows,
            (((1,), (1,)), ((), ())),
            preferred_element_type=jnp.float32,
        )
        image = live * (noise_level * search + sparse + low)
        curve_part = inner(search, image)
        if step_index == 0:
            sums = total_scalars(pack(rz_part, curve_part))[0]
            rz_now, curve = sums[:PROBES], sums[PROBES : 2 * PROBES]
        else:
            curve = total_scalars(pack(curve_part))[0, :PROBES]
        alpha = (rz_now / curve)[:, None]
        solution = solution + alpha * search
        residual = residual - alpha * image
        if step_index + 1 < ITERS:
            precon = scaling * residual
            rz_next = total_scalars(pack(inner(residual, precon)))[0, :PROBES]
            search = precon + (rz_next / rz_now)[:, None] * search
            rz_now = rz_next
    return (solution[None, None], residual[None, None])


def solution(mesh):
    fine = Mesh(mesh.devices.reshape(8, 2, 2, 2, 4), ALL)
    placed = (
        P(GX, GY, None, None),
        P(GX, GY, None, None),
        P(GX, GY, None),
        P(GX, GY),
        P(GX, GY, None, None),
        P(GX, GY, None),
        P(GY, None),
    )
    return jax.shard_map(
        on_device,
        mesh=fine,
        in_specs=placed,
        out_specs=(P(GX, GY, None, None), P(GX, GY, None, None)),
        check_vma=False,
    )
```

time: 1720 us -> 341 us (0.20)
  blocking collectives: 920 us -> 89.7 us
  waiting for transfers between devices: 637 us -> 25.9 us
  starting transfers between devices: 33.6 us -> 112 us
  matrix products: 60.6 us -> 36.5 us
  local copies, waits for them, and re-layouts: 11.2 us -> 34.5 us
    all_gather x3 -> x0, blocking collectives: 674 us -> none  [the longest x1 618 us: on_device(): centres = lax.all_gather(centre_local, ('gx', 'gy'), axis=1, tiled=True)]
    psum x4 -> x0, waiting for transfers between devices: 636 us -> none  [the longest x2 488 us: on_device(): total = lax.psum(terms, ('gx', 'gy'))]
    psum x3 -> x0, blocking collectives: 246 us -> none  [the longest x2 160 us: residual_norm(): return lax.psum(jnp.sum(left * right, axis=1), ('gx', 'gy'))]
    all_to_all x0 -> x8, blocking collectives: none -> 89.7 us  [exchange(): return lax.all_to_all(parts, axes, 0, 0, tiled=True)]
    all_to_all x0 -> x8, starting transfers between devices: none -> 63.9 us  [exchange(): return lax.all_to_all(parts, axes, 0, 0, tiled=True)]
    dot_general x8, matrix products: 59 us -> 35 us  [the longest x2 12.1 us: on_device(): terms = jnp.dot(packed, kernel_rows, preferred_element_type=jnp.float32)]
  transfers between devices with their start and end apart: 16 -> 32, of which waited for: 4 -> 15; matrix products, arithmetic and copies ran while one was open for 4% -> 23% of each run, Pallas kernels for 0% -> 0%
where the time goes in v1:
time: 341 us; the launch traced here: 339 us
  starting transfers between devices  112 us (33%)
  blocking collectives  89.7 us (26%)
  other arithmetic  37.1 us (11%)
  matrix products  36.5 us (11%)
  local copies, waits for them, and re-layouts  34.5 us (10%)
  waiting for transfers between devices  25.9 us (8%)
    all_to_all x8, blocking collectives, exchange(): return lax.all_to_all(parts, axes, 0, 0, tiled=True)  89.7 us
    all_to_all x8, starting transfers between devices, exchange(): return lax.all_to_all(parts, axes, 0, 0, tiled=True)  63.9 us
    ppermute x6, starting transfers between devices, padded(): lax.ppermute(lax.slice_in_dim(block, block.shape[dim] - width, None, axis...  23 us
    dynamic_update_slice x2, other arithmetic, on_device(): lax.map(lambda portion: inducing_rows(portion, centres), grouped)  18.7 us
    all_to_all x8, waiting for transfers between devices, exchange(): return lax.all_to_all(parts, axes, 0, 0, tiled=True)  17.1 us
    ppermute x12, starting transfers between devices, quad_partner(): return lax.ppermute(value, ('yl', 'c'), pairs)  12.8 us
    ppermute x6, starting transfers between devices, padded(): lax.ppermute(lax.slice_in_dim(block, 0, width, axis=dim), axis, backward)  12.2 us
    dot_general x2, matrix products, on_device(): terms = jnp.dot(packed, kernel_rows, preferred_element_type=jnp.float32)  12.1 us
  transfers between devices with their start and end apart: 32, of which 15 were waited for; matrix products, arithmetic and copies ran while one was open for 23% of the time, Pallas kernels for 0%

profile of v1, /device:TPU:1, one launch (start us, length us, event | category | flops | bytes accessed | tf_op | source)
XLA Modules:
  0.0 339.1 jit_solution(6115343023758432641)
XLA Ops:
  2.0 1.0 copy.97
  4.3 8.6 %all-to-all-start = ((f32[32,1,128]{2,1,0:T(1,128)}), f32[32,1,128]{2,1,0:T(1,128)S(1)}, u32[]{:S(2)}, u32[]{:S(2)}) async-start(f32[32,1,128]{2,1,0:T(1,128)} %broadcast_in_dim.140), calls=%async_computation | async-start | bytes 32768 | tf_op jit(solution)/shard_map/all_to_all | solution.py:73
  13.6 6.2 %all-to-all-done = f32[32,1,128]{2,1,0:T(1,128)S(1)} async-done(((f32[32,1,128]{2,1,0:T(1,128)}), f32[32,1,128]{2,1,0:T(1,128)S(1)}, u32[]{:S(2)}, u32[]{:S(2)}) %all-to-all-start) | async-done | bytes 16416 | tf_op jit(solution)/shard_map/all_to_all | solution.py:73
  20.4 8.2 %all-to-all-start.1 = ((f32[8,32,128]{2,1,0:T(8,128)}), f32[8,32,128]{2,1,0:T(8,128)S(1)}, u32[]{:S(2)}, u32[]{:S(2)}) async-start(f32[8,32,128]{2,1,0:T(8,128)} %broadcast_in_dim.142), calls=%async_computation.1 | async-start | bytes 262144 | tf_op jit(solution)/shard_map/all_to_all | solution.py:73
  29.5 2.9 collective-permute-start.1
  32.4 2.7 collective-permute-start
  35.1 2.3 collective-permute-start.5
  37.3 3.3 collective-permute-start.4
  41.5 3.6 %fusion.67 = (f32[128,1024]{1,0:T(8,128)}, f32[128,1024]{1,0:T(8,128)}, f32[128,1024]{1,0:T(8,128)}, f32[128,1024]{1,0:T(8,128)}) fusion(f32[512,4096]{1,0:T(8,128)} %param.21, s32[]{:T(128)S(6)} %select_n.111, s32[]{:T(128)S(6)} %select_n.113, s32[]{:T(128)S(6)} %select_n.115, s32[]{:T(128)S(6)} %select_n.119, s32[]{:T(128)S(6)} %select_n.117), kind=kLoop, calls=%fused_computation.141 | loop fusion | bytes 4194324 | tf_op jit(solution)/shard_map/dynamic_slice | solution.py:114
  46.5 19.0 %while.50 = (s32[]{:T(128)}, bf16[2,512,4096]{2,1,0:T(8,128)(2,1)}, f32[2,8,512]{2,1,0:T(8,128)S(1)}, f32[8,4096]{1,0:T(8,128)S(1)}, s32[]{:T(128)}, /*index=5*/...) while((s32[]{:T(128)}, bf16[2,512,4096]{2,1,0:T(8,128)(2,1)}, f32[2,8,512]{2,1,0:T(8,128)S(1)}, ...), condition=%wide.region_6.7_spmd, body=%wide.region_5.6_spmd.sunk | while | flops 54525960 | bytes 4636925 | solution.py:134
  46.6 9.4 %fusion.100 = bf16[2,512,4096]{2,1,0:T(8,128)(2,1)} fusion(bf16[2,512,4096]{2,1,0:T(8,128)(2,1)} %get-tuple-element.636, s32[]{:T(128)S(6)} %copy.159, f32[4096]{0:T(1024)S(1)} %bitcast.307, f32[512]{0:T(512)S(1)} %bitcast.343, f32[4096]{0:T(1024)S(1)} %bitcast.308, f32[512]{0:T(512)S(1)} %bitcast.337, f32[4096]{0:T(1024)S(1)} %bitcast.309, ...), kind=kLoop, calls=%fused_computation.5.clone.1 | loop fusion | flops 54525952 | bytes 4341764 | tf_op jit(solution)/shard_map/while/body/jit(dynamic_update_index_in_dim)/dynamic_update_slice | solution.py:134
  56.1 9.4 %fusion.100 = bf16[2,512,4096]{2,1,0:T(8,128)(2,1)} fusion(bf16[2,512,4096]{2,1,0:T(8,128)(2,1)} %get-tuple-element.636, s32[]{:T(128)S(6)} %copy.159, f32[4096]{0:T(1024)S(1)} %bitcast.307, f32[512]{0:T(512)S(1)} %bitcast.343, f32[4096]{0:T(1024)S(1)} %bitcast.308, f32[512]{0:T(512)S(1)} %bitcast.337, f32[4096]{0:T(1024)S(1)} %bitcast.309, ...), kind=kLoop, calls=%fused_computation.5.clone.1 | loop fusion | flops 54525952 | bytes 4341764 | tf_op jit(solution)/shard_map/while/body/jit(dynamic_update_index_in_dim)/dynamic_update_slice | solution.py:134
  65.5 12.0 %copy.101 = bf16[4096,1024]{1,0:T(8,128)(2,1)} copy(bf16[4096,1024]{0,1:T(8,128)(2,1)} %bitcast.300) | data formatting | bytes 16777216 | tf_op jit(solution)/shard_map/dot_general | solution.py:165
  77.4 6.4 %convolution_bitcast_fusion.3 = f32[32,16,128]{2,1,0:T(8,128)} fusion(bf16[32,128,1024]{2,1,0:T(8,128)(2,1)} %bitcast.298, bf16[1,1,16,1024]{3,2,1,0:T(8,128)(2,1)S(1)} %multiply_convert_fusion), kind=kOutput, calls=%fused_computation.54 | convolution fusion | flops 134217728 | bytes 8683520 | tf_op jit(solution)/shard_map/dot_general | solution.py:165
  83.8 5.4 %all-to-all-start.2 = ((f32[32,16,128]{2,1,0:T(8,128)}), f32[32,16,128]{2,1,0:T(8,128)S(1)}, u32[]{:S(2)}, u32[]{:S(2)}) async-start(f32[32,16,128]{2,1,0:T(8,128)} %convolution_bitcast_fusion.3), calls=%async_computation.2 | async-start | bytes 524288 | tf_op jit(solution)/shard_map/all_to_all | solution.py:73
  89.2 1.4 constant_dynamic-update-slice_fusion.2
  91.2 1.4 constant_dynamic-update-slice_fusion
  92.6 1.3 collective-permute-start.7
  93.9 4.6 %collective-permute-start.6 = (f32[3,1,8,1024]{3,2,1,0:T(8,128)}, f32[3,1,8,1024]{3,2,1,0:T(8,128)}, u32[]{:S(2)}, u32[]{:S(2)}) collective-permute-start(f32[3,1,8,1024]{3,2,1,0:T(8,128)} %constant_dynamic-update-slice_fusion), channel_id=1, source_target_pairs={{0,1},{1,2},{2,3},{3,4},{4,5},{5,6},{6,7},{8,9},{9,10},{10,11},{11... | collective-permute-start | bytes 294920 | tf_op jit(solution)/shard_map/ppermute | solution.py:30
  99.2 6.7 %all-to-all-start.3 = ((f32[8,16,128]{2,1,0:T(8,128)}), f32[8,16,128]{2,1,0:T(8,128)S(1)}, u32[]{:S(2)}, u32[]{:S(2)}) async-start(f32[8,16,128]{2,1,0:T(8,128)} %broadcast_in_dim.143), calls=%async_computation.3 | async-start | bytes 131072 | tf_op jit(solution)/shard_map/all_to_all | solution.py:73
  105.9 1.4 pad_maximum_fusion.4
  107.3 1.3 collective-permute-start.3
  108.5 4.6 %collective-permute-start.2 = (bf16[3,1,16,1024]{3,2,1,0:T(8,128)(2,1)}, bf16[3,1,16,1024]{3,2,1,0:T(8,128)(2,1)}, u32[]{:S(2)}, u32[]{:S(2)}) collective-permute-start(bf16[3,1,16,1024]{3,2,1,0:T(8,128)(2,1)} %pad_maximum_fusion.4), channel_id=1, source_target_pairs={{0,1},{1,2},{2,3},{3,4},{4,5},{5,6},{6,7},{8,9},{9,10},{10,11},{11... | collective-permute-start | bytes 294920 | tf_op jit(solution)/shard_map/ppermute | solution.py:30
  113.8 3.5 %collective-permute-start.10 = (f32[16,128]{1,0:T(8,128)}, f32[16,128]{1,0:T(8,128)S(1)}, u32[]{:S(2)}, u32[]{:S(2)}) collective-permute-start(f32[16,128]{1,0:T(8,128)} %reduce_sum.152), channel_id=1, source_target_pairs={{0,24},{8,16},{16,8},{24,0},{1,25},{9,17},{17,9},{25,1},{2,26},{10... | collective-permute-start | bytes 24584 | tf_op jit(solution)/shard_map/ppermute | solution.py:88
  117.7 1.0 pad_maximum_fusion.2
  118.9 1.2 collective-permute-done.9
  120.0 2.3 fusion.31
  123.2 9.2 %all-to-all-start.4 = ((f32[8,16,1024]{2,1,0:T(8,128)}), f32[8,16,1024]{2,1,0:T(8,128)S(1)}, u32[]{:S(2)}, u32[]{:S(2)}) async-start(f32[8,16,1024]{2,1,0:T(8,128)} %broadcast_in_dim.144), calls=%async_computation.4 | async-start | bytes 1048576 | tf_op jit(solution)/shard_map/all_to_all | solution.py:73
  132.5 15.4 %while.48 = (s32[]{:T(128)}, bf16[2,4,128,8,128]{4,2,3,1,0:T(8,128)(2,1)S(1)}, s32[2]{0:T(128)S(1)}, f32[8,8,128]{2,0,1:T(8,128)S(1)}, s32[8,8]{1,0:T(8,128)S(1)...) while((s32[]{:T(128)}, ...), condition=%wide.region_2.3_spmd, body=%wide.region_1.2_spmd.sunk | while | flops 17826924 | bytes 3855451 | solution.py:130
  134.6 5.2 %fusion.95 = bf16[1,4,128,8,128]{4,3,2,1,0:T(8,128)(2,1)S(1)} fusion(f32[4,8,128]{2,1,0:T(8,128)S(1)} %bitcast.321, f32[4,128]{1,0:T(4,128)S(1)} %get-tuple-element.577, f32[4,8,128]{2,1,0:T(8,128)S(1)} %bitcast.315, f32[4,128]{1,0:T(4,128)S(1)} %get-tuple-element.579, f32[4,8,128]{2,1,0:T(8,128)S(1)} %bitcast.316, ...), kind=kLoop, calls=%fused_computation.17.clone.1 | loop fusion | flops 17825792 | bytes 1196032 | tf_op jit(solution)/shard_map/while/body/eval_jaxpr/convert_element_type | solution.py:69
  142.2 5.2 %fusion.95 = bf16[1,4,128,8,128]{4,3,2,1,0:T(8,128)(2,1)S(1)} fusion(f32[4,8,128]{2,1,0:T(8,128)S(1)} %bitcast.321, f32[4,128]{1,0:T(4,128)S(1)} %get-tuple-element.577, f32[4,8,128]{2,1,0:T(8,128)S(1)} %bitcast.315, f32[4,128]{1,0:T(4,128)S(1)} %get-tuple-element.579, f32[4,8,128]{2,1,0:T(8,128)S(1)} %bitcast.316, ...), kind=kLoop, calls=%fused_computation.17.clone.1 | loop fusion | flops 17825792 | bytes 1196032 | tf_op jit(solution)/shard_map/while/body/eval_jaxpr/convert_element_type | solution.py:69
  147.9 3.3 fusion.64
  151.7 1.2 collective-permute-start.13
  153.2 1.0 pad_maximum_fusion.1
  156.1 9.5 %all-to-all-start.5 = ((bf16[32,16,128]{2,1,0:T(8,128)(2,1)}), bf16[32,16,128]{2,1,0:T(8,128)(2,1)S(1)}, u32[]{:S(2)}, u32[]{:S(2)}) async-start(bf16[32,16,128]{2,1,0:T(8,128)(2,1)} %broadcast_in_dim.145), calls=%async_computation.5 | async-start | bytes 262144 | tf_op jit(solution)/shard_map/all_to_all | solution.py:73
  165.6 2.2 while.49
  167.8 5.5 %all-to-all-done.5 = bf16[32,16,128]{2,1,0:T(8,128)(2,1)S(1)} async-done(((bf16[32,16,128]{2,1,0:T(8,128)(2,1)}), bf16[32,16,128]{2,1,0:T(8,128)(2,1)S(1)}, u32[]{:S(2)}, u32[]{:S(2)}) %all-to-all-start.5) | async-done | bytes 131104 | tf_op jit(solution)/shard_map/all_to_all | solution.py:73
  173.3 5.8 %fusion.26 = (f32[16]{0:T(128)S(1)}, f32[16]{0:T(128)S(1)}, f32[16,1024]{1,0:T(8,128)S(1)}) fusion(f32[1,1,16,1024]{3,2,1,0:T(8,128)S(1)} %copy-done, f32[1024]{0:T(1024)S(1)} %bitcast.345, f32[1024]{0:T(1024)S(1)} %fusion.56, bf16[1024,4096]{1,0:T(8,128)(2,1)} %bitcast.301, bf16[32,16,128]{2,1,0:T(8,128)(2,1)S(1)} %all-to-all-done.5, ...), kind=kOutput, calls=%fused_computation.76 | convolution fusion | flops 134365152 | bytes 8724608 | tf_op jit(solution)/shard_map/dot_general | solution.py:193
  179.2 10.7 %all_to_all.80 = f32[32,1,128]{2,1,0:T(1,128)S(1)} all-to-all(f32[32,1,128]{2,1,0:T(1,128)S(1)} %broadcast_in_dim.146), channel_id=1, replica_groups=mesh['z'=8,'yl'=2,'c'=2,'yh'=2,'x'=4] {'yl','c','yh','x'}, dimensions={0} | all-to-all | bytes 32768 | tf_op jit(solution)/shard_map/all_to_all | solution.py:73
  189.9 13.2 %all_to_all.81 = f32[8,1,128]{2,1,0:T(1,128)S(1)} all-to-all(f32[8,1,128]{2,1,0:T(1,128)S(1)} %broadcast_in_dim.147), channel_id=1, replica_groups=mesh['z'=8,'yl'=2,'c'=2,'yh'=2,'x'=4] {'z'}, dimensions={0} | all-to-all | bytes 8192 | tf_op jit(solution)/shard_map/all_to_all | solution.py:73
  203.5 12.1 %all_to_all.82 = f32[32,1,128]{2,1,0:T(1,128)S(1)} all-to-all(f32[32,1,128]{2,1,0:T(1,128)S(1)} %broadcast_in_dim.148), channel_id=1, replica_groups=mesh['z'=8,'yl'=2,'c'=2,'yh'=2,'x'=4] {'yl','c','yh','x'}, dimensions={0} | all-to-all | bytes 32768 | tf_op jit(solution)/shard_map/all_to_all | solution.py:73
  215.6 8.9 %all_to_all.83 = f32[8,1,128]{2,1,0:T(1,128)S(1)} all-to-all(f32[8,1,128]{2,1,0:T(1,128)S(1)} %broadcast_in_dim.149), channel_id=1, replica_groups=mesh['z'=8,'yl'=2,'c'=2,'yh'=2,'x'=4] {'z'}, dimensions={0} | all-to-all | bytes 8192 | tf_op jit(solution)/shard_map/all_to_all | solution.py:73
  224.6 5.7 %convolution_bitcast_fusion.2 = f32[32,16,128]{2,1,0:T(8,128)S(1)} fusion(bf16[32,128,1024]{2,1,0:T(8,128)(2,1)} %bitcast.299, f32[16,1024]{1,0:T(8,128)S(1)} %get-tuple-element.386), kind=kOutput, calls=%fused_computation.53 | convolution fusion | flops 134234112 | bytes 8716288 | tf_op jit(solution)/shard_map/dot_general | solution.py:165
  230.3 13.8 %all_to_all.84 = f32[32,16,128]{2,1,0:T(8,128)S(1)} all-to-all(f32[32,16,128]{2,1,0:T(8,128)S(1)} %convolution_bitcast_fusion.2), channel_id=1, replica_groups=mesh['z'=8,'yl'=2,'c'=2,'yh'=2,'x'=4] {'yh','x','yl','c'}, dimensions={0} | all-to-all | bytes 524288 | tf_op jit(solution)/shard_map/all_to_all | solution.py:73
  244.1 9.7 %all_to_all.85 = f32[8,16,128]{2,1,0:T(8,128)S(1)} all-to-all(f32[8,16,128]{2,1,0:T(8,128)S(1)} %broadcast_in_dim.151), channel_id=1, replica_groups=mesh['z'=8,'yl'=2,'c'=2,'yh'=2,'x'=4] {'z'}, dimensions={0} | all-to-all | bytes 131072 | tf_op jit(solution)/shard_map/all_to_all | solution.py:73
  253.8 2.2 collective-permute-start.20
  256.0 1.3 collective-permute-start.19
  257.3 1.2 collective-permute-done.19
  258.6 2.5 fusion.39
  261.9 3.5 %all-to-all-start.12 = ((f32[8,16,1024]{2,1,0:T(8,128)}), f32[8,16,1024]{2,1,0:T(8,128)S(1)}, u32[]{:S(2)}, u32[]{:S(2)}) async-start(f32[8,16,1024]{2,1,0:T(8,128)} %broadcast_in_dim.152), calls=%async_computation.12 | async-start | bytes 1048576 | tf_op jit(solution)/shard_map/all_to_all | solution.py:73
  265.4 3.2 collective-permute-start.15
  268.6 2.4 collective-permute-start.14
  272.1 1.3 collective-permute-start.17
  273.4 5.4 %collective-permute-start.16 = (bf16[3,1,16,1024]{3,2,1,0:T(8,128)(2,1)S(1)}, bf16[3,1,16,1024]{3,2,1,0:T(8,128)(2,1)S(1)}, u32[]{:S(2)}, u32[]{:S(2)}) collective-permute-start(bf16[3,1,16,1024]{3,2,1,0:T(8,128)(2,1)S(1)} %pad_maximum_fusion.5), channel_id=1, source_target_pairs={{0,1},{1,2},{2,3},{3,4},{4,5},{5,6},{6,7},{8,9},{9,10},{10,11},{11... | collective-permute-start | bytes 294920 | tf_op jit(solution)/shard_map/ppermute | solution.py:30
  278.9 1.7 collective-permute-done.16
  280.7 3.3 fusion.63
  284.1 3.3 collective-permute-start.23
  287.6 1.9 collective-permute-done.23
  290.6 12.8 %all-to-all-start.13 = ((bf16[32,16,128]{2,1,0:T(8,128)(2,1)}), bf16[32,16,128]{2,1,0:T(8,128)(2,1)S(1)}, u32[]{:S(2)}, u32[]{:S(2)}) async-start(bf16[32,16,128]{2,1,0:T(8,128)(2,1)} %broadcast_in_dim.153), calls=%async_computation.13 | async-start | bytes 262144 | tf_op jit(solution)/shard_map/all_to_all | solution.py:73
  303.5 2.2 while.51
  305.7 5.5 %all-to-all-done.13 = bf16[32,16,128]{2,1,0:T(8,128)(2,1)S(1)} async-done(((bf16[32,16,128]{2,1,0:T(8,128)(2,1)}), bf16[32,16,128]{2,1,0:T(8,128)(2,1)S(1)}, u32[]{:S(2)}, u32[]{:S(2)}) %all-to-all-start.13) | async-done | bytes 131104 | tf_op jit(solution)/shard_map/all_to_all | solution.py:73
  311.1 5.8 %multiply_reduce_fusion = (f32[16]{0:T(128)S(1)}, f32[16,1024]{1,0:T(8,128)S(1)}) fusion(f32[16,1024]{1,0:T(8,128)S(1)} %get-tuple-element.386, bf16[1024,4096]{1,0:T(8,128)(2,1)} %bitcast.302, f32[1024]{0:T(1024)S(1)} %fusion.56, bf16[32,16,128]{2,1,0:T(8,128)(2,1)S(1)} %all-to-all-done.13, f32[8,16,128]{2,1,0:T(8,128)S(1)} %get-tuple-element.292), kind=kOutput, calls=%fused_computation.84 | convolution fusion | flops 134299632 | bytes 8720448 | tf_op jit(solution)/shard_map/dot_general | solution.py:193
  316.9 10.7 %all_to_all.86 = f32[32,1,128]{2,1,0:T(1,128)S(1)} all-to-all(f32[32,1,128]{2,1,0:T(1,128)S(1)} %broadcast_in_dim.154), channel_id=1, replica_groups=mesh['z'=8,'yl'=2,'c'=2,'yh'=2,'x'=4] {'yl','c','yh','x'}, dimensions={0} | all-to-all | bytes 32768 | tf_op jit(solution)/shard_map/all_to_all | solution.py:73
  327.7 10.6 %all_to_all.87 = f32[8,1,128]{2,1,0:T(1,128)S(1)} all-to-all(f32[8,1,128]{2,1,0:T(1,128)S(1)} %broadcast_in_dim.155), channel_id=1, replica_groups=mesh['z'=8,'yl'=2,'c'=2,'yh'=2,'x'=4] {'z'}, dimensions={0} | all-to-all | bytes 8192 | tf_op jit(solution)/shard_map/all_to_all | solution.py:73
  (155 shorter events, 25.4 us)
Async XLA Ops:
  4.3 15.4 %all-to-all-start = ((f32[32,1,128]{2,1,0:T(1,128)}), f32[32,1,128]{2,1,0:T(1,128)S(1)}, u32[]{:S(2)}, u32[]{:S(2)}) async-start(f32[32,1,128]{2,1,0:T(1,128)} %broadcast_in_dim.140), calls=%async_computation | async-start | bytes 32768 | tf_op jit(solution)/shard_map/all_to_all | solution.py:73
  20.4 24.6 %all-to-all-start.1 = ((f32[8,32,128]{2,1,0:T(8,128)}), f32[8,32,128]{2,1,0:T(8,128)S(1)}, u32[]{:S(2)}, u32[]{:S(2)}) async-start(f32[8,32,128]{2,1,0:T(8,128)} %broadcast_in_dim.142), calls=%async_computation.1 | async-start | bytes 262144 | tf_op jit(solution)/shard_map/all_to_all | solution.py:73
  29.5 76.4 %collective-permute-start.1 = (bf16[1,1,16,1024]{3,2,1,0:T(8,128)(2,1)S(1)}, bf16[1,1,16,1024]{3,2,1,0:T(8,128)(2,1)S(1)}, u32[]{:S(2)}, u32[]{:S(2)}) collective-permute-start(bf16[1,1,16,1024]{3,2,1,0:T(8,128)(2,1)S(1)} %multiply_convert_fusion), channel_id=1, source_target_pairs={{8,0},{16,8},{24,16},{32,24},{40,32},{48,40},{56,48},{64,56},{72,6... | collective-permute-start | bytes 98312 | tf_op jit(solution)/shard_map/ppermute | solution.py:33
  32.4 73.5 %collective-permute-start = (bf16[1,1,16,1024]{3,2,1,0:T(8,128)(2,1)S(1)}, bf16[1,1,16,1024]{3,2,1,0:T(8,128)(2,1)}, u32[]{:S(2)}, u32[]{:S(2)}) collective-permute-start(bf16[1,1,16,1024]{3,2,1,0:T(8,128)(2,1)S(1)} %multiply_convert_fusion), channel_id=1, source_target_pairs={{0,8},{8,16},{16,24},{24,32},{32,40},{40,48},{48,56},{56,64},{64,7... | collective-permute-start | bytes 98312 | tf_op jit(solution)/shard_map/ppermute | solution.py:30
  35.1 56.2 %collective-permute-start.5 = (f32[1,1,8,1024]{3,2,1,0:T(8,128)}, f32[1,1,8,1024]{3,2,1,0:T(8,128)}, u32[]{:S(2)}, u32[]{:S(2)}) collective-permute-start(f32[1,1,8,1024]{3,2,1,0:T(8,128)} %param.15), channel_id=1, source_target_pairs={{8,0},{16,8},{24,16},{32,24},{40,32},{48,40},{56,48},{64,56},{72,6... | collective-permute-start | bytes 98312 | tf_op jit(solution)/shard_map/ppermute | solution.py:33
  37.3 51.9 %collective-permute-start.4 = (f32[1,1,8,1024]{3,2,1,0:T(8,128)}, f32[1,1,8,1024]{3,2,1,0:T(8,128)}, u32[]{:S(2)}, u32[]{:S(2)}) collective-permute-start(f32[1,1,8,1024]{3,2,1,0:T(8,128)} %param.15), channel_id=1, source_target_pairs={{0,8},{8,16},{16,24},{24,32},{32,40},{40,48},{48,56},{56,64},{64,7... | collective-permute-start | bytes 98312 | tf_op jit(solution)/shard_map/ppermute | solution.py:30
  45.1 1.4 copy-start.1
  83.8 36.2 %copy-start.2 = (f32[128,1024]{1,0:T(8,128)S(1)}, f32[128,1024]{1,0:T(8,128)}, u32[]{:S(2)}) copy-start(f32[128,1024]{1,0:T(8,128)} %get-tuple-element.419) | copy-start | bytes 1572868
  83.8 36.2 %copy-start.4 = (f32[128,1024]{1,0:T(8,128)S(1)}, f32[128,1024]{1,0:T(8,128)}, u32[]{:S(2)}) copy-start(f32[128,1024]{1,0:T(8,128)} %get-tuple-element.420) | copy-start | bytes 1572868
  83.8 14.7 %all-to-all-start.2 = ((f32[32,16,128]{2,1,0:T(8,128)}), f32[32,16,128]{2,1,0:T(8,128)S(1)}, u32[]{:S(2)}, u32[]{:S(2)}) async-start(f32[32,16,128]{2,1,0:T(8,128)} %convolution_bitcast_fusion.3), calls=%async_computation.2 | async-start | bytes 524288 | tf_op jit(solution)/shard_map/all_to_all | solution.py:73
  92.6 24.7 %collective-permute-start.7 = (f32[3,1,8,1024]{3,2,1,0:T(8,128)}, f32[3,1,8,1024]{3,2,1,0:T(8,128)}, u32[]{:S(2)}, u32[]{:S(2)}) collective-permute-start(f32[3,1,8,1024]{3,2,1,0:T(8,128)} %constant_dynamic-update-slice_fusion), channel_id=1, source_target_pairs={{1,0},{2,1},{3,2},{4,3},{5,4},{6,5},{7,6},{9,8},{10,9},{11,10},{12... | collective-permute-start | bytes 294920 | tf_op jit(solution)/shard_map/ppermute | solution.py:33
  93.9 23.5 %collective-permute-start.6 = (f32[3,1,8,1024]{3,2,1,0:T(8,128)}, f32[3,1,8,1024]{3,2,1,0:T(8,128)}, u32[]{:S(2)}, u32[]{:S(2)}) collective-permute-start(f32[3,1,8,1024]{3,2,1,0:T(8,128)} %constant_dynamic-update-slice_fusion), channel_id=1, source_target_pairs={{0,1},{1,2},{2,3},{3,4},{4,5},{5,6},{6,7},{8,9},{9,10},{10,11},{11... | collective-permute-start | bytes 294920 | tf_op jit(solution)/shard_map/ppermute | solution.py:30
  99.2 14.0 %all-to-all-start.3 = ((f32[8,16,128]{2,1,0:T(8,128)}), f32[8,16,128]{2,1,0:T(8,128)S(1)}, u32[]{:S(2)}, u32[]{:S(2)}) async-start(f32[8,16,128]{2,1,0:T(8,128)} %broadcast_in_dim.143), calls=%async_computation.3 | async-start | bytes 131072 | tf_op jit(solution)/shard_map/all_to_all | solution.py:73
  107.3 46.0 %collective-permute-start.3 = (bf16[3,1,16,1024]{3,2,1,0:T(8,128)(2,1)}, bf16[3,1,16,1024]{3,2,1,0:T(8,128)(2,1)}, u32[]{:S(2)}, u32[]{:S(2)}) collective-permute-start(bf16[3,1,16,1024]{3,2,1,0:T(8,128)(2,1)} %pad_maximum_fusion.4), channel_id=1, source_target_pairs={{1,0},{2,1},{3,2},{4,3},{5,4},{6,5},{7,6},{9,8},{10,9},{11,10},{12... | collective-permute-start | bytes 294920 | tf_op jit(solution)/shard_map/ppermute | solution.py:33
  108.5 44.7 %collective-permute-start.2 = (bf16[3,1,16,1024]{3,2,1,0:T(8,128)(2,1)}, bf16[3,1,16,1024]{3,2,1,0:T(8,128)(2,1)}, u32[]{:S(2)}, u32[]{:S(2)}) collective-permute-start(bf16[3,1,16,1024]{3,2,1,0:T(8,128)(2,1)} %pad_maximum_fusion.4), channel_id=1, source_target_pairs={{0,1},{1,2},{2,3},{3,4},{4,5},{5,6},{6,7},{8,9},{9,10},{10,11},{11... | collective-permute-start | bytes 294920 | tf_op jit(solution)/shard_map/ppermute | solution.py:30
  113.8 5.1 %collective-permute-start.10 = (f32[16,128]{1,0:T(8,128)}, f32[16,128]{1,0:T(8,128)S(1)}, u32[]{:S(2)}, u32[]{:S(2)}) collective-permute-start(f32[16,128]{1,0:T(8,128)} %reduce_sum.152), channel_id=1, source_target_pairs={{0,24},{8,16},{16,8},{24,0},{1,25},{9,17},{17,9},{25,1},{2,26},{10... | collective-permute-start | bytes 24584 | tf_op jit(solution)/shard_map/ppermute | solution.py:88
  117.3 2.7 collective-permute-start.9
  117.3 2.7 collective-permute-start.8
  120.0 12.4 %copy-start.5 = (s32[1,1,8,8]{3,2,1,0:T(8,128)S(1)}, s32[1,1,8,8]{3,2,1,0:T(8,128)}, u32[]{:S(2)}) copy-start(s32[1,1,8,8]{3,2,1,0:T(8,128)} %param.19) | copy-start | bytes 772
  123.2 24.6 %all-to-all-start.4 = ((f32[8,16,1024]{2,1,0:T(8,128)}), f32[8,16,1024]{2,1,0:T(8,128)S(1)}, u32[]{:S(2)}, u32[]{:S(2)}) async-start(f32[8,16,1024]{2,1,0:T(8,128)} %broadcast_in_dim.144), calls=%async_computation.4 | async-start | bytes 1048576 | tf_op jit(solution)/shard_map/all_to_all | solution.py:73
  151.3 3.1 collective-permute-start.11
  151.7 3.1 collective-permute-start.13
  152.9 2.5 collective-permute-start.12
  156.1 17.2 %all-to-all-start.5 = ((bf16[32,16,128]{2,1,0:T(8,128)(2,1)}), bf16[32,16,128]{2,1,0:T(8,128)(2,1)S(1)}, u32[]{:S(2)}, u32[]{:S(2)}) async-start(bf16[32,16,128]{2,1,0:T(8,128)(2,1)} %broadcast_in_dim.145), calls=%async_computation.5 | async-start | bytes 262144 | tf_op jit(solution)/shard_map/all_to_all | solution.py:73
  165.6 7.7 %copy-start = (f32[1,1,16,1024]{3,2,1,0:T(8,128)S(1)}, f32[1,1,16,1024]{3,2,1,0:T(8,128)}, u32[]{:S(2)}) copy-start(f32[1,1,16,1024]{3,2,1,0:T(8,128)} %param.16) | copy-start | bytes 196612
  165.6 7.7 %copy-start.6 = (f32[1,1,1024]{2,1,0:T(1,128)S(1)}, f32[1,1,1024]{2,1,0:T(1,128)}, u32[]{:S(2)}) copy-start(f32[1,1,1024]{2,1,0:T(1,128)} %param.17) | copy-start | bytes 12292
  224.6 34.0 %copy-start.3 = (f32[128,1024]{1,0:T(8,128)S(1)}, f32[128,1024]{1,0:T(8,128)}, u32[]{:S(2)}) copy-start(f32[128,1024]{1,0:T(8,128)} %get-tuple-element.419) | copy-start | bytes 1572868
  253.8 3.5 %collective-permute-start.20 = (f32[16,128]{1,0:T(8,128)S(1)}, f32[16,128]{1,0:T(8,128)S(1)}, u32[]{:S(2)}, u32[]{:S(2)}) collective-permute-start(f32[16,128]{1,0:T(8,128)S(1)} %reduce_sum.163), channel_id=1, source_target_pairs={{0,24},{8,16},{16,8},{24,0},{1,25},{9,17},{17,9},{25,1},{2,26},{10... | collective-permute-start | bytes 24584 | tf_op jit(solution)/shard_map/ppermute | solution.py:88
  256.0 2.6 collective-permute-start.19
  257.3 1.3 collective-permute-start.18
  261.9 18.7 %all-to-all-start.12 = ((f32[8,16,1024]{2,1,0:T(8,128)}), f32[8,16,1024]{2,1,0:T(8,128)S(1)}, u32[]{:S(2)}, u32[]{:S(2)}) async-start(f32[8,16,1024]{2,1,0:T(8,128)} %broadcast_in_dim.152), calls=%async_computation.12 | async-start | bytes 1048576 | tf_op jit(solution)/shard_map/all_to_all | solution.py:73
  265.4 5.8 %collective-permute-start.15 = (bf16[1,1,16,1024]{3,2,1,0:T(8,128)(2,1)S(1)}, bf16[1,1,16,1024]{3,2,1,0:T(8,128)(2,1)S(1)}, u32[]{:S(2)}, u32[]{:S(2)}) collective-permute-start(bf16[1,1,16,1024]{3,2,1,0:T(8,128)(2,1)S(1)} %get-tuple-element.385), channel_id=1, source_target_pairs={{8,0},{16,8},{24,16},{32,24},{40,32},{48,40},{56,48},{64,56},{72,6... | collective-permute-start | bytes 98312 | tf_op jit(solution)/shard_map/ppermute | solution.py:33
  268.6 3.5 %collective-permute-start.14 = (bf16[1,1,16,1024]{3,2,1,0:T(8,128)(2,1)S(1)}, bf16[1,1,16,1024]{3,2,1,0:T(8,128)(2,1)S(1)}, u32[]{:S(2)}, u32[]{:S(2)}) collective-permute-start(bf16[1,1,16,1024]{3,2,1,0:T(8,128)(2,1)S(1)} %get-tuple-element.385), channel_id=1, source_target_pairs={{0,8},{8,16},{16,24},{24,32},{32,40},{40,48},{48,56},{56,64},{64,7... | collective-permute-start | bytes 98312 | tf_op jit(solution)/shard_map/ppermute | solution.py:30
  272.1 6.8 %collective-permute-start.17 = (bf16[3,1,16,1024]{3,2,1,0:T(8,128)(2,1)S(1)}, bf16[3,1,16,1024]{3,2,1,0:T(8,128)(2,1)S(1)}, u32[]{:S(2)}, u32[]{:S(2)}) collective-permute-start(bf16[3,1,16,1024]{3,2,1,0:T(8,128)(2,1)S(1)} %pad_maximum_fusion.5), channel_id=1, source_target_pairs={{1,0},{2,1},{3,2},{4,3},{5,4},{6,5},{7,6},{9,8},{10,9},{11,10},{12... | collective-permute-start | bytes 294920 | tf_op jit(solution)/shard_map/ppermute | solution.py:33
  273.4 7.1 %collective-permute-start.16 = (bf16[3,1,16,1024]{3,2,1,0:T(8,128)(2,1)S(1)}, bf16[3,1,16,1024]{3,2,1,0:T(8,128)(2,1)S(1)}, u32[]{:S(2)}, u32[]{:S(2)}) collective-permute-start(bf16[3,1,16,1024]{3,2,1,0:T(8,128)(2,1)S(1)} %pad_maximum_fusion.5), channel_id=1, source_target_pairs={{0,1},{1,2},{2,3},{3,4},{4,5},{5,6},{6,7},{8,9},{9,10},{10,11},{11... | collective-permute-start | bytes 294920 | tf_op jit(solution)/shard_map/ppermute | solution.py:30
  284.0 3.6 %collective-permute-start.21 = (f32[16,128]{1,0:T(8,128)S(1)}, f32[16,128]{1,0:T(8,128)S(1)}, u32[]{:S(2)}, u32[]{:S(2)}) collective-permute-start(f32[16,128]{1,0:T(8,128)S(1)} %get-tuple-element.425), channel_id=1, source_target_pairs={{0,8},{8,0},{16,24},{24,16},{1,9},{9,1},{17,25},{25,17},{2,10},{10... | collective-permute-start | bytes 24584 | tf_op jit(solution)/shard_map/ppermute | solution.py:88
  284.1 5.4 %collective-permute-start.23 = (f32[16,128]{1,0:T(8,128)S(1)}, f32[16,128]{1,0:T(8,128)S(1)}, u32[]{:S(2)}, u32[]{:S(2)}) collective-permute-start(f32[16,128]{1,0:T(8,128)S(1)} %get-tuple-element.426), channel_id=1, source_target_pairs={{0,24},{8,16},{16,8},{24,0},{1,25},{9,17},{17,9},{25,1},{2,26},{10... | collective-permute-start | bytes 24584 | tf_op jit(solution)/shard_map/ppermute | solution.py:88
  287.4 2.5 collective-permute-start.22
  290.6 20.5 %all-to-all-start.13 = ((bf16[32,16,128]{2,1,0:T(8,128)(2,1)}), bf16[32,16,128]{2,1,0:T(8,128)(2,1)S(1)}, u32[]{:S(2)}, u32[]{:S(2)}) async-start(bf16[32,16,128]{2,1,0:T(8,128)(2,1)} %broadcast_in_dim.153), calls=%async_computation.13 | async-start | bytes 262144 | tf_op jit(solution)/shard_map/all_to_all | solution.py:73

commit v2 on v1

v2 whole, which is shorter than its diff:
```python
import jax
import jax.numpy as jnp
from jax import lax
from jax.experimental import pallas as pl
from jax.experimental.pallas import tpu as pltpu
from jax.sharding import Mesh, PartitionSpec as P

FEAT = 8
BLOCK = 128
PROBES = 16
PTS = 1024
SHARE = 128
CHUNK = 512
CHUNKS = 8
CAP = 8
EMPTY = 72

support_radius = 0.32
width_sq = 0.045
LOG2E = 1.4426950408889634

ALL = ("z", "yl", "c", "yh", "x")
PLANE = ("yh", "x", "yl", "c")
CELLS = ("yl", "c", "yh", "x")
GX = ("z", "yl", "c")
GY = ("yh", "x")
f32 = jnp.float32
bf16 = jnp.bfloat16

VMEM = pl.BlockSpec(memory_space=pltpu.VMEM)
SMEM = pl.BlockSpec(memory_space=pltpu.SMEM)
PARAMS = pltpu.CompilerParams(vmem_limit_bytes=32 * 1024 * 1024)


def exchange(parts, axes):
    return lax.all_to_all(parts, axes, 0, 0, tiled=True)


def spread(value, axes):
    count = lax.axis_size(axes)
    return exchange(jnp.broadcast_to(value[None], (count,) + value.shape), axes)


def quad_partner(value, step):
    pairs = [(i, i ^ step) for i in range(4)]
    return lax.ppermute(value, ("yl", "c"), pairs)


def beside(value, axes):
    count = lax.axis_size(axes)
    forward = [(i, i + 1) for i in range(count - 1)]
    backward = [(target, source) for source, target in forward]
    return lax.ppermute(value, axes, forward), lax.ppermute(value, axes, backward)


def split3(value):
    first = value.astype(bf16).astype(f32)
    rest = value - first
    second = rest.astype(bf16).astype(f32)
    return first, second, (rest - second).astype(bf16).astype(f32)


def augmented(points, scale, left):
    centred = points - 0.5
    norm = scale * jnp.sum(centred * centred, axis=0, keepdims=True)
    norms = [jnp.broadcast_to(part, points.shape) for part in split3(norm)]
    row = lax.broadcasted_iota(jnp.int32, points.shape, 0)
    if left:
        one, two, three = split3(centred)
        order = [one, one, two, one, two, three]
        base = 0
    else:
        one, two, three = split3((-2.0 * scale) * centred)
        order = [one, two, one, three, two, one]
        base = 3
    extra = jnp.where(row < 6, 1.0, 0.0)
    for index, part in enumerate(norms):
        extra = jnp.where(row == base + index, part, extra)
    return jnp.concatenate(order + [extra, jnp.zeros_like(extra)], axis=0).astype(bf16)


def as_lanes(column, offset):
    row = lax.broadcasted_iota(jnp.int32, (PROBES, 128), 0)
    lane = lax.broadcasted_iota(jnp.int32, (PROBES, 128), 1)
    return jnp.sum(jnp.where(lane == row + offset, column, 0.0), axis=0, keepdims=True)


def as_column(row_value, offset):
    row = lax.broadcasted_iota(jnp.int32, (PROBES, 128), 0)
    lane = lax.broadcasted_iota(jnp.int32, (PROBES, 128), 1)
    return jnp.sum(jnp.where(lane == row + offset, row_value, 0.0), axis=1, keepdims=True)


def live_lanes(count):
    lane = lax.broadcasted_iota(jnp.int32, (1, PTS), 1)
    return jnp.where(lane < count, 1.0, 0.0)


def nt_dot(left, right):
    return lax.dot_general(left, right, (((1,), (1,)), ((), ())), preferred_element_type=f32)


def prepare_kernel(coords, probes, precond, counts, inducing, centre_out, halo_out):
    points = coords[...]
    lane = lax.broadcasted_iota(jnp.int32, (FEAT, PTS), 1)
    short = lax.broadcasted_iota(jnp.int32, (FEAT, 128), 1)
    centre = jnp.zeros((FEAT, 128), f32)
    for index in range(16):
        picked = jnp.sum(
            jnp.where(lane == inducing[0, index], points, 0.0), axis=1, keepdims=True
        )
        centre = jnp.where(short == index, picked, centre)
    centre_out[...] = jnp.broadcast_to(centre[None], centre_out.shape)
    halo_out[:FEAT] = points
    halo_out[FEAT:] = precond[...] * (probes[...] * live_lanes(counts[0, 0]))


def prepare(coords, probes, precond, counts, inducing):
    return pl.pallas_call(
        prepare_kernel,
        out_shape=(
            jax.ShapeDtypeStruct((32, FEAT, 128), f32),
            jax.ShapeDtypeStruct((FEAT + PROBES, PTS), f32),
        ),
        in_specs=[VMEM, VMEM, VMEM, SMEM, SMEM],
        out_specs=(VMEM, VMEM),
        compiler_params=PARAMS,
        name="prepare",
    )(coords, probes, precond, counts, inducing)


def compact_kernel(parts, out):
    for tile in range(4):
        total = parts[8 * tile]
        for cell in range(1, 8):
            total = total + pltpu.roll(parts[8 * tile + cell], 16 * cell, 1)
        out[:, :, tile * 128 : (tile + 1) * 128] = jnp.broadcast_to(total[None], (8, FEAT, 128))


def compact(parts):
    return pl.pallas_call(
        compact_kernel,
        out_shape=jax.ShapeDtypeStruct((8, FEAT, CHUNK), f32),
        in_specs=[VMEM],
        out_specs=VMEM,
        compiler_params=PARAMS,
        name="compact",
    )(parts)


def rows_kernel(halo, centres, rows_out, sums_out, left, packed):
    @pl.when(pl.program_id(0) == 0)
    def _():
        left[...] = augmented(halo[:FEAT], -LOG2E / width_sq, True).astype(f32).T.astype(bf16)
        packed[...] = halo[FEAT:].astype(bf16)

    right = augmented(centres[0], -LOG2E / width_sq, False)
    power = jnp.dot(left[...], right, preferred_element_type=f32)
    rows = jnp.exp2(jnp.minimum(power, 0.0)).astype(bf16)
    rows_out[0] = rows
    sums = jnp.dot(packed[...], rows, preferred_element_type=f32)
    for part in range(4):
        sums_out[part] = sums[:, part * SHARE : (part + 1) * SHARE]


def make_rows(halo, centres):
    return pl.pallas_call(
        rows_kernel,
        grid=(CHUNKS,),
        out_shape=(
            jax.ShapeDtypeStruct((CHUNKS, PTS, CHUNK), bf16),
            jax.ShapeDtypeStruct((32, PROBES, SHARE), f32),
        ),
        in_specs=[
            pl.BlockSpec((FEAT + PROBES, PTS), lambda g: (0, 0)),
            pl.BlockSpec((1, FEAT, CHUNK), lambda g: (g, 0, 0)),
        ],
        out_specs=(
            pl.BlockSpec((1, PTS, CHUNK), lambda g: (g, 0, 0)),
            pl.BlockSpec((4, PROBES, SHARE), lambda g: (g, 0, 0)),
        ),
        scratch_shapes=[pltpu.VMEM((PTS, 64), bf16), pltpu.VMEM((PROBES, PTS), bf16)],
        compiler_params=PARAMS,
        name="rows",
    )(halo, centres)


def project_kernel(packed, rows, sums_out):
    sums = jnp.dot(packed[...], rows[0], preferred_element_type=f32)
    for part in range(4):
        sums_out[part] = sums[:, part * SHARE : (part + 1) * SHARE]


def project(packed, rows):
    height = packed.shape[0]
    return pl.pallas_call(
        project_kernel,
        grid=(CHUNKS,),
        out_shape=jax.ShapeDtypeStruct((32, height, SHARE), f32),
        in_specs=[
            pl.BlockSpec((height, PTS), lambda g: (0, 0)),
            pl.BlockSpec((1, PTS, CHUNK), lambda g: (g, 0, 0)),
        ],
        out_specs=pl.BlockSpec((4, height, SHARE), lambda g: (g, 0, 0)),
        compiler_params=PARAMS,
        name="project",
    )(packed, rows)


def fill_table(table, sources, first, last, dtype):
    for place_x in range(3):
        for place_y in range(3):
            for block in range(CAP):
                table[(place_x * 3 + place_y) * CAP + block] = sources[place_y][
                    place_x, first:last, block * BLOCK : (block + 1) * BLOCK
                ].astype(dtype)
    table[EMPTY] = jnp.zeros(table.shape[1:], dtype)


def tiles_kernel(codes, near_low, near_mid, near_high, tiles_out, sparse_out, points, values):
    block = pl.program_id(0)
    sources = (near_low, near_mid, near_high)

    @pl.when(block == 0)
    def _():
        fill_table(points, sources, 0, FEAT, f32)
        fill_table(values, sources, FEAT, FEAT + PROBES, bf16)

    scale = 1.0 / (support_radius * support_radius)
    own = augmented(points[4 * CAP + block], scale, True).astype(f32).T.astype(bf16)
    total = jnp.zeros((PROBES, BLOCK), f32)
    for entry in range(CAP):
        code = codes[block, entry]
        other = augmented(points[code], scale, False)
        square = jnp.maximum(jnp.dot(own, other, preferred_element_type=f32), 0.0)
        ratio = jnp.sqrt(square)
        remain = jnp.maximum(1.0 - ratio, 0.0)
        second = remain * remain
        fourth = second * second
        tile = (fourth * second * remain * (7.0 * ratio + 1.0)).astype(bf16)
        tiles_out[0, :, entry * BLOCK : (entry + 1) * BLOCK] = tile
        total = total + nt_dot(values[code], tile)
    sparse_out[...] = total


def make_tiles(codes, near_low, near_mid, near_high):
    whole = pl.BlockSpec((3, FEAT + PROBES, PTS), lambda b: (0, 0, 0))
    return pl.pallas_call(
        tiles_kernel,
        grid=(CAP,),
        out_shape=(
            jax.ShapeDtypeStruct((CAP, BLOCK, PTS), bf16),
            jax.ShapeDtypeStruct((PROBES, PTS), f32),
        ),
        in_specs=[SMEM, whole, whole, whole],
        out_specs=(
            pl.BlockSpec((1, BLOCK, PTS), lambda b: (b, 0, 0)),
            pl.BlockSpec((PROBES, BLOCK), lambda b: (0, b)),
        ),
        scratch_shapes=[
            pltpu.VMEM((EMPTY + 1, FEAT, BLOCK), f32),
            pltpu.VMEM((EMPTY + 1, PROBES, BLOCK), bf16),
        ],
        compiler_params=PARAMS,
        name="tiles",
    )(codes, near_low, near_mid, near_high)


def sparse_kernel(codes, near_low, near_mid, near_high, tiles, search, residual, precond, sparse_out, sums_out, values):
    fill_table(values, (near_low, near_mid, near_high), 0, PROBES, bf16)
    for block in range(CAP):
        total = jnp.zeros((PROBES, BLOCK), f32)
        for entry in range(CAP):
            total = total + nt_dot(
                values[codes[block, entry]],
                tiles[block, :, entry * BLOCK : (entry + 1) * BLOCK],
            )
        sparse_out[:, block * BLOCK : (block + 1) * BLOCK] = total
    field = search[...]
    left = residual[...]
    curve = jnp.sum(field * (field + sparse_out[...]), axis=1, keepdims=True)
    norm = jnp.sum(left * (precond[...] * left), axis=1, keepdims=True)
    lane = lax.broadcasted_iota(jnp.int32, (PROBES, 128), 1)
    sums_out[...] = jnp.where(lane == 0, curve, jnp.where(lane == 1, norm, 0.0))


def apply_tiles(codes, near_low, near_mid, near_high, tiles, search, residual, precond):
    return pl.pallas_call(
        sparse_kernel,
        out_shape=(
            jax.ShapeDtypeStruct((PROBES, PTS), f32),
            jax.ShapeDtypeStruct((PROBES, 128), f32),
        ),
        in_specs=[SMEM] + [VMEM] * 7,
        out_specs=(VMEM, VMEM),
        scratch_shapes=[pltpu.VMEM((EMPTY + 1, PROBES, BLOCK), bf16)],
        compiler_params=PARAMS,
        name="sparse",
    )(codes, near_low, near_mid, near_high, tiles, search, residual, precond)


def expand_step(weights, rows, total):
    @pl.when(pl.program_id(0) == 0)
    def _():
        total[...] = jnp.zeros_like(total)

    part = jnp.concatenate([weights[i, :PROBES] for i in range(4)], axis=1)
    total[...] += nt_dot(part, rows[0])


def image_kernel(weights, rows, counts, halo, sparse, precond, probes, image_out, sums_out, total):
    expand_step(weights, rows, total)

    @pl.when(pl.program_id(0) == CHUNKS - 1)
    def _():
        search = halo[FEAT:]
        image = live_lanes(counts[0, 0]) * (search + sparse[...] + total[...])
        image_out[...] = image
        scale = precond[...]
        norm = jnp.sum(search * (probes[...] * live_lanes(counts[0, 0])), axis=1, keepdims=True)
        curve = jnp.sum(search * image, axis=1, keepdims=True)
        square = jnp.sum(scale * image * image, axis=1, keepdims=True)
        sums_out[...] = as_lanes(norm, 0) + as_lanes(curve, 16) + as_lanes(square, 32)


def make_image(weights, rows, counts, halo, sparse, precond, probes):
    height = weights.shape[1]
    return pl.pallas_call(
        image_kernel,
        grid=(CHUNKS,),
        out_shape=(
            jax.ShapeDtypeStruct((PROBES, PTS), f32),
            jax.ShapeDtypeStruct((1, 128), f32),
        ),
        in_specs=[
            pl.BlockSpec((4, height, SHARE), lambda g: (g, 0, 0)),
            pl.BlockSpec((1, PTS, CHUNK), lambda g: (g, 0, 0)),
            SMEM,
            pl.BlockSpec((FEAT + PROBES, PTS), lambda g: (0, 0)),
            pl.BlockSpec((PROBES, PTS), lambda g: (0, 0)),
            pl.BlockSpec((1, PTS), lambda g: (0, 0)),
            pl.BlockSpec((PROBES, PTS), lambda g: (0, 0)),
        ],
        out_specs=(
            pl.BlockSpec((PROBES, PTS), lambda g: (0, 0)),
            pl.BlockSpec((1, 128), lambda g: (0, 0)),
        ),
        scratch_shapes=[pltpu.VMEM((PROBES, PTS), f32)],
        compiler_params=PARAMS,
        name="image",
    )(weights, rows, counts, halo, sparse, precond, probes)


def update_kernel(sums, halo, probes, precond, counts, image, residual_out, search_out, packed_out, solution_out):
    rz_now = as_column(sums[...], 0)
    alpha = rz_now / as_column(sums[...], 16)
    rz_next = alpha * alpha * as_column(sums[...], 32) - rz_now
    search = halo[FEAT:]
    solution_out[...] = alpha * search
    residual = probes[...] * live_lanes(counts[0, 0]) - alpha * image[...]
    residual_out[...] = residual
    following = precond[...] * residual + (rz_next / rz_now) * search
    search_out[...] = following
    rounded = following.astype(bf16)
    packed_out[:PROBES] = rounded
    packed_out[PROBES:] = (following - rounded.astype(f32)).astype(bf16)


def update(sums, halo, probes, precond, counts, image):
    field = jax.ShapeDtypeStruct((PROBES, PTS), f32)
    return pl.pallas_call(
        update_kernel,
        out_shape=(field, field, jax.ShapeDtypeStruct((2 * PROBES, PTS), bf16), field),
        in_specs=[VMEM, VMEM, VMEM, VMEM, SMEM, VMEM],
        out_specs=(VMEM,) * 4,
        compiler_params=PARAMS,
        name="update",
    )(sums, halo, probes, precond, counts, image)


def finish_kernel(weights, rows, every, counts, search, sparse, residual, solution, sums, solution_out, residual_out, total):
    expand_step(weights, rows, total)

    @pl.when(pl.program_id(0) == CHUNKS - 1)
    def _():
        field = search[...]
        image = live_lanes(counts[0, 0]) * (field + sparse[...] + total[...])
        dots = jnp.sum(every[:, PROBES:].astype(f32), axis=0)
        dot = jnp.sum(dots, axis=1, keepdims=True)
        totals = sums[...]
        curve = totals[:, 0:1] + dot
        alpha = totals[:, 1:2] / curve
        solution_out[...] = solution[...] + alpha * field
        residual_out[...] = residual[...] - alpha * image


def finish(weights, rows, counts, search, sparse, residual, solution, sums):
    field = jax.ShapeDtypeStruct((PROBES, PTS), f32)
    still = pl.BlockSpec((PROBES, PTS), lambda g: (0, 0))
    height = weights.shape[1]
    return pl.pallas_call(
        finish_kernel,
        grid=(CHUNKS,),
        out_shape=(field, field),
        in_specs=[
            pl.BlockSpec((4, height, SHARE), lambda g: (g, 0, 0)),
            pl.BlockSpec((1, PTS, CHUNK), lambda g: (g, 0, 0)),
            pl.BlockSpec((32, height, SHARE), lambda g: (0, 0, 0)),
            SMEM,
            still,
            still,
            still,
            still,
            pl.BlockSpec((PROBES, 128), lambda g: (0, 0)),
        ],
        out_specs=(still, still),
        scratch_shapes=[pltpu.VMEM((PROBES, PTS), f32)],
        compiler_params=PARAMS,
        name="finish",
    )(weights, rows, weights, counts, search, sparse, residual, solution, sums)


def on_device(coords, probes, precond, counts, neighbours, inducing, factor):
    quad = lax.axis_index("yl") * 2 + lax.axis_index("c")
    points = coords[0, 0]
    sides = probes[0, 0]
    scaling = precond[0]
    codes = neighbours[0, 0]

    centre_parts, halo = prepare(points, sides, scaling, counts, inducing[0])
    centres = exchange(compact(exchange(centre_parts, CELLS)), "z")

    columns = factor.shape[1] // 4
    factor_cols = lax.dynamic_slice_in_dim(factor, quad * columns, columns, 1)
    factor_part = jnp.concatenate(
        [
            lax.dynamic_slice_in_dim(factor_cols, (quad ^ step) * SHARE, SHARE, 0)
            for step in range(4)
        ],
        axis=0,
    )

    def surround(value):
        low, high = beside(value, GX)
        column = jnp.stack([low, value, high])
        left, right = beside(column, GY)
        return left, column, right

    near = surround(halo)
    rows, parts = make_rows(halo, centres)
    tiles, sparse = make_tiles(codes, *near)

    def weights_of(parts, sums):
        share = jnp.sum(exchange(parts, PLANE), axis=0)
        if sums is not None:
            share = jnp.concatenate([share, sums], axis=0)
        share = jnp.sum(spread(share, "z"), axis=0)
        own = share[:PROBES]
        quad_shares = jnp.concatenate(
            [own] + [quad_partner(own, step) for step in (1, 2, 3)], axis=1
        )
        terms = jnp.dot(
            quad_shares, factor_part, precision=lax.Precision.HIGHEST, preferred_element_type=f32
        )
        if sums is not None:
            terms = jnp.concatenate([terms, share[2 * PROBES :]], axis=1)
        coeffs = jnp.sum(spread(terms, GY), axis=0)
        terms = lax.dot_general(
            coeffs[:, :columns],
            factor_part,
            (((1,), (1,)), ((), ())),
            precision=lax.Precision.HIGHEST,
            preferred_element_type=f32,
        )
        totals = None
        if sums is not None:
            totals = coeffs[:, columns:]
        weights = terms[:, :SHARE]
        sent = totals
        for step in (1, 2, 3):
            part = terms[:, step * SHARE : (step + 1) * SHARE]
            if sums is None:
                weights = weights + quad_partner(part, step)
            else:
                got = quad_partner(jnp.concatenate([part, sent], axis=1), step)
                weights = weights + got[:, :SHARE]
                totals = totals + got[:, SHARE:]
        weights = weights.astype(bf16)
        if sums is not None:
            unrounded = share[:PROBES] + share[PROBES : 2 * PROBES]
            dot = jnp.sum(weights.astype(f32) * unrounded, axis=1, keepdims=True)
            first = lax.reduce_precision(dot, 8, 7)
            second = lax.reduce_precision(dot - first, 8, 7)
            third = dot - first - second
            lane = lax.broadcasted_iota(jnp.int32, (PROBES, SHARE), 1)
            row = jnp.where(
                lane == 0, first, jnp.where(lane == 1, second, jnp.where(lane == 2, third, 0.0))
            )
            weights = jnp.concatenate([weights, row.astype(bf16)], axis=0)
        return spread(weights, PLANE), totals

    weights, _ = weights_of(parts, None)
    image, row = make_image(weights, rows, counts, halo, sparse, scaling, sides)
    row = jnp.sum(spread(row, CELLS), axis=0)
    row = jnp.sum(spread(row, "z"), axis=0)
    residual, search, packed, solution = update(row, halo, sides, scaling, counts, image)

    near = surround(packed[:PROBES])
    parts = project(packed, rows)
    sparse, sums = apply_tiles(codes, *near, tiles, search, residual, scaling)
    weights, totals = weights_of(parts, sums)
    solution, residual = finish(
        weights, rows, counts, search, sparse, residual, solution, totals
    )
    return (solution[None, None], residual[None, None])


def solution(mesh):
    fine = Mesh(mesh.devices.reshape(8, 2, 2, 2, 4), ALL)
    placed = (
        P(GX, GY, None, None),
        P(GX, GY, None, None),
        P(GX, GY, None),
        P(GX, GY),
        P(GX, GY, None, None),
        P(GX, GY, None),
        P(GY, None),
    )
    return jax.shard_map(
        on_device,
        mesh=fine,
        in_specs=placed,
        out_specs=(P(GX, GY, None, None), P(GX, GY, None, None)),
        check_vma=False,
    )
```

time: 341 us -> 254 us (0.74)
  starting transfers between devices: 112 us -> 65.4 us
  other arithmetic: 37.1 us -> 0.5 us
  matrix products: 36.5 us -> 7.24 us
  Pallas kernels: 0 us -> 25.7 us
  local copies, waits for them, and re-layouts: 34.5 us -> 21.8 us
  waiting for transfers between devices: 25.9 us -> 36.1 us
  blocking collectives: 89.7 us -> 94.1 us
    all_to_all x8 -> x5, starting transfers between devices: 63.9 us -> 29.2 us  [exchange(): return lax.all_to_all(parts, axes, 0, 0, tiled=True)]
    dot_general x12 -> x4, matrix products: 36.5 us -> 7.24 us  [the longest x2 3.67 us: weights_of(): lax.dot_general(coeffs[:, :columns], factor_part, (((1,), (1,)), ((), ())...]
    pallas_call x0 -> x9, Pallas kernels: none -> 25.7 us  [the longest x1 7.19 us: make_tiles(): pl.pallas_call(tiles_kernel, grid=(CAP,), out_shape=(jax.ShapeDtypeStruct...]
    dynamic_update_slice x2 -> x0, other arithmetic: 18.7 us -> none  [on_device(): lax.map(lambda portion: inducing_rows(portion, centres), grouped)]
    ppermute x12 -> x8, starting transfers between devices: 35.2 us -> 19.4 us  [the longest x4 12.1 us: beside(): lax.ppermute(value, axes, forward)]
    unnamed x20 -> x38, local copies, waits for them, and re-layouts: 3.82 us -> 16.4 us
    dot_general x1 -> x0, local copies, waits for them, and re-layouts: 12 us -> none  [on_device(): terms = jnp.dot(packed, kernel_rows, preferred_element_type=jnp.float32)]
    convert_element_type x6 -> x2, other arithmetic: 11.3 us -> 0.09 us  [the longest x1 0.08 us: weights_of(): weights = jnp.concatenate([weights, row.astype(bf16)], axis=0)]
  transfers between devices with their start and end apart: 32 -> 25, of which waited for: 15 -> 10; matrix products, arithmetic and copies ran while one was open for 23% -> 2% of each run, Pallas kernels for 0% -> 4%
where the time goes in v2:
time: 254 us; the launch traced here: 253 us
  blocking collectives  94.1 us (37%)
  starting transfers between devices  65.4 us (26%)
  waiting for transfers between devices  36.1 us (14%)
  Pallas kernels  25.7 us (10%)
  local copies, waits for them, and re-layouts  21.8 us (9%)
  matrix products  7.24 us (3%)
    all_to_all x7, blocking collectives, exchange(): return lax.all_to_all(parts, axes, 0, 0, tiled=True)  94.1 us
    all_to_all x5, starting transfers between devices, exchange(): return lax.all_to_all(parts, axes, 0, 0, tiled=True)  29.2 us
    all_to_all x5, waiting for transfers between devices, exchange(): return lax.all_to_all(parts, axes, 0, 0, tiled=True)  26.2 us
    ppermute x12, starting transfers between devices, quad_partner(): return lax.ppermute(value, ('yl', 'c'), pairs)  16.9 us
    unnamed x38, local copies, waits for them, and re-layouts  16.4 us
    ppermute x4, starting transfers between devices, beside(): lax.ppermute(value, axes, forward)  12.1 us
    ppermute x4, starting transfers between devices, beside(): lax.ppermute(value, axes, backward)  7.26 us
    pallas_call x1, Pallas kernels, make_tiles(): pl.pallas_call(tiles_kernel, grid=(CAP,), out_shape=(jax.ShapeDtypeStruct...  7.19 us
  transfers between devices with their start and end apart: 25, of which 10 were waited for; matrix products, arithmetic and copies ran while one was open for 2% of the time, Pallas kernels for 4%

profile of v2, /device:TPU:1, one launch (start us, length us, event | category | flops | bytes accessed | tf_op | source)
XLA Modules:
  0.0 252.7 jit_solution(2206074198927170252)
XLA Ops:
  1.3 0.8 copy-done.4
  2.1 0.7 copy-done.6
  2.8 0.8 copy-done.8
  3.6 0.7 copy-done.10
  4.2 0.7 prepare.1
  4.9 16.1 %all_to_all.60.parts = f32[32,8,128]{2,1,0:T(8,128)S(1)} all-to-all(f32[32,8,128]{2,1,0:T(8,128)S(1)} %get-tuple-element.19), channel_id=1, replica_groups=mesh['z'=8,'yl'=2,'c'=2,'yh'=2,'x'=4] {'yl','c','yh','x'}, dimensions={0} | all-to-all | bytes 262144 | tf_op jit(solution)/shard_map/all_to_all | solution.py:36
  21.1 15.8 %all_to_all.61.centres = f32[8,8,512]{2,1,0:T(8,128)S(1)} all-to-all(f32[8,8,512]{2,1,0:T(8,128)S(1)} %compact.1), channel_id=1, replica_groups=mesh['z'=8,'yl'=2,'c'=2,'yh'=2,'x'=4] {'z'}, dimensions={0} | all-to-all | bytes 262144 | tf_op jit(solution)/shard_map/all_to_all | solution.py:36
  36.8 4.5 %rows.1 = (bf16[8,1024,512]{2,1,0:T(8,128)(2,1)S(1)}, f32[32,16,128]{2,1,0:T(8,128)S(1)}) custom-call(f32[24,1024]{1,0:T(8,128)S(1)} %get-tuple-element.18.halo, f32[8,8,512]{2,1,0:T(8,128)S(1)} %all_to_all.61.centres), custom_call_target="tpu_custom_call" | custom-call | tf_op jit(solution)/shard_map/rows/pallas_call | solution.py:167
  41.3 3.3 %copy-done = bf16[8,1024,512]{2,1,0:T(8,128)(2,1)} copy-done((bf16[8,1024,512]{2,1,0:T(8,128)(2,1)}, bf16[8,1024,512]{2,1,0:T(8,128)(2,1)S(1)}, u32[]{:S(2)}) %copy-start) | copy-done | bytes 8388632
  44.6 14.4 %all_to_all.62 = f32[32,16,128]{2,1,0:T(8,128)S(1)} all-to-all(f32[32,16,128]{2,1,0:T(8,128)S(1)} %get-tuple-element.20), channel_id=1, replica_groups=mesh['z'=8,'yl'=2,'c'=2,'yh'=2,'x'=4] {'yh','x','yl','c'}, dimensions={0} | all-to-all | bytes 524288 | tf_op jit(solution)/shard_map/all_to_all | solution.py:36
  59.0 0.6 broadcast_in_dim.47
  59.7 3.4 %all-to-all-start.3 = ((f32[8,16,128]{2,1,0:T(8,128)}), f32[8,16,128]{2,1,0:T(8,128)S(1)}, u32[]{:S(2)}, u32[]{:S(2)}) async-start(f32[8,16,128]{2,1,0:T(8,128)} %broadcast_in_dim.47), calls=%async_computation.3 | async-start | bytes 131072 | tf_op jit(solution)/shard_map/all_to_all | solution.py:36
  63.0 7.2 %all-to-all-done.3 = f32[8,16,128]{2,1,0:T(8,128)S(1)} async-done(((f32[8,16,128]{2,1,0:T(8,128)}), f32[8,16,128]{2,1,0:T(8,128)S(1)}, u32[]{:S(2)}, u32[]{:S(2)}) %all-to-all-start.3) | async-done | bytes 65568 | tf_op jit(solution)/shard_map/all_to_all | solution.py:36
  70.3 2.2 collective-permute-start.2
  72.4 1.3 collective-permute-start.1
  73.7 2.2 fusion.28
  76.0 1.1 fusion.2
  77.1 0.8 broadcast_in_dim.48
  78.0 3.5 %all-to-all-start.4 = ((f32[8,16,1024]{2,1,0:T(8,128)}), f32[8,16,1024]{2,1,0:T(8,128)S(1)}, u32[]{:S(2)}, u32[]{:S(2)}) async-start(f32[8,16,1024]{2,1,0:T(8,128)} %broadcast_in_dim.48), calls=%async_computation.4 | async-start | bytes 1048576 | tf_op jit(solution)/shard_map/all_to_all | solution.py:36
  81.5 2.4 collective-permute-start.7
  83.9 3.1 %collective-permute-start.6 = (f32[24,1024]{1,0:T(8,128)S(1)}, f32[24,1024]{1,0:T(8,128)S(1)}, u32[]{:S(2)}, u32[]{:S(2)}) collective-permute-start(f32[24,1024]{1,0:T(8,128)S(1)} %get-tuple-element.18.halo), channel_id=1, source_target_pairs={{0,8},{8,16},{16,24},{24,32},{32,40},{40,48},{48,56},{56,64},{64,7... | collective-permute-start | bytes 294920 | tf_op jit(solution)/shard_map/ppermute | solution.py:53
  87.1 6.1 %all-to-all-done.4 = f32[8,16,1024]{2,1,0:T(8,128)S(1)} async-done(((f32[8,16,1024]{2,1,0:T(8,128)}), f32[8,16,1024]{2,1,0:T(8,128)S(1)}, u32[]{:S(2)}, u32[]{:S(2)}) %all-to-all-start.4) | async-done | bytes 524320 | tf_op jit(solution)/shard_map/all_to_all | solution.py:36
  93.3 1.8 fusion.26
  95.1 1.2 collective-permute-start.5
  96.3 1.2 collective-permute-start.4
  97.5 2.4 collective-permute-start.8
  100.0 1.3 collective-permute-start.9
  101.3 0.7 broadcast_in_dim.84
  102.0 8.2 %all-to-all-start.5 = ((bf16[32,16,128]{2,1,0:T(8,128)(2,1)}), bf16[32,16,128]{2,1,0:T(8,128)(2,1)S(1)}, u32[]{:S(2)}, u32[]{:S(2)}) async-start(bf16[32,16,128]{2,1,0:T(8,128)(2,1)} %broadcast_in_dim.84), calls=%async_computation.5 | async-start | bytes 262144 | tf_op jit(solution)/shard_map/all_to_all | solution.py:36
  110.3 7.2 %tiles.1 = (bf16[8,128,1024]{2,1,0:T(8,128)(2,1)S(1)}, f32[16,1024]{1,0:T(8,128)S(1)}) custom-call(s32[8,8]{1,0:T(8,128)S(1)} %bitcast.28, f32[3,24,1024]{2,1,0:T(8,128)S(1)} %collective-permute-done.8.near_low, f32[3,24,1024]{2,1,0:T(8,128)S(1)} %pad_maximum_fusion.1.near_mid, f32[3,24,1024]{2,1,0:T(8,128)S(1)} %collective-permute-done.9.near_high), custom_call_target="tpu_custom_call" | custom-call | tf_op jit(solution)/shard_map/tiles/pallas_call | solution.py:248
  117.4 0.5 all-to-all-done.5.weights
  117.9 3.4 %copy-done.1 = bf16[8,1024,512]{2,1,0:T(8,128)(2,1)S(1)} copy-done((bf16[8,1024,512]{2,1,0:T(8,128)(2,1)S(1)}, bf16[8,1024,512]{2,1,0:T(8,128)(2,1)}, u32[]{:S(2)}) %copy-start.1) | copy-done | bytes 8388632
  121.3 3.2 %image.1 = (f32[16,1024]{1,0:T(8,128)S(1)}, f32[1,128]{1,0:T(1,128)S(1)}) custom-call(bf16[32,16,128]{2,1,0:T(8,128)(2,1)S(1)} %all-to-all-done.5.weights, bf16[8,1024,512]{2,1,0:T(8,128)(2,1)S(1)} %copy-done.1, s32[1,1]{1,0:T(1,128)S(6)} %copy.11.counts, f32[24,1024]{1,0:T(8,128)S(1)} %get-tuple-element.18.halo, f32[16,1024]{1,0:T(8,128)S(1)} %get-tuple-element.22.sparse, ...), custom_call_target="tpu_custom_call" | custom-call | tf_op jit(solution)/shard_map/image/pallas_call | solution.py:328
  124.6 14.9 %all_to_all.63 = f32[32,1,128]{2,1,0:T(1,128)S(1)} all-to-all(f32[32,1,128]{2,1,0:T(1,128)S(1)} %broadcast_in_dim.86), channel_id=1, replica_groups=mesh['z'=8,'yl'=2,'c'=2,'yh'=2,'x'=4] {'yl','c','yh','x'}, dimensions={0} | all-to-all | bytes 32768 | tf_op jit(solution)/shard_map/all_to_all | solution.py:36
  139.5 8.9 %all_to_all.64 = f32[8,1,128]{2,1,0:T(1,128)S(1)} all-to-all(f32[8,1,128]{2,1,0:T(1,128)S(1)} %broadcast_in_dim.87), channel_id=1, replica_groups=mesh['z'=8,'yl'=2,'c'=2,'yh'=2,'x'=4] {'z'}, dimensions={0} | all-to-all | bytes 8192 | tf_op jit(solution)/shard_map/all_to_all | solution.py:36
  148.5 3.4 %copy-done.2 = bf16[8,1024,512]{2,1,0:T(8,128)(2,1)S(1)} copy-done((bf16[8,1024,512]{2,1,0:T(8,128)(2,1)S(1)}, bf16[8,1024,512]{2,1,0:T(8,128)(2,1)}, u32[]{:S(2)}) %copy-start.2) | copy-done | bytes 8388632
  151.9 3.9 %project.1 = f32[32,32,128]{2,1,0:T(8,128)} custom-call(bf16[32,1024]{1,0:T(8,128)(2,1)S(1)} %get-tuple-element.25.packed, bf16[8,1024,512]{2,1,0:T(8,128)(2,1)S(1)} %copy-done.2), custom_call_target="tpu_custom_call" | custom-call | tf_op jit(solution)/shard_map/project/pallas_call | solution.py:196
  155.8 5.6 %all-to-all-start.8 = ((f32[32,32,128]{2,1,0:T(8,128)}), f32[32,32,128]{2,1,0:T(8,128)S(1)}, u32[]{:S(2)}, u32[]{:S(2)}) async-start(f32[32,32,128]{2,1,0:T(8,128)} %project.1), calls=%async_computation.8 | async-start | bytes 1048576 | tf_op jit(solution)/shard_map/all_to_all | solution.py:36
  161.4 2.3 collective-permute-start.11
  163.7 3.3 %collective-permute-start.10 = (bf16[16,1024]{1,0:T(8,128)(2,1)S(1)}, bf16[16,1024]{1,0:T(8,128)(2,1)S(1)}, u32[]{:S(2)}, u32[]{:S(2)}) collective-permute-start(bf16[16,1024]{1,0:T(8,128)(2,1)S(1)} %get-tuple-element.41), channel_id=1, source_target_pairs={{0,8},{8,16},{16,24},{24,32},{32,40},{40,48},{48,56},{56,64},{64,7... | collective-permute-start | bytes 98312 | tf_op jit(solution)/shard_map/ppermute | solution.py:53
  167.0 2.1 collective-permute-done.11
  169.1 3.2 %collective-permute-start.12 = (bf16[3,16,1024]{2,1,0:T(8,128)(2,1)S(1)}, bf16[3,16,1024]{2,1,0:T(8,128)(2,1)S(1)}, u32[]{:S(2)}, u32[]{:S(2)}) collective-permute-start(bf16[3,16,1024]{2,1,0:T(8,128)(2,1)S(1)} %pad_maximum_fusion.2.near_mid), channel_id=1, source_target_pairs={{0,1},{1,2},{2,3},{3,4},{4,5},{5,6},{6,7},{8,9},{9,10},{10,11},{11... | collective-permute-start | bytes 294920 | tf_op jit(solution)/shard_map/ppermute | solution.py:53
  172.3 1.3 collective-permute-start.13
  173.6 0.3 collective-permute-done.12.near_low
  173.9 4.2 %collective-permute-done.13.near_high = bf16[3,16,1024]{2,1,0:T(8,128)(2,1)S(1)} collective-permute-done((bf16[3,16,1024]{2,1,0:T(8,128)(2,1)S(1)}, bf16[3,16,1024]{2,1,0:T(8,128)(2,1)S(1)}, u32[]{:S(2)}, u32[]{:S(2)}) %collective-permute-start.13) | collective-permute-done | bytes 98336 | tf_op jit(solution)/shard_map/ppermute | solution.py:53
  178.1 1.9 sparse.1
  180.1 11.0 %all_to_all.65 = f32[8,48,128]{2,1,0:T(8,128)S(1)} all-to-all(f32[8,48,128]{2,1,0:T(8,128)S(1)} %broadcast_in_dim.88), channel_id=1, replica_groups=mesh['z'=8,'yl'=2,'c'=2,'yh'=2,'x'=4] {'z'}, dimensions={0} | all-to-all | bytes 393216 | tf_op jit(solution)/shard_map/all_to_all | solution.py:36
  191.1 4.7 %collective-permute-start.16 = (f32[16,128]{1,0:T(8,128)S(1)}, f32[16,128]{1,0:T(8,128)S(1)}, u32[]{:S(2)}, u32[]{:S(2)}) collective-permute-start(f32[16,128]{1,0:T(8,128)S(1)} %get-tuple-element.49), channel_id=1, source_target_pairs={{0,24},{8,16},{16,8},{24,0},{1,25},{9,17},{17,9},{25,1},{2,26},{10... | collective-permute-start | bytes 24584 | tf_op jit(solution)/shard_map/ppermute | solution.py:46
  195.8 3.9 %collective-permute-start.15 = (f32[16,128]{1,0:T(8,128)S(1)}, f32[16,128]{1,0:T(8,128)S(1)}, u32[]{:S(2)}, u32[]{:S(2)}) collective-permute-start(f32[16,128]{1,0:T(8,128)S(1)} %get-tuple-element.49), channel_id=1, source_target_pairs={{0,16},{8,24},{16,0},{24,8},{1,17},{9,25},{17,1},{25,9},{2,18},{10... | collective-permute-start | bytes 24584 | tf_op jit(solution)/shard_map/ppermute | solution.py:46
  199.7 1.3 collective-permute-done.15
  201.1 2.5 fusion.10
  203.6 0.9 broadcast_in_dim.89
  204.4 8.6 %all-to-all-start.10 = ((f32[8,16,1152]{2,1,0:T(8,128)}), f32[8,16,1152]{2,1,0:T(8,128)S(1)}, u32[]{:S(2)}, u32[]{:S(2)}) async-start(f32[8,16,1152]{2,1,0:T(8,128)} %broadcast_in_dim.89), calls=%async_computation.10 | async-start | bytes 1179648 | tf_op jit(solution)/shard_map/all_to_all | solution.py:36
  213.0 12.4 %all-to-all-done.10 = f32[8,16,1152]{2,1,0:T(8,128)S(1)} async-done(((f32[8,16,1152]{2,1,0:T(8,128)}), f32[8,16,1152]{2,1,0:T(8,128)S(1)}, u32[]{:S(2)}, u32[]{:S(2)}) %all-to-all-start.10) | async-done | bytes 589856 | tf_op jit(solution)/shard_map/all_to_all | solution.py:36
  225.5 1.8 fusion
  227.3 2.0 collective-permute-start.19
  229.3 0.3 collective-permute-start.18
  229.6 0.2 collective-permute-start.17
  229.8 1.4 collective-permute-done.19
  231.2 0.7 collective-permute-done.18
  231.9 0.1 fusion.19
  232.2 13.1 %all_to_all.66.weights.every = bf16[32,32,128]{2,1,0:T(8,128)(2,1)S(1)} all-to-all(bf16[32,32,128]{2,1,0:T(8,128)(2,1)S(1)} %broadcast_in_dim.94), channel_id=1, replica_groups=mesh['z'=8,'yl'=2,'c'=2,'yh'=2,'x'=4] {'yh','x','yl','c'}, dimensions={0} | all-to-all | bytes 524288 | tf_op jit(solution)/shard_map/all_to_all | solution.py:36
  245.3 3.4 %copy-done.3 = bf16[8,1024,512]{2,1,0:T(8,128)(2,1)S(1)} copy-done((bf16[8,1024,512]{2,1,0:T(8,128)(2,1)S(1)}, bf16[8,1024,512]{2,1,0:T(8,128)(2,1)}, u32[]{:S(2)}) %copy-start.3) | copy-done | bytes 8388632
  248.7 4.0 %finish.1 = (f32[16,1024]{1,0:T(8,128)}, f32[16,1024]{1,0:T(8,128)}) custom-call(bf16[32,32,128]{2,1,0:T(8,128)(2,1)S(1)} %all_to_all.66.weights.every, bf16[8,1024,512]{2,1,0:T(8,128)(2,1)S(1)} %copy-done.3, bf16[32,32,128]{2,1,0:T(8,128)(2,1)S(1)} %all_to_all.66.weights.every, s32[1,1]{1,0:T(1,128)S(6)} %copy.11.counts, ...), custom_call_target="tpu_custom_call" | custom-call | tf_op jit(solution)/shard_map/finish/pallas_call | solution.py:401
  (78 shorter events, 0.8 us)
Async XLA Ops:
  1.3 0.8 copy-start.4
  2.1 0.7 copy-start.6
  2.8 0.8 copy-start.8
  3.6 0.7 copy-start.10
  41.3 3.3 %copy-start = (bf16[8,1024,512]{2,1,0:T(8,128)(2,1)}, bf16[8,1024,512]{2,1,0:T(8,128)(2,1)S(1)}, u32[]{:S(2)}) copy-start(bf16[8,1024,512]{2,1,0:T(8,128)(2,1)S(1)} %get-tuple-element.21.rows) | copy-start | bytes 25165828
  59.7 10.6 %all-to-all-start.3 = ((f32[8,16,128]{2,1,0:T(8,128)}), f32[8,16,128]{2,1,0:T(8,128)S(1)}, u32[]{:S(2)}, u32[]{:S(2)}) async-start(f32[8,16,128]{2,1,0:T(8,128)} %broadcast_in_dim.47), calls=%async_computation.3 | async-start | bytes 131072 | tf_op jit(solution)/shard_map/all_to_all | solution.py:36
  70.3 5.7 %collective-permute-start.2 = (f32[16,128]{1,0:T(8,128)S(1)}, f32[16,128]{1,0:T(8,128)S(1)}, u32[]{:S(2)}, u32[]{:S(2)}) collective-permute-start(f32[16,128]{1,0:T(8,128)S(1)} %reduce_sum.84), channel_id=1, source_target_pairs={{0,24},{8,16},{16,8},{24,0},{1,25},{9,17},{17,9},{25,1},{2,26},{10... | collective-permute-start | bytes 24584 | tf_op jit(solution)/shard_map/ppermute | solution.py:46
  72.4 3.6 %collective-permute-start.1 = (f32[16,128]{1,0:T(8,128)S(1)}, f32[16,128]{1,0:T(8,128)S(1)}, u32[]{:S(2)}, u32[]{:S(2)}) collective-permute-start(f32[16,128]{1,0:T(8,128)S(1)} %reduce_sum.84), channel_id=1, source_target_pairs={{0,16},{8,24},{16,0},{24,8},{1,17},{9,25},{17,1},{25,9},{2,18},{10... | collective-permute-start | bytes 24584 | tf_op jit(solution)/shard_map/ppermute | solution.py:46
  73.7 2.3 collective-permute-start
  75.9 17.3 %copy-start.11 = (f32[128,1024]{1,0:T(8,128)}, f32[128,1024]{1,0:T(8,128)S(1)}, u32[]{:S(2)}) copy-start(f32[128,1024]{1,0:T(8,128)S(1)} %get-tuple-element.36) | copy-start | bytes 1572868
  76.0 17.3 %copy-start.13 = (f32[128,1024]{1,0:T(8,128)}, f32[128,1024]{1,0:T(8,128)S(1)}, u32[]{:S(2)}) copy-start(f32[128,1024]{1,0:T(8,128)S(1)} %get-tuple-element.37) | copy-start | bytes 1572868
  76.0 17.3 %copy-start.15 = (f32[128,1024]{1,0:T(8,128)}, f32[128,1024]{1,0:T(8,128)S(1)}, u32[]{:S(2)}) copy-start(f32[128,1024]{1,0:T(8,128)S(1)} %get-tuple-element.38) | copy-start | bytes 1572868
  76.0 17.3 %copy-start.17 = (f32[128,1024]{1,0:T(8,128)}, f32[128,1024]{1,0:T(8,128)S(1)}, u32[]{:S(2)}) copy-start(f32[128,1024]{1,0:T(8,128)S(1)} %get-tuple-element.39) | copy-start | bytes 1572868
  78.0 15.2 %all-to-all-start.4 = ((f32[8,16,1024]{2,1,0:T(8,128)}), f32[8,16,1024]{2,1,0:T(8,128)S(1)}, u32[]{:S(2)}, u32[]{:S(2)}) async-start(f32[8,16,1024]{2,1,0:T(8,128)} %broadcast_in_dim.48), calls=%async_computation.4 | async-start | bytes 1048576 | tf_op jit(solution)/shard_map/all_to_all | solution.py:36
  81.5 16.0 %collective-permute-start.7 = (f32[24,1024]{1,0:T(8,128)S(1)}, f32[24,1024]{1,0:T(8,128)S(1)}, u32[]{:S(2)}, u32[]{:S(2)}) collective-permute-start(f32[24,1024]{1,0:T(8,128)S(1)} %get-tuple-element.18.halo), channel_id=1, source_target_pairs={{8,0},{16,8},{24,16},{32,24},{40,32},{48,40},{56,48},{64,56},{72,6... | collective-permute-start | bytes 294920 | tf_op jit(solution)/shard_map/ppermute | solution.py:53
  83.9 13.6 %collective-permute-start.6 = (f32[24,1024]{1,0:T(8,128)S(1)}, f32[24,1024]{1,0:T(8,128)S(1)}, u32[]{:S(2)}, u32[]{:S(2)}) collective-permute-start(f32[24,1024]{1,0:T(8,128)S(1)} %get-tuple-element.18.halo), channel_id=1, source_target_pairs={{0,8},{8,16},{16,24},{24,32},{32,40},{40,48},{48,56},{56,64},{64,7... | collective-permute-start | bytes 294920 | tf_op jit(solution)/shard_map/ppermute | solution.py:53
  93.2 17.0 %copy-start.9 = (s32[1,1,8,8]{3,2,1,0:T(8,128)S(1)}, s32[1,1,8,8]{3,2,1,0:T(8,128)}, u32[]{:S(2)}) copy-start(s32[1,1,8,8]{3,2,1,0:T(8,128)} %param.11) | copy-start | bytes 772
  93.3 24.7 %copy-start.5 = (f32[1,1,16,1024]{3,2,1,0:T(8,128)S(1)}, f32[1,1,16,1024]{3,2,1,0:T(8,128)}, u32[]{:S(2)}) copy-start(f32[1,1,16,1024]{3,2,1,0:T(8,128)} %param.8) | copy-start | bytes 196612
  93.3 24.6 %copy-start.7 = (f32[1,1,1024]{2,1,0:T(1,128)S(1)}, f32[1,1,1024]{2,1,0:T(1,128)}, u32[]{:S(2)}) copy-start(f32[1,1,1024]{2,1,0:T(1,128)} %param.9) | copy-start | bytes 12292
  95.1 6.1 %collective-permute-start.5 = (f32[16,128]{1,0:T(8,128)S(1)}, f32[16,128]{1,0:T(8,128)S(1)}, u32[]{:S(2)}, u32[]{:S(2)}) collective-permute-start(f32[16,128]{1,0:T(8,128)S(1)} %get-tuple-element.47), channel_id=1, source_target_pairs={{0,24},{8,16},{16,8},{24,0},{1,25},{9,17},{17,9},{25,1},{2,26},{10... | collective-permute-start | bytes 24584 | tf_op jit(solution)/shard_map/ppermute | solution.py:46
  96.3 5.0 %collective-permute-start.4 = (f32[16,128]{1,0:T(8,128)S(1)}, f32[16,128]{1,0:T(8,128)S(1)}, u32[]{:S(2)}, u32[]{:S(2)}) collective-permute-start(f32[16,128]{1,0:T(8,128)S(1)} %get-tuple-element.48), channel_id=1, source_target_pairs={{0,16},{8,24},{16,0},{24,8},{1,17},{9,25},{17,1},{25,9},{2,18},{10... | collective-permute-start | bytes 24584 | tf_op jit(solution)/shard_map/ppermute | solution.py:46
  97.5 3.8 %collective-permute-start.3 = (f32[16,128]{1,0:T(8,128)S(1)}, f32[16,128]{1,0:T(8,128)S(1)}, u32[]{:S(2)}, u32[]{:S(2)}) collective-permute-start(f32[16,128]{1,0:T(8,128)S(1)} %get-tuple-element.46), channel_id=1, source_target_pairs={{0,8},{8,0},{16,24},{24,16},{1,9},{9,1},{17,25},{25,17},{2,10},{10... | collective-permute-start | bytes 24584 | tf_op jit(solution)/shard_map/ppermute | solution.py:46
  97.5 12.7 %collective-permute-start.8 = (f32[3,24,1024]{2,1,0:T(8,128)S(1)}, f32[3,24,1024]{2,1,0:T(8,128)S(1)}, u32[]{:S(2)}, u32[]{:S(2)}) collective-permute-start(f32[3,24,1024]{2,1,0:T(8,128)S(1)} %pad_maximum_fusion.1.near_mid), channel_id=1, source_target_pairs={{0,1},{1,2},{2,3},{3,4},{4,5},{5,6},{6,7},{8,9},{9,10},{10,11},{11... | collective-permute-start | bytes 884744 | tf_op jit(solution)/shard_map/ppermute | solution.py:53
  100.0 10.3 %collective-permute-start.9 = (f32[3,24,1024]{2,1,0:T(8,128)S(1)}, f32[3,24,1024]{2,1,0:T(8,128)S(1)}, u32[]{:S(2)}, u32[]{:S(2)}) collective-permute-start(f32[3,24,1024]{2,1,0:T(8,128)S(1)} %pad_maximum_fusion.1.near_mid), channel_id=1, source_target_pairs={{1,0},{2,1},{3,2},{4,3},{5,4},{6,5},{7,6},{9,8},{10,9},{11,10},{12... | collective-permute-start | bytes 884744 | tf_op jit(solution)/shard_map/ppermute | solution.py:53
  102.0 15.9 %all-to-all-start.5 = ((bf16[32,16,128]{2,1,0:T(8,128)(2,1)}), bf16[32,16,128]{2,1,0:T(8,128)(2,1)S(1)}, u32[]{:S(2)}, u32[]{:S(2)}) async-start(bf16[32,16,128]{2,1,0:T(8,128)(2,1)} %broadcast_in_dim.84), calls=%async_computation.5 | async-start | bytes 262144 | tf_op jit(solution)/shard_map/all_to_all | solution.py:36
  117.9 3.4 %copy-start.1 = (bf16[8,1024,512]{2,1,0:T(8,128)(2,1)S(1)}, bf16[8,1024,512]{2,1,0:T(8,128)(2,1)}, u32[]{:S(2)}) copy-start(bf16[8,1024,512]{2,1,0:T(8,128)(2,1)} %copy-done) | copy-start | bytes 25165828
  148.5 3.4 %copy-start.2 = (bf16[8,1024,512]{2,1,0:T(8,128)(2,1)S(1)}, bf16[8,1024,512]{2,1,0:T(8,128)(2,1)}, u32[]{:S(2)}) copy-start(bf16[8,1024,512]{2,1,0:T(8,128)(2,1)} %copy-done) | copy-start | bytes 25165828
  155.8 24.2 %all-to-all-start.8 = ((f32[32,32,128]{2,1,0:T(8,128)}), f32[32,32,128]{2,1,0:T(8,128)S(1)}, u32[]{:S(2)}, u32[]{:S(2)}) async-start(f32[32,32,128]{2,1,0:T(8,128)} %project.1), calls=%async_computation.8 | async-start | bytes 1048576 | tf_op jit(solution)/shard_map/all_to_all | solution.py:36
  161.4 7.6 %collective-permute-start.11 = (bf16[16,1024]{1,0:T(8,128)(2,1)S(1)}, bf16[16,1024]{1,0:T(8,128)(2,1)S(1)}, u32[]{:S(2)}, u32[]{:S(2)}) collective-permute-start(bf16[16,1024]{1,0:T(8,128)(2,1)S(1)} %get-tuple-element.41), channel_id=1, source_target_pairs={{8,0},{16,8},{24,16},{32,24},{40,32},{48,40},{56,48},{64,56},{72,6... | collective-permute-start | bytes 98312 | tf_op jit(solution)/shard_map/ppermute | solution.py:53
  163.7 5.4 %collective-permute-start.10 = (bf16[16,1024]{1,0:T(8,128)(2,1)S(1)}, bf16[16,1024]{1,0:T(8,128)(2,1)S(1)}, u32[]{:S(2)}, u32[]{:S(2)}) collective-permute-start(bf16[16,1024]{1,0:T(8,128)(2,1)S(1)} %get-tuple-element.41), channel_id=1, source_target_pairs={{0,8},{8,16},{16,24},{24,32},{32,40},{40,48},{48,56},{56,64},{64,7... | collective-permute-start | bytes 98312 | tf_op jit(solution)/shard_map/ppermute | solution.py:53
  169.1 32.0 %copy-start.12 = (f32[128,1024]{1,0:T(8,128)S(1)}, f32[128,1024]{1,0:T(8,128)}, u32[]{:S(2)}) copy-start(f32[128,1024]{1,0:T(8,128)} %copy-done.11) | copy-start | bytes 1572868
  169.1 4.9 %collective-permute-start.12 = (bf16[3,16,1024]{2,1,0:T(8,128)(2,1)S(1)}, bf16[3,16,1024]{2,1,0:T(8,128)(2,1)S(1)}, u32[]{:S(2)}, u32[]{:S(2)}) collective-permute-start(bf16[3,16,1024]{2,1,0:T(8,128)(2,1)S(1)} %pad_maximum_fusion.2.near_mid), channel_id=1, source_target_pairs={{0,1},{1,2},{2,3},{3,4},{4,5},{5,6},{6,7},{8,9},{9,10},{10,11},{11... | collective-permute-start | bytes 294920 | tf_op jit(solution)/shard_map/ppermute | solution.py:53
  172.3 5.8 %collective-permute-start.13 = (bf16[3,16,1024]{2,1,0:T(8,128)(2,1)S(1)}, bf16[3,16,1024]{2,1,0:T(8,128)(2,1)S(1)}, u32[]{:S(2)}, u32[]{:S(2)}) collective-permute-start(bf16[3,16,1024]{2,1,0:T(8,128)(2,1)S(1)} %pad_maximum_fusion.2.near_mid), channel_id=1, source_target_pairs={{1,0},{2,1},{3,2},{4,3},{5,4},{6,5},{7,6},{9,8},{10,9},{11,10},{12... | collective-permute-start | bytes 294920 | tf_op jit(solution)/shard_map/ppermute | solution.py:53
  191.1 8.6 %collective-permute-start.16 = (f32[16,128]{1,0:T(8,128)S(1)}, f32[16,128]{1,0:T(8,128)S(1)}, u32[]{:S(2)}, u32[]{:S(2)}) collective-permute-start(f32[16,128]{1,0:T(8,128)S(1)} %get-tuple-element.49), channel_id=1, source_target_pairs={{0,24},{8,16},{16,8},{24,0},{1,25},{9,17},{17,9},{25,1},{2,26},{10... | collective-permute-start | bytes 24584 | tf_op jit(solution)/shard_map/ppermute | solution.py:46
  195.8 5.2 %collective-permute-start.15 = (f32[16,128]{1,0:T(8,128)S(1)}, f32[16,128]{1,0:T(8,128)S(1)}, u32[]{:S(2)}, u32[]{:S(2)}) collective-permute-start(f32[16,128]{1,0:T(8,128)S(1)} %get-tuple-element.49), channel_id=1, source_target_pairs={{0,16},{8,24},{16,0},{24,8},{1,17},{9,25},{17,1},{25,9},{2,18},{10... | collective-permute-start | bytes 24584 | tf_op jit(solution)/shard_map/ppermute | solution.py:46
  199.7 1.3 collective-permute-start.14
  203.5 21.9 %copy-start.14 = (f32[128,1024]{1,0:T(8,128)S(1)}, f32[128,1024]{1,0:T(8,128)}, u32[]{:S(2)}) copy-start(f32[128,1024]{1,0:T(8,128)} %copy-done.13) | copy-start | bytes 1572868
  203.5 21.9 %copy-start.16 = (f32[128,1024]{1,0:T(8,128)S(1)}, f32[128,1024]{1,0:T(8,128)}, u32[]{:S(2)}) copy-start(f32[128,1024]{1,0:T(8,128)} %copy-done.15) | copy-start | bytes 1572868
  203.5 21.9 %copy-start.18 = (f32[128,1024]{1,0:T(8,128)S(1)}, f32[128,1024]{1,0:T(8,128)}, u32[]{:S(2)}) copy-start(f32[128,1024]{1,0:T(8,128)} %copy-done.17) | copy-start | bytes 1572868
  204.4 21.0 %all-to-all-start.10 = ((f32[8,16,1152]{2,1,0:T(8,128)}), f32[8,16,1152]{2,1,0:T(8,128)S(1)}, u32[]{:S(2)}, u32[]{:S(2)}) async-start(f32[8,16,1152]{2,1,0:T(8,128)} %broadcast_in_dim.89), calls=%async_computation.10 | async-start | bytes 1179648 | tf_op jit(solution)/shard_map/all_to_all | solution.py:36
  227.3 3.9 %collective-permute-start.19 = (f32[16,256]{1,0:T(8,128)S(1)}, f32[16,256]{1,0:T(8,128)S(1)}, u32[]{:S(2)}, u32[]{:S(2)}) collective-permute-start(f32[16,256]{1,0:T(8,128)S(1)} %get-tuple-element.52), channel_id=1, source_target_pairs={{0,24},{8,16},{16,8},{24,0},{1,25},{9,17},{17,9},{25,1},{2,26},{10... | collective-permute-start | bytes 49160 | tf_op jit(solution)/shard_map/ppermute | solution.py:46
  229.3 2.6 %collective-permute-start.18 = (f32[16,256]{1,0:T(8,128)S(1)}, f32[16,256]{1,0:T(8,128)S(1)}, u32[]{:S(2)}, u32[]{:S(2)}) collective-permute-start(f32[16,256]{1,0:T(8,128)S(1)} %get-tuple-element.53), channel_id=1, source_target_pairs={{0,16},{8,24},{16,0},{24,8},{1,17},{9,25},{17,1},{25,9},{2,18},{10... | collective-permute-start | bytes 49160 | tf_op jit(solution)/shard_map/ppermute | solution.py:46
  229.6 2.3 collective-permute-start.17
  245.3 3.4 %copy-start.3 = (bf16[8,1024,512]{2,1,0:T(8,128)(2,1)S(1)}, bf16[8,1024,512]{2,1,0:T(8,128)(2,1)}, u32[]{:S(2)}) copy-start(bf16[8,1024,512]{2,1,0:T(8,128)(2,1)} %copy-done) | copy-start | bytes 25165828

commit v3 on v2

v3 whole, which is shorter than its diff:
```python
import jax
import jax.numpy as jnp
from jax import lax
from jax.experimental import pallas as pl
from jax.experimental.pallas import tpu as pltpu
from jax.sharding import Mesh, PartitionSpec as P

FEAT = 8
BLOCK = 128
PROBES = 16
PTS = 1024
SHARE = 128
CHUNK = 512
CHUNKS = 8
CAP = 8
EMPTY = 72
QUARTER = 1024

support_radius = 0.32
width_sq = 0.045
LOG2E = 1.4426950408889634

ALL = ("z", "yl", "c", "yh", "x")
PLANE = ("yh", "x", "yl", "c")
CELLS = ("yl", "c", "yh", "x")
GX = ("z", "yl", "c")
GY = ("yh", "x")
f32 = jnp.float32
bf16 = jnp.bfloat16

VMEM = pl.BlockSpec(memory_space=pltpu.VMEM)
SMEM = pl.BlockSpec(memory_space=pltpu.SMEM)
SMALL = pltpu.CompilerParams(vmem_limit_bytes=16 * 1024 * 1024)
MIDDLE = pltpu.CompilerParams(vmem_limit_bytes=24 * 1024 * 1024)
LARGE = pltpu.CompilerParams(vmem_limit_bytes=57 * 1024 * 1024)


def exchange(parts, axes):
    return lax.all_to_all(parts, axes, 0, 0, tiled=True)


def quad_partner(value, step):
    pairs = [(i, i ^ step) for i in range(4)]
    return lax.ppermute(value, ("yl", "c"), pairs)


def even_pairs(value, axes):
    return lax.ppermute(value, axes, [(i, i ^ 1) for i in range(lax.axis_size(axes))])


def odd_pairs(value, axes):
    count = lax.axis_size(axes)
    pairs = [(i, i + 1) for i in range(1, count - 1, 2)]
    return lax.ppermute(value, axes, pairs + [(j, i) for i, j in pairs])


def after(value, *others):
    return lax.optimization_barrier((value,) + others)[0]


def split3(value):
    first = value.astype(bf16).astype(f32)
    rest = value - first
    second = rest.astype(bf16).astype(f32)
    return first, second, (rest - second).astype(bf16).astype(f32)


def augmented(points, scale, left):
    centred = points - 0.5
    norm = scale * jnp.sum(centred * centred, axis=0, keepdims=True)
    norms = [jnp.broadcast_to(part, points.shape) for part in split3(norm)]
    row = lax.broadcasted_iota(jnp.int32, points.shape, 0)
    if left:
        one, two, three = split3(centred)
        order = [one, one, two, one, two, three]
        base = 0
    else:
        one, two, three = split3((-2.0 * scale) * centred)
        order = [one, two, one, three, two, one]
        base = 3
    extra = jnp.where(row < 6, 1.0, 0.0)
    for index, part in enumerate(norms):
        extra = jnp.where(row == base + index, part, extra)
    return jnp.concatenate(order + [extra, jnp.zeros_like(extra)], axis=0).astype(bf16)


def as_lanes(column, offset):
    row = lax.broadcasted_iota(jnp.int32, (PROBES, 128), 0)
    lane = lax.broadcasted_iota(jnp.int32, (PROBES, 128), 1)
    return jnp.sum(jnp.where(lane == row + offset, column, 0.0), axis=0, keepdims=True)


def as_column(row_value, offset):
    row = lax.broadcasted_iota(jnp.int32, (PROBES, 128), 0)
    lane = lax.broadcasted_iota(jnp.int32, (PROBES, 128), 1)
    return jnp.sum(jnp.where(lane == row + offset, row_value, 0.0), axis=1, keepdims=True)


def live_lanes(count):
    lane = lax.broadcasted_iota(jnp.int32, (1, PTS), 1)
    return jnp.where(lane < count, 1.0, 0.0)


def nt_dot(left, right):
    return lax.dot_general(left, right, (((1,), (1,)), ((), ())), preferred_element_type=f32)


def call(kernel, name, out_shape, in_specs, args, scratch=(), grid=None, out_specs=None, params=SMALL, flops=0, moved=0):
    if out_specs is None:
        out_specs = jax.tree.map(lambda _: VMEM, out_shape)
    options = {} if grid is None else {"grid": grid}
    return pl.pallas_call(
        kernel,
        out_shape=out_shape,
        in_specs=in_specs,
        out_specs=out_specs,
        scratch_shapes=list(scratch),
        compiler_params=params,
        cost_estimate=pl.CostEstimate(flops=flops, bytes_accessed=moved, transcendentals=0),
        name=name,
        **options,
    )(*args)


def shape(*dims, dtype=f32):
    return jax.ShapeDtypeStruct(dims, dtype)


FIELD = shape(PROBES, PTS)


def prepare_kernel(coords, probes, precond, counts, inducing, centre_out, halo_out):
    points = coords[...]
    lane = lax.broadcasted_iota(jnp.int32, (FEAT, PTS), 1)
    short = lax.broadcasted_iota(jnp.int32, (FEAT, 128), 1)
    centre = jnp.zeros((FEAT, 128), f32)
    for index in range(16):
        picked = jnp.sum(
            jnp.where(lane == inducing[0, index], points, 0.0), axis=1, keepdims=True
        )
        centre = jnp.where(short == index, picked, centre)
    centre_out[...] = jnp.broadcast_to(centre[None], centre_out.shape)
    halo_out[:FEAT] = points
    halo_out[FEAT:] = precond[...] * (probes[...] * live_lanes(counts[0, 0]))


def prepare(coords, probes, precond, counts, inducing):
    return call(
        prepare_kernel,
        "prepare",
        (shape(32, FEAT, 128), shape(FEAT + PROBES, PTS)),
        [VMEM, VMEM, VMEM, SMEM, SMEM],
        (coords, probes, precond, counts, inducing),
        params=LARGE,
    )


def compact_kernel(parts, out):
    for tile in range(4):
        total = parts[8 * tile]
        for cell in range(1, 8):
            total = total + pltpu.roll(parts[8 * tile + cell], 16 * cell, 1)
        out[:, :, tile * 128 : (tile + 1) * 128] = jnp.broadcast_to(total[None], (8, FEAT, 128))


def compact(parts):
    return call(compact_kernel, "compact", shape(8, FEAT, CHUNK), [VMEM], (parts,))


def factor_kernel(quad, factor, first_out, second_out, third_out):
    first, second, third = split3(factor[...])
    first_out[...] = first.astype(bf16)
    second_out[...] = second.astype(bf16)
    third_out[...] = third.astype(bf16)


def split_factor(quad, factor):
    block = pl.BlockSpec((SHARE, QUARTER), lambda k, quad: (k, 0))
    return pl.pallas_call(
        factor_kernel,
        out_shape=(shape(4 * SHARE, QUARTER, dtype=bf16),) * 3,
        grid_spec=pltpu.PrefetchScalarGridSpec(
            num_scalar_prefetch=1,
            grid=(4,),
            in_specs=[pl.BlockSpec((SHARE, QUARTER), lambda k, quad: (quad[0] ^ k, quad[0]))],
            out_specs=(block,) * 3,
        ),
        compiler_params=LARGE,
        cost_estimate=pl.CostEstimate(flops=0, bytes_accessed=8 << 20, transcendentals=0),
        name="factor",
    )(quad, factor)


def rows_kernel(halo, centres, rows_out, sums_out, left, packed):
    @pl.when(pl.program_id(0) == 0)
    def _():
        left[...] = augmented(halo[:FEAT], -LOG2E / width_sq, True).astype(f32).T.astype(bf16)
        packed[...] = halo[FEAT:].astype(bf16)

    right = augmented(centres[0], -LOG2E / width_sq, False)
    power = jnp.dot(left[...], right, preferred_element_type=f32)
    rows = jnp.exp2(jnp.minimum(power, 0.0)).astype(bf16)
    rows_out[0] = rows
    sums = jnp.dot(packed[...], rows, preferred_element_type=f32)
    for part in range(4):
        sums_out[part] = sums[:, part * SHARE : (part + 1) * SHARE]


def make_rows(halo, centres):
    return call(
        rows_kernel,
        "rows",
        (shape(CHUNKS, PTS, CHUNK, dtype=bf16), shape(32, PROBES, SHARE)),
        [
            pl.BlockSpec((FEAT + PROBES, PTS), lambda g: (0, 0)),
            pl.BlockSpec((1, FEAT, CHUNK), lambda g: (g, 0, 0)),
        ],
        (halo, centres),
        scratch=[pltpu.VMEM((PTS, 64), bf16), pltpu.VMEM((PROBES, PTS), bf16)],
        grid=(CHUNKS,),
        out_specs=(
            pl.BlockSpec((1, PTS, CHUNK), lambda g: (g, 0, 0)),
            pl.BlockSpec((4, PROBES, SHARE), lambda g: (g, 0, 0)),
        ),
        params=MIDDLE,
        moved=16 << 20,
    )


def project_kernel(packed, rows, sums_out):
    sums = jnp.dot(packed[...], rows[0], preferred_element_type=f32)
    for part in range(4):
        sums_out[part] = sums[:, part * SHARE : (part + 1) * SHARE]


def project(packed, rows):
    height = packed.shape[0]
    return call(
        project_kernel,
        "project",
        shape(32, height, SHARE),
        [
            pl.BlockSpec((height, PTS), lambda g: (0, 0)),
            pl.BlockSpec((1, PTS, CHUNK), lambda g: (g, 0, 0)),
        ],
        (packed, rows),
        grid=(CHUNKS,),
        out_specs=pl.BlockSpec((4, height, SHARE), lambda g: (g, 0, 0)),
        params=MIDDLE,
        moved=16 << 20,
    )


def fill_table(table, sides, sources, first, last, dtype):
    places_x = (1, 2 - 2 * sides[0, 0], 2 * sides[0, 0])
    places_y = (1, 2 - 2 * sides[0, 1], 2 * sides[0, 1])
    for place_y, source in zip(places_y, sources):
        for index, place_x in enumerate(places_x):
            start = (place_x * 3 + place_y) * CAP
            values = source[index, first:last].astype(dtype)
            for block in range(CAP):
                table[start + block] = values[:, block * BLOCK : (block + 1) * BLOCK]
    table[EMPTY] = jnp.zeros(table.shape[1:], dtype)


def partners(table, codes, block):
    return jnp.concatenate([table[codes[block, entry]] for entry in range(CAP)], axis=1)


def tiles_kernel(codes, sides, near, even, odd, tiles_out, sparse_out, points, values):
    block = pl.program_id(0)

    @pl.when(block == 0)
    def _():
        fill_table(points, sides, (near, even, odd), 0, FEAT, f32)
        fill_table(values, sides, (near, even, odd), FEAT, FEAT + PROBES, bf16)

    scale = 1.0 / (support_radius * support_radius)
    own = augmented(points[4 * CAP + block], scale, True).astype(f32).T.astype(bf16)
    other = augmented(partners(points, codes, block), scale, False)
    square = jnp.maximum(jnp.dot(own, other, preferred_element_type=f32), 0.0)
    ratio = jnp.sqrt(square)
    remain = jnp.maximum(1.0 - ratio, 0.0)
    second = remain * remain
    fourth = second * second
    tile = (fourth * second * remain * (7.0 * ratio + 1.0)).astype(bf16)
    tiles_out[0] = tile
    sparse_out[...] = nt_dot(partners(values, codes, block), tile)


def make_tiles(codes, sides, near, even, odd):
    whole = pl.BlockSpec((3, FEAT + PROBES, PTS), lambda b: (0, 0, 0))
    return call(
        tiles_kernel,
        "tiles",
        (shape(CAP, BLOCK, PTS, dtype=bf16), FIELD),
        [SMEM, SMEM, whole, whole, whole],
        (codes, sides, near, even, odd),
        scratch=[
            pltpu.VMEM((EMPTY + 1, FEAT, BLOCK), f32),
            pltpu.VMEM((EMPTY + 1, PROBES, BLOCK), bf16),
        ],
        grid=(CAP,),
        out_specs=(
            pl.BlockSpec((1, BLOCK, PTS), lambda b: (b, 0, 0)),
            pl.BlockSpec((PROBES, BLOCK), lambda b: (0, b)),
        ),
        moved=16 << 20,
    )


def steps_of(row):
    rz_now = as_column(row, 0)
    alpha = rz_now / as_column(row, 16)
    return alpha, alpha * alpha * as_column(row, 32) / rz_now - 1.0


def row_total(rows):
    total = rows[0]
    for index in range(1, rows.shape[0]):
        total = total + rows[index]
    return total


def sparse_kernel(
    codes, sides, near, even, odd, tiles, search, residual, precond, sparse_out, sums_out, values
):
    fill_table(values, sides, (near, even, odd), 0, PROBES, bf16)
    for block in range(CAP):
        sparse_out[:, block * BLOCK : (block + 1) * BLOCK] = nt_dot(
            partners(values, codes, block), tiles[block]
        )
    field = search[...]
    left = residual[...]
    curve = jnp.sum(field * (field + sparse_out[...]), axis=1, keepdims=True)
    norm = jnp.sum(left * (precond[...] * left), axis=1, keepdims=True)
    lane = lax.broadcasted_iota(jnp.int32, (PROBES, 128), 1)
    sums_out[...] = jnp.where(lane == 0, curve, jnp.where(lane == 1, norm, 0.0))


def apply_tiles(codes, sides, nears, tiles, search, residual, precond):
    return call(
        sparse_kernel,
        "sparse",
        (FIELD, shape(PROBES, 128)),
        [SMEM, SMEM] + [VMEM] * 7,
        (codes, sides, *nears, tiles, search, residual, precond),
        scratch=[pltpu.VMEM((EMPTY + 1, PROBES, BLOCK), bf16)],
        moved=6 << 20,
    )


def stack_kernel(own, even, odd, out):
    out[0] = own[...]
    out[1] = even[...]
    out[2] = odd[...]


def surround(value, *first):
    column = call(
        stack_kernel,
        "stack",
        shape(3, *value.shape, dtype=value.dtype),
        [VMEM] * 3,
        (value, even_pairs(value, GX), odd_pairs(value, GX)),
    )
    column = after(column, *first)
    return column, even_pairs(column, GY), odd_pairs(column, GY)


def expand_step(weights, rows, total):
    @pl.when(pl.program_id(0) == 0)
    def _():
        total[...] = jnp.zeros_like(total)

    part = jnp.concatenate([weights[i, :PROBES] for i in range(4)], axis=1)
    total[...] += nt_dot(part, rows[0])


def image_kernel(
    weights, rows, counts, halo, sparse, precond, probes, image_out, sums_out, total
):
    expand_step(weights, rows, total)

    @pl.when(pl.program_id(0) == CHUNKS - 1)
    def _():
        search = halo[FEAT:]
        live = live_lanes(counts[0, 0])
        image = live * (search + sparse[...] + total[...])
        image_out[...] = image
        norm = jnp.sum(search * (probes[...] * live), axis=1, keepdims=True)
        curve = jnp.sum(search * image, axis=1, keepdims=True)
        square = jnp.sum(precond[...] * image * image, axis=1, keepdims=True)
        row = as_lanes(norm, 0) + as_lanes(curve, 16) + as_lanes(square, 32)
        for index in range(32):
            sums_out[index] = row


def make_image(weights, rows, counts, halo, sparse, precond, probes):
    height = weights.shape[1]
    still = pl.BlockSpec((PROBES, PTS), lambda g: (0, 0))
    return call(
        image_kernel,
        "image",
        (FIELD, shape(32, 1, 128)),
        [
            pl.BlockSpec((4, height, SHARE), lambda g: (g, 0, 0)),
            pl.BlockSpec((1, PTS, CHUNK), lambda g: (g, 0, 0)),
            SMEM,
            pl.BlockSpec((FEAT + PROBES, PTS), lambda g: (0, 0)),
            still,
            pl.BlockSpec((1, PTS), lambda g: (0, 0)),
            still,
        ],
        (weights, rows, counts, halo, sparse, precond, probes),
        scratch=[pltpu.VMEM((PROBES, PTS), f32)],
        grid=(CHUNKS,),
        out_specs=(still, pl.BlockSpec((32, 1, 128), lambda g: (0, 0, 0))),
        params=MIDDLE,
        moved=16 << 20,
    )


def update_kernel(
    rows, halo, probes, precond, counts, image,
    residual_out, search_out, packed_out, rounded_out, solution_out,
):
    alpha, beta = steps_of(row_total(rows))
    search = halo[FEAT:]
    solution_out[...] = alpha * search
    residual = probes[...] * live_lanes(counts[0, 0]) - alpha * image[...]
    residual_out[...] = residual
    following = precond[...] * residual + beta * search
    search_out[...] = following
    rounded = following.astype(bf16)
    rounded_out[...] = rounded
    packed_out[:PROBES] = rounded
    packed_out[PROBES:] = (following - rounded.astype(f32)).astype(bf16)


def update(rows, halo, probes, precond, counts, image):
    return call(
        update_kernel,
        "update",
        (
            FIELD,
            FIELD,
            shape(2 * PROBES, PTS, dtype=bf16),
            shape(PROBES, PTS, dtype=bf16),
            FIELD,
        ),
        [VMEM, VMEM, VMEM, VMEM, SMEM, VMEM],
        (rows, halo, probes, precond, counts, image),
    )


def sum_rows_kernel(rows, out):
    total = row_total(rows)
    for index in range(out.shape[0]):
        out[index] = total


def sum_rows(rows, count):
    return call(sum_rows_kernel, "sum_rows", shape(count, 1, 128), [VMEM], (rows,))


def sum_share_kernel(*refs):
    parts, out = refs[0], refs[-1]
    total = jnp.sum(parts[...], axis=0)
    if len(refs) == 3:
        total = jnp.concatenate([total, refs[1][...]], axis=0)
    out[...] = jnp.broadcast_to(total[None], out.shape)


def sum_share(parts, *sums):
    height = parts.shape[1] + sum(value.shape[0] for value in sums)
    return call(
        sum_share_kernel,
        "sum_share",
        shape(8, height, SHARE),
        [VMEM] * (1 + len(sums)),
        (parts, *sums),
    )


def sum_depth_kernel(parts, *outs):
    total = jnp.sum(parts[...], axis=0)
    for index, out in enumerate(outs):
        out[...] = total[index * PROBES : (index + 1) * PROBES]


def sum_depth(parts):
    count = parts.shape[1] // PROBES
    return call(
        sum_depth_kernel, "sum_depth", (shape(PROBES, SHARE),) * count, [VMEM], (parts,)
    )


def six_products(value, factors, dot):
    first, second, third = split3(value)
    total = dot(third.astype(bf16), factors[0][...])
    total = total + dot(second.astype(bf16), factors[1][...])
    total = total + dot(first.astype(bf16), factors[2][...])
    total = total + dot(second.astype(bf16), factors[0][...])
    total = total + dot(first.astype(bf16), factors[1][...])
    return total + dot(first.astype(bf16), factors[0][...])


def nn_dot(left, right):
    return jnp.dot(left, right, preferred_element_type=f32)


def coeffs_kernel(*refs):
    shares, factors, out = refs[:4], refs[4:7], refs[-1]
    value = jnp.concatenate([ref[...] for ref in shares], axis=1)
    terms = six_products(value, factors, nn_dot)
    if len(refs) == 9:
        terms = jnp.concatenate([terms, refs[7][...]], axis=1)
    out[...] = jnp.broadcast_to(terms[None], out.shape)


def coeff_terms(shares, factors, *sums):
    width = QUARTER + SHARE * len(sums)
    return call(
        coeffs_kernel,
        "coeffs",
        shape(8, PROBES, width),
        [VMEM] * (7 + len(sums)),
        (*shares, *factors, *sums),
    )


def weights_kernel(parts, first, second, third, *outs):
    total = jnp.sum(parts[...], axis=0)
    terms = six_products(total[:, :QUARTER], (first, second, third), nt_dot)
    for index, out in enumerate(outs):
        out[:, :SHARE] = terms[:, index * SHARE : (index + 1) * SHARE]
        if out.shape[1] > SHARE:
            out[:, SHARE:] = total[:, QUARTER:]


def weight_terms(parts, factors):
    width = SHARE + parts.shape[2] - QUARTER
    return call(
        weights_kernel,
        "weights",
        (shape(PROBES, width),) * 4,
        [VMEM] * 4,
        (parts, *factors),
    )


def gather_kernel(own, first, second, third, out):
    total = own[...] + first[...] + second[...] + third[...]
    out[...] = jnp.broadcast_to(total.astype(bf16)[None], out.shape)


def gather_weights(terms):
    return call(
        gather_kernel, "gather", shape(32, PROBES, SHARE, dtype=bf16), [VMEM] * 4, tuple(terms)
    )


def gather_last_kernel(own, first, second, third, rounded, rest, out, sums_out):
    total = own[...] + first[...] + second[...] + third[...]
    weights = total[:, :SHARE].astype(bf16)
    sums_out[...] = total[:, SHARE:]
    unrounded = rounded[...] + rest[...]
    dot = jnp.sum(weights.astype(f32) * unrounded, axis=1, keepdims=True)
    lane = lax.broadcasted_iota(jnp.int32, (PROBES, SHARE), 1)
    row = jnp.zeros((PROBES, SHARE), f32)
    for index, part in enumerate(split3(dot)):
        row = jnp.where(lane == index, part, row)
    both = jnp.concatenate([weights, row.astype(bf16)], axis=0)
    out[...] = jnp.broadcast_to(both[None], out.shape)


def gather_last(terms, rounded, rest):
    return call(
        gather_last_kernel,
        "gather_last",
        (shape(32, 2 * PROBES, SHARE, dtype=bf16), shape(PROBES, 128)),
        [VMEM] * 6,
        (*terms, rounded, rest),
    )


def finish_kernel(
    weights, rows, every, counts, search, sparse, residual, solution, sums, solution_out,
    residual_out, total,
):
    expand_step(weights, rows, total)

    @pl.when(pl.program_id(0) == CHUNKS - 1)
    def _():
        field = search[...]
        image = live_lanes(counts[0, 0]) * (field + sparse[...] + total[...])
        dots = jnp.sum(every[:, PROBES:].astype(f32), axis=0)
        dot = jnp.sum(dots, axis=1, keepdims=True)
        totals = sums[...]
        alpha = totals[:, 1:2] / (totals[:, 0:1] + dot)
        solution_out[...] = solution[...] + alpha * field
        residual_out[...] = residual[...] - alpha * image


def finish(weights, rows, counts, search, sparse, residual, solution, sums):
    still = pl.BlockSpec((PROBES, PTS), lambda g: (0, 0))
    height = weights.shape[1]
    return call(
        finish_kernel,
        "finish",
        (FIELD, FIELD),
        [
            pl.BlockSpec((4, height, SHARE), lambda g: (g, 0, 0)),
            pl.BlockSpec((1, PTS, CHUNK), lambda g: (g, 0, 0)),
            pl.BlockSpec((32, height, SHARE), lambda g: (0, 0, 0)),
            SMEM,
            still,
            still,
            still,
            still,
            pl.BlockSpec((PROBES, 128), lambda g: (0, 0)),
        ],
        (weights, rows, weights, counts, search, sparse, residual, solution, sums),
        scratch=[pltpu.VMEM((PROBES, PTS), f32)],
        grid=(CHUNKS,),
        out_specs=(still, still),
        params=MIDDLE,
        moved=16 << 20,
    )


def on_device(coords, probes, precond, counts, neighbours, inducing, factor):
    quad = lax.axis_index("yl") * 2 + lax.axis_index("c")
    sides = jnp.stack([lax.axis_index("c"), lax.axis_index("x") % 2]).reshape(1, 2)
    points = coords[0, 0]
    given = probes[0, 0]
    scaling = precond[0]
    codes = neighbours[0, 0]

    centre_parts, halo = prepare(points, given, scaling, counts, inducing[0])

    got = exchange(centre_parts, CELLS)
    factors = split_factor(after(quad.reshape(1), halo), factor)
    halos = surround(halo)
    got = after(got, halos[0], *factors)
    compacted = compact(got)
    centres = exchange(compacted, "z")
    tiles, sparse = make_tiles(codes, sides, after(halos[0], compacted), halos[1], halos[2])
    centres = after(centres, tiles, sparse)
    rows, parts = make_rows(halo, centres)

    def depth_of(got, *sums):
        return sum_depth(exchange(sum_share(got, *sums), "z"))

    def terms_of(depth):
        own = depth[0]
        shares = [own] + [quad_partner(own, step) for step in (1, 2, 3)]
        terms = exchange(coeff_terms(shares, factors, *depth[2:]), GY)
        terms = weight_terms(terms, factors)
        return [terms[0]] + [quad_partner(terms[step], step) for step in (1, 2, 3)]

    terms = terms_of(depth_of(exchange(parts, PLANE)))
    weights = exchange(gather_weights(terms), PLANE)
    image, row = make_image(weights, rows, counts, halo, sparse, scaling, given)
    row = exchange(sum_rows(exchange(row, CELLS), 8), "z")
    residual, search, packed, rounded, solution = update(
        row, halo, given, scaling, counts, image
    )

    parts = project(packed, rows)
    nears = surround(rounded, parts)
    got = exchange(after(parts, nears[0]), PLANE)
    sparse, sums = apply_tiles(
        codes, sides, (after(nears[0], got),) + nears[1:], tiles, search, residual, scaling
    )
    depth = depth_of(got, sums)
    weights, totals = gather_last(terms_of(depth), depth[0], depth[1])
    weights = exchange(weights, PLANE)
    solution, residual = finish(
        weights, rows, counts, search, sparse, residual, solution, totals
    )
    return (solution[None, None], residual[None, None])


def solution(mesh):
    fine = Mesh(mesh.devices.reshape(8, 2, 2, 2, 4), ALL)
    placed = (
        P(GX, GY, None, None),
        P(GX, GY, None, None),
        P(GX, GY, None),
        P(GX, GY),
        P(GX, GY, None, None),
        P(GX, GY, None),
        P(GY, None),
    )
    return jax.shard_map(
        on_device,
        mesh=fine,
        in_specs=placed,
        out_specs=(P(GX, GY, None, None), P(GX, GY, None, None)),
        check_vma=False,
    )
```

time: 254 us -> 233 us (0.917)
  waiting for transfers between devices: 36.1 us -> 14.1 us
  blocking collectives: 94.1 us -> 115 us
  starting transfers between devices: 65.4 us -> 53.2 us
  Pallas kernels: 25.7 us -> 35.2 us
  local copies, waits for them, and re-layouts: 21.8 us -> 12.8 us
  matrix products: 7.24 us -> 0 us
    all_to_all x7 -> x9, blocking collectives: 94.1 us -> 115 us  [exchange(): return lax.all_to_all(parts, axes, 0, 0, tiled=True)]
    all_to_all x5 -> x3, waiting for transfers between devices: 26.2 us -> 7.66 us  [exchange(): return lax.all_to_all(parts, axes, 0, 0, tiled=True)]
    pallas_call x9 -> x23, Pallas kernels: 25.7 us -> 35.2 us  [the longest x22 31 us: call(): pl.pallas_call(kernel, out_shape=out_shape, in_specs=in_specs, out_specs=...]
    all_to_all x5 -> x3, starting transfers between devices: 29.2 us -> 20.2 us  [exchange(): return lax.all_to_all(parts, axes, 0, 0, tiled=True)]
    dot_general x4 -> x0, matrix products: 7.24 us -> none  [the longest x2 3.67 us: weights_of(): lax.dot_general(coeffs[:, :columns], factor_part, (((1,), (1,)), ((), ())...]
    ppermute x8, waiting for transfers between devices: 6.54 us -> 0.02 us  [the longest x4 0.01 us: odd_pairs(): return lax.ppermute(value, axes, pairs + [(j, i) for i, j in pairs])]
    unnamed x38 -> x42, local copies, waits for them, and re-layouts: 16.4 us -> 12.8 us
    broadcast_in_dim x8 -> x0, local copies, waits for them, and re-layouts: 3.1 us -> none  [spread(): return exchange(jnp.broadcast_to(value[None], (count,) + value.shape), axes)]
  transfers between devices with their start and end apart: 25 -> 23, of which waited for: 10 -> 9; matrix products, arithmetic and copies ran while one was open for 2% -> 0% of each run, Pallas kernels for 4% -> 6%
where the time goes in v3:
time: 233 us; the launch traced here: 232 us
  blocking collectives  115 us (49%)
  starting transfers between devices  53.2 us (23%)
  Pallas kernels  35.2 us (15%)
  waiting for transfers between devices  14.1 us (6%)
  local copies, waits for them, and re-layouts  12.8 us (5%)
    all_to_all x9, blocking collectives, exchange(): return lax.all_to_all(parts, axes, 0, 0, tiled=True)  115 us
    pallas_call x22, Pallas kernels, call(): pl.pallas_call(kernel, out_shape=out_shape, in_specs=in_specs, out_specs=...  31 us
    all_to_all x3, starting transfers between devices, exchange(): return lax.all_to_all(parts, axes, 0, 0, tiled=True)  20.2 us
    ppermute x12, starting transfers between devices, quad_partner(): return lax.ppermute(value, ('yl', 'c'), pairs)  14.9 us
    unnamed x42, local copies, waits for them, and re-layouts  12.8 us
    ppermute x4, starting transfers between devices, odd_pairs(): return lax.ppermute(value, axes, pairs + [(j, i) for i, j in pairs])  10 us
    ppermute x4, starting transfers between devices, even_pairs(): lax.ppermute(value, axes, [(i, i ^ 1) for i in range(lax.axis_size(axes))])  8.19 us
    all_to_all x3, waiting for transfers between devices, exchange(): return lax.all_to_all(parts, axes, 0, 0, tiled=True)  7.66 us
  transfers between devices with their start and end apart: 23, of which 9 were waited for; matrix products, arithmetic and copies ran while one was open for 0% of the time, Pallas kernels for 6%

profile of v3, /device:TPU:1, one launch (start us, length us, event | category | flops | bytes accessed | tf_op | source)
XLA Modules:
  0.0 232.2 jit_solution(17362734128559826808)
XLA Ops:
  1.3 1.7 prepare.1
  3.0 4.7 %collective-permute-start.1 = (f32[24,1024]{1,0:T(8,128)}, f32[24,1024]{1,0:T(8,128)S(1)}, u32[]{:S(2)}, u32[]{:S(2)}) collective-permute-start(f32[24,1024]{1,0:T(8,128)} %get-tuple-element.42.own.halo), channel_id=1, source_target_pairs={{8,16},{24,32},{40,48},{56,64},{72,80},{88,96},{104,112},{120,128}... | collective-permute-start | bytes 294920 | tf_op jit(solution)/shard_map/ppermute | solution.py:54
  7.7 0.1 collective-permute-start
  7.8 7.9 %all-to-all-start = ((f32[32,8,128]{2,1,0:T(8,128)}), f32[32,8,128]{2,1,0:T(8,128)S(1)}, u32[]{:S(2)}, u32[]{:S(2)}) async-start(f32[32,8,128]{2,1,0:T(8,128)} %get-tuple-element.43), calls=%async_computation | async-start | bytes 262144 | tf_op jit(solution)/shard_map/all_to_all | solution.py:39
  15.7 0.9 copy-done.14
  16.7 0.7 collective-permute-start.3
  17.3 3.9 %collective-permute-start.2 = (f32[3,24,1024]{2,1,0:T(8,128)S(1)}, f32[3,24,1024]{2,1,0:T(8,128)S(1)}, u32[]{:S(2)}, u32[]{:S(2)}) collective-permute-start(f32[3,24,1024]{2,1,0:T(8,128)S(1)} %stack.14.near), channel_id=1, source_target_pairs={{0,1},{1,0},{2,3},{3,2},{4,5},{5,4},{6,7},{7,6},{8,9},{9,8},{10,11... | collective-permute-start | bytes 884744 | tf_op jit(solution)/shard_map/ppermute | solution.py:48
  21.2 4.1 %factor.2 = (bf16[512,1024]{1,0:T(8,128)(2,1)}, bf16[512,1024]{1,0:T(8,128)(2,1)}, bf16[512,1024]{1,0:T(8,128)(2,1)}) custom-call(s32[1]{0:T(128)} %bitcast.4.quad, f32[512,4096]{1,0:T(8,128)} %factor.3), custom_call_target="tpu_custom_call" | custom-call | bytes 8388608 | tf_op jit(solution)/shard_map/factor/pallas_call | solution.py:179
  25.4 0.8 compact.1
  26.1 7.6 %all-to-all-start.1 = ((f32[8,8,512]{2,1,0:T(8,128)}), f32[8,8,512]{2,1,0:T(8,128)S(1)}, u32[]{:S(2)}, u32[]{:S(2)}) async-start(f32[8,8,512]{2,1,0:T(8,128)} %compact.1), calls=%async_computation.1 | async-start | bytes 262144 | tf_op jit(solution)/shard_map/all_to_all | solution.py:39
  33.8 5.9 %tiles.1 = (bf16[8,128,1024]{2,1,0:T(8,128)(2,1)S(1)}, f32[16,1024]{1,0:T(8,128)S(1)}) custom-call(s32[8,8]{1,0:T(8,128)S(1)} %bitcast.19, s32[1,2]{1,0:T(1,128)S(1)} %add_bitcast_fusion.sides, f32[3,24,1024]{2,1,0:T(8,128)S(1)} %stack.14.near, f32[3,24,1024]{2,1,0:T(8,128)S(1)} %collective-permute-done.2.even, f32[3,24,1024]{2,1,0:T(8,128)S(1)} %collective-permute-done.3.odd), custom_call_target="tpu_custom_call" | custom-call | bytes 16777216 | tf_op jit(solution)/shard_map/tiles/pallas_call | solution.py:112
  39.6 1.4 copy-done.12
  41.0 0.6 all-to-all-done.1.centres
  41.6 4.5 %rows.1 = (bf16[8,1024,512]{2,1,0:T(8,128)(2,1)S(1)}, f32[32,16,128]{2,1,0:T(8,128)S(1)}) custom-call(f32[24,1024]{1,0:T(8,128)S(1)} %copy-done.15, f32[8,8,512]{2,1,0:T(8,128)S(1)} %all-to-all-done.1.centres), custom_call_target="tpu_custom_call" | custom-call | bytes 16777216 | tf_op jit(solution)/shard_map/rows/pallas_call | solution.py:112
  46.1 17.2 %all_to_all.60.refs_0_ = f32[32,16,128]{2,1,0:T(8,128)S(1)} all-to-all(f32[32,16,128]{2,1,0:T(8,128)S(1)} %get-tuple-element.53), channel_id=1, replica_groups=mesh['z'=8,'yl'=2,'c'=2,'yh'=2,'x'=4] {'yh','x','yl','c'}, dimensions={0} | all-to-all | bytes 524288 | tf_op jit(solution)/shard_map/all_to_all | solution.py:39
  63.4 12.2 %all_to_all.61.parts = f32[8,16,128]{2,1,0:T(8,128)S(1)} all-to-all(f32[8,16,128]{2,1,0:T(8,128)S(1)} %sum_share.2), channel_id=1, replica_groups=mesh['z'=8,'yl'=2,'c'=2,'yh'=2,'x'=4] {'z'}, dimensions={0} | all-to-all | bytes 131072 | tf_op jit(solution)/shard_map/all_to_all | solution.py:39
  75.6 2.6 %collective-permute-start.6 = (f32[16,128]{1,0:T(8,128)S(1)}, f32[16,128]{1,0:T(8,128)S(1)}, u32[]{:S(2)}, u32[]{:S(2)}) collective-permute-start(f32[16,128]{1,0:T(8,128)S(1)} %sum_depth.2.refs_0_), channel_id=1, source_target_pairs={{0,24},{8,16},{16,8},{24,0},{1,25},{9,17},{17,9},{25,1},{2,26},{10... | collective-permute-start | bytes 24584 | tf_op jit(solution)/shard_map/ppermute | solution.py:44
  78.1 1.3 collective-permute-start.5
  79.5 1.2 collective-permute-done.5.refs_2_
  80.7 1.2 copy-done.2
  82.0 1.2 copy-done.5
  83.2 1.2 copy-done.8
  84.4 0.9 coeffs.2
  85.3 13.5 %all_to_all.62.parts = f32[8,16,1024]{2,1,0:T(8,128)S(1)} all-to-all(f32[8,16,1024]{2,1,0:T(8,128)S(1)} %coeffs.2), channel_id=1, replica_groups=mesh['z'=8,'yl'=2,'c'=2,'yh'=2,'x'=4] {'yh','x'}, dimensions={0} | all-to-all | bytes 1048576 | tf_op jit(solution)/shard_map/all_to_all | solution.py:39
  98.8 1.2 copy-done.3
  100.0 1.2 copy-done.6
  101.3 1.2 copy-done.9
  102.5 1.7 weights.2
  104.2 2.0 collective-permute-start.7
  106.2 0.7 collective-permute-start.8
  106.9 1.0 collective-permute-start.9
  107.9 0.8 collective-permute-done.8.second
  108.7 1.3 collective-permute-done.9.third
  110.0 11.3 %all_to_all.63.weights = bf16[32,16,128]{2,1,0:T(8,128)(2,1)S(1)} all-to-all(bf16[32,16,128]{2,1,0:T(8,128)(2,1)S(1)} %gather.1), channel_id=1, replica_groups=mesh['z'=8,'yl'=2,'c'=2,'yh'=2,'x'=4] {'yh','x','yl','c'}, dimensions={0} | all-to-all | bytes 262144 | tf_op jit(solution)/shard_map/all_to_all | solution.py:39
  121.3 3.2 %image.1 = (f32[16,1024]{1,0:T(8,128)S(1)}, f32[32,1,128]{2,1,0:T(1,128)S(1)}) custom-call(bf16[32,16,128]{2,1,0:T(8,128)(2,1)S(1)} %all_to_all.63.weights, bf16[8,1024,512]{2,1,0:T(8,128)(2,1)S(1)} %get-tuple-element.58.rows, s32[1,1]{1,0:T(1,128)S(6)} %copy.9.counts, f32[24,1024]{1,0:T(8,128)S(1)} %copy-done.15, f32[16,1024]{1,0:T(8,128)S(1)} %get-tuple-element.51.sparse, ...), custom_call_target="tpu_custom_call" | custom-call | bytes 16777216 | tf_op jit(solution)/shard_map/image/pallas_call | solution.py:112
  124.6 11.0 %all_to_all.64.rows = f32[32,1,128]{2,1,0:T(1,128)S(1)} all-to-all(f32[32,1,128]{2,1,0:T(1,128)S(1)} %get-tuple-element.59), channel_id=1, replica_groups=mesh['z'=8,'yl'=2,'c'=2,'yh'=2,'x'=4] {'yl','c','yh','x'}, dimensions={0} | all-to-all | bytes 32768 | tf_op jit(solution)/shard_map/all_to_all | solution.py:39
  135.6 8.9 %all_to_all.65.rows = f32[8,1,128]{2,1,0:T(1,128)S(1)} all-to-all(f32[8,1,128]{2,1,0:T(1,128)S(1)} %sum_rows.1), channel_id=1, replica_groups=mesh['z'=8,'yl'=2,'c'=2,'yh'=2,'x'=4] {'z'}, dimensions={0} | all-to-all | bytes 8192 | tf_op jit(solution)/shard_map/all_to_all | solution.py:39
  144.5 0.1 update.1
  144.6 0.6 copy-done.17
  145.2 4.0 %collective-permute-start.11 = (bf16[16,1024]{1,0:T(8,128)(2,1)S(1)}, bf16[16,1024]{1,0:T(8,128)(2,1)S(1)}, u32[]{:S(2)}, u32[]{:S(2)}) collective-permute-start(bf16[16,1024]{1,0:T(8,128)(2,1)S(1)} %get-tuple-element.62.own), channel_id=1, source_target_pairs={{8,16},{24,32},{40,48},{56,64},{72,80},{88,96},{104,112},{120,128}... | collective-permute-start | bytes 98312 | tf_op jit(solution)/shard_map/ppermute | solution.py:54
  149.2 0.1 collective-permute-start.10
  149.3 2.3 project.1
  151.6 0.8 copy-done.11
  152.5 4.7 %all-to-all-start.8 = ((f32[32,32,128]{2,1,0:T(8,128)}), f32[32,32,128]{2,1,0:T(8,128)}, u32[]{:S(2)}, u32[]{:S(2)}) async-start(f32[32,32,128]{2,1,0:T(8,128)} %copy-done.11), calls=%async_computation.8 | async-start | bytes 1048576 | tf_op jit(solution)/shard_map/all_to_all | solution.py:39
  157.2 0.7 collective-permute-start.13
  157.8 4.1 %collective-permute-start.12 = (bf16[3,16,1024]{2,1,0:T(8,128)(2,1)S(1)}, bf16[3,16,1024]{2,1,0:T(8,128)(2,1)}, u32[]{:S(2)}, u32[]{:S(2)}) collective-permute-start(bf16[3,16,1024]{2,1,0:T(8,128)(2,1)S(1)} %stack.15.near), channel_id=1, source_target_pairs={{0,1},{1,0},{2,3},{3,2},{4,5},{5,4},{6,7},{7,6},{8,9},{9,8},{10,11... | collective-permute-start | bytes 294920 | tf_op jit(solution)/shard_map/ppermute | solution.py:48
  162.0 7.1 %all-to-all-done.8.refs_0_ = f32[32,32,128]{2,1,0:T(8,128)} async-done(((f32[32,32,128]{2,1,0:T(8,128)}), f32[32,32,128]{2,1,0:T(8,128)}, u32[]{:S(2)}, u32[]{:S(2)}) %all-to-all-start.8) | async-done | bytes 524320 | tf_op jit(solution)/shard_map/all_to_all | solution.py:39
  169.1 1.7 copy-done.13
  170.8 1.9 sparse.1
  172.7 1.1 sum_share.3
  173.8 11.2 %all_to_all.66.parts = f32[8,48,128]{2,1,0:T(8,128)S(1)} all-to-all(f32[8,48,128]{2,1,0:T(8,128)S(1)} %sum_share.3), channel_id=1, replica_groups=mesh['z'=8,'yl'=2,'c'=2,'yh'=2,'x'=4] {'z'}, dimensions={0} | all-to-all | bytes 393216 | tf_op jit(solution)/shard_map/all_to_all | solution.py:39
  185.0 2.7 %collective-permute-start.16 = (f32[16,128]{1,0:T(8,128)S(1)}, f32[16,128]{1,0:T(8,128)S(1)}, u32[]{:S(2)}, u32[]{:S(2)}) collective-permute-start(f32[16,128]{1,0:T(8,128)S(1)} %get-tuple-element.69.refs_0_.rounded), channel_id=1, source_target_pairs={{0,24},{8,16},{16,8},{24,0},{1,25},{9,17},{17,9},{25,1},{2,26},{10... | collective-permute-start | bytes 24584 | tf_op jit(solution)/shard_map/ppermute | solution.py:44
  187.7 1.8 collective-permute-start.15
  189.5 1.3 collective-permute-done.15.refs_2_
  190.9 0.9 coeffs.3
  191.8 17.3 %all_to_all.67.parts = f32[8,16,1152]{2,1,0:T(8,128)S(1)} all-to-all(f32[8,16,1152]{2,1,0:T(8,128)S(1)} %coeffs.3), channel_id=1, replica_groups=mesh['z'=8,'yl'=2,'c'=2,'yh'=2,'x'=4] {'yh','x'}, dimensions={0} | all-to-all | bytes 1179648 | tf_op jit(solution)/shard_map/all_to_all | solution.py:39
  209.1 1.7 weights.3
  210.8 1.2 collective-permute-start.17
  212.0 1.7 collective-permute-start.19
  213.7 0.9 collective-permute-done.18.second
  214.6 0.8 collective-permute-done.19.third
  215.4 0.1 gather_last.1
  215.5 12.6 %all_to_all.68.weights.every = bf16[32,32,128]{2,1,0:T(8,128)(2,1)S(1)} all-to-all(bf16[32,32,128]{2,1,0:T(8,128)(2,1)S(1)} %get-tuple-element.76), channel_id=1, replica_groups=mesh['z'=8,'yl'=2,'c'=2,'yh'=2,'x'=4] {'yh','x','yl','c'}, dimensions={0} | all-to-all | bytes 524288 | tf_op jit(solution)/shard_map/all_to_all | solution.py:39
  228.1 4.0 %finish.1 = (f32[16,1024]{1,0:T(8,128)}, f32[16,1024]{1,0:T(8,128)}) custom-call(bf16[32,32,128]{2,1,0:T(8,128)(2,1)S(1)} %all_to_all.68.weights.every, bf16[8,1024,512]{2,1,0:T(8,128)(2,1)S(1)} %copy-done.1, bf16[32,32,128]{2,1,0:T(8,128)(2,1)S(1)} %all_to_all.68.weights.every, s32[1,1]{1,0:T(1,128)S(6)} %copy.9.counts, ...), custom_call_target="tpu_custom_call" | custom-call | bytes 16777216 | tf_op jit(solution)/shard_map/finish/pallas_call | solution.py:112
  (57 shorter events, 0.4 us)
Async XLA Ops:
  0.6 33.1 %copy-start.20 = (s32[1,1,8,8]{3,2,1,0:T(8,128)S(1)}, s32[1,1,8,8]{3,2,1,0:T(8,128)}, u32[]{:S(2)}) copy-start(s32[1,1,8,8]{3,2,1,0:T(8,128)} %param.11) | copy-start | bytes 772
  3.0 38.6 %copy-start.15 = (f32[24,1024]{1,0:T(8,128)S(1)}, f32[24,1024]{1,0:T(8,128)}, u32[]{:S(2)}) copy-start(f32[24,1024]{1,0:T(8,128)} %get-tuple-element.42.own.halo) | copy-start | bytes 294916
  3.0 12.8 %collective-permute-start.1 = (f32[24,1024]{1,0:T(8,128)}, f32[24,1024]{1,0:T(8,128)S(1)}, u32[]{:S(2)}, u32[]{:S(2)}) collective-permute-start(f32[24,1024]{1,0:T(8,128)} %get-tuple-element.42.own.halo), channel_id=1, source_target_pairs={{8,16},{24,32},{40,48},{56,64},{72,80},{88,96},{104,112},{120,128}... | collective-permute-start | bytes 294920 | tf_op jit(solution)/shard_map/ppermute | solution.py:54
  7.7 8.0 %collective-permute-start = (f32[24,1024]{1,0:T(8,128)}, f32[24,1024]{1,0:T(8,128)S(1)}, u32[]{:S(2)}, u32[]{:S(2)}) collective-permute-start(f32[24,1024]{1,0:T(8,128)} %get-tuple-element.42.own.halo), channel_id=1, source_target_pairs={{0,8},{8,0},{16,24},{24,16},{32,40},{40,32},{48,56},{56,48},{64,72... | collective-permute-start | bytes 294920 | tf_op jit(solution)/shard_map/ppermute | solution.py:48
  7.8 17.6 %all-to-all-start = ((f32[32,8,128]{2,1,0:T(8,128)}), f32[32,8,128]{2,1,0:T(8,128)S(1)}, u32[]{:S(2)}, u32[]{:S(2)}) async-start(f32[32,8,128]{2,1,0:T(8,128)} %get-tuple-element.43), calls=%async_computation | async-start | bytes 262144 | tf_op jit(solution)/shard_map/all_to_all | solution.py:39
  15.7 0.9 copy-start.14
  16.7 17.1 %collective-permute-start.3 = (f32[3,24,1024]{2,1,0:T(8,128)S(1)}, f32[3,24,1024]{2,1,0:T(8,128)S(1)}, u32[]{:S(2)}, u32[]{:S(2)}) collective-permute-start(f32[3,24,1024]{2,1,0:T(8,128)S(1)} %stack.14.near), channel_id=1, source_target_pairs={{1,2},{3,4},{5,6},{2,1},{4,3},{6,5},{9,10},{11,12},{13,14},{10,9},... | collective-permute-start | bytes 884744 | tf_op jit(solution)/shard_map/ppermute | solution.py:54
  17.3 16.4 %collective-permute-start.2 = (f32[3,24,1024]{2,1,0:T(8,128)S(1)}, f32[3,24,1024]{2,1,0:T(8,128)S(1)}, u32[]{:S(2)}, u32[]{:S(2)}) collective-permute-start(f32[3,24,1024]{2,1,0:T(8,128)S(1)} %stack.14.near), channel_id=1, source_target_pairs={{0,1},{1,0},{2,3},{3,2},{4,5},{5,4},{6,7},{7,6},{8,9},{9,8},{10,11... | collective-permute-start | bytes 884744 | tf_op jit(solution)/shard_map/ppermute | solution.py:48
  21.2 100.1 %copy-start.16 = (f32[1,1,16,1024]{3,2,1,0:T(8,128)S(1)}, f32[1,1,16,1024]{3,2,1,0:T(8,128)}, u32[]{:S(2)}) copy-start(f32[1,1,16,1024]{3,2,1,0:T(8,128)} %param.8) | copy-start | bytes 196612
  21.2 100.1 %copy-start.19 = (f32[1,1,1024]{2,1,0:T(1,128)S(1)}, f32[1,1,1024]{2,1,0:T(1,128)}, u32[]{:S(2)}) copy-start(f32[1,1,1024]{2,1,0:T(1,128)} %param.9) | copy-start | bytes 12292
  26.1 15.5 %all-to-all-start.1 = ((f32[8,8,512]{2,1,0:T(8,128)}), f32[8,8,512]{2,1,0:T(8,128)S(1)}, u32[]{:S(2)}, u32[]{:S(2)}) async-start(f32[8,8,512]{2,1,0:T(8,128)} %compact.1), calls=%async_computation.1 | async-start | bytes 262144 | tf_op jit(solution)/shard_map/all_to_all | solution.py:39
  39.6 1.4 copy-start.12
  46.1 103.2 %copy-start = (bf16[8,1024,512]{2,1,0:T(8,128)(2,1)}, bf16[8,1024,512]{2,1,0:T(8,128)(2,1)S(1)}, u32[]{:S(2)}) copy-start(bf16[8,1024,512]{2,1,0:T(8,128)(2,1)S(1)} %get-tuple-element.58.rows) | copy-start | bytes 25165828
  75.6 3.9 %collective-permute-start.6 = (f32[16,128]{1,0:T(8,128)S(1)}, f32[16,128]{1,0:T(8,128)S(1)}, u32[]{:S(2)}, u32[]{:S(2)}) collective-permute-start(f32[16,128]{1,0:T(8,128)S(1)} %sum_depth.2.refs_0_), channel_id=1, source_target_pairs={{0,24},{8,16},{16,8},{24,0},{1,25},{9,17},{17,9},{25,1},{2,26},{10... | collective-permute-start | bytes 24584 | tf_op jit(solution)/shard_map/ppermute | solution.py:44
  78.1 2.6 %collective-permute-start.5 = (f32[16,128]{1,0:T(8,128)S(1)}, f32[16,128]{1,0:T(8,128)S(1)}, u32[]{:S(2)}, u32[]{:S(2)}) collective-permute-start(f32[16,128]{1,0:T(8,128)S(1)} %sum_depth.2.refs_0_), channel_id=1, source_target_pairs={{0,16},{8,24},{16,0},{24,8},{1,17},{9,25},{17,1},{25,9},{2,18},{10... | collective-permute-start | bytes 24584 | tf_op jit(solution)/shard_map/ppermute | solution.py:44
  79.4 1.3 collective-permute-start.4
  80.7 1.2 copy-start.2
  82.0 1.2 copy-start.5
  83.2 1.2 copy-start.8
  98.8 1.2 copy-start.3
  100.0 1.2 copy-start.6
  101.3 1.2 copy-start.9
  104.2 3.7 %collective-permute-start.7 = (f32[16,128]{1,0:T(8,128)S(1)}, f32[16,128]{1,0:T(8,128)S(1)}, u32[]{:S(2)}, u32[]{:S(2)}) collective-permute-start(f32[16,128]{1,0:T(8,128)S(1)} %get-tuple-element.55), channel_id=1, source_target_pairs={{0,8},{8,0},{16,24},{24,16},{1,9},{9,1},{17,25},{25,17},{2,10},{10... | collective-permute-start | bytes 24584 | tf_op jit(solution)/shard_map/ppermute | solution.py:44
  106.2 2.5 %collective-permute-start.8 = (f32[16,128]{1,0:T(8,128)S(1)}, f32[16,128]{1,0:T(8,128)S(1)}, u32[]{:S(2)}, u32[]{:S(2)}) collective-permute-start(f32[16,128]{1,0:T(8,128)S(1)} %get-tuple-element.56), channel_id=1, source_target_pairs={{0,16},{8,24},{16,0},{24,8},{1,17},{9,25},{17,1},{25,9},{2,18},{10... | collective-permute-start | bytes 24584 | tf_op jit(solution)/shard_map/ppermute | solution.py:44
  106.9 3.1 %collective-permute-start.9 = (f32[16,128]{1,0:T(8,128)S(1)}, f32[16,128]{1,0:T(8,128)S(1)}, u32[]{:S(2)}, u32[]{:S(2)}) collective-permute-start(f32[16,128]{1,0:T(8,128)S(1)} %get-tuple-element.57), channel_id=1, source_target_pairs={{0,24},{8,16},{16,8},{24,0},{1,25},{9,17},{17,9},{25,1},{2,26},{10... | collective-permute-start | bytes 24584 | tf_op jit(solution)/shard_map/ppermute | solution.py:44
  124.6 66.3 %copy-start.4 = (bf16[512,1024]{1,0:T(8,128)(2,1)S(1)}, bf16[512,1024]{1,0:T(8,128)(2,1)}, u32[]{:S(2)}) copy-start(bf16[512,1024]{1,0:T(8,128)(2,1)} %get-tuple-element.45.refs_4_.first) | copy-start | bytes 3145732
  124.6 66.3 %copy-start.7 = (bf16[512,1024]{1,0:T(8,128)(2,1)S(1)}, bf16[512,1024]{1,0:T(8,128)(2,1)}, u32[]{:S(2)}) copy-start(bf16[512,1024]{1,0:T(8,128)(2,1)} %get-tuple-element.46.refs_5_.second) | copy-start | bytes 3145732
  124.6 66.3 %copy-start.10 = (bf16[512,1024]{1,0:T(8,128)(2,1)S(1)}, bf16[512,1024]{1,0:T(8,128)(2,1)}, u32[]{:S(2)}) copy-start(bf16[512,1024]{1,0:T(8,128)(2,1)} %get-tuple-element.47.refs_6_.third) | copy-start | bytes 3145732
  144.6 0.6 copy-start.17
  145.2 7.2 %collective-permute-start.11 = (bf16[16,1024]{1,0:T(8,128)(2,1)S(1)}, bf16[16,1024]{1,0:T(8,128)(2,1)S(1)}, u32[]{:S(2)}, u32[]{:S(2)}) collective-permute-start(bf16[16,1024]{1,0:T(8,128)(2,1)S(1)} %get-tuple-element.62.own), channel_id=1, source_target_pairs={{8,16},{24,32},{40,48},{56,64},{72,80},{88,96},{104,112},{120,128}... | collective-permute-start | bytes 98312 | tf_op jit(solution)/shard_map/ppermute | solution.py:54
  149.2 3.3 %collective-permute-start.10 = (bf16[16,1024]{1,0:T(8,128)(2,1)S(1)}, bf16[16,1024]{1,0:T(8,128)(2,1)S(1)}, u32[]{:S(2)}, u32[]{:S(2)}) collective-permute-start(bf16[16,1024]{1,0:T(8,128)(2,1)S(1)} %get-tuple-element.62.own), channel_id=1, source_target_pairs={{0,8},{8,0},{16,24},{24,16},{32,40},{40,32},{48,56},{56,48},{64,72... | collective-permute-start | bytes 98312 | tf_op jit(solution)/shard_map/ppermute | solution.py:48
  151.6 0.8 copy-start.11
  152.5 75.7 %copy-start.18 = (f32[16,1024]{1,0:T(8,128)S(1)}, f32[16,1024]{1,0:T(8,128)}, u32[]{:S(2)}) copy-start(f32[16,1024]{1,0:T(8,128)} %copy-done.17) | copy-start | bytes 196612
  152.5 16.6 %all-to-all-start.8 = ((f32[32,32,128]{2,1,0:T(8,128)}), f32[32,32,128]{2,1,0:T(8,128)}, u32[]{:S(2)}, u32[]{:S(2)}) async-start(f32[32,32,128]{2,1,0:T(8,128)} %copy-done.11), calls=%async_computation.8 | async-start | bytes 1048576 | tf_op jit(solution)/shard_map/all_to_all | solution.py:39
  157.2 11.9 %collective-permute-start.13 = (bf16[3,16,1024]{2,1,0:T(8,128)(2,1)S(1)}, bf16[3,16,1024]{2,1,0:T(8,128)(2,1)S(1)}, u32[]{:S(2)}, u32[]{:S(2)}) collective-permute-start(bf16[3,16,1024]{2,1,0:T(8,128)(2,1)S(1)} %stack.15.near), channel_id=1, source_target_pairs={{1,2},{3,4},{5,6},{2,1},{4,3},{6,5},{9,10},{11,12},{13,14},{10,9},... | collective-permute-start | bytes 294920 | tf_op jit(solution)/shard_map/ppermute | solution.py:54
  157.8 11.2 %collective-permute-start.12 = (bf16[3,16,1024]{2,1,0:T(8,128)(2,1)S(1)}, bf16[3,16,1024]{2,1,0:T(8,128)(2,1)}, u32[]{:S(2)}, u32[]{:S(2)}) collective-permute-start(bf16[3,16,1024]{2,1,0:T(8,128)(2,1)S(1)} %stack.15.near), channel_id=1, source_target_pairs={{0,1},{1,0},{2,3},{3,2},{4,5},{5,4},{6,7},{7,6},{8,9},{9,8},{10,11... | collective-permute-start | bytes 294920 | tf_op jit(solution)/shard_map/ppermute | solution.py:48
  169.0 59.1 %copy-start.1 = (bf16[8,1024,512]{2,1,0:T(8,128)(2,1)S(1)}, bf16[8,1024,512]{2,1,0:T(8,128)(2,1)}, u32[]{:S(2)}) copy-start(bf16[8,1024,512]{2,1,0:T(8,128)(2,1)} %copy-done) | copy-start | bytes 25165828
  169.1 1.7 copy-start.13
  185.0 4.5 %collective-permute-start.16 = (f32[16,128]{1,0:T(8,128)S(1)}, f32[16,128]{1,0:T(8,128)S(1)}, u32[]{:S(2)}, u32[]{:S(2)}) collective-permute-start(f32[16,128]{1,0:T(8,128)S(1)} %get-tuple-element.69.refs_0_.rounded), channel_id=1, source_target_pairs={{0,24},{8,16},{16,8},{24,0},{1,25},{9,17},{17,9},{25,1},{2,26},{10... | collective-permute-start | bytes 24584 | tf_op jit(solution)/shard_map/ppermute | solution.py:44
  187.7 3.1 %collective-permute-start.15 = (f32[16,128]{1,0:T(8,128)S(1)}, f32[16,128]{1,0:T(8,128)S(1)}, u32[]{:S(2)}, u32[]{:S(2)}) collective-permute-start(f32[16,128]{1,0:T(8,128)S(1)} %get-tuple-element.69.refs_0_.rounded), channel_id=1, source_target_pairs={{0,16},{8,24},{16,0},{24,8},{1,17},{9,25},{17,1},{25,9},{2,18},{10... | collective-permute-start | bytes 24584 | tf_op jit(solution)/shard_map/ppermute | solution.py:44
  189.5 1.3 collective-permute-start.14
  210.8 2.9 %collective-permute-start.17 = (f32[16,256]{1,0:T(8,128)S(1)}, f32[16,256]{1,0:T(8,128)S(1)}, u32[]{:S(2)}, u32[]{:S(2)}) collective-permute-start(f32[16,256]{1,0:T(8,128)S(1)} %get-tuple-element.72), channel_id=1, source_target_pairs={{0,8},{8,0},{16,24},{24,16},{1,9},{9,1},{17,25},{25,17},{2,10},{10... | collective-permute-start | bytes 49160 | tf_op jit(solution)/shard_map/ppermute | solution.py:44
  212.0 2.6 %collective-permute-start.18 = (f32[16,256]{1,0:T(8,128)S(1)}, f32[16,256]{1,0:T(8,128)S(1)}, u32[]{:S(2)}, u32[]{:S(2)}) collective-permute-start(f32[16,256]{1,0:T(8,128)S(1)} %get-tuple-element.73), channel_id=1, source_target_pairs={{0,16},{8,24},{16,0},{24,8},{1,17},{9,25},{17,1},{25,9},{2,18},{10... | collective-permute-start | bytes 49160 | tf_op jit(solution)/shard_map/ppermute | solution.py:44
  212.0 3.4 %collective-permute-start.19 = (f32[16,256]{1,0:T(8,128)S(1)}, f32[16,256]{1,0:T(8,128)S(1)}, u32[]{:S(2)}, u32[]{:S(2)}) collective-permute-start(f32[16,256]{1,0:T(8,128)S(1)} %get-tuple-element.74), channel_id=1, source_target_pairs={{0,24},{8,16},{16,8},{24,0},{1,25},{9,17},{17,9},{25,1},{2,26},{10... | collective-permute-start | bytes 49160 | tf_op jit(solution)/shard_map/ppermute | solution.py:44

commit v4 on v3

--- a/solution.py
+++ b/solution.py
@@ -1,3 +1,5 @@
+import functools
+
 import jax
 import jax.numpy as jnp
 from jax import lax
@@ -14,6 +16,7 @@
 CHUNKS = 8
 CAP = 8
 EMPTY = 72
+HALF = 4
 QUARTER = 1024
 
 support_radius = 0.32
@@ -22,7 +25,6 @@
 
 ALL = ("z", "yl", "c", "yh", "x")
 PLANE = ("yh", "x", "yl", "c")
-CELLS = ("yl", "c", "yh", "x")
 GX = ("z", "yl", "c")
 GY = ("yh", "x")
 f32 = jnp.float32
@@ -129,7 +131,7 @@
 FIELD = shape(PROBES, PTS)
 
 
-def prepare_kernel(coords, probes, precond, counts, inducing, centre_out, halo_out):
+def prepare_kernel(place, coords, probes, precond, counts, inducing, centre_out, halo_out):
     points = coords[...]
     lane = lax.broadcasted_iota(jnp.int32, (FEAT, PTS), 1)
     short = lax.broadcasted_iota(jnp.int32, (FEAT, 128), 1)
@@ -139,56 +141,53 @@
             jnp.where(lane == inducing[0, index], points, 0.0), axis=1, keepdims=True
         )
         centre = jnp.where(short == index, picked, centre)
-    centre_out[...] = jnp.broadcast_to(centre[None], centre_out.shape)
+    row = centre[:1]
+    for feature in range(1, FEAT):
+        row = row + pltpu.roll(centre, 128 - 16 * feature, 1)[feature : feature + 1]
+    centre_out[...] = jnp.broadcast_to(row[None], centre_out.shape)
     halo_out[:FEAT] = points
     halo_out[FEAT:] = precond[...] * (probes[...] * live_lanes(counts[0, 0]))
 
 
-def prepare(coords, probes, precond, counts, inducing):
+def prepare(place, coords, probes, precond, counts, inducing):
     return call(
         prepare_kernel,
         "prepare",
-        (shape(32, FEAT, 128), shape(FEAT + PROBES, PTS)),
-        [VMEM, VMEM, VMEM, SMEM, SMEM],
-        (coords, probes, precond, counts, inducing),
+        (shape(256, 1, 128), shape(FEAT + PROBES, PTS)),
+        [SMEM, VMEM, VMEM, VMEM, SMEM, SMEM],
+        (place, coords, probes, precond, counts, inducing),
         params=LARGE,
     )
 
 
-def compact_kernel(parts, out):
-    for tile in range(4):
-        total = parts[8 * tile]
-        for cell in range(1, 8):
-            total = total + pltpu.roll(parts[8 * tile + cell], 16 * cell, 1)
-        out[:, :, tile * 128 : (tile + 1) * 128] = jnp.broadcast_to(total[None], (8, FEAT, 128))
-
-
-def compact(parts):
-    return call(compact_kernel, "compact", shape(8, FEAT, CHUNK), [VMEM], (parts,))
-
-
-def factor_kernel(quad, factor, first_out, second_out, third_out):
-    first, second, third = split3(factor[...])
-    first_out[...] = first.astype(bf16)
-    second_out[...] = second.astype(bf16)
-    third_out[...] = third.astype(bf16)
-
-
-def split_factor(quad, factor):
-    block = pl.BlockSpec((SHARE, QUARTER), lambda k, quad: (k, 0))
-    return pl.pallas_call(
+def factor_kernel(place, columns, first_out, second_out, third_out):
+    for index in range(4):
+        start = pl.multiple_of((place[0, 0] ^ index) * SHARE, SHARE)
+        parts = split3(columns[pl.ds(start, SHARE), :])
+        for out, part in zip((first_out, second_out, third_out), parts):
+            out[index * SHARE : (index + 1) * SHARE] = part.astype(bf16)
+
+
+def split_factor(place, columns):
+    return call(
         factor_kernel,
-        out_shape=(shape(4 * SHARE, QUARTER, dtype=bf16),) * 3,
-        grid_spec=pltpu.PrefetchScalarGridSpec(
-            num_scalar_prefetch=1,
-            grid=(4,),
-            in_specs=[pl.BlockSpec((SHARE, QUARTER), lambda k, quad: (quad[0] ^ k, quad[0]))],
-            out_specs=(block,) * 3,
-        ),
-        compiler_params=LARGE,
-        cost_estimate=pl.CostEstimate(flops=0, bytes_accessed=8 << 20, transcendentals=0),
-        name="factor",
-    )(quad, factor)
+        "factor",
+        (shape(4 * SHARE, QUARTER, dtype=bf16),) * 3,
+        [SMEM, VMEM],
+        (place, columns),
+        moved=8 << 20,
+    )
+
+
+def centre_columns(parts):
+    group = lax.broadcasted_iota(jnp.int32, (8, 128), 1) // 16
+    tiles = []
+    for index in range(4):
+        tile = pltpu.roll(parts[8 * index : 8 * index + 8], 0, 1, stride=16, stride_axis=0)
+        for bit in (1, 2, 4):
+            tile = jnp.where(group & bit != 0, pltpu.roll(tile, 8 - bit, 0), tile)
+        tiles.append(pltpu.roll(tile, 0, 1, stride=16, stride_axis=0))
+    return jnp.concatenate(tiles, axis=1)
 
 
 def rows_kernel(halo, centres, rows_out, sums_out, left, packed):
@@ -197,7 +196,7 @@
         left[...] = augmented(halo[:FEAT], -LOG2E / width_sq, True).astype(f32).T.astype(bf16)
         packed[...] = halo[FEAT:].astype(bf16)
 
-    right = augmented(centres[0], -LOG2E / width_sq, False)
+    right = augmented(centre_columns(centres[...]), -LOG2E / width_sq, False)
     power = jnp.dot(left[...], right, preferred_element_type=f32)
     rows = jnp.exp2(jnp.minimum(power, 0.0)).astype(bf16)
     rows_out[0] = rows
@@ -213,7 +212,7 @@
         (shape(CHUNKS, PTS, CHUNK, dtype=bf16), shape(32, PROBES, SHARE)),
         [
             pl.BlockSpec((FEAT + PROBES, PTS), lambda g: (0, 0)),
-            pl.BlockSpec((1, FEAT, CHUNK), lambda g: (g, 0, 0)),
+            pl.BlockSpec((32, 128), lambda g: (g, 0)),
         ],
         (halo, centres),
         scratch=[pltpu.VMEM((PTS, 64), bf16), pltpu.VMEM((PROBES, PTS), bf16)],
@@ -251,9 +250,9 @@
     )
 
 
-def fill_table(table, sides, sources, first, last, dtype):
-    places_x = (1, 2 - 2 * sides[0, 0], 2 * sides[0, 0])
-    places_y = (1, 2 - 2 * sides[0, 1], 2 * sides[0, 1])
+def fill_table(table, place, sources, first, last, dtype):
+    places_x = (1, 2 - 2 * place[0, 1], 2 * place[0, 1])
+    places_y = (1, 2 - 2 * place[0, 2], 2 * place[0, 2])
     for place_y, source in zip(places_y, sources):
         for index, place_x in enumerate(places_x):
             start = (place_x * 3 + place_y) * CAP
@@ -267,13 +266,13 @@
     return jnp.concatenate([table[codes[block, entry]] for entry in range(CAP)], axis=1)
 
 
-def tiles_kernel(codes, sides, near, even, odd, tiles_out, sparse_out, points, values):
-    block = pl.program_id(0)
-
-    @pl.when(block == 0)
+def tiles_kernel(base, codes, place, near, even, odd, tiles_out, sparse_out, points, values):
+    block = base + pl.program_id(0)
+
+    @pl.when(pl.program_id(0) == 0)
     def _():
-        fill_table(points, sides, (near, even, odd), 0, FEAT, f32)
-        fill_table(values, sides, (near, even, odd), FEAT, FEAT + PROBES, bf16)
+        fill_table(points, place, (near, even, odd), 0, FEAT, f32)
+        fill_table(values, place, (near, even, odd), FEAT, FEAT + PROBES, bf16)
 
     scale = 1.0 / (support_radius * support_radius)
     own = augmented(points[4 * CAP + block], scale, True).astype(f32).T.astype(bf16)
@@ -288,24 +287,24 @@
     sparse_out[...] = nt_dot(partners(values, codes, block), tile)
 
 
-def make_tiles(codes, sides, near, even, odd):
+def make_tiles(half, codes, place, near, even, odd):
     whole = pl.BlockSpec((3, FEAT + PROBES, PTS), lambda b: (0, 0, 0))
     return call(
-        tiles_kernel,
+        functools.partial(tiles_kernel, half * HALF),
         "tiles",
-        (shape(CAP, BLOCK, PTS, dtype=bf16), FIELD),
+        (shape(HALF, BLOCK, PTS, dtype=bf16), shape(PROBES, HALF * BLOCK)),
         [SMEM, SMEM, whole, whole, whole],
-        (codes, sides, near, even, odd),
+        (codes, place, near, even, odd),
         scratch=[
             pltpu.VMEM((EMPTY + 1, FEAT, BLOCK), f32),
             pltpu.VMEM((EMPTY + 1, PROBES, BLOCK), bf16),
         ],
-        grid=(CAP,),
+        grid=(HALF,),
         out_specs=(
             pl.BlockSpec((1, BLOCK, PTS), lambda b: (b, 0, 0)),
             pl.BlockSpec((PROBES, BLOCK), lambda b: (0, b)),
         ),
-        moved=16 << 20,
+        moved=8 << 20,
     )
 
 
@@ -315,20 +314,14 @@
     return alpha, alpha * alpha * as_column(row, 32) / rz_now - 1.0
 
 
-def row_total(rows):
-    total = rows[0]
-    for index in range(1, rows.shape[0]):
-        total = total + rows[index]
-    return total
-
-
 def sparse_kernel(
-    codes, sides, near, even, odd, tiles, search, residual, precond, sparse_out, sums_out, values
+    codes, place, near, even, odd, tiles_low, tiles_high, search, residual, precond,
+    sparse_out, sums_out, values,
 ):
-    fill_table(values, sides, (near, even, odd), 0, PROBES, bf16)
+    fill_table(values, place, (near, even, odd), 0, PROBES, bf16)
     for block in range(CAP):
         sparse_out[:, block * BLOCK : (block + 1) * BLOCK] = nt_dot(
-            partners(values, codes, block), tiles[block]
+            partners(values, codes, block), (tiles_low, tiles_high)[block // HALF][block % HALF]
         )
     field = search[...]
     left = residual[...]
@@ -338,13 +331,13 @@
     sums_out[...] = jnp.where(lane == 0, curve, jnp.where(lane == 1, norm, 0.0))
 
 
-def apply_tiles(codes, sides, nears, tiles, search, residual, precond):
+def apply_tiles(codes, place, nears, tiles, search, residual, precond):
     return call(
         sparse_kernel,
         "sparse",
         (FIELD, shape(PROBES, 128)),
-        [SMEM, SMEM] + [VMEM] * 7,
-        (codes, sides, *nears, tiles, search, residual, precond),
+        [SMEM, SMEM] + [VMEM] * 8,
+        (codes, place, *nears, *tiles, search, residual, precond),
         scratch=[pltpu.VMEM((EMPTY + 1, PROBES, BLOCK), bf16)],
         moved=6 << 20,
     )
@@ -356,15 +349,14 @@
     out[2] = odd[...]
 
 
-def surround(value, *first):
+def surround(value, even, odd):
     column = call(
         stack_kernel,
         "stack",
         shape(3, *value.shape, dtype=value.dtype),
         [VMEM] * 3,
-        (value, even_pairs(value, GX), odd_pairs(value, GX)),
-    )
-    column = after(column, *first)
+        (value, even, odd),
+    )
     return column, even_pairs(column, GY), odd_pairs(column, GY)
 
 
@@ -378,7 +370,7 @@
 
 
 def image_kernel(
-    weights, rows, counts, halo, sparse, precond, probes, image_out, sums_out, total
+    weights, rows, counts, halo, sparse_low, sparse_high, precond, probes, image_out, sums_out, total
 ):
     expand_step(weights, rows, total)
 
@@ -386,36 +378,38 @@
     def _():
         search = halo[FEAT:]
         live = live_lanes(counts[0, 0])
-        image = live * (search + sparse[...] + total[...])
+        sparse = jnp.concatenate([sparse_low[...], sparse_high[...]], axis=1)
+        image = live * (search + sparse + total[...])
         image_out[...] = image
         norm = jnp.sum(search * (probes[...] * live), axis=1, keepdims=True)
         curve = jnp.sum(search * image, axis=1, keepdims=True)
         square = jnp.sum(precond[...] * image * image, axis=1, keepdims=True)
         row = as_lanes(norm, 0) + as_lanes(curve, 16) + as_lanes(square, 32)
-        for index in range(32):
-            sums_out[index] = row
+        sums_out[...] = jnp.broadcast_to(row[None], sums_out.shape)
 
 
 def make_image(weights, rows, counts, halo, sparse, precond, probes):
     height = weights.shape[1]
     still = pl.BlockSpec((PROBES, PTS), lambda g: (0, 0))
+    half = pl.BlockSpec((PROBES, HALF * BLOCK), lambda g: (0, 0))
     return call(
         image_kernel,
         "image",
-        (FIELD, shape(32, 1, 128)),
+        (FIELD, shape(256, 1, 128)),
         [
             pl.BlockSpec((4, height, SHARE), lambda g: (g, 0, 0)),
             pl.BlockSpec((1, PTS, CHUNK), lambda g: (g, 0, 0)),
             SMEM,
             pl.BlockSpec((FEAT + PROBES, PTS), lambda g: (0, 0)),
-            still,
+            half,
+            half,
             pl.BlockSpec((1, PTS), lambda g: (0, 0)),
             still,
         ],
-        (weights, rows, counts, halo, sparse, precond, probes),
+        (weights, rows, counts, halo, *sparse, precond, probes),
         scratch=[pltpu.VMEM((PROBES, PTS), f32)],
         grid=(CHUNKS,),
-        out_specs=(still, pl.BlockSpec((32, 1, 128), lambda g: (0, 0, 0))),
+        out_specs=(still, pl.BlockSpec((256, 1, 128), lambda g: (0, 0, 0))),
         params=MIDDLE,
         moved=16 << 20,
     )
@@ -425,7 +419,7 @@
     rows, halo, probes, precond, counts, image,
     residual_out, search_out, packed_out, rounded_out, solution_out,
 ):
-    alpha, beta = steps_of(row_total(rows))
+    alpha, beta = steps_of(jnp.sum(rows[...], axis=0))
     search = halo[FEAT:]
     solution_out[...] = alpha * search
     residual = probes[...] * live_lanes(counts[0, 0]) - alpha * image[...]
@@ -454,16 +448,6 @@
     )
 
 
-def sum_rows_kernel(rows, out):
-    total = row_total(rows)
-    for index in range(out.shape[0]):
-        out[index] = total
-
-
-def sum_rows(rows, count):
-    return call(sum_rows_kernel, "sum_rows", shape(count, 1, 128), [VMEM], (rows,))
-
-
 def sum_share_kernel(*refs):
     parts, out = refs[0], refs[-1]
     total = jnp.sum(parts[...], axis=0)
@@ -498,12 +482,13 @@
 
 def six_products(value, factors, dot):
     first, second, third = split3(value)
-    total = dot(third.astype(bf16), factors[0][...])
-    total = total + dot(second.astype(bf16), factors[1][...])
-    total = total + dot(first.astype(bf16), factors[2][...])
-    total = total + dot(second.astype(bf16), factors[0][...])
-    total = total + dot(first.astype(bf16), factors[1][...])
-    return total + dot(first.astype(bf16), factors[0][...])
+    stacked = jnp.concatenate([third, second, first], axis=0).astype(bf16)
+    by_first = dot(stacked, factors[0][...])
+    by_second = dot(stacked[PROBES:], factors[1][...])
+    by_third = dot(stacked[2 * PROBES :], factors[2][...])
+    small = by_first[:PROBES] + by_second[:PROBES] + by_third
+    middle = by_first[PROBES : 2 * PROBES] + by_second[PROBES:]
+    return by_first[2 * PROBES :] + (middle + small)
 
 
 def nn_dot(left, right):
@@ -632,50 +617,59 @@
 
 def on_device(coords, probes, precond, counts, neighbours, inducing, factor):
     quad = lax.axis_index("yl") * 2 + lax.axis_index("c")
-    sides = jnp.stack([lax.axis_index("c"), lax.axis_index("x") % 2]).reshape(1, 2)
+    place = jnp.stack([quad, lax.axis_index("c"), lax.axis_index("x") & 1]).reshape(1, 3)
     points = coords[0, 0]
     given = probes[0, 0]
     scaling = precond[0]
     codes = neighbours[0, 0]
 
-    centre_parts, halo = prepare(points, given, scaling, counts, inducing[0])
-
-    got = exchange(centre_parts, CELLS)
-    factors = split_factor(after(quad.reshape(1), halo), factor)
-    halos = surround(halo)
-    got = after(got, halos[0], *factors)
-    compacted = compact(got)
-    centres = exchange(compacted, "z")
-    tiles, sparse = make_tiles(codes, sides, after(halos[0], compacted), halos[1], halos[2])
-    centres = after(centres, tiles, sparse)
-    rows, parts = make_rows(halo, centres)
+    centre_parts, halo = prepare(place, points, given, scaling, counts, inducing[0])
+
+    even, odd = even_pairs(halo, GX), odd_pairs(halo, GX)
+    centres = exchange(centre_parts, ALL).reshape(256, 128)
+    halos = surround(after(halo, centres), even, odd)
+    columns = lax.dynamic_slice_in_dim(after(factor, halos[0]), quad * QUARTER, QUARTER, 1)
+    factors = split_factor(place, columns)
+    rows, parts = make_rows(halo, after(centres, halos[0], *factors))
+    parts = after(parts, *halos)
 
     def depth_of(got, *sums):
         return sum_depth(exchange(sum_share(got, *sums), "z"))
 
-    def terms_of(depth):
+    def coeffs_of(depth, beside):
         own = depth[0]
         shares = [own] + [quad_partner(own, step) for step in (1, 2, 3)]
-        terms = exchange(coeff_terms(shares, factors, *depth[2:]), GY)
-        terms = weight_terms(terms, factors)
+        shares[0] = after(own, *beside)
+        return exchange(coeff_terms(shares, factors, *depth[2:]), GY)
+
+    def terms_of(coeffs):
+        terms = weight_terms(coeffs, factors)
         return [terms[0]] + [quad_partner(terms[step], step) for step in (1, 2, 3)]
 
-    terms = terms_of(depth_of(exchange(parts, PLANE)))
+    depth = depth_of(exchange(parts, PLANE))
+    low = make_tiles(0, codes, place, after(halos[0], depth[0]), *halos[1:])
+    coeffs = coeffs_of(depth, low)
+    terms = weight_terms(coeffs, factors)
+    high = make_tiles(1, codes, place, after(halos[0], terms[0]), *halos[1:])
+    terms = [after(terms[0], *high)] + [quad_partner(terms[step], step) for step in (1, 2, 3)]
     weights = exchange(gather_weights(terms), PLANE)
+    tiles, sparse = zip(low, high)
     image, row = make_image(weights, rows, counts, halo, sparse, scaling, given)
-    row = exchange(sum_rows(exchange(row, CELLS), 8), "z")
+    row = exchange(row, ALL)
     residual, search, packed, rounded, solution = update(
         row, halo, given, scaling, counts, image
     )
 
+    even, odd = even_pairs(rounded, GX), odd_pairs(rounded, GX)
     parts = project(packed, rows)
-    nears = surround(rounded, parts)
+
+    nears = surround(after(rounded, parts), even, odd)
     got = exchange(after(parts, nears[0]), PLANE)
     sparse, sums = apply_tiles(
-        codes, sides, (after(nears[0], got),) + nears[1:], tiles, search, residual, scaling
+        codes, place, (after(nears[0], got),) + nears[1:], tiles, search, residual, scaling
     )
     depth = depth_of(got, sums)
-    weights, totals = gather_last(terms_of(depth), depth[0], depth[1])
+    weights, totals = gather_last(terms_of(coeffs_of(depth, ())), depth[0], depth[1])
     weights = exchange(weights, PLANE)
     solution, residual = finish(
         weights, rows, counts, search, sparse, residual, solution, totals

time: 233 us -> 226 us (0.970)
  waiting for transfers between devices: 14.1 us -> 19.5 us
  blocking collectives: 115 us -> 110 us
  starting transfers between devices: 53.2 us -> 49.4 us
  Pallas kernels: 35.2 us -> 32.3 us
    all_to_all x3 -> x2, waiting for transfers between devices: 7.66 us -> 16.4 us  [exchange(): return lax.all_to_all(parts, axes, 0, 0, tiled=True)]
    all_to_all x9 -> x8, blocking collectives: 115 us -> 110 us  [exchange(): return lax.all_to_all(parts, axes, 0, 0, tiled=True)]
    pallas_call x1 -> x0, Pallas kernels: 4.14 us -> none  [split_factor(): pl.pallas_call(factor_kernel, out_shape=(shape(4 * SHARE, QUARTER, dtype=...]
    ppermute x12, waiting for transfers between devices: 6.43 us -> 3.06 us  [quad_partner(): return lax.ppermute(value, ('yl', 'c'), pairs)]
    unnamed x42 -> x34, local copies, waits for them, and re-layouts: 12.8 us -> 9.68 us
    ppermute x4, starting transfers between devices: 8.19 us -> 5.56 us  [even_pairs(): lax.ppermute(value, axes, [(i, i ^ 1) for i in range(lax.axis_size(axes))])]
    all_to_all x3 -> x2, starting transfers between devices: 20.2 us -> 20.3 us  [exchange(): return lax.all_to_all(parts, axes, 0, 0, tiled=True)]
  transfers between devices with their start and end apart: 23 -> 22, of which waited for: 9 -> 5; matrix products, arithmetic and copies ran while one was open for 0% -> 1% of each run, Pallas kernels for 6% -> 7%
where the time goes in v4:
time: 226 us; the launch traced here: 225 us
  blocking collectives  110 us (49%)
  starting transfers between devices  49.4 us (22%)
  Pallas kernels  32.3 us (14%)
  waiting for transfers between devices  19.5 us (9%)
  local copies, waits for them, and re-layouts  11.4 us (5%)
    all_to_all x8, blocking collectives, exchange(): return lax.all_to_all(parts, axes, 0, 0, tiled=True)  110 us
    pallas_call x22, Pallas kernels, call(): pl.pallas_call(kernel, out_shape=out_shape, in_specs=in_specs, out_specs=...  32.3 us
    all_to_all x2, starting transfers between devices, exchange(): return lax.all_to_all(parts, axes, 0, 0, tiled=True)  20.3 us
    all_to_all x2, waiting for transfers between devices, exchange(): return lax.all_to_all(parts, axes, 0, 0, tiled=True)  16.4 us
    ppermute x12, starting transfers between devices, quad_partner(): return lax.ppermute(value, ('yl', 'c'), pairs)  14.8 us
    unnamed x34, local copies, waits for them, and re-layouts  9.68 us
    ppermute x4, starting transfers between devices, odd_pairs(): return lax.ppermute(value, axes, pairs + [(j, i) for i, j in pairs])  8.75 us
    ppermute x4, starting transfers between devices, even_pairs(): lax.ppermute(value, axes, [(i, i ^ 1) for i in range(lax.axis_size(axes))])  5.56 us
  transfers between devices with their start and end apart: 22, of which 5 were waited for; matrix products, arithmetic and copies ran while one was open for 1% of the time, Pallas kernels for 7%

profile of v4, /device:TPU:1, one launch (start us, length us, event | category | flops | bytes accessed | tf_op | source)
XLA Modules:
  0.0 224.8 jit_solution(1969934738702893726)
XLA Ops:
  1.3 0.7 add_bitcast_fusion.place
  2.0 1.8 prepare.1
  3.8 15.7 %all-to-all-start = ((f32[256,1,128]{2,1,0:T(1,128)}), f32[256,1,128]{2,1,0:T(1,128)S(1)}, u32[]{:S(2)}, u32[]{:S(2)}) async-start(f32[256,1,128]{2,1,0:T(1,128)} %get-tuple-element.49), calls=%async_computation | async-start | bytes 262144 | tf_op jit(solution)/shard_map/all_to_all | solution.py:41
  19.4 3.5 %collective-permute-start.1 = (f32[24,1024]{1,0:T(8,128)}, f32[24,1024]{1,0:T(8,128)S(1)}, u32[]{:S(2)}, u32[]{:S(2)}) collective-permute-start(f32[24,1024]{1,0:T(8,128)} %get-tuple-element.50.own.halo), channel_id=1, source_target_pairs={{8,16},{24,32},{40,48},{56,64},{72,80},{88,96},{104,112},{120,128}... | collective-permute-start | bytes 294920 | tf_op jit(solution)/shard_map/ppermute | solution.py:56
  23.0 0.1 collective-permute-start
  23.1 9.2 %all-to-all-done = f32[256,1,128]{2,1,0:T(1,128)S(1)} async-done(((f32[256,1,128]{2,1,0:T(1,128)}), f32[256,1,128]{2,1,0:T(1,128)S(1)}, u32[]{:S(2)}, u32[]{:S(2)}) %all-to-all-start) | async-done | bytes 131104 | tf_op jit(solution)/shard_map/all_to_all | solution.py:41
  32.3 0.7 copy-done.11
  32.9 0.9 copy-done.3
  33.8 1.4 collective-permute-start.3
  35.2 1.4 collective-permute-start.2
  36.7 1.8 constant_dynamic-slice_fusion.columns
  38.4 0.7 copy-done.15
  39.1 1.1 factor.1
  40.3 0.9 copy-done.4
  41.2 0.9 copy-done.12
  42.1 5.7 %rows.1 = (bf16[8,1024,512]{2,1,0:T(8,128)(2,1)S(1)}, f32[32,16,128]{2,1,0:T(8,128)S(1)}) custom-call(f32[24,1024]{1,0:T(8,128)S(1)} %copy-done.4, f32[256,128]{1,0:T(8,128)S(1)} %bitcast.16), custom_call_target="tpu_custom_call" | custom-call | bytes 16777216 | tf_op jit(solution)/shard_map/rows/pallas_call | solution.py:114
  47.7 0.0 collective-permute-done.3.odd
  47.7 0.0 collective-permute-done.2.even
  47.7 15.5 %all_to_all.50.refs_0_ = f32[32,16,128]{2,1,0:T(8,128)S(1)} all-to-all(f32[32,16,128]{2,1,0:T(8,128)S(1)} %get-tuple-element.57), channel_id=1, replica_groups=mesh['z'=8,'yl'=2,'c'=2,'yh'=2,'x'=4] {'yh','x','yl','c'}, dimensions={0} | all-to-all | bytes 524288 | tf_op jit(solution)/shard_map/all_to_all | solution.py:41
  63.3 10.7 %all_to_all.51.parts = f32[8,16,128]{2,1,0:T(8,128)S(1)} all-to-all(f32[8,16,128]{2,1,0:T(8,128)S(1)} %sum_share.2), channel_id=1, replica_groups=mesh['z'=8,'yl'=2,'c'=2,'yh'=2,'x'=4] {'z'}, dimensions={0} | all-to-all | bytes 131072 | tf_op jit(solution)/shard_map/all_to_all | solution.py:41
  73.9 2.6 %collective-permute-start.6 = (f32[16,128]{1,0:T(8,128)S(1)}, f32[16,128]{1,0:T(8,128)S(1)}, u32[]{:S(2)}, u32[]{:S(2)}) collective-permute-start(f32[16,128]{1,0:T(8,128)S(1)} %sum_depth.2.refs_0_), channel_id=1, source_target_pairs={{0,24},{8,16},{16,8},{24,0},{1,25},{9,17},{17,9},{25,1},{2,26},{10... | collective-permute-start | bytes 24584 | tf_op jit(solution)/shard_map/ppermute | solution.py:46
  76.5 1.3 collective-permute-start.5
  77.8 0.0 collective-permute-start.4
  77.8 3.7 %tiles.2 = (bf16[4,128,1024]{2,1,0:T(8,128)(2,1)S(1)}, f32[16,512]{1,0:T(8,128)S(1)}) custom-call(s32[8,8]{1,0:T(8,128)S(1)} %bitcast.21, s32[1,3]{1,0:T(1,128)S(1)} %copy-done.16, f32[3,24,1024]{2,1,0:T(8,128)S(1)} %stack.18.near, f32[3,24,1024]{2,1,0:T(8,128)} %collective-permute-done.2.even, f32[3,24,1024]{2,1,0:T(8,128)} %collective-permute-done.3.odd), custom_call_target="tpu_custom_call" | custom-call | bytes 8388608 | tf_op jit(solution)/shard_map/tiles/pallas_call | solution.py:114
  81.5 1.0 copy-done.6
  82.5 0.6 coeffs.2
  83.1 13.3 %all_to_all.52.parts = f32[8,16,1024]{2,1,0:T(8,128)S(1)} all-to-all(f32[8,16,1024]{2,1,0:T(8,128)S(1)} %coeffs.2), channel_id=1, replica_groups=mesh['z'=8,'yl'=2,'c'=2,'yh'=2,'x'=4] {'yh','x'}, dimensions={0} | all-to-all | bytes 1048576 | tf_op jit(solution)/shard_map/all_to_all | solution.py:41
  96.3 1.0 weights.2
  97.3 1.9 collective-permute-start.7
  99.2 0.3 collective-permute-start.8
  99.5 1.4 collective-permute-start.9
  100.9 3.7 %tiles.3 = (bf16[4,128,1024]{2,1,0:T(8,128)(2,1)S(1)}, f32[16,512]{1,0:T(8,128)S(1)}) custom-call(s32[8,8]{1,0:T(8,128)S(1)} %bitcast.22, s32[1,3]{1,0:T(1,128)S(1)} %copy-done.16, f32[3,24,1024]{2,1,0:T(8,128)S(1)} %stack.18.near, f32[3,24,1024]{2,1,0:T(8,128)} %collective-permute-done.2.even, f32[3,24,1024]{2,1,0:T(8,128)} %collective-permute-done.3.odd), custom_call_target="tpu_custom_call" | custom-call | bytes 8388608 | tf_op jit(solution)/shard_map/tiles/pallas_call | solution.py:114
  104.6 1.0 copy-done.8
  105.6 0.0 collective-permute-done.7.first
  105.7 10.6 %all_to_all.53.weights = bf16[32,16,128]{2,1,0:T(8,128)(2,1)S(1)} all-to-all(bf16[32,16,128]{2,1,0:T(8,128)(2,1)S(1)} %gather.1), channel_id=1, replica_groups=mesh['z'=8,'yl'=2,'c'=2,'yh'=2,'x'=4] {'yh','x','yl','c'}, dimensions={0} | all-to-all | bytes 262144 | tf_op jit(solution)/shard_map/all_to_all | solution.py:41
  116.3 3.3 %image.1 = (f32[16,1024]{1,0:T(8,128)S(1)}, f32[256,1,128]{2,1,0:T(1,128)S(1)}) custom-call(bf16[32,16,128]{2,1,0:T(8,128)(2,1)S(1)} %all_to_all.53.weights, bf16[8,1024,512]{2,1,0:T(8,128)(2,1)S(1)} %get-tuple-element.70.rows, s32[1,1]{1,0:T(1,128)S(6)} %copy.10.counts, f32[24,1024]{1,0:T(8,128)S(1)} %copy-done.5, ...), custom_call_target="tpu_custom_call" | custom-call | bytes 16777216 | tf_op jit(solution)/shard_map/image/pallas_call | solution.py:114
  119.6 18.6 %all_to_all.54.rows = f32[256,1,128]{2,1,0:T(1,128)S(1)} all-to-all(f32[256,1,128]{2,1,0:T(1,128)S(1)} %get-tuple-element.71), channel_id=1, replica_groups=mesh['z'=8,'yl'=2,'c'=2,'yh'=2,'x'=4] {'z','yl','c','yh','x'}, dimensions={0} | all-to-all | bytes 262144 | tf_op jit(solution)/shard_map/all_to_all | solution.py:41
  138.2 0.4 update.1
  138.6 3.1 %collective-permute-start.11 = (bf16[16,1024]{1,0:T(8,128)(2,1)S(1)}, bf16[16,1024]{1,0:T(8,128)(2,1)S(1)}, u32[]{:S(2)}, u32[]{:S(2)}) collective-permute-start(bf16[16,1024]{1,0:T(8,128)(2,1)S(1)} %get-tuple-element.75.own), channel_id=1, source_target_pairs={{8,16},{24,32},{40,48},{56,64},{72,80},{88,96},{104,112},{120,128}... | collective-permute-start | bytes 98312 | tf_op jit(solution)/shard_map/ppermute | solution.py:56
  141.8 0.1 collective-permute-start.10
  141.9 2.3 %project.1 = f32[32,32,128]{2,1,0:T(8,128)S(1)} custom-call(bf16[32,1024]{1,0:T(8,128)(2,1)S(1)} %get-tuple-element.73.packed, bf16[8,1024,512]{2,1,0:T(8,128)(2,1)S(1)} %get-tuple-element.70.rows), custom_call_target="tpu_custom_call" | custom-call | bytes 16777216 | tf_op jit(solution)/shard_map/project/pallas_call | solution.py:114
  144.2 0.8 copy-done.2
  145.0 4.7 %all-to-all-start.6 = ((f32[32,32,128]{2,1,0:T(8,128)}), f32[32,32,128]{2,1,0:T(8,128)}, u32[]{:S(2)}, u32[]{:S(2)}) async-start(f32[32,32,128]{2,1,0:T(8,128)} %copy-done.2), calls=%async_computation.6 | async-start | bytes 1048576 | tf_op jit(solution)/shard_map/all_to_all | solution.py:41
  149.7 0.7 collective-permute-start.13
  150.4 3.9 %collective-permute-start.12 = (bf16[3,16,1024]{2,1,0:T(8,128)(2,1)S(1)}, bf16[3,16,1024]{2,1,0:T(8,128)(2,1)}, u32[]{:S(2)}, u32[]{:S(2)}) collective-permute-start(bf16[3,16,1024]{2,1,0:T(8,128)(2,1)S(1)} %stack.19.near), channel_id=1, source_target_pairs={{0,1},{1,0},{2,3},{3,2},{4,5},{5,4},{6,7},{7,6},{8,9},{9,8},{10,11... | collective-permute-start | bytes 294920 | tf_op jit(solution)/shard_map/ppermute | solution.py:50
  154.3 7.2 %all-to-all-done.6.refs_0_ = f32[32,32,128]{2,1,0:T(8,128)} async-done(((f32[32,32,128]{2,1,0:T(8,128)}), f32[32,32,128]{2,1,0:T(8,128)}, u32[]{:S(2)}, u32[]{:S(2)}) %all-to-all-start.6) | async-done | bytes 524320 | tf_op jit(solution)/shard_map/all_to_all | solution.py:41
  161.6 1.4 copy-done.7
  163.0 1.4 copy-done.9
  164.4 1.8 sparse.1
  166.2 1.1 sum_share.3
  167.3 11.6 %all_to_all.55.parts = f32[8,48,128]{2,1,0:T(8,128)S(1)} all-to-all(f32[8,48,128]{2,1,0:T(8,128)S(1)} %sum_share.3), channel_id=1, replica_groups=mesh['z'=8,'yl'=2,'c'=2,'yh'=2,'x'=4] {'z'}, dimensions={0} | all-to-all | bytes 393216 | tf_op jit(solution)/shard_map/all_to_all | solution.py:41
  178.9 2.7 %collective-permute-start.16 = (f32[16,128]{1,0:T(8,128)S(1)}, f32[16,128]{1,0:T(8,128)S(1)}, u32[]{:S(2)}, u32[]{:S(2)}) collective-permute-start(f32[16,128]{1,0:T(8,128)S(1)} %get-tuple-element.81.refs_0_.rounded), channel_id=1, source_target_pairs={{0,24},{8,16},{16,8},{24,0},{1,25},{9,17},{17,9},{25,1},{2,26},{10... | collective-permute-start | bytes 24584 | tf_op jit(solution)/shard_map/ppermute | solution.py:46
  181.7 1.8 collective-permute-start.15
  183.4 1.3 collective-permute-done.15.refs_2_
  184.8 0.6 coeffs.3
  185.4 17.1 %all_to_all.56.parts = f32[8,16,1152]{2,1,0:T(8,128)S(1)} all-to-all(f32[8,16,1152]{2,1,0:T(8,128)S(1)} %coeffs.3), channel_id=1, replica_groups=mesh['z'=8,'yl'=2,'c'=2,'yh'=2,'x'=4] {'yh','x'}, dimensions={0} | all-to-all | bytes 1179648 | tf_op jit(solution)/shard_map/all_to_all | solution.py:41
  202.5 1.0 weights.3
  203.5 1.2 collective-permute-start.17
  204.6 1.7 collective-permute-start.19
  206.3 0.9 collective-permute-done.18.second
  207.2 0.8 collective-permute-done.19.third
  208.0 0.1 gather_last.1
  208.2 12.6 %all_to_all.57.weights.every = bf16[32,32,128]{2,1,0:T(8,128)(2,1)S(1)} all-to-all(bf16[32,32,128]{2,1,0:T(8,128)(2,1)S(1)} %get-tuple-element.88), channel_id=1, replica_groups=mesh['z'=8,'yl'=2,'c'=2,'yh'=2,'x'=4] {'yh','x','yl','c'}, dimensions={0} | all-to-all | bytes 524288 | tf_op jit(solution)/shard_map/all_to_all | solution.py:41
  220.8 4.0 %finish.1 = (f32[16,1024]{1,0:T(8,128)}, f32[16,1024]{1,0:T(8,128)}) custom-call(bf16[32,32,128]{2,1,0:T(8,128)(2,1)S(1)} %all_to_all.57.weights.every, bf16[8,1024,512]{2,1,0:T(8,128)(2,1)S(1)} %copy-done.1, bf16[32,32,128]{2,1,0:T(8,128)(2,1)S(1)} %all_to_all.57.weights.every, s32[1,1]{1,0:T(1,128)S(6)} %copy.10.counts, ...), custom_call_target="tpu_custom_call" | custom-call | bytes 16777216 | tf_op jit(solution)/shard_map/finish/pallas_call | solution.py:114
  (46 shorter events, 0.2 us)
Async XLA Ops:
  0.6 77.1 %copy-start.14 = (s32[1,1,8,8]{3,2,1,0:T(8,128)S(1)}, s32[1,1,8,8]{3,2,1,0:T(8,128)}, u32[]{:S(2)}) copy-start(s32[1,1,8,8]{3,2,1,0:T(8,128)} %param.11) | copy-start | bytes 772
  2.0 75.8 %copy-start.16 = (s32[1,3]{1,0:T(1,128)S(1)}, s32[1,3]{1,0:T(1,128)}, u32[]{:S(2)}) copy-start(s32[1,3]{1,0:T(1,128)} %add_bitcast_fusion.place) | copy-start | bytes 40
  3.8 28.5 %all-to-all-start = ((f32[256,1,128]{2,1,0:T(1,128)}), f32[256,1,128]{2,1,0:T(1,128)S(1)}, u32[]{:S(2)}, u32[]{:S(2)}) async-start(f32[256,1,128]{2,1,0:T(1,128)} %get-tuple-element.49), calls=%async_computation | async-start | bytes 262144 | tf_op jit(solution)/shard_map/all_to_all | solution.py:41
  19.4 13.5 %collective-permute-start.1 = (f32[24,1024]{1,0:T(8,128)}, f32[24,1024]{1,0:T(8,128)S(1)}, u32[]{:S(2)}, u32[]{:S(2)}) collective-permute-start(f32[24,1024]{1,0:T(8,128)} %get-tuple-element.50.own.halo), channel_id=1, source_target_pairs={{8,16},{24,32},{40,48},{56,64},{72,80},{88,96},{104,112},{120,128}... | collective-permute-start | bytes 294920 | tf_op jit(solution)/shard_map/ppermute | solution.py:56
  23.0 9.9 %collective-permute-start = (f32[24,1024]{1,0:T(8,128)}, f32[24,1024]{1,0:T(8,128)S(1)}, u32[]{:S(2)}, u32[]{:S(2)}) collective-permute-start(f32[24,1024]{1,0:T(8,128)} %get-tuple-element.50.own.halo), channel_id=1, source_target_pairs={{0,8},{8,0},{16,24},{24,16},{32,40},{40,32},{48,56},{56,48},{64,72... | collective-permute-start | bytes 294920 | tf_op jit(solution)/shard_map/ppermute | solution.py:50
  32.3 0.7 copy-start.11
  32.9 0.9 copy-start.3
  33.8 13.9 %collective-permute-start.3 = (f32[3,24,1024]{2,1,0:T(8,128)S(1)}, f32[3,24,1024]{2,1,0:T(8,128)}, u32[]{:S(2)}, u32[]{:S(2)}) collective-permute-start(f32[3,24,1024]{2,1,0:T(8,128)S(1)} %stack.18.near), channel_id=1, source_target_pairs={{1,2},{3,4},{5,6},{2,1},{4,3},{6,5},{9,10},{11,12},{13,14},{10,9},... | collective-permute-start | bytes 884744 | tf_op jit(solution)/shard_map/ppermute | solution.py:56
  35.2 12.5 %collective-permute-start.2 = (f32[3,24,1024]{2,1,0:T(8,128)S(1)}, f32[3,24,1024]{2,1,0:T(8,128)}, u32[]{:S(2)}, u32[]{:S(2)}) collective-permute-start(f32[3,24,1024]{2,1,0:T(8,128)S(1)} %stack.18.near), channel_id=1, source_target_pairs={{0,1},{1,0},{2,3},{3,2},{4,5},{5,4},{6,7},{7,6},{8,9},{9,8},{10,11... | collective-permute-start | bytes 884744 | tf_op jit(solution)/shard_map/ppermute | solution.py:50
  36.7 79.6 %copy-start.5 = (f32[24,1024]{1,0:T(8,128)S(1)}, f32[24,1024]{1,0:T(8,128)}, u32[]{:S(2)}) copy-start(f32[24,1024]{1,0:T(8,128)} %get-tuple-element.50.own.halo) | copy-start | bytes 294916
  36.7 79.6 %copy-start.10 = (f32[1,1,16,1024]{3,2,1,0:T(8,128)S(1)}, f32[1,1,16,1024]{3,2,1,0:T(8,128)}, u32[]{:S(2)}) copy-start(f32[1,1,16,1024]{3,2,1,0:T(8,128)} %param.8) | copy-start | bytes 196612
  36.7 79.6 %copy-start.13 = (f32[1,1,1024]{2,1,0:T(1,128)S(1)}, f32[1,1,1024]{2,1,0:T(1,128)}, u32[]{:S(2)}) copy-start(f32[1,1,1024]{2,1,0:T(1,128)} %param.9) | copy-start | bytes 12292
  38.4 0.7 copy-start.15
  40.3 0.9 copy-start.4
  41.2 0.9 copy-start.12
  47.7 94.1 %copy-start = (bf16[8,1024,512]{2,1,0:T(8,128)(2,1)}, bf16[8,1024,512]{2,1,0:T(8,128)(2,1)S(1)}, u32[]{:S(2)}) copy-start(bf16[8,1024,512]{2,1,0:T(8,128)(2,1)S(1)} %get-tuple-element.70.rows) | copy-start | bytes 25165828
  73.9 8.5 %collective-permute-start.6 = (f32[16,128]{1,0:T(8,128)S(1)}, f32[16,128]{1,0:T(8,128)S(1)}, u32[]{:S(2)}, u32[]{:S(2)}) collective-permute-start(f32[16,128]{1,0:T(8,128)S(1)} %sum_depth.2.refs_0_), channel_id=1, source_target_pairs={{0,24},{8,16},{16,8},{24,0},{1,25},{9,17},{17,9},{25,1},{2,26},{10... | collective-permute-start | bytes 24584 | tf_op jit(solution)/shard_map/ppermute | solution.py:46
  76.5 6.0 %collective-permute-start.5 = (f32[16,128]{1,0:T(8,128)S(1)}, f32[16,128]{1,0:T(8,128)S(1)}, u32[]{:S(2)}, u32[]{:S(2)}) collective-permute-start(f32[16,128]{1,0:T(8,128)S(1)} %sum_depth.2.refs_0_), channel_id=1, source_target_pairs={{0,16},{8,24},{16,0},{24,8},{1,17},{9,25},{17,1},{25,9},{2,18},{10... | collective-permute-start | bytes 24584 | tf_op jit(solution)/shard_map/ppermute | solution.py:46
  77.8 4.7 %collective-permute-start.4 = (f32[16,128]{1,0:T(8,128)S(1)}, f32[16,128]{1,0:T(8,128)S(1)}, u32[]{:S(2)}, u32[]{:S(2)}) collective-permute-start(f32[16,128]{1,0:T(8,128)S(1)} %sum_depth.2.refs_0_), channel_id=1, source_target_pairs={{0,8},{8,0},{16,24},{24,16},{1,9},{9,1},{17,25},{25,17},{2,10},{10... | collective-permute-start | bytes 24584 | tf_op jit(solution)/shard_map/ppermute | solution.py:46
  81.5 1.0 copy-start.6
  97.3 8.3 %collective-permute-start.7 = (f32[16,128]{1,0:T(8,128)S(1)}, f32[16,128]{1,0:T(8,128)S(1)}, u32[]{:S(2)}, u32[]{:S(2)}) collective-permute-start(f32[16,128]{1,0:T(8,128)S(1)} %get-tuple-element.67), channel_id=1, source_target_pairs={{0,8},{8,0},{16,24},{24,16},{1,9},{9,1},{17,25},{25,17},{2,10},{10... | collective-permute-start | bytes 24584 | tf_op jit(solution)/shard_map/ppermute | solution.py:46
  99.2 6.4 %collective-permute-start.8 = (f32[16,128]{1,0:T(8,128)S(1)}, f32[16,128]{1,0:T(8,128)S(1)}, u32[]{:S(2)}, u32[]{:S(2)}) collective-permute-start(f32[16,128]{1,0:T(8,128)S(1)} %get-tuple-element.68), channel_id=1, source_target_pairs={{0,16},{8,24},{16,0},{24,8},{1,17},{9,25},{17,1},{25,9},{2,18},{10... | collective-permute-start | bytes 24584 | tf_op jit(solution)/shard_map/ppermute | solution.py:46
  99.5 6.1 %collective-permute-start.9 = (f32[16,128]{1,0:T(8,128)S(1)}, f32[16,128]{1,0:T(8,128)S(1)}, u32[]{:S(2)}, u32[]{:S(2)}) collective-permute-start(f32[16,128]{1,0:T(8,128)S(1)} %get-tuple-element.69), channel_id=1, source_target_pairs={{0,24},{8,16},{16,8},{24,0},{1,25},{9,17},{17,9},{25,1},{2,26},{10... | collective-permute-start | bytes 24584 | tf_op jit(solution)/shard_map/ppermute | solution.py:46
  104.6 1.0 copy-start.8
  138.6 6.4 %collective-permute-start.11 = (bf16[16,1024]{1,0:T(8,128)(2,1)S(1)}, bf16[16,1024]{1,0:T(8,128)(2,1)S(1)}, u32[]{:S(2)}, u32[]{:S(2)}) collective-permute-start(bf16[16,1024]{1,0:T(8,128)(2,1)S(1)} %get-tuple-element.75.own), channel_id=1, source_target_pairs={{8,16},{24,32},{40,48},{56,64},{72,80},{88,96},{104,112},{120,128}... | collective-permute-start | bytes 98312 | tf_op jit(solution)/shard_map/ppermute | solution.py:56
  141.8 3.2 %collective-permute-start.10 = (bf16[16,1024]{1,0:T(8,128)(2,1)S(1)}, bf16[16,1024]{1,0:T(8,128)(2,1)S(1)}, u32[]{:S(2)}, u32[]{:S(2)}) collective-permute-start(bf16[16,1024]{1,0:T(8,128)(2,1)S(1)} %get-tuple-element.75.own), channel_id=1, source_target_pairs={{0,8},{8,0},{16,24},{24,16},{32,40},{40,32},{48,56},{56,48},{64,72... | collective-permute-start | bytes 98312 | tf_op jit(solution)/shard_map/ppermute | solution.py:50
  144.2 0.8 copy-start.2
  145.0 16.6 %all-to-all-start.6 = ((f32[32,32,128]{2,1,0:T(8,128)}), f32[32,32,128]{2,1,0:T(8,128)}, u32[]{:S(2)}, u32[]{:S(2)}) async-start(f32[32,32,128]{2,1,0:T(8,128)} %copy-done.2), calls=%async_computation.6 | async-start | bytes 1048576 | tf_op jit(solution)/shard_map/all_to_all | solution.py:41
  149.7 11.9 %collective-permute-start.13 = (bf16[3,16,1024]{2,1,0:T(8,128)(2,1)S(1)}, bf16[3,16,1024]{2,1,0:T(8,128)(2,1)S(1)}, u32[]{:S(2)}, u32[]{:S(2)}) collective-permute-start(bf16[3,16,1024]{2,1,0:T(8,128)(2,1)S(1)} %stack.19.near), channel_id=1, source_target_pairs={{1,2},{3,4},{5,6},{2,1},{4,3},{6,5},{9,10},{11,12},{13,14},{10,9},... | collective-permute-start | bytes 294920 | tf_op jit(solution)/shard_map/ppermute | solution.py:56
  150.4 11.2 %collective-permute-start.12 = (bf16[3,16,1024]{2,1,0:T(8,128)(2,1)S(1)}, bf16[3,16,1024]{2,1,0:T(8,128)(2,1)}, u32[]{:S(2)}, u32[]{:S(2)}) collective-permute-start(bf16[3,16,1024]{2,1,0:T(8,128)(2,1)S(1)} %stack.19.near), channel_id=1, source_target_pairs={{0,1},{1,0},{2,3},{3,2},{4,5},{5,4},{6,7},{7,6},{8,9},{9,8},{10,11... | collective-permute-start | bytes 294920 | tf_op jit(solution)/shard_map/ppermute | solution.py:50
  161.6 59.2 %copy-start.1 = (bf16[8,1024,512]{2,1,0:T(8,128)(2,1)S(1)}, bf16[8,1024,512]{2,1,0:T(8,128)(2,1)}, u32[]{:S(2)}) copy-start(bf16[8,1024,512]{2,1,0:T(8,128)(2,1)} %copy-done) | copy-start | bytes 25165828
  161.6 1.4 copy-start.7
  163.0 1.4 copy-start.9
  178.9 4.5 %collective-permute-start.16 = (f32[16,128]{1,0:T(8,128)S(1)}, f32[16,128]{1,0:T(8,128)S(1)}, u32[]{:S(2)}, u32[]{:S(2)}) collective-permute-start(f32[16,128]{1,0:T(8,128)S(1)} %get-tuple-element.81.refs_0_.rounded), channel_id=1, source_target_pairs={{0,24},{8,16},{16,8},{24,0},{1,25},{9,17},{17,9},{25,1},{2,26},{10... | collective-permute-start | bytes 24584 | tf_op jit(solution)/shard_map/ppermute | solution.py:46
  181.7 3.1 %collective-permute-start.15 = (f32[16,128]{1,0:T(8,128)S(1)}, f32[16,128]{1,0:T(8,128)S(1)}, u32[]{:S(2)}, u32[]{:S(2)}) collective-permute-start(f32[16,128]{1,0:T(8,128)S(1)} %get-tuple-element.81.refs_0_.rounded), channel_id=1, source_target_pairs={{0,16},{8,24},{16,0},{24,8},{1,17},{9,25},{17,1},{25,9},{2,18},{10... | collective-permute-start | bytes 24584 | tf_op jit(solution)/shard_map/ppermute | solution.py:46
  183.4 1.3 collective-permute-start.14
  203.5 2.9 %collective-permute-start.17 = (f32[16,256]{1,0:T(8,128)S(1)}, f32[16,256]{1,0:T(8,128)S(1)}, u32[]{:S(2)}, u32[]{:S(2)}) collective-permute-start(f32[16,256]{1,0:T(8,128)S(1)} %get-tuple-element.84), channel_id=1, source_target_pairs={{0,8},{8,0},{16,24},{24,16},{1,9},{9,1},{17,25},{25,17},{2,10},{10... | collective-permute-start | bytes 49160 | tf_op jit(solution)/shard_map/ppermute | solution.py:46
  204.6 2.6 %collective-permute-start.18 = (f32[16,256]{1,0:T(8,128)S(1)}, f32[16,256]{1,0:T(8,128)S(1)}, u32[]{:S(2)}, u32[]{:S(2)}) collective-permute-start(f32[16,256]{1,0:T(8,128)S(1)} %get-tuple-element.85), channel_id=1, source_target_pairs={{0,16},{8,24},{16,0},{24,8},{1,17},{9,25},{17,1},{25,9},{2,18},{10... | collective-permute-start | bytes 49160 | tf_op jit(solution)/shard_map/ppermute | solution.py:46
  204.6 3.4 %collective-permute-start.19 = (f32[16,256]{1,0:T(8,128)S(1)}, f32[16,256]{1,0:T(8,128)S(1)}, u32[]{:S(2)}, u32[]{:S(2)}) collective-permute-start(f32[16,256]{1,0:T(8,128)S(1)} %get-tuple-element.86), channel_id=1, source_target_pairs={{0,24},{8,16},{16,8},{24,0},{1,25},{9,17},{17,9},{25,1},{2,26},{10... | collective-permute-start | bytes 49160 | tf_op jit(solution)/shard_map/ppermute | solution.py:46

commit v5 on v4

--- a/solution.py
+++ b/solution.py
@@ -39,6 +39,10 @@
 
 def exchange(parts, axes):
     return lax.all_to_all(parts, axes, 0, 0, tiled=True)
+
+
+def quad_index():
+    return lax.axis_index("yl") * 2 + lax.axis_index("c")
 
 
 def quad_partner(value, step):
@@ -131,7 +135,7 @@
 FIELD = shape(PROBES, PTS)
 
 
-def prepare_kernel(place, coords, probes, precond, counts, inducing, centre_out, halo_out):
+def prepare_kernel(coords, probes, precond, counts, inducing, centre_out, halo_out):
     points = coords[...]
     lane = lax.broadcasted_iota(jnp.int32, (FEAT, PTS), 1)
     short = lax.broadcasted_iota(jnp.int32, (FEAT, 128), 1)
@@ -149,32 +153,33 @@
     halo_out[FEAT:] = precond[...] * (probes[...] * live_lanes(counts[0, 0]))
 
 
-def prepare(place, coords, probes, precond, counts, inducing):
+def prepare(coords, probes, precond, counts, inducing):
     return call(
         prepare_kernel,
         "prepare",
         (shape(256, 1, 128), shape(FEAT + PROBES, PTS)),
-        [SMEM, VMEM, VMEM, VMEM, SMEM, SMEM],
-        (place, coords, probes, precond, counts, inducing),
+        [VMEM, VMEM, VMEM, SMEM, SMEM],
+        (coords, probes, precond, counts, inducing),
         params=LARGE,
     )
 
 
-def factor_kernel(place, columns, first_out, second_out, third_out):
+def factor_kernel(columns, first_out, second_out, third_out):
+    quad = quad_index()
     for index in range(4):
-        start = pl.multiple_of((place[0, 0] ^ index) * SHARE, SHARE)
+        start = pl.multiple_of((quad ^ index) * SHARE, SHARE)
         parts = split3(columns[pl.ds(start, SHARE), :])
         for out, part in zip((first_out, second_out, third_out), parts):
             out[index * SHARE : (index + 1) * SHARE] = part.astype(bf16)
 
 
-def split_factor(place, columns):
+def split_factor(columns):
     return call(
         factor_kernel,
         "factor",
         (shape(4 * SHARE, QUARTER, dtype=bf16),) * 3,
-        [SMEM, VMEM],
-        (place, columns),
+        [VMEM],
+        (columns,),
         moved=8 << 20,
     )
 
@@ -191,18 +196,21 @@
 
 
 def rows_kernel(halo, centres, rows_out, sums_out, left, packed):
-    @pl.when(pl.program_id(0) == 0)
-    def _():
-        left[...] = augmented(halo[:FEAT], -LOG2E / width_sq, True).astype(f32).T.astype(bf16)
-        packed[...] = halo[FEAT:].astype(bf16)
-
-    right = augmented(centre_columns(centres[...]), -LOG2E / width_sq, False)
-    power = jnp.dot(left[...], right, preferred_element_type=f32)
-    rows = jnp.exp2(jnp.minimum(power, 0.0)).astype(bf16)
-    rows_out[0] = rows
-    sums = jnp.dot(packed[...], rows, preferred_element_type=f32)
-    for part in range(4):
-        sums_out[part] = sums[:, part * SHARE : (part + 1) * SHARE]
+    left[...] = augmented(halo[:FEAT], -LOG2E / width_sq, True).astype(f32).T.astype(bf16)
+    packed[...] = halo[FEAT:].astype(bf16)
+
+    def chunk(step, carry):
+        cells = centres[pl.ds(pl.multiple_of(step * 32, 32), 32), :]
+        right = augmented(centre_columns(cells), -LOG2E / width_sq, False)
+        power = jnp.dot(left[...], right, preferred_element_type=f32)
+        rows = jnp.exp2(jnp.minimum(power, 0.0)).astype(bf16)
+        rows_out[step] = rows
+        sums = jnp.dot(packed[...], rows, preferred_element_type=f32)
+        for part in range(4):
+            sums_out[4 * step + part] = sums[:, part * SHARE : (part + 1) * SHARE]
+        return carry
+
+    lax.fori_loop(0, CHUNKS, chunk, 0, unroll=2)
 
 
 def make_rows(halo, centres):
@@ -210,49 +218,37 @@
         rows_kernel,
         "rows",
         (shape(CHUNKS, PTS, CHUNK, dtype=bf16), shape(32, PROBES, SHARE)),
-        [
-            pl.BlockSpec((FEAT + PROBES, PTS), lambda g: (0, 0)),
-            pl.BlockSpec((32, 128), lambda g: (g, 0)),
-        ],
+        [VMEM, VMEM],
         (halo, centres),
         scratch=[pltpu.VMEM((PTS, 64), bf16), pltpu.VMEM((PROBES, PTS), bf16)],
-        grid=(CHUNKS,),
-        out_specs=(
-            pl.BlockSpec((1, PTS, CHUNK), lambda g: (g, 0, 0)),
-            pl.BlockSpec((4, PROBES, SHARE), lambda g: (g, 0, 0)),
-        ),
         params=MIDDLE,
         moved=16 << 20,
     )
 
 
 def project_kernel(packed, rows, sums_out):
-    sums = jnp.dot(packed[...], rows[0], preferred_element_type=f32)
-    for part in range(4):
-        sums_out[part] = sums[:, part * SHARE : (part + 1) * SHARE]
+    for step in range(CHUNKS):
+        sums = jnp.dot(packed[...], rows[step], preferred_element_type=f32)
+        for part in range(4):
+            sums_out[4 * step + part] = sums[:, part * SHARE : (part + 1) * SHARE]
 
 
 def project(packed, rows):
-    height = packed.shape[0]
     return call(
         project_kernel,
         "project",
-        shape(32, height, SHARE),
-        [
-            pl.BlockSpec((height, PTS), lambda g: (0, 0)),
-            pl.BlockSpec((1, PTS, CHUNK), lambda g: (g, 0, 0)),
-        ],
+        shape(32, packed.shape[0], SHARE),
+        [VMEM, VMEM],
         (packed, rows),
-        grid=(CHUNKS,),
-        out_specs=pl.BlockSpec((4, height, SHARE), lambda g: (g, 0, 0)),
         params=MIDDLE,
         moved=16 << 20,
     )
 
 
-def fill_table(table, place, sources, first, last, dtype):
-    places_x = (1, 2 - 2 * place[0, 1], 2 * place[0, 1])
-    places_y = (1, 2 - 2 * place[0, 2], 2 * place[0, 2])
+def fill_table(table, sources, first, last, dtype):
+    side_x, side_y = lax.axis_index("c"), lax.axis_index("x") & 1
+    places_x = (1, 2 - 2 * side_x, 2 * side_x)
+    places_y = (1, 2 - 2 * side_y, 2 * side_y)
     for place_y, source in zip(places_y, sources):
         for index, place_x in enumerate(places_x):
             start = (place_x * 3 + place_y) * CAP
@@ -266,44 +262,37 @@
     return jnp.concatenate([table[codes[block, entry]] for entry in range(CAP)], axis=1)
 
 
-def tiles_kernel(base, codes, place, near, even, odd, tiles_out, sparse_out, points, values):
-    block = base + pl.program_id(0)
-
-    @pl.when(pl.program_id(0) == 0)
-    def _():
-        fill_table(points, place, (near, even, odd), 0, FEAT, f32)
-        fill_table(values, place, (near, even, odd), FEAT, FEAT + PROBES, bf16)
-
+def tiles_kernel(base, codes, near, even, odd, tiles_out, sparse_out, points, values):
+    fill_table(points, (near, even, odd), 0, FEAT, f32)
+    fill_table(values, (near, even, odd), FEAT, FEAT + PROBES, bf16)
     scale = 1.0 / (support_radius * support_radius)
-    own = augmented(points[4 * CAP + block], scale, True).astype(f32).T.astype(bf16)
-    other = augmented(partners(points, codes, block), scale, False)
-    square = jnp.maximum(jnp.dot(own, other, preferred_element_type=f32), 0.0)
-    ratio = jnp.sqrt(square)
-    remain = jnp.maximum(1.0 - ratio, 0.0)
-    second = remain * remain
-    fourth = second * second
-    tile = (fourth * second * remain * (7.0 * ratio + 1.0)).astype(bf16)
-    tiles_out[0] = tile
-    sparse_out[...] = nt_dot(partners(values, codes, block), tile)
-
-
-def make_tiles(half, codes, place, near, even, odd):
-    whole = pl.BlockSpec((3, FEAT + PROBES, PTS), lambda b: (0, 0, 0))
+    for index in range(HALF):
+        block = base + index
+        own = augmented(points[4 * CAP + block], scale, True).astype(f32).T.astype(bf16)
+        other = augmented(partners(points, codes, block), scale, False)
+        square = jnp.maximum(jnp.dot(own, other, preferred_element_type=f32), 0.0)
+        ratio = jnp.sqrt(square)
+        remain = jnp.maximum(1.0 - ratio, 0.0)
+        second = remain * remain
+        fourth = second * second
+        tile = (fourth * second * remain * (7.0 * ratio + 1.0)).astype(bf16)
+        tiles_out[index] = tile
+        sparse_out[:, index * BLOCK : (index + 1) * BLOCK] = nt_dot(
+            partners(values, codes, block), tile
+        )
+
+
+def make_tiles(half, codes, near, even, odd):
     return call(
         functools.partial(tiles_kernel, half * HALF),
         "tiles",
         (shape(HALF, BLOCK, PTS, dtype=bf16), shape(PROBES, HALF * BLOCK)),
-        [SMEM, SMEM, whole, whole, whole],
-        (codes, place, near, even, odd),
+        [SMEM, VMEM, VMEM, VMEM],
+        (codes, near, even, odd),
         scratch=[
             pltpu.VMEM((EMPTY + 1, FEAT, BLOCK), f32),
             pltpu.VMEM((EMPTY + 1, PROBES, BLOCK), bf16),
         ],
-        grid=(HALF,),
-        out_specs=(
-            pl.BlockSpec((1, BLOCK, PTS), lambda b: (b, 0, 0)),
-            pl.BlockSpec((PROBES, BLOCK), lambda b: (0, b)),
-        ),
         moved=8 << 20,
     )
 
@@ -315,10 +304,10 @@
 
 
 def sparse_kernel(
-    codes, place, near, even, odd, tiles_low, tiles_high, search, residual, precond,
+    codes, near, even, odd, tiles_low, tiles_high, search, residual, precond,
     sparse_out, sums_out, values,
 ):
-    fill_table(values, place, (near, even, odd), 0, PROBES, bf16)
+    fill_table(values, (near, even, odd), 0, PROBES, bf16)
     for block in range(CAP):
         sparse_out[:, block * BLOCK : (block + 1) * BLOCK] = nt_dot(
             partners(values, codes, block), (tiles_low, tiles_high)[block // HALF][block % HALF]
@@ -331,13 +320,13 @@
     sums_out[...] = jnp.where(lane == 0, curve, jnp.where(lane == 1, norm, 0.0))
 
 
-def apply_tiles(codes, place, nears, tiles, search, residual, precond):
+def apply_tiles(codes, nears, tiles, search, residual, precond):
     return call(
         sparse_kernel,
         "sparse",
         (FIELD, shape(PROBES, 128)),
-        [SMEM, SMEM] + [VMEM] * 8,
-        (codes, place, *nears, *tiles, search, residual, precond),
+        [SMEM] + [VMEM] * 8,
+        (codes, *nears, *tiles, search, residual, precond),
         scratch=[pltpu.VMEM((EMPTY + 1, PROBES, BLOCK), bf16)],
         moved=6 << 20,
     )
@@ -360,56 +349,36 @@
     return column, even_pairs(column, GY), odd_pairs(column, GY)
 
 
-def expand_step(weights, rows, total):
-    @pl.when(pl.program_id(0) == 0)
-    def _():
-        total[...] = jnp.zeros_like(total)
-
-    part = jnp.concatenate([weights[i, :PROBES] for i in range(4)], axis=1)
-    total[...] += nt_dot(part, rows[0])
+def expand(weights, rows):
+    total = jnp.zeros((PROBES, PTS), f32)
+    for step in range(CHUNKS):
+        part = jnp.concatenate([weights[4 * step + i, :PROBES] for i in range(4)], axis=1)
+        total = total + nt_dot(part, rows[step])
+    return total
 
 
 def image_kernel(
-    weights, rows, counts, halo, sparse_low, sparse_high, precond, probes, image_out, sums_out, total
+    weights, rows, counts, halo, sparse_low, sparse_high, precond, probes, image_out, sums_out
 ):
-    expand_step(weights, rows, total)
-
-    @pl.when(pl.program_id(0) == CHUNKS - 1)
-    def _():
-        search = halo[FEAT:]
-        live = live_lanes(counts[0, 0])
-        sparse = jnp.concatenate([sparse_low[...], sparse_high[...]], axis=1)
-        image = live * (search + sparse + total[...])
-        image_out[...] = image
-        norm = jnp.sum(search * (probes[...] * live), axis=1, keepdims=True)
-        curve = jnp.sum(search * image, axis=1, keepdims=True)
-        square = jnp.sum(precond[...] * image * image, axis=1, keepdims=True)
-        row = as_lanes(norm, 0) + as_lanes(curve, 16) + as_lanes(square, 32)
-        sums_out[...] = jnp.broadcast_to(row[None], sums_out.shape)
+    search = halo[FEAT:]
+    live = live_lanes(counts[0, 0])
+    sparse = jnp.concatenate([sparse_low[...], sparse_high[...]], axis=1)
+    image = live * (search + sparse + expand(weights, rows))
+    image_out[...] = image
+    norm = jnp.sum(search * (probes[...] * live), axis=1, keepdims=True)
+    curve = jnp.sum(search * image, axis=1, keepdims=True)
+    square = jnp.sum(precond[...] * image * image, axis=1, keepdims=True)
+    row = as_lanes(norm, 0) + as_lanes(curve, 16) + as_lanes(square, 32)
+    sums_out[...] = jnp.broadcast_to(row[None], sums_out.shape)
 
 
 def make_image(weights, rows, counts, halo, sparse, precond, probes):
-    height = weights.shape[1]
-    still = pl.BlockSpec((PROBES, PTS), lambda g: (0, 0))
-    half = pl.BlockSpec((PROBES, HALF * BLOCK), lambda g: (0, 0))
     return call(
         image_kernel,
         "image",
         (FIELD, shape(256, 1, 128)),
-        [
-            pl.BlockSpec((4, height, SHARE), lambda g: (g, 0, 0)),
-            pl.BlockSpec((1, PTS, CHUNK), lambda g: (g, 0, 0)),
-            SMEM,
-            pl.BlockSpec((FEAT + PROBES, PTS), lambda g: (0, 0)),
-            half,
-            half,
-            pl.BlockSpec((1, PTS), lambda g: (0, 0)),
-            still,
-        ],
+        [VMEM, VMEM, SMEM] + [VMEM] * 5,
         (weights, rows, counts, halo, *sparse, precond, probes),
-        scratch=[pltpu.VMEM((PROBES, PTS), f32)],
-        grid=(CHUNKS,),
-        out_specs=(still, pl.BlockSpec((256, 1, 128), lambda g: (0, 0, 0))),
         params=MIDDLE,
         moved=16 << 20,
     )
@@ -571,65 +540,44 @@
 
 
 def finish_kernel(
-    weights, rows, every, counts, search, sparse, residual, solution, sums, solution_out,
-    residual_out, total,
+    weights, rows, counts, search, sparse, residual, solution, sums, solution_out, residual_out
 ):
-    expand_step(weights, rows, total)
-
-    @pl.when(pl.program_id(0) == CHUNKS - 1)
-    def _():
-        field = search[...]
-        image = live_lanes(counts[0, 0]) * (field + sparse[...] + total[...])
-        dots = jnp.sum(every[:, PROBES:].astype(f32), axis=0)
-        dot = jnp.sum(dots, axis=1, keepdims=True)
-        totals = sums[...]
-        alpha = totals[:, 1:2] / (totals[:, 0:1] + dot)
-        solution_out[...] = solution[...] + alpha * field
-        residual_out[...] = residual[...] - alpha * image
+    field = search[...]
+    image = live_lanes(counts[0, 0]) * (field + sparse[...] + expand(weights, rows))
+    dots = jnp.sum(weights[:, PROBES:].astype(f32), axis=0)
+    dot = jnp.sum(dots, axis=1, keepdims=True)
+    totals = sums[...]
+    alpha = totals[:, 1:2] / (totals[:, 0:1] + dot)
+    solution_out[...] = solution[...] + alpha * field
+    residual_out[...] = residual[...] - alpha * image
 
 
 def finish(weights, rows, counts, search, sparse, residual, solution, sums):
-    still = pl.BlockSpec((PROBES, PTS), lambda g: (0, 0))
-    height = weights.shape[1]
     return call(
         finish_kernel,
         "finish",
         (FIELD, FIELD),
-        [
-            pl.BlockSpec((4, height, SHARE), lambda g: (g, 0, 0)),
-            pl.BlockSpec((1, PTS, CHUNK), lambda g: (g, 0, 0)),
-            pl.BlockSpec((32, height, SHARE), lambda g: (0, 0, 0)),
-            SMEM,
-            still,
-            still,
-            still,
-            still,
-            pl.BlockSpec((PROBES, 128), lambda g: (0, 0)),
-        ],
-        (weights, rows, weights, counts, search, sparse, residual, solution, sums),
-        scratch=[pltpu.VMEM((PROBES, PTS), f32)],
-        grid=(CHUNKS,),
-        out_specs=(still, still),
+        [VMEM, VMEM, SMEM] + [VMEM] * 5,
+        (weights, rows, counts, search, sparse, residual, solution, sums),
         params=MIDDLE,
         moved=16 << 20,
     )
 
 
 def on_device(coords, probes, precond, counts, neighbours, inducing, factor):
-    quad = lax.axis_index("yl") * 2 + lax.axis_index("c")
-    place = jnp.stack([quad, lax.axis_index("c"), lax.axis_index("x") & 1]).reshape(1, 3)
     points = coords[0, 0]
     given = probes[0, 0]
     scaling = precond[0]
     codes = neighbours[0, 0]
 
-    centre_parts, halo = prepare(place, points, given, scaling, counts, inducing[0])
+    centre_parts, halo = prepare(points, given, scaling, counts, inducing[0])
 
     even, odd = even_pairs(halo, GX), odd_pairs(halo, GX)
     centres = exchange(centre_parts, ALL).reshape(256, 128)
+    columns = lax.dynamic_slice_in_dim(factor, quad_index() * QUARTER, QUARTER, 1)
+    centres = after(centres, columns)
     halos = surround(after(halo, centres), even, odd)
-    columns = lax.dynamic_slice_in_dim(after(factor, halos[0]), quad * QUARTER, QUARTER, 1)
-    factors = split_factor(place, columns)
+    factors = split_factor(after(columns, halos[0]))
     rows, parts = make_rows(halo, after(centres, halos[0], *factors))
     parts = after(parts, *halos)
 
@@ -647,10 +595,10 @@
         return [terms[0]] + [quad_partner(terms[step], step) for step in (1, 2, 3)]
 
     depth = depth_of(exchange(parts, PLANE))
-    low = make_tiles(0, codes, place, after(halos[0], depth[0]), *halos[1:])
+    low = make_tiles(0, codes, after(halos[0], depth[0]), *halos[1:])
     coeffs = coeffs_of(depth, low)
     terms = weight_terms(coeffs, factors)
-    high = make_tiles(1, codes, place, after(halos[0], terms[0]), *halos[1:])
+    high = make_tiles(1, codes, after(halos[0], terms[0]), *halos[1:])
     terms = [after(terms[0], *high)] + [quad_partner(terms[step], step) for step in (1, 2, 3)]
     weights = exchange(gather_weights(terms), PLANE)
     tiles, sparse = zip(low, high)
@@ -666,7 +614,7 @@
     nears = surround(after(rounded, parts), even, odd)
     got = exchange(after(parts, nears[0]), PLANE)
     sparse, sums = apply_tiles(
-        codes, place, (after(nears[0], got),) + nears[1:], tiles, search, residual, scaling
+        codes, (after(nears[0], got),) + nears[1:], tiles, search, residual, scaling
     )
     depth = depth_of(got, sums)
     weights, totals = gather_last(terms_of(coeffs_of(depth, ())), depth[0], depth[1])

time: 226 us -> 216 us (0.956)
  Pallas kernels: 32.3 us -> 24.9 us
  waiting for transfers between devices: 19.5 us -> 16.3 us
    pallas_call x22, Pallas kernels: 32.3 us -> 24.9 us  [call(): pl.pallas_call(kernel, out_shape=out_shape, in_specs=in_specs, out_specs=...]
    all_to_all x2, waiting for transfers between devices: 16.4 us -> 13.2 us  [exchange(): return lax.all_to_all(parts, axes, 0, 0, tiled=True)]
    unnamed x34 -> x26, local copies, waits for them, and re-layouts: 9.68 us -> 9.07 us
  transfers between devices with their start and end apart: 22 -> 22, of which waited for: 5 -> 5; matrix products, arithmetic and copies ran while one was open for 1% -> 1% of each run, Pallas kernels for 7% -> 5%
where the time goes in v5:
time: 216 us
  blocking collectives  111 us (51%)
  starting transfers between devices  49.4 us (23%)
  Pallas kernels  24.9 us (12%)
  waiting for transfers between devices  16.3 us (8%)
  local copies, waits for them, and re-layouts  12.3 us (6%)
    all_to_all x8, blocking collectives, exchange(): return lax.all_to_all(parts, axes, 0, 0, tiled=True)  111 us
    pallas_call x22, Pallas kernels, call(): pl.pallas_call(kernel, out_shape=out_shape, in_specs=in_specs, out_specs=...  24.9 us
    all_to_all x2, starting transfers between devices, exchange(): return lax.all_to_all(parts, axes, 0, 0, tiled=True)  20.4 us
    ppermute x12, starting transfers between devices, quad_partner(): return lax.ppermute(value, ('yl', 'c'), pairs)  14.8 us
    all_to_all x2, waiting for transfers between devices, exchange(): return lax.all_to_all(parts, axes, 0, 0, tiled=True)  13.2 us
    unnamed x26, local copies, waits for them, and re-layouts  9.07 us
    ppermute x4, starting transfers between devices, odd_pairs(): return lax.ppermute(value, axes, pairs + [(j, i) for i, j in pairs])  8.04 us
    ppermute x4, starting transfers between devices, even_pairs(): lax.ppermute(value, axes, [(i, i ^ 1) for i in range(lax.axis_size(axes))])  6.26 us
  transfers between devices with their start and end apart: 22, of which 5 were waited for; matrix products, arithmetic and copies ran while one was open for 1% of the time, Pallas kernels for 5%

profile of v5, /device:TPU:1, one launch (start us, length us, event | category | flops | bytes accessed | tf_op | source)
XLA Modules:
  0.0 215.5 jit_solution(9798698069830629485)
XLA Ops:
  1.3 1.8 prepare.1
  3.1 15.7 %all-to-all-start = ((f32[256,1,128]{2,1,0:T(1,128)}), f32[256,1,128]{2,1,0:T(1,128)S(1)}, u32[]{:S(2)}, u32[]{:S(2)}) async-start(f32[256,1,128]{2,1,0:T(1,128)} %get-tuple-element.50), calls=%async_computation | async-start | bytes 262144 | tf_op jit(solution)/shard_map/all_to_all | solution.py:41
  18.7 3.5 %collective-permute-start.1 = (f32[24,1024]{1,0:T(8,128)}, f32[24,1024]{1,0:T(8,128)S(1)}, u32[]{:S(2)}, u32[]{:S(2)}) collective-permute-start(f32[24,1024]{1,0:T(8,128)} %get-tuple-element.52.own.halo), channel_id=1, source_target_pairs={{8,16},{24,32},{40,48},{56,64},{72,80},{88,96},{104,112},{120,128}... | collective-permute-start | bytes 294920 | tf_op jit(solution)/shard_map/ppermute | solution.py:60
  22.3 0.1 collective-permute-start
  22.4 0.0 copy-start.10
  22.4 0.0 copy-start.11
  22.4 3.2 %constant_dynamic-slice_fusion.columns = f32[512,1024]{1,0:T(8,128)} fusion(f32[512,4096]{1,0:T(8,128)} %param.13, s32[]{:T(128)S(6)} %select_n.3), kind=kLoop, calls=%fused_computation | loop fusion | bytes 4194308 | tf_op jit(solution)/shard_map/dynamic_slice | solution.py:577
  25.6 5.9 %all-to-all-done = f32[256,1,128]{2,1,0:T(1,128)S(1)} async-done(((f32[256,1,128]{2,1,0:T(1,128)}), f32[256,1,128]{2,1,0:T(1,128)S(1)}, u32[]{:S(2)}, u32[]{:S(2)}) %all-to-all-start) | async-done | bytes 131104 | tf_op jit(solution)/shard_map/all_to_all | solution.py:41
  31.6 0.9 copy-done.4
  32.5 0.7 collective-permute-start.3
  33.2 2.1 collective-permute-start.2
  35.3 1.6 copy-done.2
  36.9 0.6 factor.1
  37.5 0.9 copy-done.5
  38.4 4.5 %rows.1 = (bf16[8,1024,512]{2,1,0:T(8,128)(2,1)S(1)}, f32[32,16,128]{2,1,0:T(8,128)S(1)}) custom-call(f32[24,1024]{1,0:T(8,128)S(1)} %copy-done.5, f32[256,128]{1,0:T(8,128)S(1)} %bitcast.11), custom_call_target="tpu_custom_call" | custom-call | bytes 16777216 | tf_op jit(solution)/shard_map/rows/pallas_call | solution.py:118
  43.0 15.9 %all_to_all.50.refs_0_ = f32[32,16,128]{2,1,0:T(8,128)S(1)} all-to-all(f32[32,16,128]{2,1,0:T(8,128)S(1)} %get-tuple-element.59), channel_id=1, replica_groups=mesh['z'=8,'yl'=2,'c'=2,'yh'=2,'x'=4] {'yh','x','yl','c'}, dimensions={0} | all-to-all | bytes 524288 | tf_op jit(solution)/shard_map/all_to_all | solution.py:41
  59.0 10.9 %all_to_all.51.parts = f32[8,16,128]{2,1,0:T(8,128)S(1)} all-to-all(f32[8,16,128]{2,1,0:T(8,128)S(1)} %sum_share.2), channel_id=1, replica_groups=mesh['z'=8,'yl'=2,'c'=2,'yh'=2,'x'=4] {'z'}, dimensions={0} | all-to-all | bytes 131072 | tf_op jit(solution)/shard_map/all_to_all | solution.py:41
  69.9 2.6 %collective-permute-start.6 = (f32[16,128]{1,0:T(8,128)S(1)}, f32[16,128]{1,0:T(8,128)S(1)}, u32[]{:S(2)}, u32[]{:S(2)}) collective-permute-start(f32[16,128]{1,0:T(8,128)S(1)} %sum_depth.2.refs_0_), channel_id=1, source_target_pairs={{0,24},{8,16},{16,8},{24,0},{1,25},{9,17},{17,9},{25,1},{2,26},{10... | collective-permute-start | bytes 24584 | tf_op jit(solution)/shard_map/ppermute | solution.py:50
  72.4 1.3 collective-permute-start.5
  73.7 0.0 collective-permute-start.4
  73.7 2.2 %tiles.2 = (bf16[4,128,1024]{2,1,0:T(8,128)(2,1)S(1)}, f32[16,512]{1,0:T(8,128)S(1)}) custom-call(s32[8,8]{1,0:T(8,128)S(1)} %bitcast.16, f32[3,24,1024]{2,1,0:T(8,128)S(1)} %stack.2.near, f32[3,24,1024]{2,1,0:T(8,128)S(1)} %collective-permute-done.2.even, f32[3,24,1024]{2,1,0:T(8,128)S(1)} %collective-permute-done.3.odd), custom_call_target="tpu_custom_call" | custom-call | bytes 8388608 | tf_op jit(solution)/shard_map/tiles/pallas_call | solution.py:118
  75.9 1.0 copy-done.6
  76.9 0.0 collective-permute-done.6.refs_3_
  76.9 0.0 collective-permute-done.5.refs_2_
  76.9 0.0 collective-permute-done.4.refs_1_
  76.9 0.6 coeffs.2
  77.5 13.3 %all_to_all.52.parts = f32[8,16,1024]{2,1,0:T(8,128)S(1)} all-to-all(f32[8,16,1024]{2,1,0:T(8,128)S(1)} %coeffs.2), channel_id=1, replica_groups=mesh['z'=8,'yl'=2,'c'=2,'yh'=2,'x'=4] {'yh','x'}, dimensions={0} | all-to-all | bytes 1048576 | tf_op jit(solution)/shard_map/all_to_all | solution.py:41
  90.8 1.0 weights.2
  91.7 1.9 collective-permute-start.7
  93.7 0.3 collective-permute-start.8
  94.0 1.4 collective-permute-start.9
  95.4 2.2 %tiles.3 = (bf16[4,128,1024]{2,1,0:T(8,128)(2,1)S(1)}, f32[16,512]{1,0:T(8,128)S(1)}) custom-call(s32[8,8]{1,0:T(8,128)S(1)} %bitcast.17, f32[3,24,1024]{2,1,0:T(8,128)S(1)} %stack.2.near, f32[3,24,1024]{2,1,0:T(8,128)S(1)} %collective-permute-done.2.even, f32[3,24,1024]{2,1,0:T(8,128)S(1)} %collective-permute-done.3.odd), custom_call_target="tpu_custom_call" | custom-call | bytes 8388608 | tf_op jit(solution)/shard_map/tiles/pallas_call | solution.py:118
  97.6 1.0 copy-done.8
  98.6 0.0 collective-permute-done.7.first
  98.6 10.6 %all_to_all.53.weights = bf16[32,16,128]{2,1,0:T(8,128)(2,1)S(1)} all-to-all(bf16[32,16,128]{2,1,0:T(8,128)(2,1)S(1)} %gather.1), channel_id=1, replica_groups=mesh['z'=8,'yl'=2,'c'=2,'yh'=2,'x'=4] {'yh','x','yl','c'}, dimensions={0} | all-to-all | bytes 262144 | tf_op jit(solution)/shard_map/all_to_all | solution.py:41
  109.2 2.4 %image.1 = (f32[16,1024]{1,0:T(8,128)S(1)}, f32[256,1,128]{2,1,0:T(1,128)S(1)}) custom-call(bf16[32,16,128]{2,1,0:T(8,128)(2,1)S(1)} %all_to_all.53.weights, bf16[8,1024,512]{2,1,0:T(8,128)(2,1)S(1)} %get-tuple-element.72.rows, s32[1,1]{1,0:T(1,128)S(6)} %copy.10.counts, f32[24,1024]{1,0:T(8,128)S(1)} %copy-done.5, ...), custom_call_target="tpu_custom_call" | custom-call | bytes 16777216 | tf_op jit(solution)/shard_map/image/pallas_call | solution.py:118
  111.7 18.4 %all_to_all.54.rows = f32[256,1,128]{2,1,0:T(1,128)S(1)} all-to-all(f32[256,1,128]{2,1,0:T(1,128)S(1)} %get-tuple-element.73), channel_id=1, replica_groups=mesh['z'=8,'yl'=2,'c'=2,'yh'=2,'x'=4] {'z','yl','c','yh','x'}, dimensions={0} | all-to-all | bytes 262144 | tf_op jit(solution)/shard_map/all_to_all | solution.py:41
  130.1 0.4 update.1
  130.5 3.1 %collective-permute-start.11 = (bf16[16,1024]{1,0:T(8,128)(2,1)S(1)}, bf16[16,1024]{1,0:T(8,128)(2,1)S(1)}, u32[]{:S(2)}, u32[]{:S(2)}) collective-permute-start(bf16[16,1024]{1,0:T(8,128)(2,1)S(1)} %get-tuple-element.77.own), channel_id=1, source_target_pairs={{8,16},{24,32},{40,48},{56,64},{72,80},{88,96},{104,112},{120,128}... | collective-permute-start | bytes 98312 | tf_op jit(solution)/shard_map/ppermute | solution.py:60
  133.6 0.1 collective-permute-start.10
  133.8 1.5 project.1
  135.3 0.8 copy-done.3
  136.1 4.7 %all-to-all-start.6 = ((f32[32,32,128]{2,1,0:T(8,128)}), f32[32,32,128]{2,1,0:T(8,128)}, u32[]{:S(2)}, u32[]{:S(2)}) async-start(f32[32,32,128]{2,1,0:T(8,128)} %copy-done.3), calls=%async_computation.6 | async-start | bytes 1048576 | tf_op jit(solution)/shard_map/all_to_all | solution.py:41
  140.8 0.7 collective-permute-start.13
  141.5 3.9 %collective-permute-start.12 = (bf16[3,16,1024]{2,1,0:T(8,128)(2,1)S(1)}, bf16[3,16,1024]{2,1,0:T(8,128)(2,1)}, u32[]{:S(2)}, u32[]{:S(2)}) collective-permute-start(bf16[3,16,1024]{2,1,0:T(8,128)(2,1)S(1)} %stack.3.near), channel_id=1, source_target_pairs={{0,1},{1,0},{2,3},{3,2},{4,5},{5,4},{6,7},{7,6},{8,9},{9,8},{10,11... | collective-permute-start | bytes 294920 | tf_op jit(solution)/shard_map/ppermute | solution.py:54
  145.4 7.2 %all-to-all-done.6.refs_0_ = f32[32,32,128]{2,1,0:T(8,128)} async-done(((f32[32,32,128]{2,1,0:T(8,128)}), f32[32,32,128]{2,1,0:T(8,128)}, u32[]{:S(2)}, u32[]{:S(2)}) %all-to-all-start.6) | async-done | bytes 524320 | tf_op jit(solution)/shard_map/all_to_all | solution.py:41
  152.7 1.4 copy-done.7
  154.1 1.4 copy-done.9
  155.5 1.8 sparse.1
  157.4 1.1 sum_share.3
  158.5 12.3 %all_to_all.55.parts = f32[8,48,128]{2,1,0:T(8,128)S(1)} all-to-all(f32[8,48,128]{2,1,0:T(8,128)S(1)} %sum_share.3), channel_id=1, replica_groups=mesh['z'=8,'yl'=2,'c'=2,'yh'=2,'x'=4] {'z'}, dimensions={0} | all-to-all | bytes 393216 | tf_op jit(solution)/shard_map/all_to_all | solution.py:41
  170.8 2.7 %collective-permute-start.16 = (f32[16,128]{1,0:T(8,128)S(1)}, f32[16,128]{1,0:T(8,128)S(1)}, u32[]{:S(2)}, u32[]{:S(2)}) collective-permute-start(f32[16,128]{1,0:T(8,128)S(1)} %get-tuple-element.83.refs_0_.rounded), channel_id=1, source_target_pairs={{0,24},{8,16},{16,8},{24,0},{1,25},{9,17},{17,9},{25,1},{2,26},{10... | collective-permute-start | bytes 24584 | tf_op jit(solution)/shard_map/ppermute | solution.py:50
  173.5 1.8 collective-permute-start.15
  175.3 1.3 collective-permute-done.15.refs_2_
  176.6 0.6 coeffs.3
  177.2 17.1 %all_to_all.56.parts = f32[8,16,1152]{2,1,0:T(8,128)S(1)} all-to-all(f32[8,16,1152]{2,1,0:T(8,128)S(1)} %coeffs.3), channel_id=1, replica_groups=mesh['z'=8,'yl'=2,'c'=2,'yh'=2,'x'=4] {'yh','x'}, dimensions={0} | all-to-all | bytes 1179648 | tf_op jit(solution)/shard_map/all_to_all | solution.py:41
  194.3 1.0 weights.3
  195.3 1.2 collective-permute-start.17
  196.5 1.7 collective-permute-start.19
  198.2 0.9 collective-permute-done.18.second
  199.1 0.8 collective-permute-done.19.third
  199.9 0.1 gather_last.1
  200.0 12.6 %all_to_all.57.weights = bf16[32,32,128]{2,1,0:T(8,128)(2,1)S(1)} all-to-all(bf16[32,32,128]{2,1,0:T(8,128)(2,1)S(1)} %get-tuple-element.90), channel_id=1, replica_groups=mesh['z'=8,'yl'=2,'c'=2,'yh'=2,'x'=4] {'yh','x','yl','c'}, dimensions={0} | all-to-all | bytes 524288 | tf_op jit(solution)/shard_map/all_to_all | solution.py:41
  212.6 2.9 %finish.1 = (f32[16,1024]{1,0:T(8,128)}, f32[16,1024]{1,0:T(8,128)}) custom-call(bf16[32,32,128]{2,1,0:T(8,128)(2,1)S(1)} %all_to_all.57.weights, bf16[8,1024,512]{2,1,0:T(8,128)(2,1)S(1)} %copy-done.1, s32[1,1]{1,0:T(1,128)S(6)} %copy.10.counts, f32[16,1024]{1,0:T(8,128)S(1)} %get-tuple-element.80.search, f32[16,1024]{1,0:T(8,128)S(1)} %get-tuple-element.91.sparse, ...), custom_call_target="tpu_custom_call" | custom-call | bytes 16777216 | tf_op jit(solution)/shard_map/finish/pallas_call | solution.py:118
  (37 shorter events, 0.2 us)
Async XLA Ops:
  0.6 73.0 %copy-start.12 = (s32[1,1,8,8]{3,2,1,0:T(8,128)S(1)}, s32[1,1,8,8]{3,2,1,0:T(8,128)}, u32[]{:S(2)}) copy-start(s32[1,1,8,8]{3,2,1,0:T(8,128)} %param.11) | copy-start | bytes 772
  3.1 28.5 %all-to-all-start = ((f32[256,1,128]{2,1,0:T(1,128)}), f32[256,1,128]{2,1,0:T(1,128)S(1)}, u32[]{:S(2)}, u32[]{:S(2)}) async-start(f32[256,1,128]{2,1,0:T(1,128)} %get-tuple-element.50), calls=%async_computation | async-start | bytes 262144 | tf_op jit(solution)/shard_map/all_to_all | solution.py:41
  18.7 12.8 %collective-permute-start.1 = (f32[24,1024]{1,0:T(8,128)}, f32[24,1024]{1,0:T(8,128)S(1)}, u32[]{:S(2)}, u32[]{:S(2)}) collective-permute-start(f32[24,1024]{1,0:T(8,128)} %get-tuple-element.52.own.halo), channel_id=1, source_target_pairs={{8,16},{24,32},{40,48},{56,64},{72,80},{88,96},{104,112},{120,128}... | collective-permute-start | bytes 294920 | tf_op jit(solution)/shard_map/ppermute | solution.py:60
  22.3 9.3 %collective-permute-start = (f32[24,1024]{1,0:T(8,128)}, f32[24,1024]{1,0:T(8,128)S(1)}, u32[]{:S(2)}, u32[]{:S(2)}) collective-permute-start(f32[24,1024]{1,0:T(8,128)} %get-tuple-element.52.own.halo), channel_id=1, source_target_pairs={{0,8},{8,0},{16,24},{24,16},{32,40},{40,32},{48,56},{56,48},{64,72... | collective-permute-start | bytes 294920 | tf_op jit(solution)/shard_map/ppermute | solution.py:54
  22.4 86.8 %copy-start.10 = (f32[1,1,16,1024]{3,2,1,0:T(8,128)S(1)}, f32[1,1,16,1024]{3,2,1,0:T(8,128)}, u32[]{:S(2)}) copy-start(f32[1,1,16,1024]{3,2,1,0:T(8,128)} %param.8) | copy-start | bytes 196612
  22.4 86.8 %copy-start.11 = (f32[1,1,1024]{2,1,0:T(1,128)S(1)}, f32[1,1,1024]{2,1,0:T(1,128)}, u32[]{:S(2)}) copy-start(f32[1,1,1024]{2,1,0:T(1,128)} %param.9) | copy-start | bytes 12292
  31.6 0.9 copy-start.4
  32.5 10.5 %collective-permute-start.3 = (f32[3,24,1024]{2,1,0:T(8,128)S(1)}, f32[3,24,1024]{2,1,0:T(8,128)S(1)}, u32[]{:S(2)}, u32[]{:S(2)}) collective-permute-start(f32[3,24,1024]{2,1,0:T(8,128)S(1)} %stack.2.near), channel_id=1, source_target_pairs={{1,2},{3,4},{5,6},{2,1},{4,3},{6,5},{9,10},{11,12},{13,14},{10,9},... | collective-permute-start | bytes 884744 | tf_op jit(solution)/shard_map/ppermute | solution.py:60
  33.2 9.8 %collective-permute-start.2 = (f32[3,24,1024]{2,1,0:T(8,128)S(1)}, f32[3,24,1024]{2,1,0:T(8,128)S(1)}, u32[]{:S(2)}, u32[]{:S(2)}) collective-permute-start(f32[3,24,1024]{2,1,0:T(8,128)S(1)} %stack.2.near), channel_id=1, source_target_pairs={{0,1},{1,0},{2,3},{3,2},{4,5},{5,4},{6,7},{7,6},{8,9},{9,8},{10,11... | collective-permute-start | bytes 884744 | tf_op jit(solution)/shard_map/ppermute | solution.py:54
  35.3 1.6 copy-start.2
  37.5 0.9 copy-start.5
  43.0 90.8 %copy-start = (bf16[8,1024,512]{2,1,0:T(8,128)(2,1)}, bf16[8,1024,512]{2,1,0:T(8,128)(2,1)S(1)}, u32[]{:S(2)}) copy-start(bf16[8,1024,512]{2,1,0:T(8,128)(2,1)S(1)} %get-tuple-element.72.rows) | copy-start | bytes 25165828
  69.9 7.1 %collective-permute-start.6 = (f32[16,128]{1,0:T(8,128)S(1)}, f32[16,128]{1,0:T(8,128)S(1)}, u32[]{:S(2)}, u32[]{:S(2)}) collective-permute-start(f32[16,128]{1,0:T(8,128)S(1)} %sum_depth.2.refs_0_), channel_id=1, source_target_pairs={{0,24},{8,16},{16,8},{24,0},{1,25},{9,17},{17,9},{25,1},{2,26},{10... | collective-permute-start | bytes 24584 | tf_op jit(solution)/shard_map/ppermute | solution.py:50
  72.4 4.5 %collective-permute-start.5 = (f32[16,128]{1,0:T(8,128)S(1)}, f32[16,128]{1,0:T(8,128)S(1)}, u32[]{:S(2)}, u32[]{:S(2)}) collective-permute-start(f32[16,128]{1,0:T(8,128)S(1)} %sum_depth.2.refs_0_), channel_id=1, source_target_pairs={{0,16},{8,24},{16,0},{24,8},{1,17},{9,25},{17,1},{25,9},{2,18},{10... | collective-permute-start | bytes 24584 | tf_op jit(solution)/shard_map/ppermute | solution.py:50
  73.7 3.3 %collective-permute-start.4 = (f32[16,128]{1,0:T(8,128)S(1)}, f32[16,128]{1,0:T(8,128)S(1)}, u32[]{:S(2)}, u32[]{:S(2)}) collective-permute-start(f32[16,128]{1,0:T(8,128)S(1)} %sum_depth.2.refs_0_), channel_id=1, source_target_pairs={{0,8},{8,0},{16,24},{24,16},{1,9},{9,1},{17,25},{25,17},{2,10},{10... | collective-permute-start | bytes 24584 | tf_op jit(solution)/shard_map/ppermute | solution.py:50
  75.9 1.0 copy-start.6
  91.7 6.9 %collective-permute-start.7 = (f32[16,128]{1,0:T(8,128)S(1)}, f32[16,128]{1,0:T(8,128)S(1)}, u32[]{:S(2)}, u32[]{:S(2)}) collective-permute-start(f32[16,128]{1,0:T(8,128)S(1)} %get-tuple-element.69), channel_id=1, source_target_pairs={{0,8},{8,0},{16,24},{24,16},{1,9},{9,1},{17,25},{25,17},{2,10},{10... | collective-permute-start | bytes 24584 | tf_op jit(solution)/shard_map/ppermute | solution.py:50
  93.7 4.9 %collective-permute-start.8 = (f32[16,128]{1,0:T(8,128)S(1)}, f32[16,128]{1,0:T(8,128)S(1)}, u32[]{:S(2)}, u32[]{:S(2)}) collective-permute-start(f32[16,128]{1,0:T(8,128)S(1)} %get-tuple-element.70), channel_id=1, source_target_pairs={{0,16},{8,24},{16,0},{24,8},{1,17},{9,25},{17,1},{25,9},{2,18},{10... | collective-permute-start | bytes 24584 | tf_op jit(solution)/shard_map/ppermute | solution.py:50
  94.0 4.7 %collective-permute-start.9 = (f32[16,128]{1,0:T(8,128)S(1)}, f32[16,128]{1,0:T(8,128)S(1)}, u32[]{:S(2)}, u32[]{:S(2)}) collective-permute-start(f32[16,128]{1,0:T(8,128)S(1)} %get-tuple-element.71), channel_id=1, source_target_pairs={{0,24},{8,16},{16,8},{24,0},{1,25},{9,17},{17,9},{25,1},{2,26},{10... | collective-permute-start | bytes 24584 | tf_op jit(solution)/shard_map/ppermute | solution.py:50
  97.6 1.0 copy-start.8
  130.5 5.6 %collective-permute-start.11 = (bf16[16,1024]{1,0:T(8,128)(2,1)S(1)}, bf16[16,1024]{1,0:T(8,128)(2,1)S(1)}, u32[]{:S(2)}, u32[]{:S(2)}) collective-permute-start(bf16[16,1024]{1,0:T(8,128)(2,1)S(1)} %get-tuple-element.77.own), channel_id=1, source_target_pairs={{8,16},{24,32},{40,48},{56,64},{72,80},{88,96},{104,112},{120,128}... | collective-permute-start | bytes 98312 | tf_op jit(solution)/shard_map/ppermute | solution.py:60
  133.6 2.5 %collective-permute-start.10 = (bf16[16,1024]{1,0:T(8,128)(2,1)S(1)}, bf16[16,1024]{1,0:T(8,128)(2,1)S(1)}, u32[]{:S(2)}, u32[]{:S(2)}) collective-permute-start(bf16[16,1024]{1,0:T(8,128)(2,1)S(1)} %get-tuple-element.77.own), channel_id=1, source_target_pairs={{0,8},{8,0},{16,24},{24,16},{32,40},{40,32},{48,56},{56,48},{64,72... | collective-permute-start | bytes 98312 | tf_op jit(solution)/shard_map/ppermute | solution.py:54
  135.3 0.8 copy-start.3
  136.1 16.6 %all-to-all-start.6 = ((f32[32,32,128]{2,1,0:T(8,128)}), f32[32,32,128]{2,1,0:T(8,128)}, u32[]{:S(2)}, u32[]{:S(2)}) async-start(f32[32,32,128]{2,1,0:T(8,128)} %copy-done.3), calls=%async_computation.6 | async-start | bytes 1048576 | tf_op jit(solution)/shard_map/all_to_all | solution.py:41
  140.8 11.9 %collective-permute-start.13 = (bf16[3,16,1024]{2,1,0:T(8,128)(2,1)S(1)}, bf16[3,16,1024]{2,1,0:T(8,128)(2,1)S(1)}, u32[]{:S(2)}, u32[]{:S(2)}) collective-permute-start(bf16[3,16,1024]{2,1,0:T(8,128)(2,1)S(1)} %stack.3.near), channel_id=1, source_target_pairs={{1,2},{3,4},{5,6},{2,1},{4,3},{6,5},{9,10},{11,12},{13,14},{10,9},... | collective-permute-start | bytes 294920 | tf_op jit(solution)/shard_map/ppermute | solution.py:60
  141.5 11.2 %collective-permute-start.12 = (bf16[3,16,1024]{2,1,0:T(8,128)(2,1)S(1)}, bf16[3,16,1024]{2,1,0:T(8,128)(2,1)}, u32[]{:S(2)}, u32[]{:S(2)}) collective-permute-start(bf16[3,16,1024]{2,1,0:T(8,128)(2,1)S(1)} %stack.3.near), channel_id=1, source_target_pairs={{0,1},{1,0},{2,3},{3,2},{4,5},{5,4},{6,7},{7,6},{8,9},{9,8},{10,11... | collective-permute-start | bytes 294920 | tf_op jit(solution)/shard_map/ppermute | solution.py:54
  152.7 59.9 %copy-start.1 = (bf16[8,1024,512]{2,1,0:T(8,128)(2,1)S(1)}, bf16[8,1024,512]{2,1,0:T(8,128)(2,1)}, u32[]{:S(2)}) copy-start(bf16[8,1024,512]{2,1,0:T(8,128)(2,1)} %copy-done) | copy-start | bytes 25165828
  152.7 1.4 copy-start.7
  154.1 1.4 copy-start.9
  170.8 4.5 %collective-permute-start.16 = (f32[16,128]{1,0:T(8,128)S(1)}, f32[16,128]{1,0:T(8,128)S(1)}, u32[]{:S(2)}, u32[]{:S(2)}) collective-permute-start(f32[16,128]{1,0:T(8,128)S(1)} %get-tuple-element.83.refs_0_.rounded), channel_id=1, source_target_pairs={{0,24},{8,16},{16,8},{24,0},{1,25},{9,17},{17,9},{25,1},{2,26},{10... | collective-permute-start | bytes 24584 | tf_op jit(solution)/shard_map/ppermute | solution.py:50
  173.5 3.1 %collective-permute-start.15 = (f32[16,128]{1,0:T(8,128)S(1)}, f32[16,128]{1,0:T(8,128)S(1)}, u32[]{:S(2)}, u32[]{:S(2)}) collective-permute-start(f32[16,128]{1,0:T(8,128)S(1)} %get-tuple-element.83.refs_0_.rounded), channel_id=1, source_target_pairs={{0,16},{8,24},{16,0},{24,8},{1,17},{9,25},{17,1},{25,9},{2,18},{10... | collective-permute-start | bytes 24584 | tf_op jit(solution)/shard_map/ppermute | solution.py:50
  175.3 1.3 collective-permute-start.14
  195.3 2.9 %collective-permute-start.17 = (f32[16,256]{1,0:T(8,128)S(1)}, f32[16,256]{1,0:T(8,128)S(1)}, u32[]{:S(2)}, u32[]{:S(2)}) collective-permute-start(f32[16,256]{1,0:T(8,128)S(1)} %get-tuple-element.86), channel_id=1, source_target_pairs={{0,8},{8,0},{16,24},{24,16},{1,9},{9,1},{17,25},{25,17},{2,10},{10... | collective-permute-start | bytes 49160 | tf_op jit(solution)/shard_map/ppermute | solution.py:50
  196.5 2.6 %collective-permute-start.18 = (f32[16,256]{1,0:T(8,128)S(1)}, f32[16,256]{1,0:T(8,128)S(1)}, u32[]{:S(2)}, u32[]{:S(2)}) collective-permute-start(f32[16,256]{1,0:T(8,128)S(1)} %get-tuple-element.87), channel_id=1, source_target_pairs={{0,16},{8,24},{16,0},{24,8},{1,17},{9,25},{17,1},{25,9},{2,18},{10... | collective-permute-start | bytes 49160 | tf_op jit(solution)/shard_map/ppermute | solution.py:50
  196.5 3.4 %collective-permute-start.19 = (f32[16,256]{1,0:T(8,128)S(1)}, f32[16,256]{1,0:T(8,128)S(1)}, u32[]{:S(2)}, u32[]{:S(2)}) collective-permute-start(f32[16,256]{1,0:T(8,128)S(1)} %get-tuple-element.88), channel_id=1, source_target_pairs={{0,24},{8,16},{16,8},{24,0},{1,25},{9,17},{17,9},{25,1},{2,26},{10... | collective-permute-start | bytes 49160 | tf_op jit(solution)/shard_map/ppermute | solution.py:50

commit v6 on v5

--- a/solution.py
+++ b/solution.py
@@ -90,18 +90,6 @@
     return jnp.concatenate(order + [extra, jnp.zeros_like(extra)], axis=0).astype(bf16)
 
 
-def as_lanes(column, offset):
-    row = lax.broadcasted_iota(jnp.int32, (PROBES, 128), 0)
-    lane = lax.broadcasted_iota(jnp.int32, (PROBES, 128), 1)
-    return jnp.sum(jnp.where(lane == row + offset, column, 0.0), axis=0, keepdims=True)
-
-
-def as_column(row_value, offset):
-    row = lax.broadcasted_iota(jnp.int32, (PROBES, 128), 0)
-    lane = lax.broadcasted_iota(jnp.int32, (PROBES, 128), 1)
-    return jnp.sum(jnp.where(lane == row + offset, row_value, 0.0), axis=1, keepdims=True)
-
-
 def live_lanes(count):
     lane = lax.broadcasted_iota(jnp.int32, (1, PTS), 1)
     return jnp.where(lane < count, 1.0, 0.0)
@@ -230,14 +218,16 @@
     for step in range(CHUNKS):
         sums = jnp.dot(packed[...], rows[step], preferred_element_type=f32)
         for part in range(4):
-            sums_out[4 * step + part] = sums[:, part * SHARE : (part + 1) * SHARE]
+            here = sums[:, part * SHARE : (part + 1) * SHARE]
+            sums_out[4 * step + part, :PROBES] = here[:PROBES] + here[PROBES : 2 * PROBES]
+            sums_out[4 * step + part, PROBES:] = here[2 * PROBES :]
 
 
 def project(packed, rows):
     return call(
         project_kernel,
         "project",
-        shape(32, packed.shape[0], SHARE),
+        shape(32, 2 * PROBES, SHARE),
         [VMEM, VMEM],
         (packed, rows),
         params=MIDDLE,
@@ -297,37 +287,48 @@
     )
 
 
-def steps_of(row):
-    rz_now = as_column(row, 0)
-    alpha = rz_now / as_column(row, 16)
-    return alpha, alpha * alpha * as_column(row, 32) / rz_now - 1.0
+def steps_of(sums):
+    alpha = sums[:, 0:1] / sums[:, 1:2]
+    return alpha, alpha * alpha * sums[:, 2:3] / sums[:, 0:1] - 1.0
 
 
 def sparse_kernel(
-    codes, near, even, odd, tiles_low, tiles_high, search, residual, precond,
-    sparse_out, sums_out, values,
+    codes, near, even, odd, tiles_low, tiles_high, halo, image, scaled, sparse_low, sparse_high,
+    precond, sparse_out, sums_out, values,
 ):
-    fill_table(values, (near, even, odd), 0, PROBES, bf16)
+    fill_table(values, (near, even, odd), 0, 2 * PROBES, bf16)
     for block in range(CAP):
-        sparse_out[:, block * BLOCK : (block + 1) * BLOCK] = nt_dot(
+        both = nt_dot(
             partners(values, codes, block), (tiles_low, tiles_high)[block // HALF][block % HALF]
         )
-    field = search[...]
-    left = residual[...]
-    curve = jnp.sum(field * (field + sparse_out[...]), axis=1, keepdims=True)
-    norm = jnp.sum(left * (precond[...] * left), axis=1, keepdims=True)
+        sparse_out[:, block * BLOCK : (block + 1) * BLOCK] = both[:PROBES] + both[PROBES:]
+    old = halo[FEAT:]
+    new = scaled[...]
+    by_old = old + jnp.concatenate([sparse_low[...], sparse_high[...]], axis=1)
+    by_new = new + sparse_out[...]
+    products = (
+        old * (old / precond[...]),
+        old * image[...],
+        new * image[...],
+        old * by_old,
+        old * by_new + new * by_old,
+        new * by_new,
+    )
     lane = lax.broadcasted_iota(jnp.int32, (PROBES, 128), 1)
-    sums_out[...] = jnp.where(lane == 0, curve, jnp.where(lane == 1, norm, 0.0))
-
-
-def apply_tiles(codes, nears, tiles, search, residual, precond):
+    row = jnp.zeros((PROBES, 128), f32)
+    for index, product in enumerate(products):
+        row = jnp.where(lane == index, jnp.sum(product, axis=1, keepdims=True), row)
+    sums_out[...] = row
+
+
+def apply_tiles(codes, nears, tiles, halo, image, scaled, sparse, precond):
     return call(
         sparse_kernel,
         "sparse",
         (FIELD, shape(PROBES, 128)),
-        [SMEM] + [VMEM] * 8,
-        (codes, *nears, *tiles, search, residual, precond),
-        scratch=[pltpu.VMEM((EMPTY + 1, PROBES, BLOCK), bf16)],
+        [SMEM] + [VMEM] * 11,
+        (codes, *nears, *tiles, halo, image, scaled, *sparse, precond),
+        scratch=[pltpu.VMEM((EMPTY + 1, 2 * PROBES, BLOCK), bf16)],
         moved=6 << 20,
     )
 
@@ -358,62 +359,39 @@
 
 
 def image_kernel(
-    weights, rows, counts, halo, sparse_low, sparse_high, precond, probes, image_out, sums_out
+    weights, rows, counts, halo, sparse_low, sparse_high, precond,
+    image_out, scaled_out, halo_out, packed_out,
 ):
     search = halo[FEAT:]
-    live = live_lanes(counts[0, 0])
     sparse = jnp.concatenate([sparse_low[...], sparse_high[...]], axis=1)
-    image = live * (search + sparse + expand(weights, rows))
+    image = live_lanes(counts[0, 0]) * (search + sparse + expand(weights, rows))
     image_out[...] = image
-    norm = jnp.sum(search * (probes[...] * live), axis=1, keepdims=True)
-    curve = jnp.sum(search * image, axis=1, keepdims=True)
-    square = jnp.sum(precond[...] * image * image, axis=1, keepdims=True)
-    row = as_lanes(norm, 0) + as_lanes(curve, 16) + as_lanes(square, 32)
-    sums_out[...] = jnp.broadcast_to(row[None], sums_out.shape)
-
-
-def make_image(weights, rows, counts, halo, sparse, precond, probes):
+    scaled = precond[...] * image
+    scaled_out[...] = scaled
+    first = scaled.astype(bf16)
+    second = (scaled - first.astype(f32)).astype(bf16)
+    rest = (search - search.astype(bf16).astype(f32)).astype(bf16)
+    halo_out[:PROBES] = first
+    halo_out[PROBES:] = second
+    packed_out[:PROBES] = first
+    packed_out[PROBES : 2 * PROBES] = second
+    packed_out[2 * PROBES :] = rest
+
+
+def make_image(weights, rows, counts, halo, sparse, precond):
     return call(
         image_kernel,
         "image",
-        (FIELD, shape(256, 1, 128)),
-        [VMEM, VMEM, SMEM] + [VMEM] * 5,
-        (weights, rows, counts, halo, *sparse, precond, probes),
-        params=MIDDLE,
-        moved=16 << 20,
-    )
-
-
-def update_kernel(
-    rows, halo, probes, precond, counts, image,
-    residual_out, search_out, packed_out, rounded_out, solution_out,
-):
-    alpha, beta = steps_of(jnp.sum(rows[...], axis=0))
-    search = halo[FEAT:]
-    solution_out[...] = alpha * search
-    residual = probes[...] * live_lanes(counts[0, 0]) - alpha * image[...]
-    residual_out[...] = residual
-    following = precond[...] * residual + beta * search
-    search_out[...] = following
-    rounded = following.astype(bf16)
-    rounded_out[...] = rounded
-    packed_out[:PROBES] = rounded
-    packed_out[PROBES:] = (following - rounded.astype(f32)).astype(bf16)
-
-
-def update(rows, halo, probes, precond, counts, image):
-    return call(
-        update_kernel,
-        "update",
         (
             FIELD,
             FIELD,
             shape(2 * PROBES, PTS, dtype=bf16),
-            shape(PROBES, PTS, dtype=bf16),
-            FIELD,
+            shape(3 * PROBES, PTS, dtype=bf16),
         ),
-        [VMEM, VMEM, VMEM, VMEM, SMEM, VMEM],
-        (rows, halo, probes, precond, counts, image),
+        [VMEM, VMEM, SMEM] + [VMEM] * 4,
+        (weights, rows, counts, halo, *sparse, precond),
+        params=MIDDLE,
+        moved=16 << 20,
     )
 
 
@@ -504,23 +482,32 @@
     )
 
 
-def gather_kernel(own, first, second, third, out):
+def gather_kernel(own, first, second, third, out, total_out):
     total = own[...] + first[...] + second[...] + third[...]
+    total_out[...] = total
     out[...] = jnp.broadcast_to(total.astype(bf16)[None], out.shape)
 
 
 def gather_weights(terms):
     return call(
-        gather_kernel, "gather", shape(32, PROBES, SHARE, dtype=bf16), [VMEM] * 4, tuple(terms)
-    )
-
-
-def gather_last_kernel(own, first, second, third, rounded, rest, out, sums_out):
+        gather_kernel,
+        "gather",
+        (shape(32, PROBES, SHARE, dtype=bf16), shape(PROBES, SHARE)),
+        [VMEM] * 4,
+        tuple(terms),
+    )
+
+
+def gather_last_kernel(
+    own, first, second, third, new_share, rest_share, old_share, old_weights, out, sums_out
+):
     total = own[...] + first[...] + second[...] + third[...]
-    weights = total[:, :SHARE].astype(bf16)
-    sums_out[...] = total[:, SHARE:]
-    unrounded = rounded[...] + rest[...]
-    dot = jnp.sum(weights.astype(f32) * unrounded, axis=1, keepdims=True)
+    sums = total[:, SHARE:]
+    sums_out[...] = sums
+    alpha, beta = steps_of(sums)
+    weights = ((1.0 + beta) * old_weights[...] - alpha * total[:, :SHARE]).astype(bf16)
+    share = (1.0 + beta) * (old_share[...] + rest_share[...]) - alpha * new_share[...]
+    dot = jnp.sum(weights.astype(f32) * share, axis=1, keepdims=True)
     lane = lax.broadcasted_iota(jnp.int32, (PROBES, SHARE), 1)
     row = jnp.zeros((PROBES, SHARE), f32)
     for index, part in enumerate(split3(dot)):
@@ -529,36 +516,48 @@
     out[...] = jnp.broadcast_to(both[None], out.shape)
 
 
-def gather_last(terms, rounded, rest):
+def gather_last(terms, new_share, rest_share, old_share, old_weights):
     return call(
         gather_last_kernel,
         "gather_last",
         (shape(32, 2 * PROBES, SHARE, dtype=bf16), shape(PROBES, 128)),
-        [VMEM] * 6,
-        (*terms, rounded, rest),
+        [VMEM] * 8,
+        (*terms, new_share, rest_share, old_share, old_weights),
     )
 
 
 def finish_kernel(
-    weights, rows, counts, search, sparse, residual, solution, sums, solution_out, residual_out
+    weights, rows, counts, halo, probes, image, scaled, sparse_low, sparse_high, sparse, sums,
+    solution_out, residual_out,
 ):
-    field = search[...]
-    image = live_lanes(counts[0, 0]) * (field + sparse[...] + expand(weights, rows))
+    totals = sums[...]
+    alpha, beta = steps_of(totals)
+    scale = 1.0 + beta
+    old = halo[FEAT:]
+    field = scale * old - alpha * scaled[...]
+    by_old = jnp.concatenate([sparse_low[...], sparse_high[...]], axis=1)
+    live = live_lanes(counts[0, 0])
+    following = live * (
+        field + (scale * by_old - alpha * sparse[...]) + expand(weights, rows)
+    )
     dots = jnp.sum(weights[:, PROBES:].astype(f32), axis=0)
-    dot = jnp.sum(dots, axis=1, keepdims=True)
-    totals = sums[...]
-    alpha = totals[:, 1:2] / (totals[:, 0:1] + dot)
-    solution_out[...] = solution[...] + alpha * field
-    residual_out[...] = residual[...] - alpha * image
-
-
-def finish(weights, rows, counts, search, sparse, residual, solution, sums):
+    curve = jnp.sum(dots, axis=1, keepdims=True) + (
+        scale * scale * totals[:, 3:4]
+        - alpha * scale * totals[:, 4:5]
+        + alpha * alpha * totals[:, 5:6]
+    )
+    step = beta * totals[:, 0:1] / curve
+    solution_out[...] = alpha * old + step * field
+    residual_out[...] = (probes[...] * live - alpha * image[...]) - step * following
+
+
+def finish(weights, rows, counts, halo, probes, image, scaled, old_sparse, sparse, sums):
     return call(
         finish_kernel,
         "finish",
         (FIELD, FIELD),
-        [VMEM, VMEM, SMEM] + [VMEM] * 5,
-        (weights, rows, counts, search, sparse, residual, solution, sums),
+        [VMEM, VMEM, SMEM] + [VMEM] * 8,
+        (weights, rows, counts, halo, probes, image, scaled, *old_sparse, sparse, sums),
         params=MIDDLE,
         moved=16 << 20,
     )
@@ -600,27 +599,26 @@
     terms = weight_terms(coeffs, factors)
     high = make_tiles(1, codes, after(halos[0], terms[0]), *halos[1:])
     terms = [after(terms[0], *high)] + [quad_partner(terms[step], step) for step in (1, 2, 3)]
-    weights = exchange(gather_weights(terms), PLANE)
-    tiles, sparse = zip(low, high)
-    image, row = make_image(weights, rows, counts, halo, sparse, scaling, given)
-    row = exchange(row, ALL)
-    residual, search, packed, rounded, solution = update(
-        row, halo, given, scaling, counts, image
-    )
-
-    even, odd = even_pairs(rounded, GX), odd_pairs(rounded, GX)
+    old_share = depth[0]
+    weights, old_weights = gather_weights(terms)
+    weights = exchange(weights, PLANE)
+    tiles, old_sparse = zip(low, high)
+    image, scaled, sent, packed = make_image(weights, rows, counts, halo, old_sparse, scaling)
+    even, odd = even_pairs(sent, GX), odd_pairs(sent, GX)
     parts = project(packed, rows)
 
-    nears = surround(after(rounded, parts), even, odd)
+    nears = surround(after(sent, parts), even, odd)
     got = exchange(after(parts, nears[0]), PLANE)
     sparse, sums = apply_tiles(
-        codes, (after(nears[0], got),) + nears[1:], tiles, search, residual, scaling
+        codes, (after(nears[0], got),) + nears[1:], tiles, halo, image, scaled, old_sparse, scaling
     )
     depth = depth_of(got, sums)
-    weights, totals = gather_last(terms_of(coeffs_of(depth, ())), depth[0], depth[1])
+    weights, totals = gather_last(
+        terms_of(coeffs_of(depth, ())), depth[0], depth[1], old_share, old_weights
+    )
     weights = exchange(weights, PLANE)
     solution, residual = finish(
-        weights, rows, counts, search, sparse, residual, solution, totals
+        weights, rows, counts, halo, given, image, scaled, old_sparse, sparse, totals
     )
     return (solution[None, None], residual[None, None])
 

time: 216 us -> 202 us (0.935)
  blocking collectives: 111 us -> 93.4 us
  local copies, waits for them, and re-layouts: 12.3 us -> 15.3 us
    all_to_all x8 -> x7, blocking collectives: 111 us -> 93.4 us  [exchange(): return lax.all_to_all(parts, axes, 0, 0, tiled=True)]
    unnamed x26 -> x40, local copies, waits for them, and re-layouts: 9.07 us -> 12.1 us
    pallas_call x22 -> x21, Pallas kernels: 24.9 us -> 24.6 us  [call(): pl.pallas_call(kernel, out_shape=out_shape, in_specs=in_specs, out_specs=...]
  transfers between devices with their start and end apart: 22 -> 22, of which waited for: 5 -> 8; matrix products, arithmetic and copies ran while one was open for 1% -> 2% of each run, Pallas kernels for 5% -> 5%
where the time goes in v6:
time: 202 us; the launch traced here: 201 us
  blocking collectives  93.4 us (46%)
  starting transfers between devices  48.7 us (24%)
  Pallas kernels  24.6 us (12%)
  waiting for transfers between devices  17.6 us (9%)
  local copies, waits for them, and re-layouts  15.3 us (8%)
    all_to_all x7, blocking collectives, exchange(): return lax.all_to_all(parts, axes, 0, 0, tiled=True)  93.4 us
    pallas_call x21, Pallas kernels, call(): pl.pallas_call(kernel, out_shape=out_shape, in_specs=in_specs, out_specs=...  24.6 us
    all_to_all x2, starting transfers between devices, exchange(): return lax.all_to_all(parts, axes, 0, 0, tiled=True)  20.1 us
    ppermute x12, starting transfers between devices, quad_partner(): return lax.ppermute(value, ('yl', 'c'), pairs)  14.8 us
    all_to_all x2, waiting for transfers between devices, exchange(): return lax.all_to_all(parts, axes, 0, 0, tiled=True)  13.2 us
    unnamed x40, local copies, waits for them, and re-layouts  12.1 us
    ppermute x4, starting transfers between devices, odd_pairs(): return lax.ppermute(value, axes, pairs + [(j, i) for i, j in pairs])  8.34 us
    ppermute x4, starting transfers between devices, even_pairs(): lax.ppermute(value, axes, [(i, i ^ 1) for i in range(lax.axis_size(axes))])  5.46 us
  transfers between devices with their start and end apart: 22, of which 8 were waited for; matrix products, arithmetic and copies ran while one was open for 2% of the time, Pallas kernels for 5%

profile of v6, /device:TPU:1, one launch (start us, length us, event | category | flops | bytes accessed | tf_op | source)
XLA Modules:
  0.0 201.2 jit_solution(12678369613479768318)
XLA Ops:
  1.3 1.8 prepare.1
  3.1 15.7 %all-to-all-start = ((f32[256,1,128]{2,1,0:T(1,128)}), f32[256,1,128]{2,1,0:T(1,128)S(1)}, u32[]{:S(2)}, u32[]{:S(2)}) async-start(f32[256,1,128]{2,1,0:T(1,128)} %get-tuple-element.49), calls=%async_computation | async-start | bytes 262144 | tf_op jit(solution)/shard_map/all_to_all | solution.py:41
  18.8 3.5 %collective-permute-start.1 = (f32[24,1024]{1,0:T(8,128)}, f32[24,1024]{1,0:T(8,128)S(1)}, u32[]{:S(2)}, u32[]{:S(2)}) collective-permute-start(f32[24,1024]{1,0:T(8,128)} %get-tuple-element.51.own.halo), channel_id=1, source_target_pairs={{8,16},{24,32},{40,48},{56,64},{72,80},{88,96},{104,112},{120,128}... | collective-permute-start | bytes 294920 | tf_op jit(solution)/shard_map/ppermute | solution.py:60
  22.3 0.1 collective-permute-start
  22.4 0.0 copy-start.19
  22.4 3.2 %constant_dynamic-slice_fusion.columns = f32[512,1024]{1,0:T(8,128)} fusion(f32[512,4096]{1,0:T(8,128)} %param.13, s32[]{:T(128)S(6)} %select_n.3), kind=kLoop, calls=%fused_computation | loop fusion | bytes 4194308 | tf_op jit(solution)/shard_map/dynamic_slice | solution.py:576
  25.7 5.9 %all-to-all-done = f32[256,1,128]{2,1,0:T(1,128)S(1)} async-done(((f32[256,1,128]{2,1,0:T(1,128)}), f32[256,1,128]{2,1,0:T(1,128)S(1)}, u32[]{:S(2)}, u32[]{:S(2)}) %all-to-all-start) | async-done | bytes 131104 | tf_op jit(solution)/shard_map/all_to_all | solution.py:41
  31.6 0.9 copy-done.3
  32.5 0.7 collective-permute-start.3
  33.2 2.1 %collective-permute-start.2 = (f32[3,24,1024]{2,1,0:T(8,128)S(1)}, f32[3,24,1024]{2,1,0:T(8,128)S(1)}, u32[]{:S(2)}, u32[]{:S(2)}) collective-permute-start(f32[3,24,1024]{2,1,0:T(8,128)S(1)} %stack.2.near), channel_id=1, source_target_pairs={{0,1},{1,0},{2,3},{3,2},{4,5},{5,4},{6,7},{7,6},{8,9},{9,8},{10,11... | collective-permute-start | bytes 884744 | tf_op jit(solution)/shard_map/ppermute | solution.py:54
  35.4 1.6 copy-done.2
  37.0 0.6 factor.1
  37.6 0.9 copy-done.4
  38.4 4.5 %rows.1 = (bf16[8,1024,512]{2,1,0:T(8,128)(2,1)S(1)}, f32[32,16,128]{2,1,0:T(8,128)S(1)}) custom-call(f32[24,1024]{1,0:T(8,128)S(1)} %copy-done.4, f32[256,128]{1,0:T(8,128)S(1)} %bitcast.8), custom_call_target="tpu_custom_call" | custom-call | bytes 16777216 | tf_op jit(solution)/shard_map/rows/pallas_call | solution.py:106
  43.0 16.0 %all_to_all.45.refs_0_ = f32[32,16,128]{2,1,0:T(8,128)S(1)} all-to-all(f32[32,16,128]{2,1,0:T(8,128)S(1)} %get-tuple-element.58), channel_id=1, replica_groups=mesh['z'=8,'yl'=2,'c'=2,'yh'=2,'x'=4] {'yh','x','yl','c'}, dimensions={0} | all-to-all | bytes 524288 | tf_op jit(solution)/shard_map/all_to_all | solution.py:41
  59.0 10.8 %all_to_all.46.parts = f32[8,16,128]{2,1,0:T(8,128)S(1)} all-to-all(f32[8,16,128]{2,1,0:T(8,128)S(1)} %sum_share.2), channel_id=1, replica_groups=mesh['z'=8,'yl'=2,'c'=2,'yh'=2,'x'=4] {'z'}, dimensions={0} | all-to-all | bytes 131072 | tf_op jit(solution)/shard_map/all_to_all | solution.py:41
  69.9 2.6 %collective-permute-start.6 = (f32[16,128]{1,0:T(8,128)S(1)}, f32[16,128]{1,0:T(8,128)S(1)}, u32[]{:S(2)}, u32[]{:S(2)}) collective-permute-start(f32[16,128]{1,0:T(8,128)S(1)} %sum_depth.2.refs_0_.old_share), channel_id=1, source_target_pairs={{0,24},{8,16},{16,8},{24,0},{1,25},{9,17},{17,9},{25,1},{2,26},{10... | collective-permute-start | bytes 24584 | tf_op jit(solution)/shard_map/ppermute | solution.py:50
  72.4 1.3 collective-permute-start.5
  73.7 2.2 %tiles.2 = (bf16[4,128,1024]{2,1,0:T(8,128)(2,1)S(1)}, f32[16,512]{1,0:T(8,128)S(1)}) custom-call(s32[8,8]{1,0:T(8,128)S(1)} %bitcast.11, f32[3,24,1024]{2,1,0:T(8,128)S(1)} %stack.2.near, f32[3,24,1024]{2,1,0:T(8,128)S(1)} %collective-permute-done.2.even, f32[3,24,1024]{2,1,0:T(8,128)S(1)} %collective-permute-done.3.odd), custom_call_target="tpu_custom_call" | custom-call | bytes 8388608 | tf_op jit(solution)/shard_map/tiles/pallas_call | solution.py:106
  75.9 1.0 copy-done.7
  76.9 0.6 coeffs.2
  77.5 13.3 %all_to_all.47.parts = f32[8,16,1024]{2,1,0:T(8,128)S(1)} all-to-all(f32[8,16,1024]{2,1,0:T(8,128)S(1)} %coeffs.2), channel_id=1, replica_groups=mesh['z'=8,'yl'=2,'c'=2,'yh'=2,'x'=4] {'yh','x'}, dimensions={0} | all-to-all | bytes 1048576 | tf_op jit(solution)/shard_map/all_to_all | solution.py:41
  90.8 1.0 weights.2
  91.7 1.9 collective-permute-start.7
  93.7 0.3 collective-permute-start.8
  94.0 1.4 collective-permute-start.9
  95.4 2.2 %tiles.3 = (bf16[4,128,1024]{2,1,0:T(8,128)(2,1)S(1)}, f32[16,512]{1,0:T(8,128)S(1)}) custom-call(s32[8,8]{1,0:T(8,128)S(1)} %bitcast.12, f32[3,24,1024]{2,1,0:T(8,128)S(1)} %stack.2.near, f32[3,24,1024]{2,1,0:T(8,128)S(1)} %collective-permute-done.2.even, f32[3,24,1024]{2,1,0:T(8,128)S(1)} %collective-permute-done.3.odd), custom_call_target="tpu_custom_call" | custom-call | bytes 8388608 | tf_op jit(solution)/shard_map/tiles/pallas_call | solution.py:106
  97.6 1.0 copy-done.9
  98.6 10.6 %all_to_all.48.weights = bf16[32,16,128]{2,1,0:T(8,128)(2,1)S(1)} all-to-all(bf16[32,16,128]{2,1,0:T(8,128)(2,1)S(1)} %get-tuple-element.71), channel_id=1, replica_groups=mesh['z'=8,'yl'=2,'c'=2,'yh'=2,'x'=4] {'yh','x','yl','c'}, dimensions={0} | all-to-all | bytes 262144 | tf_op jit(solution)/shard_map/all_to_all | solution.py:41
  109.2 2.3 %image.1 = (f32[16,1024]{1,0:T(8,128)S(1)}, f32[16,1024]{1,0:T(8,128)S(1)}, bf16[32,1024]{1,0:T(8,128)(2,1)S(1)}, bf16[48,1024]{1,0:T(8,128)(2,1)S(1)}) custom-call(bf16[32,16,128]{2,1,0:T(8,128)(2,1)S(1)} %all_to_all.48.weights, bf16[8,1024,512]{2,1,0:T(8,128)(2,1)S(1)} %get-tuple-element.72.rows, s32[1,1]{1,0:T(1,128)S(6)} %copy.10.counts, ...), custom_call_target="tpu_custom_call" | custom-call | bytes 16777216 | tf_op jit(solution)/shard_map/image/pallas_call | solution.py:106
  111.5 0.6 copy-done.11
  112.2 0.6 copy-done.14
  112.8 2.8 %collective-permute-start.11 = (bf16[32,1024]{1,0:T(8,128)(2,1)S(1)}, bf16[32,1024]{1,0:T(8,128)(2,1)S(1)}, u32[]{:S(2)}, u32[]{:S(2)}) collective-permute-start(bf16[32,1024]{1,0:T(8,128)(2,1)S(1)} %get-tuple-element.75.own), channel_id=1, source_target_pairs={{8,16},{24,32},{40,48},{56,64},{72,80},{88,96},{104,112},{120,128}... | collective-permute-start | bytes 196616 | tf_op jit(solution)/shard_map/ppermute | solution.py:60
  115.6 0.1 collective-permute-start.10
  115.7 1.4 project.1
  117.1 0.8 copy-done.6
  117.9 0.4 collective-permute-done.11.odd
  118.4 4.4 %all-to-all-start.5 = ((f32[32,32,128]{2,1,0:T(8,128)}), f32[32,32,128]{2,1,0:T(8,128)}, u32[]{:S(2)}, u32[]{:S(2)}) async-start(f32[32,32,128]{2,1,0:T(8,128)} %copy-done.6), calls=%async_computation.5 | async-start | bytes 1048576 | tf_op jit(solution)/shard_map/all_to_all | solution.py:41
  122.8 1.3 collective-permute-start.13
  124.1 3.1 %collective-permute-start.12 = (bf16[3,32,1024]{2,1,0:T(8,128)(2,1)S(1)}, bf16[3,32,1024]{2,1,0:T(8,128)(2,1)}, u32[]{:S(2)}, u32[]{:S(2)}) collective-permute-start(bf16[3,32,1024]{2,1,0:T(8,128)(2,1)S(1)} %stack.3.near), channel_id=1, source_target_pairs={{0,1},{1,0},{2,3},{3,2},{4,5},{5,4},{6,7},{7,6},{8,9},{9,8},{10,11... | collective-permute-start | bytes 589832 | tf_op jit(solution)/shard_map/ppermute | solution.py:54
  127.3 7.2 %all-to-all-done.5.refs_0_ = f32[32,32,128]{2,1,0:T(8,128)} async-done(((f32[32,32,128]{2,1,0:T(8,128)}), f32[32,32,128]{2,1,0:T(8,128)}, u32[]{:S(2)}, u32[]{:S(2)}) %all-to-all-start.5) | async-done | bytes 524320 | tf_op jit(solution)/shard_map/all_to_all | solution.py:41
  134.5 0.3 collective-permute-done.12.even
  134.8 1.4 copy-done.8
  136.2 1.6 copy-done.10
  137.7 0.8 copy-done.12
  138.6 0.8 copy-done.15
  139.4 2.0 sparse.1
  141.4 1.1 sum_share.3
  142.5 12.7 %all_to_all.49.parts = f32[8,48,128]{2,1,0:T(8,128)S(1)} all-to-all(f32[8,48,128]{2,1,0:T(8,128)S(1)} %sum_share.3), channel_id=1, replica_groups=mesh['z'=8,'yl'=2,'c'=2,'yh'=2,'x'=4] {'z'}, dimensions={0} | all-to-all | bytes 393216 | tf_op jit(solution)/shard_map/all_to_all | solution.py:41
  155.2 4.1 %collective-permute-start.16 = (f32[16,128]{1,0:T(8,128)S(1)}, f32[16,128]{1,0:T(8,128)S(1)}, u32[]{:S(2)}, u32[]{:S(2)}) collective-permute-start(f32[16,128]{1,0:T(8,128)S(1)} %get-tuple-element.81.refs_0_.new_share), channel_id=1, source_target_pairs={{0,24},{8,16},{16,8},{24,0},{1,25},{9,17},{17,9},{25,1},{2,26},{10... | collective-permute-start | bytes 24584 | tf_op jit(solution)/shard_map/ppermute | solution.py:50
  159.2 0.2 collective-permute-start.15
  159.4 0.3 collective-permute-start.14
  159.7 1.0 collective-permute-done.16.refs_3_
  160.8 1.0 collective-permute-done.15.refs_2_
  161.7 0.6 coeffs.3
  162.3 17.5 %all_to_all.50.parts = f32[8,16,1152]{2,1,0:T(8,128)S(1)} all-to-all(f32[8,16,1152]{2,1,0:T(8,128)S(1)} %coeffs.3), channel_id=1, replica_groups=mesh['z'=8,'yl'=2,'c'=2,'yh'=2,'x'=4] {'yh','x'}, dimensions={0} | all-to-all | bytes 1179648 | tf_op jit(solution)/shard_map/all_to_all | solution.py:41
  179.8 1.0 weights.3
  180.8 1.1 collective-permute-start.17
  182.0 1.7 collective-permute-start.19
  183.7 0.9 collective-permute-done.18.second
  184.5 0.8 collective-permute-done.19.third
  185.4 0.2 gather_last.1
  185.6 12.6 %all_to_all.51.weights = bf16[32,32,128]{2,1,0:T(8,128)(2,1)S(1)} all-to-all(bf16[32,32,128]{2,1,0:T(8,128)(2,1)S(1)} %get-tuple-element.89), channel_id=1, replica_groups=mesh['z'=8,'yl'=2,'c'=2,'yh'=2,'x'=4] {'yh','x','yl','c'}, dimensions={0} | all-to-all | bytes 524288 | tf_op jit(solution)/shard_map/all_to_all | solution.py:41
  198.3 2.9 %finish.1 = (f32[16,1024]{1,0:T(8,128)}, f32[16,1024]{1,0:T(8,128)}) custom-call(bf16[32,32,128]{2,1,0:T(8,128)(2,1)S(1)} %all_to_all.51.weights, bf16[8,1024,512]{2,1,0:T(8,128)(2,1)S(1)} %copy-done.1, s32[1,1]{1,0:T(1,128)S(6)} %copy.10.counts, f32[24,1024]{1,0:T(8,128)S(1)} %copy-done.5, f32[16,1024]{1,0:T(8,128)S(1)} %bitcast.10, ...), custom_call_target="tpu_custom_call" | custom-call | bytes 16777216 | tf_op jit(solution)/shard_map/finish/pallas_call | solution.py:106
  (49 shorter events, 0.2 us)
Async XLA Ops:
  0.6 73.1 %copy-start.18 = (s32[1,1,8,8]{3,2,1,0:T(8,128)S(1)}, s32[1,1,8,8]{3,2,1,0:T(8,128)}, u32[]{:S(2)}) copy-start(s32[1,1,8,8]{3,2,1,0:T(8,128)} %param.11) | copy-start | bytes 772
  3.1 28.5 %all-to-all-start = ((f32[256,1,128]{2,1,0:T(1,128)}), f32[256,1,128]{2,1,0:T(1,128)S(1)}, u32[]{:S(2)}, u32[]{:S(2)}) async-start(f32[256,1,128]{2,1,0:T(1,128)} %get-tuple-element.49), calls=%async_computation | async-start | bytes 262144 | tf_op jit(solution)/shard_map/all_to_all | solution.py:41
  18.8 12.8 %collective-permute-start.1 = (f32[24,1024]{1,0:T(8,128)}, f32[24,1024]{1,0:T(8,128)S(1)}, u32[]{:S(2)}, u32[]{:S(2)}) collective-permute-start(f32[24,1024]{1,0:T(8,128)} %get-tuple-element.51.own.halo), channel_id=1, source_target_pairs={{8,16},{24,32},{40,48},{56,64},{72,80},{88,96},{104,112},{120,128}... | collective-permute-start | bytes 294920 | tf_op jit(solution)/shard_map/ppermute | solution.py:60
  22.3 9.3 %collective-permute-start = (f32[24,1024]{1,0:T(8,128)}, f32[24,1024]{1,0:T(8,128)S(1)}, u32[]{:S(2)}, u32[]{:S(2)}) collective-permute-start(f32[24,1024]{1,0:T(8,128)} %get-tuple-element.51.own.halo), channel_id=1, source_target_pairs={{0,8},{8,0},{16,24},{24,16},{32,40},{40,32},{48,56},{56,48},{64,72... | collective-permute-start | bytes 294920 | tf_op jit(solution)/shard_map/ppermute | solution.py:54
  22.4 86.8 %copy-start.5 = (f32[24,1024]{1,0:T(8,128)S(1)}, f32[24,1024]{1,0:T(8,128)}, u32[]{:S(2)}) copy-start(f32[24,1024]{1,0:T(8,128)} %get-tuple-element.51.own.halo) | copy-start | bytes 294916
  22.4 86.8 %copy-start.19 = (f32[1,1,1024]{2,1,0:T(1,128)S(1)}, f32[1,1,1024]{2,1,0:T(1,128)}, u32[]{:S(2)}) copy-start(f32[1,1,1024]{2,1,0:T(1,128)} %param.9) | copy-start | bytes 12292
  31.6 0.9 copy-start.3
  32.5 10.5 %collective-permute-start.3 = (f32[3,24,1024]{2,1,0:T(8,128)S(1)}, f32[3,24,1024]{2,1,0:T(8,128)S(1)}, u32[]{:S(2)}, u32[]{:S(2)}) collective-permute-start(f32[3,24,1024]{2,1,0:T(8,128)S(1)} %stack.2.near), channel_id=1, source_target_pairs={{1,2},{3,4},{5,6},{2,1},{4,3},{6,5},{9,10},{11,12},{13,14},{10,9},... | collective-permute-start | bytes 884744 | tf_op jit(solution)/shard_map/ppermute | solution.py:60
  33.2 9.8 %collective-permute-start.2 = (f32[3,24,1024]{2,1,0:T(8,128)S(1)}, f32[3,24,1024]{2,1,0:T(8,128)S(1)}, u32[]{:S(2)}, u32[]{:S(2)}) collective-permute-start(f32[3,24,1024]{2,1,0:T(8,128)S(1)} %stack.2.near), channel_id=1, source_target_pairs={{0,1},{1,0},{2,3},{3,2},{4,5},{5,4},{6,7},{7,6},{8,9},{9,8},{10,11... | collective-permute-start | bytes 884744 | tf_op jit(solution)/shard_map/ppermute | solution.py:54
  35.4 1.6 copy-start.2
  37.6 0.9 copy-start.4
  43.0 72.7 %copy-start = (bf16[8,1024,512]{2,1,0:T(8,128)(2,1)}, bf16[8,1024,512]{2,1,0:T(8,128)(2,1)S(1)}, u32[]{:S(2)}) copy-start(bf16[8,1024,512]{2,1,0:T(8,128)(2,1)S(1)} %get-tuple-element.72.rows) | copy-start | bytes 25165828
  69.9 7.0 %collective-permute-start.6 = (f32[16,128]{1,0:T(8,128)S(1)}, f32[16,128]{1,0:T(8,128)S(1)}, u32[]{:S(2)}, u32[]{:S(2)}) collective-permute-start(f32[16,128]{1,0:T(8,128)S(1)} %sum_depth.2.refs_0_.old_share), channel_id=1, source_target_pairs={{0,24},{8,16},{16,8},{24,0},{1,25},{9,17},{17,9},{25,1},{2,26},{10... | collective-permute-start | bytes 24584 | tf_op jit(solution)/shard_map/ppermute | solution.py:50
  72.4 4.5 %collective-permute-start.5 = (f32[16,128]{1,0:T(8,128)S(1)}, f32[16,128]{1,0:T(8,128)S(1)}, u32[]{:S(2)}, u32[]{:S(2)}) collective-permute-start(f32[16,128]{1,0:T(8,128)S(1)} %sum_depth.2.refs_0_.old_share), channel_id=1, source_target_pairs={{0,16},{8,24},{16,0},{24,8},{1,17},{9,25},{17,1},{25,9},{2,18},{10... | collective-permute-start | bytes 24584 | tf_op jit(solution)/shard_map/ppermute | solution.py:50
  73.7 3.2 %collective-permute-start.4 = (f32[16,128]{1,0:T(8,128)S(1)}, f32[16,128]{1,0:T(8,128)S(1)}, u32[]{:S(2)}, u32[]{:S(2)}) collective-permute-start(f32[16,128]{1,0:T(8,128)S(1)} %sum_depth.2.refs_0_.old_share), channel_id=1, source_target_pairs={{0,8},{8,0},{16,24},{24,16},{1,9},{9,1},{17,25},{25,17},{2,10},{10... | collective-permute-start | bytes 24584 | tf_op jit(solution)/shard_map/ppermute | solution.py:50
  75.9 1.0 copy-start.7
  91.7 6.9 %collective-permute-start.7 = (f32[16,128]{1,0:T(8,128)S(1)}, f32[16,128]{1,0:T(8,128)S(1)}, u32[]{:S(2)}, u32[]{:S(2)}) collective-permute-start(f32[16,128]{1,0:T(8,128)S(1)} %get-tuple-element.68), channel_id=1, source_target_pairs={{0,8},{8,0},{16,24},{24,16},{1,9},{9,1},{17,25},{25,17},{2,10},{10... | collective-permute-start | bytes 24584 | tf_op jit(solution)/shard_map/ppermute | solution.py:50
  93.7 4.9 %collective-permute-start.8 = (f32[16,128]{1,0:T(8,128)S(1)}, f32[16,128]{1,0:T(8,128)S(1)}, u32[]{:S(2)}, u32[]{:S(2)}) collective-permute-start(f32[16,128]{1,0:T(8,128)S(1)} %get-tuple-element.69), channel_id=1, source_target_pairs={{0,16},{8,24},{16,0},{24,8},{1,17},{9,25},{17,1},{25,9},{2,18},{10... | collective-permute-start | bytes 24584 | tf_op jit(solution)/shard_map/ppermute | solution.py:50
  94.0 4.7 %collective-permute-start.9 = (f32[16,128]{1,0:T(8,128)S(1)}, f32[16,128]{1,0:T(8,128)S(1)}, u32[]{:S(2)}, u32[]{:S(2)}) collective-permute-start(f32[16,128]{1,0:T(8,128)S(1)} %get-tuple-element.70), channel_id=1, source_target_pairs={{0,24},{8,16},{16,8},{24,0},{1,25},{9,17},{17,9},{25,1},{2,26},{10... | collective-permute-start | bytes 24584 | tf_op jit(solution)/shard_map/ppermute | solution.py:50
  97.6 1.0 copy-start.9
  111.5 0.6 copy-start.11
  112.2 0.6 copy-start.14
  112.8 5.6 %collective-permute-start.11 = (bf16[32,1024]{1,0:T(8,128)(2,1)S(1)}, bf16[32,1024]{1,0:T(8,128)(2,1)S(1)}, u32[]{:S(2)}, u32[]{:S(2)}) collective-permute-start(bf16[32,1024]{1,0:T(8,128)(2,1)S(1)} %get-tuple-element.75.own), channel_id=1, source_target_pairs={{8,16},{24,32},{40,48},{56,64},{72,80},{88,96},{104,112},{120,128}... | collective-permute-start | bytes 196616 | tf_op jit(solution)/shard_map/ppermute | solution.py:60
  115.6 2.8 %collective-permute-start.10 = (bf16[32,1024]{1,0:T(8,128)(2,1)S(1)}, bf16[32,1024]{1,0:T(8,128)(2,1)S(1)}, u32[]{:S(2)}, u32[]{:S(2)}) collective-permute-start(bf16[32,1024]{1,0:T(8,128)(2,1)S(1)} %get-tuple-element.75.own), channel_id=1, source_target_pairs={{0,8},{8,0},{16,24},{24,16},{32,40},{40,32},{48,56},{56,48},{64,72... | collective-permute-start | bytes 196616 | tf_op jit(solution)/shard_map/ppermute | solution.py:54
  117.1 0.8 copy-start.6
  118.4 16.1 %all-to-all-start.5 = ((f32[32,32,128]{2,1,0:T(8,128)}), f32[32,32,128]{2,1,0:T(8,128)}, u32[]{:S(2)}, u32[]{:S(2)}) async-start(f32[32,32,128]{2,1,0:T(8,128)} %copy-done.6), calls=%async_computation.5 | async-start | bytes 1048576 | tf_op jit(solution)/shard_map/all_to_all | solution.py:41
  122.8 11.7 %collective-permute-start.13 = (bf16[3,32,1024]{2,1,0:T(8,128)(2,1)S(1)}, bf16[3,32,1024]{2,1,0:T(8,128)(2,1)}, u32[]{:S(2)}, u32[]{:S(2)}) collective-permute-start(bf16[3,32,1024]{2,1,0:T(8,128)(2,1)S(1)} %stack.3.near), channel_id=1, source_target_pairs={{1,2},{3,4},{5,6},{2,1},{4,3},{6,5},{9,10},{11,12},{13,14},{10,9},... | collective-permute-start | bytes 589832 | tf_op jit(solution)/shard_map/ppermute | solution.py:60
  124.1 10.7 %collective-permute-start.12 = (bf16[3,32,1024]{2,1,0:T(8,128)(2,1)S(1)}, bf16[3,32,1024]{2,1,0:T(8,128)(2,1)}, u32[]{:S(2)}, u32[]{:S(2)}) collective-permute-start(bf16[3,32,1024]{2,1,0:T(8,128)(2,1)S(1)} %stack.3.near), channel_id=1, source_target_pairs={{0,1},{1,0},{2,3},{3,2},{4,5},{5,4},{6,7},{7,6},{8,9},{9,8},{10,11... | collective-permute-start | bytes 589832 | tf_op jit(solution)/shard_map/ppermute | solution.py:54
  134.5 63.7 %copy-start.1 = (bf16[8,1024,512]{2,1,0:T(8,128)(2,1)S(1)}, bf16[8,1024,512]{2,1,0:T(8,128)(2,1)}, u32[]{:S(2)}) copy-start(bf16[8,1024,512]{2,1,0:T(8,128)(2,1)} %copy-done) | copy-start | bytes 25165828
  134.8 1.4 copy-start.8
  136.2 1.6 copy-start.10
  137.7 0.8 copy-start.12
  138.6 0.8 copy-start.15
  139.4 58.8 %copy-start.13 = (f32[16,1024]{1,0:T(8,128)S(1)}, f32[16,1024]{1,0:T(8,128)}, u32[]{:S(2)}) copy-start(f32[16,1024]{1,0:T(8,128)} %copy-done.11) | copy-start | bytes 196612
  139.4 58.8 %copy-start.16 = (f32[16,1024]{1,0:T(8,128)S(1)}, f32[16,1024]{1,0:T(8,128)}, u32[]{:S(2)}) copy-start(f32[16,1024]{1,0:T(8,128)} %copy-done.14) | copy-start | bytes 196612
  139.4 58.8 %copy-start.17 = (f32[1,1,16,1024]{3,2,1,0:T(8,128)S(1)}, f32[1,1,16,1024]{3,2,1,0:T(8,128)}, u32[]{:S(2)}) copy-start(f32[1,1,16,1024]{3,2,1,0:T(8,128)} %param.8) | copy-start | bytes 196612
  155.2 5.6 %collective-permute-start.16 = (f32[16,128]{1,0:T(8,128)S(1)}, f32[16,128]{1,0:T(8,128)S(1)}, u32[]{:S(2)}, u32[]{:S(2)}) collective-permute-start(f32[16,128]{1,0:T(8,128)S(1)} %get-tuple-element.81.refs_0_.new_share), channel_id=1, source_target_pairs={{0,24},{8,16},{16,8},{24,0},{1,25},{9,17},{17,9},{25,1},{2,26},{10... | collective-permute-start | bytes 24584 | tf_op jit(solution)/shard_map/ppermute | solution.py:50
  159.2 2.5 %collective-permute-start.15 = (f32[16,128]{1,0:T(8,128)S(1)}, f32[16,128]{1,0:T(8,128)S(1)}, u32[]{:S(2)}, u32[]{:S(2)}) collective-permute-start(f32[16,128]{1,0:T(8,128)S(1)} %get-tuple-element.81.refs_0_.new_share), channel_id=1, source_target_pairs={{0,16},{8,24},{16,0},{24,8},{1,17},{9,25},{17,1},{25,9},{2,18},{10... | collective-permute-start | bytes 24584 | tf_op jit(solution)/shard_map/ppermute | solution.py:50
  159.4 2.3 %collective-permute-start.14 = (f32[16,128]{1,0:T(8,128)S(1)}, f32[16,128]{1,0:T(8,128)S(1)}, u32[]{:S(2)}, u32[]{:S(2)}) collective-permute-start(f32[16,128]{1,0:T(8,128)S(1)} %get-tuple-element.81.refs_0_.new_share), channel_id=1, source_target_pairs={{0,8},{8,0},{16,24},{24,16},{1,9},{9,1},{17,25},{25,17},{2,10},{10... | collective-permute-start | bytes 24584 | tf_op jit(solution)/shard_map/ppermute | solution.py:50
  180.8 2.8 %collective-permute-start.17 = (f32[16,256]{1,0:T(8,128)S(1)}, f32[16,256]{1,0:T(8,128)S(1)}, u32[]{:S(2)}, u32[]{:S(2)}) collective-permute-start(f32[16,256]{1,0:T(8,128)S(1)} %get-tuple-element.84), channel_id=1, source_target_pairs={{0,8},{8,0},{16,24},{24,16},{1,9},{9,1},{17,25},{25,17},{2,10},{10... | collective-permute-start | bytes 49160 | tf_op jit(solution)/shard_map/ppermute | solution.py:50
  182.0 2.6 %collective-permute-start.18 = (f32[16,256]{1,0:T(8,128)S(1)}, f32[16,256]{1,0:T(8,128)S(1)}, u32[]{:S(2)}, u32[]{:S(2)}) collective-permute-start(f32[16,256]{1,0:T(8,128)S(1)} %get-tuple-element.85), channel_id=1, source_target_pairs={{0,16},{8,24},{16,0},{24,8},{1,17},{9,25},{17,1},{25,9},{2,18},{10... | collective-permute-start | bytes 49160 | tf_op jit(solution)/shard_map/ppermute | solution.py:50
  182.0 3.4 %collective-permute-start.19 = (f32[16,256]{1,0:T(8,128)S(1)}, f32[16,256]{1,0:T(8,128)S(1)}, u32[]{:S(2)}, u32[]{:S(2)}) collective-permute-start(f32[16,256]{1,0:T(8,128)S(1)} %get-tuple-element.86), channel_id=1, source_target_pairs={{0,24},{8,16},{16,8},{24,0},{1,25},{9,17},{17,9},{25,1},{2,26},{10... | collective-permute-start | bytes 49160 | tf_op jit(solution)/shard_map/ppermute | solution.py:50

commit v7 on v6

--- a/solution.py
+++ b/solution.py
@@ -296,12 +296,11 @@
     codes, near, even, odd, tiles_low, tiles_high, halo, image, scaled, sparse_low, sparse_high,
     precond, sparse_out, sums_out, values,
 ):
-    fill_table(values, (near, even, odd), 0, 2 * PROBES, bf16)
+    fill_table(values, (near, even, odd), 0, PROBES, bf16)
     for block in range(CAP):
-        both = nt_dot(
+        sparse_out[:, block * BLOCK : (block + 1) * BLOCK] = nt_dot(
             partners(values, codes, block), (tiles_low, tiles_high)[block // HALF][block % HALF]
         )
-        sparse_out[:, block * BLOCK : (block + 1) * BLOCK] = both[:PROBES] + both[PROBES:]
     old = halo[FEAT:]
     new = scaled[...]
     by_old = old + jnp.concatenate([sparse_low[...], sparse_high[...]], axis=1)
@@ -328,7 +327,7 @@
         (FIELD, shape(PROBES, 128)),
         [SMEM] + [VMEM] * 11,
         (codes, *nears, *tiles, halo, image, scaled, *sparse, precond),
-        scratch=[pltpu.VMEM((EMPTY + 1, 2 * PROBES, BLOCK), bf16)],
+        scratch=[pltpu.VMEM((EMPTY + 1, PROBES, BLOCK), bf16)],
         moved=6 << 20,
     )
 
@@ -371,8 +370,7 @@
     first = scaled.astype(bf16)
     second = (scaled - first.astype(f32)).astype(bf16)
     rest = (search - search.astype(bf16).astype(f32)).astype(bf16)
-    halo_out[:PROBES] = first
-    halo_out[PROBES:] = second
+    halo_out[...] = first
     packed_out[:PROBES] = first
     packed_out[PROBES : 2 * PROBES] = second
     packed_out[2 * PROBES :] = rest
@@ -385,7 +383,7 @@
         (
             FIELD,
             FIELD,
-            shape(2 * PROBES, PTS, dtype=bf16),
+            shape(PROBES, PTS, dtype=bf16),
             shape(3 * PROBES, PTS, dtype=bf16),
         ),
         [VMEM, VMEM, SMEM] + [VMEM] * 4,
@@ -608,7 +606,7 @@
     parts = project(packed, rows)
 
     nears = surround(after(sent, parts), even, odd)
-    got = exchange(after(parts, nears[0]), PLANE)
+    got = exchange(after(parts, *nears), PLANE)
     sparse, sums = apply_tiles(
         codes, (after(nears[0], got),) + nears[1:], tiles, halo, image, scaled, old_sparse, scaling
     )

time: 202 us -> 197 us (0.975)
  blocking collectives: 93.4 us -> 110 us
  local copies, waits for them, and re-layouts: 15.3 us -> 3.56 us
  starting transfers between devices: 48.7 us -> 43.4 us
  waiting for transfers between devices: 17.6 us -> 15.1 us
    all_to_all x7 -> x8, blocking collectives: 93.4 us -> 110 us  [exchange(): return lax.all_to_all(parts, axes, 0, 0, tiled=True)]
    unnamed x40 -> x12, local copies, waits for them, and re-layouts: 12.1 us -> 1.8 us
    all_to_all x2 -> x1, waiting for transfers between devices: 13.2 us -> 7.39 us  [exchange(): return lax.all_to_all(parts, axes, 0, 0, tiled=True)]
    all_to_all x2 -> x1, starting transfers between devices: 20.1 us -> 15.7 us  [exchange(): return lax.all_to_all(parts, axes, 0, 0, tiled=True)]
    ppermute x4, waiting for transfers between devices: 0.28 us -> 3.62 us  [even_pairs(): lax.ppermute(value, axes, [(i, i ^ 1) for i in range(lax.axis_size(axes))])]
  transfers between devices with their start and end apart: 22 -> 21, of which waited for: 8 -> 7; matrix products, arithmetic and copies ran while one was open for 2% -> 1% of each run, Pallas kernels for 5% -> 6%
where the time goes in v7:
time: 197 us; the launch traced here: 196 us
  blocking collectives  110 us (56%)
  starting transfers between devices  43.4 us (22%)
  Pallas kernels  22.9 us (12%)
  waiting for transfers between devices  15.1 us (8%)
  local copies, waits for them, and re-layouts  3.56 us (2%)
    all_to_all x8, blocking collectives, exchange(): return lax.all_to_all(parts, axes, 0, 0, tiled=True)  110 us
    pallas_call x21, Pallas kernels, call(): pl.pallas_call(kernel, out_shape=out_shape, in_specs=in_specs, out_specs=...  22.9 us
    ppermute x12, starting transfers between devices, quad_partner(): return lax.ppermute(value, ('yl', 'c'), pairs)  15.8 us
    all_to_all x1, starting transfers between devices, exchange(): return lax.all_to_all(parts, axes, 0, 0, tiled=True)  15.7 us
    ppermute x4, starting transfers between devices, odd_pairs(): return lax.ppermute(value, axes, pairs + [(j, i) for i, j in pairs])  7.68 us
    all_to_all x1, waiting for transfers between devices, exchange(): return lax.all_to_all(parts, axes, 0, 0, tiled=True)  7.39 us
    ppermute x4, starting transfers between devices, even_pairs(): lax.ppermute(value, axes, [(i, i ^ 1) for i in range(lax.axis_size(axes))])  4.27 us
  transfers between devices with their start and end apart: 21, of which 7 were waited for; matrix products, arithmetic and copies ran while one was open for 1% of the time, Pallas kernels for 6%

profile of v7, /device:TPU:1, one launch (start us, length us, event | category | flops | bytes accessed | tf_op | source)
XLA Modules:
  0.0 196.0 jit_solution(13970911617563818411)
XLA Ops:
  1.3 1.8 prepare.1
  3.1 15.7 %all-to-all-start = ((f32[256,1,128]{2,1,0:T(1,128)}), f32[256,1,128]{2,1,0:T(1,128)S(1)}, u32[]{:S(2)}, u32[]{:S(2)}) async-start(f32[256,1,128]{2,1,0:T(1,128)} %get-tuple-element.49), calls=%async_computation | async-start | bytes 262144 | tf_op jit(solution)/shard_map/all_to_all | solution.py:41
  18.7 3.5 %collective-permute-start.1 = (f32[24,1024]{1,0:T(8,128)}, f32[24,1024]{1,0:T(8,128)S(1)}, u32[]{:S(2)}, u32[]{:S(2)}) collective-permute-start(f32[24,1024]{1,0:T(8,128)} %get-tuple-element.51.own.halo), channel_id=1, source_target_pairs={{8,16},{24,32},{40,48},{56,64},{72,80},{88,96},{104,112},{120,128}... | collective-permute-start | bytes 294920 | tf_op jit(solution)/shard_map/ppermute | solution.py:60
  22.3 0.1 collective-permute-start
  22.4 0.0 copy-start.5
  22.4 1.8 constant_dynamic-slice_fusion.columns
  24.2 7.4 %all-to-all-done = f32[256,1,128]{2,1,0:T(1,128)S(1)} async-done(((f32[256,1,128]{2,1,0:T(1,128)}), f32[256,1,128]{2,1,0:T(1,128)S(1)}, u32[]{:S(2)}, u32[]{:S(2)}) %all-to-all-start) | async-done | bytes 131104 | tf_op jit(solution)/shard_map/all_to_all | solution.py:41
  31.6 0.0 collective-permute-done.1.odd
  31.6 0.0 collective-permute-done.even
  31.6 0.9 copy-done
  32.5 0.7 collective-permute-start.3
  33.2 2.1 %collective-permute-start.2 = (f32[3,24,1024]{2,1,0:T(8,128)S(1)}, f32[3,24,1024]{2,1,0:T(8,128)S(1)}, u32[]{:S(2)}, u32[]{:S(2)}) collective-permute-start(f32[3,24,1024]{2,1,0:T(8,128)S(1)} %stack.2.near), channel_id=1, source_target_pairs={{0,1},{1,0},{2,3},{3,2},{4,5},{5,4},{6,7},{7,6},{8,9},{9,8},{10,11... | collective-permute-start | bytes 884744 | tf_op jit(solution)/shard_map/ppermute | solution.py:54
  35.3 0.6 factor.1
  35.9 0.9 copy-done.1
  36.8 4.5 %rows.1 = (bf16[8,1024,512]{2,1,0:T(8,128)(2,1)S(1)}, f32[32,16,128]{2,1,0:T(8,128)S(1)}) custom-call(f32[24,1024]{1,0:T(8,128)S(1)} %copy-done.1, f32[256,128]{1,0:T(8,128)S(1)} %bitcast.8), custom_call_target="tpu_custom_call" | custom-call | bytes 16777216 | tf_op jit(solution)/shard_map/rows/pallas_call | solution.py:106
  41.4 0.0 collective-permute-done.3.odd
  41.4 0.7 collective-permute-done.2.even
  42.1 16.9 %all_to_all.45.refs_0_ = f32[32,16,128]{2,1,0:T(8,128)S(1)} all-to-all(f32[32,16,128]{2,1,0:T(8,128)S(1)} %get-tuple-element.58), channel_id=1, replica_groups=mesh['z'=8,'yl'=2,'c'=2,'yh'=2,'x'=4] {'yh','x','yl','c'}, dimensions={0} | all-to-all | bytes 524288 | tf_op jit(solution)/shard_map/all_to_all | solution.py:41
  59.0 10.8 %all_to_all.46.parts = f32[8,16,128]{2,1,0:T(8,128)S(1)} all-to-all(f32[8,16,128]{2,1,0:T(8,128)S(1)} %sum_share.2), channel_id=1, replica_groups=mesh['z'=8,'yl'=2,'c'=2,'yh'=2,'x'=4] {'z'}, dimensions={0} | all-to-all | bytes 131072 | tf_op jit(solution)/shard_map/all_to_all | solution.py:41
  69.8 2.6 %collective-permute-start.6 = (f32[16,128]{1,0:T(8,128)S(1)}, f32[16,128]{1,0:T(8,128)S(1)}, u32[]{:S(2)}, u32[]{:S(2)}) collective-permute-start(f32[16,128]{1,0:T(8,128)S(1)} %sum_depth.2.refs_0_.old_share), channel_id=1, source_target_pairs={{0,24},{8,16},{16,8},{24,0},{1,25},{9,17},{17,9},{25,1},{2,26},{10... | collective-permute-start | bytes 24584 | tf_op jit(solution)/shard_map/ppermute | solution.py:50
  72.4 1.3 collective-permute-start.5
  73.6 0.0 collective-permute-start.4
  73.6 2.2 %tiles.2 = (bf16[4,128,1024]{2,1,0:T(8,128)(2,1)S(1)}, f32[16,512]{1,0:T(8,128)S(1)}) custom-call(s32[8,8]{1,0:T(8,128)S(1)} %bitcast.11, f32[3,24,1024]{2,1,0:T(8,128)S(1)} %stack.2.near, f32[3,24,1024]{2,1,0:T(8,128)S(1)} %collective-permute-done.2.even, f32[3,24,1024]{2,1,0:T(8,128)S(1)} %collective-permute-done.3.odd), custom_call_target="tpu_custom_call" | custom-call | bytes 8388608 | tf_op jit(solution)/shard_map/tiles/pallas_call | solution.py:106
  75.9 0.0 collective-permute-done.6.refs_3_
  75.9 0.0 collective-permute-done.5.refs_2_
  75.9 0.0 collective-permute-done.4.refs_1_
  75.9 0.6 coeffs.2
  76.5 13.2 %all_to_all.47.parts = f32[8,16,1024]{2,1,0:T(8,128)S(1)} all-to-all(f32[8,16,1024]{2,1,0:T(8,128)S(1)} %coeffs.2), channel_id=1, replica_groups=mesh['z'=8,'yl'=2,'c'=2,'yh'=2,'x'=4] {'yh','x'}, dimensions={0} | all-to-all | bytes 1048576 | tf_op jit(solution)/shard_map/all_to_all | solution.py:41
  89.8 1.0 weights.2
  90.8 1.9 collective-permute-start.7
  92.7 0.3 collective-permute-start.8
  93.0 1.4 collective-permute-start.9
  94.4 2.2 %tiles.3 = (bf16[4,128,1024]{2,1,0:T(8,128)(2,1)S(1)}, f32[16,512]{1,0:T(8,128)S(1)}) custom-call(s32[8,8]{1,0:T(8,128)S(1)} %bitcast.12, f32[3,24,1024]{2,1,0:T(8,128)S(1)} %stack.2.near, f32[3,24,1024]{2,1,0:T(8,128)S(1)} %collective-permute-done.2.even, f32[3,24,1024]{2,1,0:T(8,128)S(1)} %collective-permute-done.3.odd), custom_call_target="tpu_custom_call" | custom-call | bytes 8388608 | tf_op jit(solution)/shard_map/tiles/pallas_call | solution.py:106
  96.6 0.0 collective-permute-done.7.first
  96.6 0.0 collective-permute-done.8.second
  96.6 0.0 collective-permute-done.9.third
  96.7 10.7 %all_to_all.48.weights = bf16[32,16,128]{2,1,0:T(8,128)(2,1)S(1)} all-to-all(bf16[32,16,128]{2,1,0:T(8,128)(2,1)S(1)} %get-tuple-element.71), channel_id=1, replica_groups=mesh['z'=8,'yl'=2,'c'=2,'yh'=2,'x'=4] {'yh','x','yl','c'}, dimensions={0} | all-to-all | bytes 262144 | tf_op jit(solution)/shard_map/all_to_all | solution.py:41
  107.4 2.3 %image.1 = (f32[16,1024]{1,0:T(8,128)S(1)}, f32[16,1024]{1,0:T(8,128)S(1)}, bf16[16,1024]{1,0:T(8,128)(2,1)S(1)}, bf16[48,1024]{1,0:T(8,128)(2,1)S(1)}) custom-call(bf16[32,16,128]{2,1,0:T(8,128)(2,1)S(1)} %all_to_all.48.weights, bf16[8,1024,512]{2,1,0:T(8,128)(2,1)S(1)} %get-tuple-element.72.rows, s32[1,1]{1,0:T(1,128)S(6)} %copy.10.counts, ...), custom_call_target="tpu_custom_call" | custom-call | bytes 16777216 | tf_op jit(solution)/shard_map/image/pallas_call | solution.py:106
  109.7 2.8 %collective-permute-start.11 = (bf16[16,1024]{1,0:T(8,128)(2,1)S(1)}, bf16[16,1024]{1,0:T(8,128)(2,1)S(1)}, u32[]{:S(2)}, u32[]{:S(2)}) collective-permute-start(bf16[16,1024]{1,0:T(8,128)(2,1)S(1)} %get-tuple-element.75.own), channel_id=1, source_target_pairs={{8,16},{24,32},{40,48},{56,64},{72,80},{88,96},{104,112},{120,128}... | collective-permute-start | bytes 98312 | tf_op jit(solution)/shard_map/ppermute | solution.py:60
  112.5 0.1 collective-permute-start.10
  112.6 1.4 project.1
  114.0 0.9 collective-permute-done.11.odd
  114.9 0.7 collective-permute-start.13
  115.6 2.0 %collective-permute-start.12 = (bf16[3,16,1024]{2,1,0:T(8,128)(2,1)S(1)}, bf16[3,16,1024]{2,1,0:T(8,128)(2,1)S(1)}, u32[]{:S(2)}, u32[]{:S(2)}) collective-permute-start(bf16[3,16,1024]{2,1,0:T(8,128)(2,1)S(1)} %stack.3.near), channel_id=1, source_target_pairs={{0,1},{1,0},{2,3},{3,2},{4,5},{5,4},{6,7},{7,6},{8,9},{9,8},{10,11... | collective-permute-start | bytes 294920 | tf_op jit(solution)/shard_map/ppermute | solution.py:54
  117.6 2.9 %collective-permute-done.12.even = bf16[3,16,1024]{2,1,0:T(8,128)(2,1)S(1)} collective-permute-done((bf16[3,16,1024]{2,1,0:T(8,128)(2,1)S(1)}, bf16[3,16,1024]{2,1,0:T(8,128)(2,1)S(1)}, u32[]{:S(2)}, u32[]{:S(2)}) %collective-permute-start.12) | collective-permute-done | bytes 98336 | tf_op jit(solution)/shard_map/ppermute | solution.py:54
  120.5 19.8 %all_to_all.49.refs_0_ = f32[32,32,128]{2,1,0:T(8,128)S(1)} all-to-all(f32[32,32,128]{2,1,0:T(8,128)S(1)} %project.1), channel_id=1, replica_groups=mesh['z'=8,'yl'=2,'c'=2,'yh'=2,'x'=4] {'yh','x','yl','c'}, dimensions={0} | all-to-all | bytes 1048576 | tf_op jit(solution)/shard_map/all_to_all | solution.py:41
  140.3 1.4 sparse.1
  141.7 11.3 %all_to_all.50.parts = f32[8,48,128]{2,1,0:T(8,128)S(1)} all-to-all(f32[8,48,128]{2,1,0:T(8,128)S(1)} %sum_share.3), channel_id=1, replica_groups=mesh['z'=8,'yl'=2,'c'=2,'yh'=2,'x'=4] {'z'}, dimensions={0} | all-to-all | bytes 393216 | tf_op jit(solution)/shard_map/all_to_all | solution.py:41
  153.1 2.3 %collective-permute-start.16 = (f32[16,128]{1,0:T(8,128)S(1)}, f32[16,128]{1,0:T(8,128)S(1)}, u32[]{:S(2)}, u32[]{:S(2)}) collective-permute-start(f32[16,128]{1,0:T(8,128)S(1)} %get-tuple-element.81.refs_0_.new_share), channel_id=1, source_target_pairs={{0,24},{8,16},{16,8},{24,0},{1,25},{9,17},{17,9},{25,1},{2,26},{10... | collective-permute-start | bytes 24584 | tf_op jit(solution)/shard_map/ppermute | solution.py:50
  155.4 1.9 collective-permute-start.15
  157.2 0.0 collective-permute-done.16.refs_3_
  157.2 1.3 collective-permute-done.15.refs_2_
  158.5 0.6 coeffs.3
  159.1 14.2 %all_to_all.51.parts = f32[8,16,1152]{2,1,0:T(8,128)S(1)} all-to-all(f32[8,16,1152]{2,1,0:T(8,128)S(1)} %coeffs.3), channel_id=1, replica_groups=mesh['z'=8,'yl'=2,'c'=2,'yh'=2,'x'=4] {'yh','x'}, dimensions={0} | all-to-all | bytes 1179648 | tf_op jit(solution)/shard_map/all_to_all | solution.py:41
  173.4 1.0 weights.3
  174.3 2.5 %collective-permute-start.17 = (f32[16,256]{1,0:T(8,128)S(1)}, f32[16,256]{1,0:T(8,128)S(1)}, u32[]{:S(2)}, u32[]{:S(2)}) collective-permute-start(f32[16,256]{1,0:T(8,128)S(1)} %get-tuple-element.84), channel_id=1, source_target_pairs={{0,8},{8,0},{16,24},{24,16},{1,9},{9,1},{17,25},{25,17},{2,10},{10... | collective-permute-start | bytes 49160 | tf_op jit(solution)/shard_map/ppermute | solution.py:50
  176.8 0.2 collective-permute-start.18
  177.0 1.5 collective-permute-start.19
  178.5 0.0 collective-permute-done.17.first
  178.5 0.9 collective-permute-done.18.second
  179.4 0.9 collective-permute-done.19.third
  180.3 0.2 gather_last.1
  180.6 12.5 %all_to_all.52.weights = bf16[32,32,128]{2,1,0:T(8,128)(2,1)S(1)} all-to-all(bf16[32,32,128]{2,1,0:T(8,128)(2,1)S(1)} %get-tuple-element.89), channel_id=1, replica_groups=mesh['z'=8,'yl'=2,'c'=2,'yh'=2,'x'=4] {'yh','x','yl','c'}, dimensions={0} | all-to-all | bytes 524288 | tf_op jit(solution)/shard_map/all_to_all | solution.py:41
  193.1 2.9 %finish.1 = (f32[16,1024]{1,0:T(8,128)}, f32[16,1024]{1,0:T(8,128)}) custom-call(bf16[32,32,128]{2,1,0:T(8,128)(2,1)S(1)} %all_to_all.52.weights, bf16[8,1024,512]{2,1,0:T(8,128)(2,1)S(1)} %get-tuple-element.72.rows, s32[1,1]{1,0:T(1,128)S(6)} %copy.10.counts, f32[24,1024]{1,0:T(8,128)S(1)} %copy-done.2, f32[16,1024]{1,0:T(8,128)S(1)} %bitcast.10, ...), custom_call_target="tpu_custom_call" | custom-call | bytes 16777216 | tf_op jit(solution)/shard_map/finish/pallas_call | solution.py:106
  (20 shorter events, 0.2 us)
Async XLA Ops:
  0.6 73.0 %copy-start.4 = (s32[1,1,8,8]{3,2,1,0:T(8,128)S(1)}, s32[1,1,8,8]{3,2,1,0:T(8,128)}, u32[]{:S(2)}) copy-start(s32[1,1,8,8]{3,2,1,0:T(8,128)} %param.11) | copy-start | bytes 772
  3.1 28.5 %all-to-all-start = ((f32[256,1,128]{2,1,0:T(1,128)}), f32[256,1,128]{2,1,0:T(1,128)S(1)}, u32[]{:S(2)}, u32[]{:S(2)}) async-start(f32[256,1,128]{2,1,0:T(1,128)} %get-tuple-element.49), calls=%async_computation | async-start | bytes 262144 | tf_op jit(solution)/shard_map/all_to_all | solution.py:41
  18.7 12.8 %collective-permute-start.1 = (f32[24,1024]{1,0:T(8,128)}, f32[24,1024]{1,0:T(8,128)S(1)}, u32[]{:S(2)}, u32[]{:S(2)}) collective-permute-start(f32[24,1024]{1,0:T(8,128)} %get-tuple-element.51.own.halo), channel_id=1, source_target_pairs={{8,16},{24,32},{40,48},{56,64},{72,80},{88,96},{104,112},{120,128}... | collective-permute-start | bytes 294920 | tf_op jit(solution)/shard_map/ppermute | solution.py:60
  22.3 9.3 %collective-permute-start = (f32[24,1024]{1,0:T(8,128)}, f32[24,1024]{1,0:T(8,128)S(1)}, u32[]{:S(2)}, u32[]{:S(2)}) collective-permute-start(f32[24,1024]{1,0:T(8,128)} %get-tuple-element.51.own.halo), channel_id=1, source_target_pairs={{0,8},{8,0},{16,24},{24,16},{32,40},{40,32},{48,56},{56,48},{64,72... | collective-permute-start | bytes 294920 | tf_op jit(solution)/shard_map/ppermute | solution.py:54
  22.4 85.0 %copy-start.2 = (f32[24,1024]{1,0:T(8,128)S(1)}, f32[24,1024]{1,0:T(8,128)}, u32[]{:S(2)}) copy-start(f32[24,1024]{1,0:T(8,128)} %get-tuple-element.51.own.halo) | copy-start | bytes 294916
  22.4 85.0 %copy-start.5 = (f32[1,1,1024]{2,1,0:T(1,128)S(1)}, f32[1,1,1024]{2,1,0:T(1,128)}, u32[]{:S(2)}) copy-start(f32[1,1,1024]{2,1,0:T(1,128)} %param.9) | copy-start | bytes 12292
  31.6 0.9 copy-start
  32.5 8.9 %collective-permute-start.3 = (f32[3,24,1024]{2,1,0:T(8,128)S(1)}, f32[3,24,1024]{2,1,0:T(8,128)S(1)}, u32[]{:S(2)}, u32[]{:S(2)}) collective-permute-start(f32[3,24,1024]{2,1,0:T(8,128)S(1)} %stack.2.near), channel_id=1, source_target_pairs={{1,2},{3,4},{5,6},{2,1},{4,3},{6,5},{9,10},{11,12},{13,14},{10,9},... | collective-permute-start | bytes 884744 | tf_op jit(solution)/shard_map/ppermute | solution.py:60
  33.2 8.9 %collective-permute-start.2 = (f32[3,24,1024]{2,1,0:T(8,128)S(1)}, f32[3,24,1024]{2,1,0:T(8,128)S(1)}, u32[]{:S(2)}, u32[]{:S(2)}) collective-permute-start(f32[3,24,1024]{2,1,0:T(8,128)S(1)} %stack.2.near), channel_id=1, source_target_pairs={{0,1},{1,0},{2,3},{3,2},{4,5},{5,4},{6,7},{7,6},{8,9},{9,8},{10,11... | collective-permute-start | bytes 884744 | tf_op jit(solution)/shard_map/ppermute | solution.py:54
  35.9 0.9 copy-start.1
  69.8 6.0 %collective-permute-start.6 = (f32[16,128]{1,0:T(8,128)S(1)}, f32[16,128]{1,0:T(8,128)S(1)}, u32[]{:S(2)}, u32[]{:S(2)}) collective-permute-start(f32[16,128]{1,0:T(8,128)S(1)} %sum_depth.2.refs_0_.old_share), channel_id=1, source_target_pairs={{0,24},{8,16},{16,8},{24,0},{1,25},{9,17},{17,9},{25,1},{2,26},{10... | collective-permute-start | bytes 24584 | tf_op jit(solution)/shard_map/ppermute | solution.py:50
  72.4 3.5 %collective-permute-start.5 = (f32[16,128]{1,0:T(8,128)S(1)}, f32[16,128]{1,0:T(8,128)S(1)}, u32[]{:S(2)}, u32[]{:S(2)}) collective-permute-start(f32[16,128]{1,0:T(8,128)S(1)} %sum_depth.2.refs_0_.old_share), channel_id=1, source_target_pairs={{0,16},{8,24},{16,0},{24,8},{1,17},{9,25},{17,1},{25,9},{2,18},{10... | collective-permute-start | bytes 24584 | tf_op jit(solution)/shard_map/ppermute | solution.py:50
  73.6 2.3 %collective-permute-start.4 = (f32[16,128]{1,0:T(8,128)S(1)}, f32[16,128]{1,0:T(8,128)S(1)}, u32[]{:S(2)}, u32[]{:S(2)}) collective-permute-start(f32[16,128]{1,0:T(8,128)S(1)} %sum_depth.2.refs_0_.old_share), channel_id=1, source_target_pairs={{0,8},{8,0},{16,24},{24,16},{1,9},{9,1},{17,25},{25,17},{2,10},{10... | collective-permute-start | bytes 24584 | tf_op jit(solution)/shard_map/ppermute | solution.py:50
  90.8 5.8 %collective-permute-start.7 = (f32[16,128]{1,0:T(8,128)S(1)}, f32[16,128]{1,0:T(8,128)S(1)}, u32[]{:S(2)}, u32[]{:S(2)}) collective-permute-start(f32[16,128]{1,0:T(8,128)S(1)} %get-tuple-element.68), channel_id=1, source_target_pairs={{0,8},{8,0},{16,24},{24,16},{1,9},{9,1},{17,25},{25,17},{2,10},{10... | collective-permute-start | bytes 24584 | tf_op jit(solution)/shard_map/ppermute | solution.py:50
  92.7 3.9 %collective-permute-start.8 = (f32[16,128]{1,0:T(8,128)S(1)}, f32[16,128]{1,0:T(8,128)S(1)}, u32[]{:S(2)}, u32[]{:S(2)}) collective-permute-start(f32[16,128]{1,0:T(8,128)S(1)} %get-tuple-element.69), channel_id=1, source_target_pairs={{0,16},{8,24},{16,0},{24,8},{1,17},{9,25},{17,1},{25,9},{2,18},{10... | collective-permute-start | bytes 24584 | tf_op jit(solution)/shard_map/ppermute | solution.py:50
  93.0 3.7 %collective-permute-start.9 = (f32[16,128]{1,0:T(8,128)S(1)}, f32[16,128]{1,0:T(8,128)S(1)}, u32[]{:S(2)}, u32[]{:S(2)}) collective-permute-start(f32[16,128]{1,0:T(8,128)S(1)} %get-tuple-element.70), channel_id=1, source_target_pairs={{0,24},{8,16},{16,8},{24,0},{1,25},{9,17},{17,9},{25,1},{2,26},{10... | collective-permute-start | bytes 24584 | tf_op jit(solution)/shard_map/ppermute | solution.py:50
  109.7 5.2 %collective-permute-start.11 = (bf16[16,1024]{1,0:T(8,128)(2,1)S(1)}, bf16[16,1024]{1,0:T(8,128)(2,1)S(1)}, u32[]{:S(2)}, u32[]{:S(2)}) collective-permute-start(bf16[16,1024]{1,0:T(8,128)(2,1)S(1)} %get-tuple-element.75.own), channel_id=1, source_target_pairs={{8,16},{24,32},{40,48},{56,64},{72,80},{88,96},{104,112},{120,128}... | collective-permute-start | bytes 98312 | tf_op jit(solution)/shard_map/ppermute | solution.py:60
  112.5 2.4 %collective-permute-start.10 = (bf16[16,1024]{1,0:T(8,128)(2,1)S(1)}, bf16[16,1024]{1,0:T(8,128)(2,1)S(1)}, u32[]{:S(2)}, u32[]{:S(2)}) collective-permute-start(bf16[16,1024]{1,0:T(8,128)(2,1)S(1)} %get-tuple-element.75.own), channel_id=1, source_target_pairs={{0,8},{8,0},{16,24},{24,16},{32,40},{40,32},{48,56},{56,48},{64,72... | collective-permute-start | bytes 98312 | tf_op jit(solution)/shard_map/ppermute | solution.py:54
  114.0 79.1 %copy-start.3 = (f32[1,1,16,1024]{3,2,1,0:T(8,128)S(1)}, f32[1,1,16,1024]{3,2,1,0:T(8,128)}, u32[]{:S(2)}) copy-start(f32[1,1,16,1024]{3,2,1,0:T(8,128)} %param.8) | copy-start | bytes 196612
  114.9 2.6 %collective-permute-start.13 = (bf16[3,16,1024]{2,1,0:T(8,128)(2,1)S(1)}, bf16[3,16,1024]{2,1,0:T(8,128)(2,1)S(1)}, u32[]{:S(2)}, u32[]{:S(2)}) collective-permute-start(bf16[3,16,1024]{2,1,0:T(8,128)(2,1)S(1)} %stack.3.near), channel_id=1, source_target_pairs={{1,2},{3,4},{5,6},{2,1},{4,3},{6,5},{9,10},{11,12},{13,14},{10,9},... | collective-permute-start | bytes 294920 | tf_op jit(solution)/shard_map/ppermute | solution.py:60
  115.6 4.9 %collective-permute-start.12 = (bf16[3,16,1024]{2,1,0:T(8,128)(2,1)S(1)}, bf16[3,16,1024]{2,1,0:T(8,128)(2,1)S(1)}, u32[]{:S(2)}, u32[]{:S(2)}) collective-permute-start(bf16[3,16,1024]{2,1,0:T(8,128)(2,1)S(1)} %stack.3.near), channel_id=1, source_target_pairs={{0,1},{1,0},{2,3},{3,2},{4,5},{5,4},{6,7},{7,6},{8,9},{9,8},{10,11... | collective-permute-start | bytes 294920 | tf_op jit(solution)/shard_map/ppermute | solution.py:54
  153.1 4.1 %collective-permute-start.16 = (f32[16,128]{1,0:T(8,128)S(1)}, f32[16,128]{1,0:T(8,128)S(1)}, u32[]{:S(2)}, u32[]{:S(2)}) collective-permute-start(f32[16,128]{1,0:T(8,128)S(1)} %get-tuple-element.81.refs_0_.new_share), channel_id=1, source_target_pairs={{0,24},{8,16},{16,8},{24,0},{1,25},{9,17},{17,9},{25,1},{2,26},{10... | collective-permute-start | bytes 24584 | tf_op jit(solution)/shard_map/ppermute | solution.py:50
  155.4 3.2 %collective-permute-start.15 = (f32[16,128]{1,0:T(8,128)S(1)}, f32[16,128]{1,0:T(8,128)S(1)}, u32[]{:S(2)}, u32[]{:S(2)}) collective-permute-start(f32[16,128]{1,0:T(8,128)S(1)} %get-tuple-element.81.refs_0_.new_share), channel_id=1, source_target_pairs={{0,16},{8,24},{16,0},{24,8},{1,17},{9,25},{17,1},{25,9},{2,18},{10... | collective-permute-start | bytes 24584 | tf_op jit(solution)/shard_map/ppermute | solution.py:50
  157.2 1.3 collective-permute-start.14
  174.3 4.2 %collective-permute-start.17 = (f32[16,256]{1,0:T(8,128)S(1)}, f32[16,256]{1,0:T(8,128)S(1)}, u32[]{:S(2)}, u32[]{:S(2)}) collective-permute-start(f32[16,256]{1,0:T(8,128)S(1)} %get-tuple-element.84), channel_id=1, source_target_pairs={{0,8},{8,0},{16,24},{24,16},{1,9},{9,1},{17,25},{25,17},{2,10},{10... | collective-permute-start | bytes 49160 | tf_op jit(solution)/shard_map/ppermute | solution.py:50
  176.8 2.6 %collective-permute-start.18 = (f32[16,256]{1,0:T(8,128)S(1)}, f32[16,256]{1,0:T(8,128)S(1)}, u32[]{:S(2)}, u32[]{:S(2)}) collective-permute-start(f32[16,256]{1,0:T(8,128)S(1)} %get-tuple-element.85), channel_id=1, source_target_pairs={{0,16},{8,24},{16,0},{24,8},{1,17},{9,25},{17,1},{25,9},{2,18},{10... | collective-permute-start | bytes 49160 | tf_op jit(solution)/shard_map/ppermute | solution.py:50
  177.0 3.3 %collective-permute-start.19 = (f32[16,256]{1,0:T(8,128)S(1)}, f32[16,256]{1,0:T(8,128)S(1)}, u32[]{:S(2)}, u32[]{:S(2)}) collective-permute-start(f32[16,256]{1,0:T(8,128)S(1)} %get-tuple-element.86), channel_id=1, source_target_pairs={{0,24},{8,16},{16,8},{24,0},{1,25},{9,17},{17,9},{25,1},{2,26},{10... | collective-permute-start | bytes 49160 | tf_op jit(solution)/shard_map/ppermute | solution.py:50

commit v8 on v7

--- a/solution.py
+++ b/solution.py
@@ -198,7 +198,7 @@
             sums_out[4 * step + part] = sums[:, part * SHARE : (part + 1) * SHARE]
         return carry
 
-    lax.fori_loop(0, CHUNKS, chunk, 0, unroll=2)
+    lax.fori_loop(0, CHUNKS, chunk, 0, unroll=4)
 
 
 def make_rows(halo, centres):

time: 197 us -> 197 us (level)
  transfers between devices with their start and end apart: 21 -> 21, of which waited for: 7 -> 7; matrix products, arithmetic and copies ran while one was open for 1% -> 1% of each run, Pallas kernels for 6% -> 5%
where the time goes in v8:
time: 197 us; the launch traced here: 196 us
  blocking collectives  109 us (55%)
  starting transfers between devices  43.4 us (22%)
  Pallas kernels  22.3 us (11%)
  waiting for transfers between devices  15.7 us (8%)
  local copies, waits for them, and re-layouts  3.56 us (2%)
    all_to_all x8, blocking collectives, exchange(): return lax.all_to_all(parts, axes, 0, 0, tiled=True)  109 us
    pallas_call x21, Pallas kernels, call(): pl.pallas_call(kernel, out_shape=out_shape, in_specs=in_specs, out_specs=...  22.3 us
    ppermute x12, starting transfers between devices, quad_partner(): return lax.ppermute(value, ('yl', 'c'), pairs)  15.8 us
    all_to_all x1, starting transfers between devices, exchange(): return lax.all_to_all(parts, axes, 0, 0, tiled=True)  15.7 us
    ppermute x4, starting transfers between devices, odd_pairs(): return lax.ppermute(value, axes, pairs + [(j, i) for i, j in pairs])  7.68 us
    all_to_all x1, waiting for transfers between devices, exchange(): return lax.all_to_all(parts, axes, 0, 0, tiled=True)  7.39 us
    ppermute x4, starting transfers between devices, even_pairs(): lax.ppermute(value, axes, [(i, i ^ 1) for i in range(lax.axis_size(axes))])  4.27 us
    ppermute x4, waiting for transfers between devices, even_pairs(): lax.ppermute(value, axes, [(i, i ^ 1) for i in range(lax.axis_size(axes))])  4.17 us
  transfers between devices with their start and end apart: 21, of which 7 were waited for; matrix products, arithmetic and copies ran while one was open for 1% of the time, Pallas kernels for 5%

profile of v8, /device:TPU:1, one launch (start us, length us, event | category | flops | bytes accessed | tf_op | source)
XLA Modules:
  0.0 196.0 jit_solution(8325888248557674322)
XLA Ops:
  1.3 1.8 prepare.1
  3.1 15.7 %all-to-all-start = ((f32[256,1,128]{2,1,0:T(1,128)}), f32[256,1,128]{2,1,0:T(1,128)S(1)}, u32[]{:S(2)}, u32[]{:S(2)}) async-start(f32[256,1,128]{2,1,0:T(1,128)} %get-tuple-element.49), calls=%async_computation | async-start | bytes 262144 | tf_op jit(solution)/shard_map/all_to_all | solution.py:41
  18.7 3.5 %collective-permute-start.1 = (f32[24,1024]{1,0:T(8,128)}, f32[24,1024]{1,0:T(8,128)S(1)}, u32[]{:S(2)}, u32[]{:S(2)}) collective-permute-start(f32[24,1024]{1,0:T(8,128)} %get-tuple-element.51.own.halo), channel_id=1, source_target_pairs={{8,16},{24,32},{40,48},{56,64},{72,80},{88,96},{104,112},{120,128}... | collective-permute-start | bytes 294920 | tf_op jit(solution)/shard_map/ppermute | solution.py:60
  22.3 0.1 collective-permute-start
  22.4 0.0 copy-start.5
  22.4 1.8 constant_dynamic-slice_fusion.columns
  24.2 7.4 %all-to-all-done = f32[256,1,128]{2,1,0:T(1,128)S(1)} async-done(((f32[256,1,128]{2,1,0:T(1,128)}), f32[256,1,128]{2,1,0:T(1,128)S(1)}, u32[]{:S(2)}, u32[]{:S(2)}) %all-to-all-start) | async-done | bytes 131104 | tf_op jit(solution)/shard_map/all_to_all | solution.py:41
  31.6 0.0 collective-permute-done.1.odd
  31.6 0.0 collective-permute-done.even
  31.6 0.9 copy-done
  32.5 0.7 collective-permute-start.3
  33.2 2.1 %collective-permute-start.2 = (f32[3,24,1024]{2,1,0:T(8,128)S(1)}, f32[3,24,1024]{2,1,0:T(8,128)S(1)}, u32[]{:S(2)}, u32[]{:S(2)}) collective-permute-start(f32[3,24,1024]{2,1,0:T(8,128)S(1)} %stack.2.near), channel_id=1, source_target_pairs={{0,1},{1,0},{2,3},{3,2},{4,5},{5,4},{6,7},{7,6},{8,9},{9,8},{10,11... | collective-permute-start | bytes 884744 | tf_op jit(solution)/shard_map/ppermute | solution.py:54
  35.3 0.6 factor.1
  35.9 0.9 copy-done.1
  36.8 4.0 %rows.1 = (bf16[8,1024,512]{2,1,0:T(8,128)(2,1)S(1)}, f32[32,16,128]{2,1,0:T(8,128)S(1)}) custom-call(f32[24,1024]{1,0:T(8,128)S(1)} %copy-done.1, f32[256,128]{1,0:T(8,128)S(1)} %bitcast.8), custom_call_target="tpu_custom_call" | custom-call | bytes 16777216 | tf_op jit(solution)/shard_map/rows/pallas_call | solution.py:106
  40.8 1.2 collective-permute-done.2.even
  42.1 16.9 %all_to_all.45.refs_0_ = f32[32,16,128]{2,1,0:T(8,128)S(1)} all-to-all(f32[32,16,128]{2,1,0:T(8,128)S(1)} %get-tuple-element.58), channel_id=1, replica_groups=mesh['z'=8,'yl'=2,'c'=2,'yh'=2,'x'=4] {'yh','x','yl','c'}, dimensions={0} | all-to-all | bytes 524288 | tf_op jit(solution)/shard_map/all_to_all | solution.py:41
  59.0 10.8 %all_to_all.46.parts = f32[8,16,128]{2,1,0:T(8,128)S(1)} all-to-all(f32[8,16,128]{2,1,0:T(8,128)S(1)} %sum_share.2), channel_id=1, replica_groups=mesh['z'=8,'yl'=2,'c'=2,'yh'=2,'x'=4] {'z'}, dimensions={0} | all-to-all | bytes 131072 | tf_op jit(solution)/shard_map/all_to_all | solution.py:41
  69.8 2.6 %collective-permute-start.6 = (f32[16,128]{1,0:T(8,128)S(1)}, f32[16,128]{1,0:T(8,128)S(1)}, u32[]{:S(2)}, u32[]{:S(2)}) collective-permute-start(f32[16,128]{1,0:T(8,128)S(1)} %sum_depth.2.refs_0_.old_share), channel_id=1, source_target_pairs={{0,24},{8,16},{16,8},{24,0},{1,25},{9,17},{17,9},{25,1},{2,26},{10... | collective-permute-start | bytes 24584 | tf_op jit(solution)/shard_map/ppermute | solution.py:50
  72.4 1.3 collective-permute-start.5
  73.6 2.2 %tiles.2 = (bf16[4,128,1024]{2,1,0:T(8,128)(2,1)S(1)}, f32[16,512]{1,0:T(8,128)S(1)}) custom-call(s32[8,8]{1,0:T(8,128)S(1)} %bitcast.11, f32[3,24,1024]{2,1,0:T(8,128)S(1)} %stack.2.near, f32[3,24,1024]{2,1,0:T(8,128)S(1)} %collective-permute-done.2.even, f32[3,24,1024]{2,1,0:T(8,128)S(1)} %collective-permute-done.3.odd), custom_call_target="tpu_custom_call" | custom-call | bytes 8388608 | tf_op jit(solution)/shard_map/tiles/pallas_call | solution.py:106
  75.9 0.0 collective-permute-done.6.refs_3_
  75.9 0.0 collective-permute-done.5.refs_2_
  75.9 0.0 collective-permute-done.4.refs_1_
  75.9 0.6 coeffs.2
  76.5 13.2 %all_to_all.47.parts = f32[8,16,1024]{2,1,0:T(8,128)S(1)} all-to-all(f32[8,16,1024]{2,1,0:T(8,128)S(1)} %coeffs.2), channel_id=1, replica_groups=mesh['z'=8,'yl'=2,'c'=2,'yh'=2,'x'=4] {'yh','x'}, dimensions={0} | all-to-all | bytes 1048576 | tf_op jit(solution)/shard_map/all_to_all | solution.py:41
  89.8 1.0 weights.2
  90.8 1.9 collective-permute-start.7
  92.7 0.3 collective-permute-start.8
  93.0 1.4 collective-permute-start.9
  94.4 2.2 %tiles.3 = (bf16[4,128,1024]{2,1,0:T(8,128)(2,1)S(1)}, f32[16,512]{1,0:T(8,128)S(1)}) custom-call(s32[8,8]{1,0:T(8,128)S(1)} %bitcast.12, f32[3,24,1024]{2,1,0:T(8,128)S(1)} %stack.2.near, f32[3,24,1024]{2,1,0:T(8,128)S(1)} %collective-permute-done.2.even, f32[3,24,1024]{2,1,0:T(8,128)S(1)} %collective-permute-done.3.odd), custom_call_target="tpu_custom_call" | custom-call | bytes 8388608 | tf_op jit(solution)/shard_map/tiles/pallas_call | solution.py:106
  96.6 0.0 collective-permute-done.7.first
  96.6 0.0 collective-permute-done.8.second
  96.6 0.0 collective-permute-done.9.third
  96.7 10.7 %all_to_all.48.weights = bf16[32,16,128]{2,1,0:T(8,128)(2,1)S(1)} all-to-all(bf16[32,16,128]{2,1,0:T(8,128)(2,1)S(1)} %get-tuple-element.71), channel_id=1, replica_groups=mesh['z'=8,'yl'=2,'c'=2,'yh'=2,'x'=4] {'yh','x','yl','c'}, dimensions={0} | all-to-all | bytes 262144 | tf_op jit(solution)/shard_map/all_to_all | solution.py:41
  107.4 2.3 %image.1 = (f32[16,1024]{1,0:T(8,128)S(1)}, f32[16,1024]{1,0:T(8,128)S(1)}, bf16[16,1024]{1,0:T(8,128)(2,1)S(1)}, bf16[48,1024]{1,0:T(8,128)(2,1)S(1)}) custom-call(bf16[32,16,128]{2,1,0:T(8,128)(2,1)S(1)} %all_to_all.48.weights, bf16[8,1024,512]{2,1,0:T(8,128)(2,1)S(1)} %get-tuple-element.72.rows, s32[1,1]{1,0:T(1,128)S(6)} %copy.10.counts, ...), custom_call_target="tpu_custom_call" | custom-call | bytes 16777216 | tf_op jit(solution)/shard_map/image/pallas_call | solution.py:106
  109.7 2.8 %collective-permute-start.11 = (bf16[16,1024]{1,0:T(8,128)(2,1)S(1)}, bf16[16,1024]{1,0:T(8,128)(2,1)S(1)}, u32[]{:S(2)}, u32[]{:S(2)}) collective-permute-start(bf16[16,1024]{1,0:T(8,128)(2,1)S(1)} %get-tuple-element.75.own), channel_id=1, source_target_pairs={{8,16},{24,32},{40,48},{56,64},{72,80},{88,96},{104,112},{120,128}... | collective-permute-start | bytes 98312 | tf_op jit(solution)/shard_map/ppermute | solution.py:60
  112.5 0.1 collective-permute-start.10
  112.6 1.4 project.1
  114.0 0.9 collective-permute-done.11.odd
  114.9 0.0 collective-permute-done.10.even
  114.9 0.7 collective-permute-start.13
  115.6 2.0 %collective-permute-start.12 = (bf16[3,16,1024]{2,1,0:T(8,128)(2,1)S(1)}, bf16[3,16,1024]{2,1,0:T(8,128)(2,1)S(1)}, u32[]{:S(2)}, u32[]{:S(2)}) collective-permute-start(bf16[3,16,1024]{2,1,0:T(8,128)(2,1)S(1)} %stack.3.near), channel_id=1, source_target_pairs={{0,1},{1,0},{2,3},{3,2},{4,5},{5,4},{6,7},{7,6},{8,9},{9,8},{10,11... | collective-permute-start | bytes 294920 | tf_op jit(solution)/shard_map/ppermute | solution.py:54
  117.6 0.0 collective-permute-done.13.odd
  117.6 2.9 %collective-permute-done.12.even = bf16[3,16,1024]{2,1,0:T(8,128)(2,1)S(1)} collective-permute-done((bf16[3,16,1024]{2,1,0:T(8,128)(2,1)S(1)}, bf16[3,16,1024]{2,1,0:T(8,128)(2,1)S(1)}, u32[]{:S(2)}, u32[]{:S(2)}) %collective-permute-start.12) | collective-permute-done | bytes 98336 | tf_op jit(solution)/shard_map/ppermute | solution.py:54
  120.5 19.8 %all_to_all.49.refs_0_ = f32[32,32,128]{2,1,0:T(8,128)S(1)} all-to-all(f32[32,32,128]{2,1,0:T(8,128)S(1)} %project.1), channel_id=1, replica_groups=mesh['z'=8,'yl'=2,'c'=2,'yh'=2,'x'=4] {'yh','x','yl','c'}, dimensions={0} | all-to-all | bytes 1048576 | tf_op jit(solution)/shard_map/all_to_all | solution.py:41
  140.3 1.4 sparse.1
  141.7 11.3 %all_to_all.50.parts = f32[8,48,128]{2,1,0:T(8,128)S(1)} all-to-all(f32[8,48,128]{2,1,0:T(8,128)S(1)} %sum_share.3), channel_id=1, replica_groups=mesh['z'=8,'yl'=2,'c'=2,'yh'=2,'x'=4] {'z'}, dimensions={0} | all-to-all | bytes 393216 | tf_op jit(solution)/shard_map/all_to_all | solution.py:41
  153.0 2.3 %collective-permute-start.16 = (f32[16,128]{1,0:T(8,128)S(1)}, f32[16,128]{1,0:T(8,128)S(1)}, u32[]{:S(2)}, u32[]{:S(2)}) collective-permute-start(f32[16,128]{1,0:T(8,128)S(1)} %get-tuple-element.81.refs_0_.new_share), channel_id=1, source_target_pairs={{0,24},{8,16},{16,8},{24,0},{1,25},{9,17},{17,9},{25,1},{2,26},{10... | collective-permute-start | bytes 24584 | tf_op jit(solution)/shard_map/ppermute | solution.py:50
  155.3 1.9 collective-permute-start.15
  157.2 0.0 collective-permute-start.14
  157.2 0.0 collective-permute-done.16.refs_3_
  157.2 1.3 collective-permute-done.15.refs_2_
  158.5 0.6 coeffs.3
  159.1 14.2 %all_to_all.51.parts = f32[8,16,1152]{2,1,0:T(8,128)S(1)} all-to-all(f32[8,16,1152]{2,1,0:T(8,128)S(1)} %coeffs.3), channel_id=1, replica_groups=mesh['z'=8,'yl'=2,'c'=2,'yh'=2,'x'=4] {'yh','x'}, dimensions={0} | all-to-all | bytes 1179648 | tf_op jit(solution)/shard_map/all_to_all | solution.py:41
  173.3 1.0 weights.3
  174.3 2.5 %collective-permute-start.17 = (f32[16,256]{1,0:T(8,128)S(1)}, f32[16,256]{1,0:T(8,128)S(1)}, u32[]{:S(2)}, u32[]{:S(2)}) collective-permute-start(f32[16,256]{1,0:T(8,128)S(1)} %get-tuple-element.84), channel_id=1, source_target_pairs={{0,8},{8,0},{16,24},{24,16},{1,9},{9,1},{17,25},{25,17},{2,10},{10... | collective-permute-start | bytes 49160 | tf_op jit(solution)/shard_map/ppermute | solution.py:50
  176.8 0.2 collective-permute-start.18
  177.0 1.5 collective-permute-start.19
  178.5 0.9 collective-permute-done.18.second
  179.4 0.9 collective-permute-done.19.third
  180.3 0.2 gather_last.1
  180.6 12.5 %all_to_all.52.weights = bf16[32,32,128]{2,1,0:T(8,128)(2,1)S(1)} all-to-all(bf16[32,32,128]{2,1,0:T(8,128)(2,1)S(1)} %get-tuple-element.89), channel_id=1, replica_groups=mesh['z'=8,'yl'=2,'c'=2,'yh'=2,'x'=4] {'yh','x','yl','c'}, dimensions={0} | all-to-all | bytes 524288 | tf_op jit(solution)/shard_map/all_to_all | solution.py:41
  193.1 2.9 %finish.1 = (f32[16,1024]{1,0:T(8,128)}, f32[16,1024]{1,0:T(8,128)}) custom-call(bf16[32,32,128]{2,1,0:T(8,128)(2,1)S(1)} %all_to_all.52.weights, bf16[8,1024,512]{2,1,0:T(8,128)(2,1)S(1)} %get-tuple-element.72.rows, s32[1,1]{1,0:T(1,128)S(6)} %copy.10.counts, f32[24,1024]{1,0:T(8,128)S(1)} %copy-done.2, f32[16,1024]{1,0:T(8,128)S(1)} %bitcast.10, ...), custom_call_target="tpu_custom_call" | custom-call | bytes 16777216 | tf_op jit(solution)/shard_map/finish/pallas_call | solution.py:106
  (20 shorter events, 0.2 us)
Async XLA Ops:
  0.6 73.0 %copy-start.4 = (s32[1,1,8,8]{3,2,1,0:T(8,128)S(1)}, s32[1,1,8,8]{3,2,1,0:T(8,128)}, u32[]{:S(2)}) copy-start(s32[1,1,8,8]{3,2,1,0:T(8,128)} %param.11) | copy-start | bytes 772
  3.1 28.5 %all-to-all-start = ((f32[256,1,128]{2,1,0:T(1,128)}), f32[256,1,128]{2,1,0:T(1,128)S(1)}, u32[]{:S(2)}, u32[]{:S(2)}) async-start(f32[256,1,128]{2,1,0:T(1,128)} %get-tuple-element.49), calls=%async_computation | async-start | bytes 262144 | tf_op jit(solution)/shard_map/all_to_all | solution.py:41
  18.7 12.8 %collective-permute-start.1 = (f32[24,1024]{1,0:T(8,128)}, f32[24,1024]{1,0:T(8,128)S(1)}, u32[]{:S(2)}, u32[]{:S(2)}) collective-permute-start(f32[24,1024]{1,0:T(8,128)} %get-tuple-element.51.own.halo), channel_id=1, source_target_pairs={{8,16},{24,32},{40,48},{56,64},{72,80},{88,96},{104,112},{120,128}... | collective-permute-start | bytes 294920 | tf_op jit(solution)/shard_map/ppermute | solution.py:60
  22.3 9.3 %collective-permute-start = (f32[24,1024]{1,0:T(8,128)}, f32[24,1024]{1,0:T(8,128)S(1)}, u32[]{:S(2)}, u32[]{:S(2)}) collective-permute-start(f32[24,1024]{1,0:T(8,128)} %get-tuple-element.51.own.halo), channel_id=1, source_target_pairs={{0,8},{8,0},{16,24},{24,16},{32,40},{40,32},{48,56},{56,48},{64,72... | collective-permute-start | bytes 294920 | tf_op jit(solution)/shard_map/ppermute | solution.py:54
  22.4 85.0 %copy-start.2 = (f32[24,1024]{1,0:T(8,128)S(1)}, f32[24,1024]{1,0:T(8,128)}, u32[]{:S(2)}) copy-start(f32[24,1024]{1,0:T(8,128)} %get-tuple-element.51.own.halo) | copy-start | bytes 294916
  22.4 85.0 %copy-start.5 = (f32[1,1,1024]{2,1,0:T(1,128)S(1)}, f32[1,1,1024]{2,1,0:T(1,128)}, u32[]{:S(2)}) copy-start(f32[1,1,1024]{2,1,0:T(1,128)} %param.9) | copy-start | bytes 12292
  31.6 0.9 copy-start
  32.5 8.3 %collective-permute-start.3 = (f32[3,24,1024]{2,1,0:T(8,128)S(1)}, f32[3,24,1024]{2,1,0:T(8,128)S(1)}, u32[]{:S(2)}, u32[]{:S(2)}) collective-permute-start(f32[3,24,1024]{2,1,0:T(8,128)S(1)} %stack.2.near), channel_id=1, source_target_pairs={{1,2},{3,4},{5,6},{2,1},{4,3},{6,5},{9,10},{11,12},{13,14},{10,9},... | collective-permute-start | bytes 884744 | tf_op jit(solution)/shard_map/ppermute | solution.py:60
  33.2 8.9 %collective-permute-start.2 = (f32[3,24,1024]{2,1,0:T(8,128)S(1)}, f32[3,24,1024]{2,1,0:T(8,128)S(1)}, u32[]{:S(2)}, u32[]{:S(2)}) collective-permute-start(f32[3,24,1024]{2,1,0:T(8,128)S(1)} %stack.2.near), channel_id=1, source_target_pairs={{0,1},{1,0},{2,3},{3,2},{4,5},{5,4},{6,7},{7,6},{8,9},{9,8},{10,11... | collective-permute-start | bytes 884744 | tf_op jit(solution)/shard_map/ppermute | solution.py:54
  35.9 0.9 copy-start.1
  69.8 6.0 %collective-permute-start.6 = (f32[16,128]{1,0:T(8,128)S(1)}, f32[16,128]{1,0:T(8,128)S(1)}, u32[]{:S(2)}, u32[]{:S(2)}) collective-permute-start(f32[16,128]{1,0:T(8,128)S(1)} %sum_depth.2.refs_0_.old_share), channel_id=1, source_target_pairs={{0,24},{8,16},{16,8},{24,0},{1,25},{9,17},{17,9},{25,1},{2,26},{10... | collective-permute-start | bytes 24584 | tf_op jit(solution)/shard_map/ppermute | solution.py:50
  72.4 3.5 %collective-permute-start.5 = (f32[16,128]{1,0:T(8,128)S(1)}, f32[16,128]{1,0:T(8,128)S(1)}, u32[]{:S(2)}, u32[]{:S(2)}) collective-permute-start(f32[16,128]{1,0:T(8,128)S(1)} %sum_depth.2.refs_0_.old_share), channel_id=1, source_target_pairs={{0,16},{8,24},{16,0},{24,8},{1,17},{9,25},{17,1},{25,9},{2,18},{10... | collective-permute-start | bytes 24584 | tf_op jit(solution)/shard_map/ppermute | solution.py:50
  73.6 2.3 %collective-permute-start.4 = (f32[16,128]{1,0:T(8,128)S(1)}, f32[16,128]{1,0:T(8,128)S(1)}, u32[]{:S(2)}, u32[]{:S(2)}) collective-permute-start(f32[16,128]{1,0:T(8,128)S(1)} %sum_depth.2.refs_0_.old_share), channel_id=1, source_target_pairs={{0,8},{8,0},{16,24},{24,16},{1,9},{9,1},{17,25},{25,17},{2,10},{10... | collective-permute-start | bytes 24584 | tf_op jit(solution)/shard_map/ppermute | solution.py:50
  90.8 5.8 %collective-permute-start.7 = (f32[16,128]{1,0:T(8,128)S(1)}, f32[16,128]{1,0:T(8,128)S(1)}, u32[]{:S(2)}, u32[]{:S(2)}) collective-permute-start(f32[16,128]{1,0:T(8,128)S(1)} %get-tuple-element.68), channel_id=1, source_target_pairs={{0,8},{8,0},{16,24},{24,16},{1,9},{9,1},{17,25},{25,17},{2,10},{10... | collective-permute-start | bytes 24584 | tf_op jit(solution)/shard_map/ppermute | solution.py:50
  92.7 3.9 %collective-permute-start.8 = (f32[16,128]{1,0:T(8,128)S(1)}, f32[16,128]{1,0:T(8,128)S(1)}, u32[]{:S(2)}, u32[]{:S(2)}) collective-permute-start(f32[16,128]{1,0:T(8,128)S(1)} %get-tuple-element.69), channel_id=1, source_target_pairs={{0,16},{8,24},{16,0},{24,8},{1,17},{9,25},{17,1},{25,9},{2,18},{10... | collective-permute-start | bytes 24584 | tf_op jit(solution)/shard_map/ppermute | solution.py:50
  93.0 3.7 %collective-permute-start.9 = (f32[16,128]{1,0:T(8,128)S(1)}, f32[16,128]{1,0:T(8,128)S(1)}, u32[]{:S(2)}, u32[]{:S(2)}) collective-permute-start(f32[16,128]{1,0:T(8,128)S(1)} %get-tuple-element.70), channel_id=1, source_target_pairs={{0,24},{8,16},{16,8},{24,0},{1,25},{9,17},{17,9},{25,1},{2,26},{10... | collective-permute-start | bytes 24584 | tf_op jit(solution)/shard_map/ppermute | solution.py:50
  109.7 5.2 %collective-permute-start.11 = (bf16[16,1024]{1,0:T(8,128)(2,1)S(1)}, bf16[16,1024]{1,0:T(8,128)(2,1)S(1)}, u32[]{:S(2)}, u32[]{:S(2)}) collective-permute-start(bf16[16,1024]{1,0:T(8,128)(2,1)S(1)} %get-tuple-element.75.own), channel_id=1, source_target_pairs={{8,16},{24,32},{40,48},{56,64},{72,80},{88,96},{104,112},{120,128}... | collective-permute-start | bytes 98312 | tf_op jit(solution)/shard_map/ppermute | solution.py:60
  112.5 2.4 %collective-permute-start.10 = (bf16[16,1024]{1,0:T(8,128)(2,1)S(1)}, bf16[16,1024]{1,0:T(8,128)(2,1)S(1)}, u32[]{:S(2)}, u32[]{:S(2)}) collective-permute-start(bf16[16,1024]{1,0:T(8,128)(2,1)S(1)} %get-tuple-element.75.own), channel_id=1, source_target_pairs={{0,8},{8,0},{16,24},{24,16},{32,40},{40,32},{48,56},{56,48},{64,72... | collective-permute-start | bytes 98312 | tf_op jit(solution)/shard_map/ppermute | solution.py:54
  114.0 79.1 %copy-start.3 = (f32[1,1,16,1024]{3,2,1,0:T(8,128)S(1)}, f32[1,1,16,1024]{3,2,1,0:T(8,128)}, u32[]{:S(2)}) copy-start(f32[1,1,16,1024]{3,2,1,0:T(8,128)} %param.8) | copy-start | bytes 196612
  114.9 2.6 %collective-permute-start.13 = (bf16[3,16,1024]{2,1,0:T(8,128)(2,1)S(1)}, bf16[3,16,1024]{2,1,0:T(8,128)(2,1)S(1)}, u32[]{:S(2)}, u32[]{:S(2)}) collective-permute-start(bf16[3,16,1024]{2,1,0:T(8,128)(2,1)S(1)} %stack.3.near), channel_id=1, source_target_pairs={{1,2},{3,4},{5,6},{2,1},{4,3},{6,5},{9,10},{11,12},{13,14},{10,9},... | collective-permute-start | bytes 294920 | tf_op jit(solution)/shard_map/ppermute | solution.py:60
  115.6 4.9 %collective-permute-start.12 = (bf16[3,16,1024]{2,1,0:T(8,128)(2,1)S(1)}, bf16[3,16,1024]{2,1,0:T(8,128)(2,1)S(1)}, u32[]{:S(2)}, u32[]{:S(2)}) collective-permute-start(bf16[3,16,1024]{2,1,0:T(8,128)(2,1)S(1)} %stack.3.near), channel_id=1, source_target_pairs={{0,1},{1,0},{2,3},{3,2},{4,5},{5,4},{6,7},{7,6},{8,9},{9,8},{10,11... | collective-permute-start | bytes 294920 | tf_op jit(solution)/shard_map/ppermute | solution.py:54
  153.0 4.2 %collective-permute-start.16 = (f32[16,128]{1,0:T(8,128)S(1)}, f32[16,128]{1,0:T(8,128)S(1)}, u32[]{:S(2)}, u32[]{:S(2)}) collective-permute-start(f32[16,128]{1,0:T(8,128)S(1)} %get-tuple-element.81.refs_0_.new_share), channel_id=1, source_target_pairs={{0,24},{8,16},{16,8},{24,0},{1,25},{9,17},{17,9},{25,1},{2,26},{10... | collective-permute-start | bytes 24584 | tf_op jit(solution)/shard_map/ppermute | solution.py:50
  155.3 3.2 %collective-permute-start.15 = (f32[16,128]{1,0:T(8,128)S(1)}, f32[16,128]{1,0:T(8,128)S(1)}, u32[]{:S(2)}, u32[]{:S(2)}) collective-permute-start(f32[16,128]{1,0:T(8,128)S(1)} %get-tuple-element.81.refs_0_.new_share), channel_id=1, source_target_pairs={{0,16},{8,24},{16,0},{24,8},{1,17},{9,25},{17,1},{25,9},{2,18},{10... | collective-permute-start | bytes 24584 | tf_op jit(solution)/shard_map/ppermute | solution.py:50
  157.2 1.3 collective-permute-start.14
  174.3 4.2 %collective-permute-start.17 = (f32[16,256]{1,0:T(8,128)S(1)}, f32[16,256]{1,0:T(8,128)S(1)}, u32[]{:S(2)}, u32[]{:S(2)}) collective-permute-start(f32[16,256]{1,0:T(8,128)S(1)} %get-tuple-element.84), channel_id=1, source_target_pairs={{0,8},{8,0},{16,24},{24,16},{1,9},{9,1},{17,25},{25,17},{2,10},{10... | collective-permute-start | bytes 49160 | tf_op jit(solution)/shard_map/ppermute | solution.py:50
  176.8 2.6 %collective-permute-start.18 = (f32[16,256]{1,0:T(8,128)S(1)}, f32[16,256]{1,0:T(8,128)S(1)}, u32[]{:S(2)}, u32[]{:S(2)}) collective-permute-start(f32[16,256]{1,0:T(8,128)S(1)} %get-tuple-element.85), channel_id=1, source_target_pairs={{0,16},{8,24},{16,0},{24,8},{1,17},{9,25},{17,1},{25,9},{2,18},{10... | collective-permute-start | bytes 49160 | tf_op jit(solution)/shard_map/ppermute | solution.py:50
  177.0 3.3 %collective-permute-start.19 = (f32[16,256]{1,0:T(8,128)S(1)}, f32[16,256]{1,0:T(8,128)S(1)}, u32[]{:S(2)}, u32[]{:S(2)}) collective-permute-start(f32[16,256]{1,0:T(8,128)S(1)} %get-tuple-element.86), channel_id=1, source_target_pairs={{0,24},{8,16},{16,8},{24,0},{1,25},{9,17},{17,9},{25,1},{2,26},{10... | collective-permute-start | bytes 49160 | tf_op jit(solution)/shard_map/ppermute | solution.py:50

commit v9 on v7

--- a/solution.py
+++ b/solution.py
@@ -148,7 +148,7 @@
         (shape(256, 1, 128), shape(FEAT + PROBES, PTS)),
         [VMEM, VMEM, VMEM, SMEM, SMEM],
         (coords, probes, precond, counts, inducing),
-        params=LARGE,
+        params=MIDDLE,
     )
 
 

time: 197 us -> 198 us (level)
  no operation moved by 1% of the time
where the time goes in v9:
time: 198 us
  blocking collectives  109 us (55%)
  starting transfers between devices  43.4 us (22%)
  Pallas kernels  22.6 us (11%)
  waiting for transfers between devices  16 us (8%)
  local copies, waits for them, and re-layouts  4.68 us (2%)
    all_to_all x8, blocking collectives, exchange(): return lax.all_to_all(parts, axes, 0, 0, tiled=True)  109 us
    pallas_call x21, Pallas kernels, call(): pl.pallas_call(kernel, out_shape=out_shape, in_specs=in_specs, out_specs=...  22.6 us
    ppermute x12, starting transfers between devices, quad_partner(): return lax.ppermute(value, ('yl', 'c'), pairs)  15.8 us
    all_to_all x1, starting transfers between devices, exchange(): return lax.all_to_all(parts, axes, 0, 0, tiled=True)  15.7 us
    ppermute x4, starting transfers between devices, odd_pairs(): return lax.ppermute(value, axes, pairs + [(j, i) for i, j in pairs])  7.68 us
    all_to_all x1, waiting for transfers between devices, exchange(): return lax.all_to_all(parts, axes, 0, 0, tiled=True)  7.42 us
    ppermute x4, waiting for transfers between devices, even_pairs(): lax.ppermute(value, axes, [(i, i ^ 1) for i in range(lax.axis_size(axes))])  4.52 us
    ppermute x4, starting transfers between devices, even_pairs(): lax.ppermute(value, axes, [(i, i ^ 1) for i in range(lax.axis_size(axes))])  4.29 us
  transfers between devices with their start and end apart: 21, of which 7 were waited for; matrix products, arithmetic and copies ran while one was open for 1% of the time, Pallas kernels for 6%

profile of v9, /device:TPU:1, one launch (start us, length us, event | category | flops | bytes accessed | tf_op | source)
XLA Modules:
  0.0 197.5 jit_solution(6526802398689936303)
XLA Ops:
  1.3 0.0 copy-start
  1.3 0.8 copy-done
  2.1 0.7 copy-done.3
  2.8 0.8 copy-done.5
  3.6 0.7 copy-done.6
  4.2 1.5 prepare.1
  5.7 15.7 %all-to-all-start = ((f32[256,1,128]{2,1,0:T(1,128)}), f32[256,1,128]{2,1,0:T(1,128)S(1)}, u32[]{:S(2)}, u32[]{:S(2)}) async-start(f32[256,1,128]{2,1,0:T(1,128)} %get-tuple-element.49), calls=%async_computation | async-start | bytes 262144 | tf_op jit(solution)/shard_map/all_to_all | solution.py:41
  21.4 3.5 %collective-permute-start.1 = (f32[24,1024]{1,0:T(8,128)S(1)}, f32[24,1024]{1,0:T(8,128)S(1)}, u32[]{:S(2)}, u32[]{:S(2)}) collective-permute-start(f32[24,1024]{1,0:T(8,128)S(1)} %get-tuple-element.51.own.halo), channel_id=1, source_target_pairs={{8,16},{24,32},{40,48},{56,64},{72,80},{88,96},{104,112},{120,128}... | collective-permute-start | bytes 294920 | tf_op jit(solution)/shard_map/ppermute | solution.py:60
  24.9 0.1 collective-permute-start
  25.0 0.0 copy-start.4
  25.0 1.7 constant_dynamic-slice_fusion.columns
  26.8 7.4 %all-to-all-done = f32[256,1,128]{2,1,0:T(1,128)S(1)} async-done(((f32[256,1,128]{2,1,0:T(1,128)}), f32[256,1,128]{2,1,0:T(1,128)S(1)}, u32[]{:S(2)}, u32[]{:S(2)}) %all-to-all-start) | async-done | bytes 131104 | tf_op jit(solution)/shard_map/all_to_all | solution.py:41
  34.2 0.0 collective-permute-done.even
  34.2 0.7 collective-permute-start.3
  34.9 2.1 %collective-permute-start.2 = (f32[3,24,1024]{2,1,0:T(8,128)S(1)}, f32[3,24,1024]{2,1,0:T(8,128)S(1)}, u32[]{:S(2)}, u32[]{:S(2)}) collective-permute-start(f32[3,24,1024]{2,1,0:T(8,128)S(1)} %stack.2.near), channel_id=1, source_target_pairs={{0,1},{1,0},{2,3},{3,2},{4,5},{5,4},{6,7},{7,6},{8,9},{9,8},{10,11... | collective-permute-start | bytes 884744 | tf_op jit(solution)/shard_map/ppermute | solution.py:54
  37.1 0.6 factor.1
  37.7 4.5 %rows.1 = (bf16[8,1024,512]{2,1,0:T(8,128)(2,1)S(1)}, f32[32,16,128]{2,1,0:T(8,128)S(1)}) custom-call(f32[24,1024]{1,0:T(8,128)S(1)} %get-tuple-element.51.own.halo, f32[256,128]{1,0:T(8,128)S(1)} %bitcast.8), custom_call_target="tpu_custom_call" | custom-call | bytes 16777216 | tf_op jit(solution)/shard_map/rows/pallas_call | solution.py:106
  42.2 1.6 collective-permute-done.2.even
  43.8 16.9 %all_to_all.45.refs_0_ = f32[32,16,128]{2,1,0:T(8,128)S(1)} all-to-all(f32[32,16,128]{2,1,0:T(8,128)S(1)} %get-tuple-element.58), channel_id=1, replica_groups=mesh['z'=8,'yl'=2,'c'=2,'yh'=2,'x'=4] {'yh','x','yl','c'}, dimensions={0} | all-to-all | bytes 524288 | tf_op jit(solution)/shard_map/all_to_all | solution.py:41
  60.7 10.6 %all_to_all.46.parts = f32[8,16,128]{2,1,0:T(8,128)S(1)} all-to-all(f32[8,16,128]{2,1,0:T(8,128)S(1)} %sum_share.2), channel_id=1, replica_groups=mesh['z'=8,'yl'=2,'c'=2,'yh'=2,'x'=4] {'z'}, dimensions={0} | all-to-all | bytes 131072 | tf_op jit(solution)/shard_map/all_to_all | solution.py:41
  71.4 2.6 %collective-permute-start.6 = (f32[16,128]{1,0:T(8,128)S(1)}, f32[16,128]{1,0:T(8,128)S(1)}, u32[]{:S(2)}, u32[]{:S(2)}) collective-permute-start(f32[16,128]{1,0:T(8,128)S(1)} %sum_depth.2.refs_0_.old_share), channel_id=1, source_target_pairs={{0,24},{8,16},{16,8},{24,0},{1,25},{9,17},{17,9},{25,1},{2,26},{10... | collective-permute-start | bytes 24584 | tf_op jit(solution)/shard_map/ppermute | solution.py:50
  73.9 1.3 collective-permute-start.5
  75.2 0.0 collective-permute-start.4
  75.2 2.2 %tiles.2 = (bf16[4,128,1024]{2,1,0:T(8,128)(2,1)S(1)}, f32[16,512]{1,0:T(8,128)S(1)}) custom-call(s32[8,8]{1,0:T(8,128)S(1)} %bitcast.11, f32[3,24,1024]{2,1,0:T(8,128)S(1)} %stack.2.near, f32[3,24,1024]{2,1,0:T(8,128)S(1)} %collective-permute-done.2.even, f32[3,24,1024]{2,1,0:T(8,128)S(1)} %collective-permute-done.3.odd), custom_call_target="tpu_custom_call" | custom-call | bytes 8388608 | tf_op jit(solution)/shard_map/tiles/pallas_call | solution.py:106
  77.4 0.0 collective-permute-done.5.refs_2_
  77.4 0.0 collective-permute-done.4.refs_1_
  77.5 0.6 coeffs.2
  78.1 13.2 %all_to_all.47.parts = f32[8,16,1024]{2,1,0:T(8,128)S(1)} all-to-all(f32[8,16,1024]{2,1,0:T(8,128)S(1)} %coeffs.2), channel_id=1, replica_groups=mesh['z'=8,'yl'=2,'c'=2,'yh'=2,'x'=4] {'yh','x'}, dimensions={0} | all-to-all | bytes 1048576 | tf_op jit(solution)/shard_map/all_to_all | solution.py:41
  91.3 1.0 weights.2
  92.3 1.9 collective-permute-start.7
  94.2 0.3 collective-permute-start.8
  94.5 1.4 collective-permute-start.9
  95.9 2.2 %tiles.3 = (bf16[4,128,1024]{2,1,0:T(8,128)(2,1)S(1)}, f32[16,512]{1,0:T(8,128)S(1)}) custom-call(s32[8,8]{1,0:T(8,128)S(1)} %bitcast.12, f32[3,24,1024]{2,1,0:T(8,128)S(1)} %stack.2.near, f32[3,24,1024]{2,1,0:T(8,128)S(1)} %collective-permute-done.2.even, f32[3,24,1024]{2,1,0:T(8,128)S(1)} %collective-permute-done.3.odd), custom_call_target="tpu_custom_call" | custom-call | bytes 8388608 | tf_op jit(solution)/shard_map/tiles/pallas_call | solution.py:106
  98.1 0.0 collective-permute-done.7.first
  98.1 0.0 collective-permute-done.8.second
  98.2 0.0 collective-permute-done.9.third
  98.2 10.7 %all_to_all.48.weights = bf16[32,16,128]{2,1,0:T(8,128)(2,1)S(1)} all-to-all(bf16[32,16,128]{2,1,0:T(8,128)(2,1)S(1)} %get-tuple-element.71), channel_id=1, replica_groups=mesh['z'=8,'yl'=2,'c'=2,'yh'=2,'x'=4] {'yh','x','yl','c'}, dimensions={0} | all-to-all | bytes 262144 | tf_op jit(solution)/shard_map/all_to_all | solution.py:41
  108.9 2.3 %image.1 = (f32[16,1024]{1,0:T(8,128)S(1)}, f32[16,1024]{1,0:T(8,128)S(1)}, bf16[16,1024]{1,0:T(8,128)(2,1)S(1)}, bf16[48,1024]{1,0:T(8,128)(2,1)S(1)}) custom-call(bf16[32,16,128]{2,1,0:T(8,128)(2,1)S(1)} %all_to_all.48.weights, bf16[8,1024,512]{2,1,0:T(8,128)(2,1)S(1)} %get-tuple-element.72.rows, s32[1,1]{1,0:T(1,128)S(6)} %copy.10.counts, ...), custom_call_target="tpu_custom_call" | custom-call | bytes 16777216 | tf_op jit(solution)/shard_map/image/pallas_call | solution.py:106
  111.2 2.8 %collective-permute-start.11 = (bf16[16,1024]{1,0:T(8,128)(2,1)S(1)}, bf16[16,1024]{1,0:T(8,128)(2,1)S(1)}, u32[]{:S(2)}, u32[]{:S(2)}) collective-permute-start(bf16[16,1024]{1,0:T(8,128)(2,1)S(1)} %get-tuple-element.75.own), channel_id=1, source_target_pairs={{8,16},{24,32},{40,48},{56,64},{72,80},{88,96},{104,112},{120,128}... | collective-permute-start | bytes 98312 | tf_op jit(solution)/shard_map/ppermute | solution.py:60
  114.0 0.1 collective-permute-start.10
  114.1 1.4 project.1
  115.5 0.9 collective-permute-done.11.odd
  116.4 0.0 collective-permute-done.10.even
  116.5 0.7 collective-permute-start.13
  117.1 2.0 collective-permute-start.12
  119.1 2.9 %collective-permute-done.12.even = bf16[3,16,1024]{2,1,0:T(8,128)(2,1)S(1)} collective-permute-done((bf16[3,16,1024]{2,1,0:T(8,128)(2,1)S(1)}, bf16[3,16,1024]{2,1,0:T(8,128)(2,1)S(1)}, u32[]{:S(2)}, u32[]{:S(2)}) %collective-permute-start.12) | collective-permute-done | bytes 98336 | tf_op jit(solution)/shard_map/ppermute | solution.py:54
  122.0 19.8 %all_to_all.49.refs_0_ = f32[32,32,128]{2,1,0:T(8,128)S(1)} all-to-all(f32[32,32,128]{2,1,0:T(8,128)S(1)} %project.1), channel_id=1, replica_groups=mesh['z'=8,'yl'=2,'c'=2,'yh'=2,'x'=4] {'yh','x','yl','c'}, dimensions={0} | all-to-all | bytes 1048576 | tf_op jit(solution)/shard_map/all_to_all | solution.py:41
  141.8 1.4 sparse.1
  143.2 11.3 %all_to_all.50.parts = f32[8,48,128]{2,1,0:T(8,128)S(1)} all-to-all(f32[8,48,128]{2,1,0:T(8,128)S(1)} %sum_share.3), channel_id=1, replica_groups=mesh['z'=8,'yl'=2,'c'=2,'yh'=2,'x'=4] {'z'}, dimensions={0} | all-to-all | bytes 393216 | tf_op jit(solution)/shard_map/all_to_all | solution.py:41
  154.6 2.3 %collective-permute-start.16 = (f32[16,128]{1,0:T(8,128)S(1)}, f32[16,128]{1,0:T(8,128)S(1)}, u32[]{:S(2)}, u32[]{:S(2)}) collective-permute-start(f32[16,128]{1,0:T(8,128)S(1)} %get-tuple-element.81.refs_0_.new_share), channel_id=1, source_target_pairs={{0,24},{8,16},{16,8},{24,0},{1,25},{9,17},{17,9},{25,1},{2,26},{10... | collective-permute-start | bytes 24584 | tf_op jit(solution)/shard_map/ppermute | solution.py:50
  156.9 1.9 collective-permute-start.15
  158.7 1.3 collective-permute-done.15.refs_2_
  160.1 0.6 coeffs.3
  160.7 14.2 %all_to_all.51.parts = f32[8,16,1152]{2,1,0:T(8,128)S(1)} all-to-all(f32[8,16,1152]{2,1,0:T(8,128)S(1)} %coeffs.3), channel_id=1, replica_groups=mesh['z'=8,'yl'=2,'c'=2,'yh'=2,'x'=4] {'yh','x'}, dimensions={0} | all-to-all | bytes 1179648 | tf_op jit(solution)/shard_map/all_to_all | solution.py:41
  174.9 1.0 weights.3
  175.8 2.5 %collective-permute-start.17 = (f32[16,256]{1,0:T(8,128)S(1)}, f32[16,256]{1,0:T(8,128)S(1)}, u32[]{:S(2)}, u32[]{:S(2)}) collective-permute-start(f32[16,256]{1,0:T(8,128)S(1)} %get-tuple-element.84), channel_id=1, source_target_pairs={{0,8},{8,0},{16,24},{24,16},{1,9},{9,1},{17,25},{25,17},{2,10},{10... | collective-permute-start | bytes 49160 | tf_op jit(solution)/shard_map/ppermute | solution.py:50
  178.3 0.2 collective-permute-start.18
  178.6 1.5 collective-permute-start.19
  180.0 0.0 collective-permute-done.17.first
  180.0 0.9 collective-permute-done.18.second
  180.9 0.9 collective-permute-done.19.third
  181.9 0.2 gather_last.1
  182.1 12.5 %all_to_all.52.weights = bf16[32,32,128]{2,1,0:T(8,128)(2,1)S(1)} all-to-all(bf16[32,32,128]{2,1,0:T(8,128)(2,1)S(1)} %get-tuple-element.89), channel_id=1, replica_groups=mesh['z'=8,'yl'=2,'c'=2,'yh'=2,'x'=4] {'yh','x','yl','c'}, dimensions={0} | all-to-all | bytes 524288 | tf_op jit(solution)/shard_map/all_to_all | solution.py:41
  194.6 2.9 %finish.1 = (f32[16,1024]{1,0:T(8,128)}, f32[16,1024]{1,0:T(8,128)}) custom-call(bf16[32,32,128]{2,1,0:T(8,128)(2,1)S(1)} %all_to_all.52.weights, bf16[8,1024,512]{2,1,0:T(8,128)(2,1)S(1)} %get-tuple-element.72.rows, s32[1,1]{1,0:T(1,128)S(6)} %copy.10.counts, f32[24,1024]{1,0:T(8,128)S(1)} %get-tuple-element.51.own.halo, f32[16,1024]{1,0:T(8,128)S(1)} %bitcast.10, ...), custom_call_target="tpu_custom_call" | custom-call | bytes 16777216 | tf_op jit(solution)/shard_map/finish/pallas_call | solution.py:106
  (22 shorter events, 0.2 us)
Async XLA Ops:
  0.6 74.5 %copy-start.2 = (s32[1,1,8,8]{3,2,1,0:T(8,128)S(1)}, s32[1,1,8,8]{3,2,1,0:T(8,128)}, u32[]{:S(2)}) copy-start(s32[1,1,8,8]{3,2,1,0:T(8,128)} %param.11) | copy-start | bytes 772
  1.3 0.8 copy-start
  2.1 0.7 copy-start.3
  2.8 0.8 copy-start.5
  3.6 0.7 copy-start.6
  5.7 28.5 %all-to-all-start = ((f32[256,1,128]{2,1,0:T(1,128)}), f32[256,1,128]{2,1,0:T(1,128)S(1)}, u32[]{:S(2)}, u32[]{:S(2)}) async-start(f32[256,1,128]{2,1,0:T(1,128)} %get-tuple-element.49), calls=%async_computation | async-start | bytes 262144 | tf_op jit(solution)/shard_map/all_to_all | solution.py:41
  21.4 12.8 %collective-permute-start.1 = (f32[24,1024]{1,0:T(8,128)S(1)}, f32[24,1024]{1,0:T(8,128)S(1)}, u32[]{:S(2)}, u32[]{:S(2)}) collective-permute-start(f32[24,1024]{1,0:T(8,128)S(1)} %get-tuple-element.51.own.halo), channel_id=1, source_target_pairs={{8,16},{24,32},{40,48},{56,64},{72,80},{88,96},{104,112},{120,128}... | collective-permute-start | bytes 294920 | tf_op jit(solution)/shard_map/ppermute | solution.py:60
  24.9 9.3 %collective-permute-start = (f32[24,1024]{1,0:T(8,128)S(1)}, f32[24,1024]{1,0:T(8,128)S(1)}, u32[]{:S(2)}, u32[]{:S(2)}) collective-permute-start(f32[24,1024]{1,0:T(8,128)S(1)} %get-tuple-element.51.own.halo), channel_id=1, source_target_pairs={{0,8},{8,0},{16,24},{24,16},{32,40},{40,32},{48,56},{56,48},{64,72... | collective-permute-start | bytes 294920 | tf_op jit(solution)/shard_map/ppermute | solution.py:54
  25.0 83.9 %copy-start.4 = (f32[1,1,1024]{2,1,0:T(1,128)S(1)}, f32[1,1,1024]{2,1,0:T(1,128)}, u32[]{:S(2)}) copy-start(f32[1,1,1024]{2,1,0:T(1,128)} %param.9) | copy-start | bytes 12292
  34.2 8.0 %collective-permute-start.3 = (f32[3,24,1024]{2,1,0:T(8,128)S(1)}, f32[3,24,1024]{2,1,0:T(8,128)S(1)}, u32[]{:S(2)}, u32[]{:S(2)}) collective-permute-start(f32[3,24,1024]{2,1,0:T(8,128)S(1)} %stack.2.near), channel_id=1, source_target_pairs={{1,2},{3,4},{5,6},{2,1},{4,3},{6,5},{9,10},{11,12},{13,14},{10,9},... | collective-permute-start | bytes 884744 | tf_op jit(solution)/shard_map/ppermute | solution.py:60
  34.9 8.9 %collective-permute-start.2 = (f32[3,24,1024]{2,1,0:T(8,128)S(1)}, f32[3,24,1024]{2,1,0:T(8,128)S(1)}, u32[]{:S(2)}, u32[]{:S(2)}) collective-permute-start(f32[3,24,1024]{2,1,0:T(8,128)S(1)} %stack.2.near), channel_id=1, source_target_pairs={{0,1},{1,0},{2,3},{3,2},{4,5},{5,4},{6,7},{7,6},{8,9},{9,8},{10,11... | collective-permute-start | bytes 884744 | tf_op jit(solution)/shard_map/ppermute | solution.py:54
  71.4 6.0 %collective-permute-start.6 = (f32[16,128]{1,0:T(8,128)S(1)}, f32[16,128]{1,0:T(8,128)S(1)}, u32[]{:S(2)}, u32[]{:S(2)}) collective-permute-start(f32[16,128]{1,0:T(8,128)S(1)} %sum_depth.2.refs_0_.old_share), channel_id=1, source_target_pairs={{0,24},{8,16},{16,8},{24,0},{1,25},{9,17},{17,9},{25,1},{2,26},{10... | collective-permute-start | bytes 24584 | tf_op jit(solution)/shard_map/ppermute | solution.py:50
  73.9 3.5 %collective-permute-start.5 = (f32[16,128]{1,0:T(8,128)S(1)}, f32[16,128]{1,0:T(8,128)S(1)}, u32[]{:S(2)}, u32[]{:S(2)}) collective-permute-start(f32[16,128]{1,0:T(8,128)S(1)} %sum_depth.2.refs_0_.old_share), channel_id=1, source_target_pairs={{0,16},{8,24},{16,0},{24,8},{1,17},{9,25},{17,1},{25,9},{2,18},{10... | collective-permute-start | bytes 24584 | tf_op jit(solution)/shard_map/ppermute | solution.py:50
  75.2 2.3 %collective-permute-start.4 = (f32[16,128]{1,0:T(8,128)S(1)}, f32[16,128]{1,0:T(8,128)S(1)}, u32[]{:S(2)}, u32[]{:S(2)}) collective-permute-start(f32[16,128]{1,0:T(8,128)S(1)} %sum_depth.2.refs_0_.old_share), channel_id=1, source_target_pairs={{0,8},{8,0},{16,24},{24,16},{1,9},{9,1},{17,25},{25,17},{2,10},{10... | collective-permute-start | bytes 24584 | tf_op jit(solution)/shard_map/ppermute | solution.py:50
  92.3 5.8 %collective-permute-start.7 = (f32[16,128]{1,0:T(8,128)S(1)}, f32[16,128]{1,0:T(8,128)S(1)}, u32[]{:S(2)}, u32[]{:S(2)}) collective-permute-start(f32[16,128]{1,0:T(8,128)S(1)} %get-tuple-element.68), channel_id=1, source_target_pairs={{0,8},{8,0},{16,24},{24,16},{1,9},{9,1},{17,25},{25,17},{2,10},{10... | collective-permute-start | bytes 24584 | tf_op jit(solution)/shard_map/ppermute | solution.py:50
  94.2 3.9 %collective-permute-start.8 = (f32[16,128]{1,0:T(8,128)S(1)}, f32[16,128]{1,0:T(8,128)S(1)}, u32[]{:S(2)}, u32[]{:S(2)}) collective-permute-start(f32[16,128]{1,0:T(8,128)S(1)} %get-tuple-element.69), channel_id=1, source_target_pairs={{0,16},{8,24},{16,0},{24,8},{1,17},{9,25},{17,1},{25,9},{2,18},{10... | collective-permute-start | bytes 24584 | tf_op jit(solution)/shard_map/ppermute | solution.py:50
  94.5 3.7 %collective-permute-start.9 = (f32[16,128]{1,0:T(8,128)S(1)}, f32[16,128]{1,0:T(8,128)S(1)}, u32[]{:S(2)}, u32[]{:S(2)}) collective-permute-start(f32[16,128]{1,0:T(8,128)S(1)} %get-tuple-element.70), channel_id=1, source_target_pairs={{0,24},{8,16},{16,8},{24,0},{1,25},{9,17},{17,9},{25,1},{2,26},{10... | collective-permute-start | bytes 24584 | tf_op jit(solution)/shard_map/ppermute | solution.py:50
  111.2 5.2 %collective-permute-start.11 = (bf16[16,1024]{1,0:T(8,128)(2,1)S(1)}, bf16[16,1024]{1,0:T(8,128)(2,1)S(1)}, u32[]{:S(2)}, u32[]{:S(2)}) collective-permute-start(bf16[16,1024]{1,0:T(8,128)(2,1)S(1)} %get-tuple-element.75.own), channel_id=1, source_target_pairs={{8,16},{24,32},{40,48},{56,64},{72,80},{88,96},{104,112},{120,128}... | collective-permute-start | bytes 98312 | tf_op jit(solution)/shard_map/ppermute | solution.py:60
  114.0 2.4 %collective-permute-start.10 = (bf16[16,1024]{1,0:T(8,128)(2,1)S(1)}, bf16[16,1024]{1,0:T(8,128)(2,1)S(1)}, u32[]{:S(2)}, u32[]{:S(2)}) collective-permute-start(bf16[16,1024]{1,0:T(8,128)(2,1)S(1)} %get-tuple-element.75.own), channel_id=1, source_target_pairs={{0,8},{8,0},{16,24},{24,16},{32,40},{40,32},{48,56},{56,48},{64,72... | collective-permute-start | bytes 98312 | tf_op jit(solution)/shard_map/ppermute | solution.py:54
  115.5 79.1 %copy-start.1 = (f32[1,1,16,1024]{3,2,1,0:T(8,128)S(1)}, f32[1,1,16,1024]{3,2,1,0:T(8,128)}, u32[]{:S(2)}) copy-start(f32[1,1,16,1024]{3,2,1,0:T(8,128)} %param.8) | copy-start | bytes 196612
  116.5 2.6 %collective-permute-start.13 = (bf16[3,16,1024]{2,1,0:T(8,128)(2,1)S(1)}, bf16[3,16,1024]{2,1,0:T(8,128)(2,1)S(1)}, u32[]{:S(2)}, u32[]{:S(2)}) collective-permute-start(bf16[3,16,1024]{2,1,0:T(8,128)(2,1)S(1)} %stack.3.near), channel_id=1, source_target_pairs={{1,2},{3,4},{5,6},{2,1},{4,3},{6,5},{9,10},{11,12},{13,14},{10,9},... | collective-permute-start | bytes 294920 | tf_op jit(solution)/shard_map/ppermute | solution.py:60
  117.1 4.9 %collective-permute-start.12 = (bf16[3,16,1024]{2,1,0:T(8,128)(2,1)S(1)}, bf16[3,16,1024]{2,1,0:T(8,128)(2,1)S(1)}, u32[]{:S(2)}, u32[]{:S(2)}) collective-permute-start(bf16[3,16,1024]{2,1,0:T(8,128)(2,1)S(1)} %stack.3.near), channel_id=1, source_target_pairs={{0,1},{1,0},{2,3},{3,2},{4,5},{5,4},{6,7},{7,6},{8,9},{9,8},{10,11... | collective-permute-start | bytes 294920 | tf_op jit(solution)/shard_map/ppermute | solution.py:54
  154.6 4.1 %collective-permute-start.16 = (f32[16,128]{1,0:T(8,128)S(1)}, f32[16,128]{1,0:T(8,128)S(1)}, u32[]{:S(2)}, u32[]{:S(2)}) collective-permute-start(f32[16,128]{1,0:T(8,128)S(1)} %get-tuple-element.81.refs_0_.new_share), channel_id=1, source_target_pairs={{0,24},{8,16},{16,8},{24,0},{1,25},{9,17},{17,9},{25,1},{2,26},{10... | collective-permute-start | bytes 24584 | tf_op jit(solution)/shard_map/ppermute | solution.py:50
  156.9 3.2 %collective-permute-start.15 = (f32[16,128]{1,0:T(8,128)S(1)}, f32[16,128]{1,0:T(8,128)S(1)}, u32[]{:S(2)}, u32[]{:S(2)}) collective-permute-start(f32[16,128]{1,0:T(8,128)S(1)} %get-tuple-element.81.refs_0_.new_share), channel_id=1, source_target_pairs={{0,16},{8,24},{16,0},{24,8},{1,17},{9,25},{17,1},{25,9},{2,18},{10... | collective-permute-start | bytes 24584 | tf_op jit(solution)/shard_map/ppermute | solution.py:50
  158.7 1.3 collective-permute-start.14
  175.8 4.2 %collective-permute-start.17 = (f32[16,256]{1,0:T(8,128)S(1)}, f32[16,256]{1,0:T(8,128)S(1)}, u32[]{:S(2)}, u32[]{:S(2)}) collective-permute-start(f32[16,256]{1,0:T(8,128)S(1)} %get-tuple-element.84), channel_id=1, source_target_pairs={{0,8},{8,0},{16,24},{24,16},{1,9},{9,1},{17,25},{25,17},{2,10},{10... | collective-permute-start | bytes 49160 | tf_op jit(solution)/shard_map/ppermute | solution.py:50
  178.3 2.6 %collective-permute-start.18 = (f32[16,256]{1,0:T(8,128)S(1)}, f32[16,256]{1,0:T(8,128)S(1)}, u32[]{:S(2)}, u32[]{:S(2)}) collective-permute-start(f32[16,256]{1,0:T(8,128)S(1)} %get-tuple-element.85), channel_id=1, source_target_pairs={{0,16},{8,24},{16,0},{24,8},{1,17},{9,25},{17,1},{25,9},{2,18},{10... | collective-permute-start | bytes 49160 | tf_op jit(solution)/shard_map/ppermute | solution.py:50
  178.6 3.3 %collective-permute-start.19 = (f32[16,256]{1,0:T(8,128)S(1)}, f32[16,256]{1,0:T(8,128)S(1)}, u32[]{:S(2)}, u32[]{:S(2)}) collective-permute-start(f32[16,256]{1,0:T(8,128)S(1)} %get-tuple-element.86), channel_id=1, source_target_pairs={{0,24},{8,16},{16,8},{24,0},{1,25},{9,17},{17,9},{25,1},{2,26},{10... | collective-permute-start | bytes 49160 | tf_op jit(solution)/shard_map/ppermute | solution.py:50
